TPU v7x, 128 devices: a whole 4x4x4 slice. The times are simulated.
128 devices in a mesh: blk: 16 (over x_hi, z, core), head: 8 (over y, x_lo).
Axes of the slice: x: 4 (x_hi: 2, x_lo: 2; x = x_hi * 2 + x_lo), y: 4, z: 4, core: 2. Of those that a mesh axis runs over, the one named last changes fastest.
Arguments:
- queries: bfloat16 [1024, 8192], P('blk', 'head'), may hold values from -20 to 20
- question_keys: bfloat16 [1024, 1024], P('blk', 'head'), may hold values from -40 to 40
- question_values: bfloat16 [1024, 1024], P('blk', 'head'), may hold values from -6 to 6
- question_ids: int32 [1024], P('blk'), may hold values from 0 to 1023, as said below
- live_rows: int32 [16], P('blk'), may hold values from 16 to 64, as said below
- prefix_keys: bfloat16 [32768, 1024], P('blk', 'head'), may hold values from -40 to 40
- prefix_values: bfloat16 [32768, 1024], P('blk', 'head'), may hold values from -6 to 6
- out_weight: bfloat16 [8192, 8192], P('head', 'blk'), may hold values from -0.0625 to 0.0625
Outputs:
- projected: bfloat16 [1024, 8192], P('head', 'blk')
Inputs may be any that keep to these rules, and one draw needn't show every extreme that they name: `question_ids`: each question lies inside the 64 row slots of one owner; a row's id is the index of its question's first row slot, so ids never fall along the rows; the last row slot of all is a question of one row. `live_rows`: counts of live question rows per owner; one owner has all 64 slots live and another only 16.
All inputs are finite; a program needn't handle non-finite values.
Results may differ from a plain program's by a relative error of at most 0.0048.
Values may be sent and summed in bfloat16 or wider, within the bound.
No kernel may reach another device: no remote copies, remote signals or barrier semaphores. Data moves between devices by JAX's collectives and lax.ppermute only.
A program may use at most 64 MiB of HBM per device.

v0:
```python
import jax
import jax.numpy as jnp
from jax import lax
from jax.sharding import PartitionSpec as P

DH = 128


floor_score = -1e30


def shifted(array, axis, by):
    peers = lax.axis_size(axis)
    return lax.ppermute(array, axis, [(i, (i + by) % peers) for i in range(peers)])


def block_partial(query_rows, key_rows, value_rows, allowed):
    positions = key_rows.shape[0]
    kv_heads = query_rows.shape[1]
    scaling = query_rows.shape[3] ** (-0.5)
    key_heads = key_rows.reshape(positions, kv_heads, -1)
    value_heads = value_rows.reshape(positions, kv_heads, -1)
    scores = (
        jnp.einsum("qkgd,pkd->kgqp", query_rows, key_heads, preferred_element_type=jnp.float32)
        * scaling
    )
    if allowed is not None:
        scores = jnp.where(allowed, scores, floor_score)
    highest = jnp.max(scores, axis=-1)
    weights = jnp.exp(scores - highest[..., None]).astype(jnp.bfloat16)
    totals = jnp.sum(weights, axis=-1, dtype=jnp.float32)
    summed = jnp.einsum("kgqp,pkd->kgqd", weights, value_heads, preferred_element_type=jnp.float32)
    return (highest, totals, summed)


def merge_parts(former, latter):
    highest = jnp.maximum(former[0], latter[0])
    first_scale = jnp.exp(former[0] - highest)
    second_scale = jnp.exp(latter[0] - highest)
    totals = first_scale * former[1] + second_scale * latter[1]
    summed = first_scale[..., None] * former[2] + second_scale[..., None] * latter[2]
    return (highest, totals, summed)


def shards(
    queries,
    question_keys,
    question_values,
    question_ids,
    live_rows,
    prefix_keys,
    prefix_values,
    out_weight,
):
    row_count = queries.shape[0]
    kv_local = prefix_keys.shape[1] // DH
    group_size = queries.shape[1] // (kv_local * DH)
    query_rows = queries.reshape(row_count, kv_local, group_size, DH)
    row_index = jnp.arange(row_count, dtype=jnp.int32)
    allowed = (question_ids[:, None] == question_ids[None, :]) & (
        row_index[None, :] <= row_index[:, None]
    )
    own_part = block_partial(query_rows, question_keys, question_values, allowed)
    blocks = lax.axis_size("blk")
    combined = merge_parts(own_part, block_partial(query_rows, prefix_keys, prefix_values, None))

    def advance(turn_index, running):
        key_rows, value_rows, partial_state = running
        key_rows, value_rows = shifted((key_rows, value_rows), "blk", 1)
        return (
            key_rows,
            value_rows,
            merge_parts(partial_state, block_partial(query_rows, key_rows, value_rows, None)),
        )

    _, _, combined = lax.fori_loop(1, blocks, advance, (prefix_keys, prefix_values, combined))
    attention = combined[2] / combined[1][..., None]
    attention = jnp.transpose(attention, (2, 0, 1, 3)).reshape(row_count, -1)
    live_mask = row_index < live_rows[0]
    attention = jnp.where(live_mask[:, None], attention, 0.0).astype(jnp.bfloat16)
    terms = jnp.dot(
        lax.all_gather(attention, "blk", axis=0, tiled=True),
        out_weight,
        preferred_element_type=jnp.float32,
    )
    return lax.psum_scatter(terms, "head", scatter_dimension=0, tiled=True).astype(jnp.bfloat16)


def solution(mesh):
    return jax.shard_map(
        shards,
        mesh=mesh,
        in_specs=(
            P("blk", "head"),
            P("blk", "head"),
            P("blk", "head"),
            P("blk"),
            P("blk"),
            P("blk", "head"),
            P("blk", "head"),
            P("head", "blk"),
        ),
        out_specs=P("head", "blk"),
        check_vma=False,
    )
```

profile of v0, /device:TPU:1, one launch (start us, length us, event | category | flops | bytes accessed | tf_op | source)
XLA Modules:
  0.0 412.9 jit_solution(2853586223683762569)
XLA Ops:
  6.5 1.1 copy.56
  7.7 1.1 copy.57
  9.6 1.7 bitcast_reduce_fusion.1
  11.6 1.6 copy-done.1
  13.2 0.8 convert_reduce_fusion.1
  14.4 3.0 fusion.33
  17.5 269.8 %while.18 = (s32[]{:T(128)}, bf16[2048,128]{1,0:T(8,128)(2,1)S(1)}, bf16[2048,128]{1,0:T(8,128)(2,1)S(1)}, f32[1,8,64]{2,1,0:T(8,128)S(1)}, f32[1,8,64]{2,1,0:T(...) while((s32[]{:T(128)}, bf16[2048,128]{1,0:T(8,128)(2,1)S(1)}, ...), condition=%wide.region_7.8_spmd, body=%wide.region_4.7_spmd.sunk | while | flops 547555840 | bytes 20617380 | solution.py:76
  17.5 3.1 collective-permute-start
  20.6 6.0 %collective-permute-done = bf16[2048,128]{1,0:T(8,128)(2,1)S(1)} collective-permute-done((bf16[2048,128]{1,0:T(8,128)(2,1)S(1)}, bf16[2048,128]{1,0:T(8,128)(2,1)S(1)}, u32[]{:S(2)}, u32[]{:S(2)}) %collective-permute-start) | collective-permute-done | bytes 524320 | tf_op jit(solution)/shard_map/while/body/eval_jaxpr/ppermute | solution.py:14
  27.5 0.8 convert_reduce_fusion.4
  28.4 3.9 collective-permute-done.1
  32.3 0.9 fusion.72
  33.2 2.5 collective-permute-start
  35.9 6.0 %collective-permute-done = bf16[2048,128]{1,0:T(8,128)(2,1)S(1)} collective-permute-done((bf16[2048,128]{1,0:T(8,128)(2,1)S(1)}, bf16[2048,128]{1,0:T(8,128)(2,1)S(1)}, u32[]{:S(2)}, u32[]{:S(2)}) %collective-permute-start) | collective-permute-done | bytes 524320 | tf_op jit(solution)/shard_map/while/body/eval_jaxpr/ppermute | solution.py:14
  42.7 0.8 convert_reduce_fusion.4
  43.6 3.9 collective-permute-done.1
  47.6 0.9 fusion.72
  48.4 2.5 collective-permute-start
  51.1 7.6 %collective-permute-done = bf16[2048,128]{1,0:T(8,128)(2,1)S(1)} collective-permute-done((bf16[2048,128]{1,0:T(8,128)(2,1)S(1)}, bf16[2048,128]{1,0:T(8,128)(2,1)S(1)}, u32[]{:S(2)}, u32[]{:S(2)}) %collective-permute-start) | collective-permute-done | bytes 524320 | tf_op jit(solution)/shard_map/while/body/eval_jaxpr/ppermute | solution.py:14
  59.5 0.8 convert_reduce_fusion.4
  60.4 2.3 collective-permute-done.1
  62.8 0.9 fusion.72
  63.7 2.5 collective-permute-start
  66.3 11.2 %collective-permute-done = bf16[2048,128]{1,0:T(8,128)(2,1)S(1)} collective-permute-done((bf16[2048,128]{1,0:T(8,128)(2,1)S(1)}, bf16[2048,128]{1,0:T(8,128)(2,1)S(1)}, u32[]{:S(2)}, u32[]{:S(2)}) %collective-permute-start) | collective-permute-done | bytes 524320 | tf_op jit(solution)/shard_map/while/body/eval_jaxpr/ppermute | solution.py:14
  78.3 0.8 convert_reduce_fusion.4
  79.3 0.9 fusion.72
  80.2 1.3 collective-permute-start
  81.5 14.8 %collective-permute-done = bf16[2048,128]{1,0:T(8,128)(2,1)S(1)} collective-permute-done((bf16[2048,128]{1,0:T(8,128)(2,1)S(1)}, bf16[2048,128]{1,0:T(8,128)(2,1)S(1)}, u32[]{:S(2)}, u32[]{:S(2)}) %collective-permute-start) | collective-permute-done | bytes 524320 | tf_op jit(solution)/shard_map/while/body/eval_jaxpr/ppermute | solution.py:14
  97.1 0.8 convert_reduce_fusion.4
  98.1 0.9 fusion.72
  99.2 16.0 %collective-permute-done = bf16[2048,128]{1,0:T(8,128)(2,1)S(1)} collective-permute-done((bf16[2048,128]{1,0:T(8,128)(2,1)S(1)}, bf16[2048,128]{1,0:T(8,128)(2,1)S(1)}, u32[]{:S(2)}, u32[]{:S(2)}) %collective-permute-start) | collective-permute-done | bytes 524320 | tf_op jit(solution)/shard_map/while/body/eval_jaxpr/ppermute | solution.py:14
  116.0 0.8 convert_reduce_fusion.4
  116.9 0.9 fusion.72
  118.0 16.0 %collective-permute-done = bf16[2048,128]{1,0:T(8,128)(2,1)S(1)} collective-permute-done((bf16[2048,128]{1,0:T(8,128)(2,1)S(1)}, bf16[2048,128]{1,0:T(8,128)(2,1)S(1)}, u32[]{:S(2)}, u32[]{:S(2)}) %collective-permute-start) | collective-permute-done | bytes 524320 | tf_op jit(solution)/shard_map/while/body/eval_jaxpr/ppermute | solution.py:14
  134.8 0.8 convert_reduce_fusion.4
  135.8 0.9 fusion.72
  136.8 16.0 %collective-permute-done = bf16[2048,128]{1,0:T(8,128)(2,1)S(1)} collective-permute-done((bf16[2048,128]{1,0:T(8,128)(2,1)S(1)}, bf16[2048,128]{1,0:T(8,128)(2,1)S(1)}, u32[]{:S(2)}, u32[]{:S(2)}) %collective-permute-start) | collective-permute-done | bytes 524320 | tf_op jit(solution)/shard_map/while/body/eval_jaxpr/ppermute | solution.py:14
  153.6 0.8 convert_reduce_fusion.4
  154.6 0.9 fusion.72
  155.6 16.0 %collective-permute-done = bf16[2048,128]{1,0:T(8,128)(2,1)S(1)} collective-permute-done((bf16[2048,128]{1,0:T(8,128)(2,1)S(1)}, bf16[2048,128]{1,0:T(8,128)(2,1)S(1)}, u32[]{:S(2)}, u32[]{:S(2)}) %collective-permute-start) | collective-permute-done | bytes 524320 | tf_op jit(solution)/shard_map/while/body/eval_jaxpr/ppermute | solution.py:14
  172.5 0.8 convert_reduce_fusion.4
  173.4 0.9 fusion.72
  174.5 16.0 %collective-permute-done = bf16[2048,128]{1,0:T(8,128)(2,1)S(1)} collective-permute-done((bf16[2048,128]{1,0:T(8,128)(2,1)S(1)}, bf16[2048,128]{1,0:T(8,128)(2,1)S(1)}, u32[]{:S(2)}, u32[]{:S(2)}) %collective-permute-start) | collective-permute-done | bytes 524320 | tf_op jit(solution)/shard_map/while/body/eval_jaxpr/ppermute | solution.py:14
  191.3 0.8 convert_reduce_fusion.4
  192.3 0.9 fusion.72
  193.3 16.0 %collective-permute-done = bf16[2048,128]{1,0:T(8,128)(2,1)S(1)} collective-permute-done((bf16[2048,128]{1,0:T(8,128)(2,1)S(1)}, bf16[2048,128]{1,0:T(8,128)(2,1)S(1)}, u32[]{:S(2)}, u32[]{:S(2)}) %collective-permute-start) | collective-permute-done | bytes 524320 | tf_op jit(solution)/shard_map/while/body/eval_jaxpr/ppermute | solution.py:14
  210.1 0.8 convert_reduce_fusion.4
  211.1 0.9 fusion.72
  212.1 16.0 %collective-permute-done = bf16[2048,128]{1,0:T(8,128)(2,1)S(1)} collective-permute-done((bf16[2048,128]{1,0:T(8,128)(2,1)S(1)}, bf16[2048,128]{1,0:T(8,128)(2,1)S(1)}, u32[]{:S(2)}, u32[]{:S(2)}) %collective-permute-start) | collective-permute-done | bytes 524320 | tf_op jit(solution)/shard_map/while/body/eval_jaxpr/ppermute | solution.py:14
  229.0 0.8 convert_reduce_fusion.4
  229.9 0.9 fusion.72
  231.0 16.0 %collective-permute-done = bf16[2048,128]{1,0:T(8,128)(2,1)S(1)} collective-permute-done((bf16[2048,128]{1,0:T(8,128)(2,1)S(1)}, bf16[2048,128]{1,0:T(8,128)(2,1)S(1)}, u32[]{:S(2)}, u32[]{:S(2)}) %collective-permute-start) | collective-permute-done | bytes 524320 | tf_op jit(solution)/shard_map/while/body/eval_jaxpr/ppermute | solution.py:14
  247.8 0.8 convert_reduce_fusion.4
  248.7 0.9 fusion.72
  249.8 16.0 %collective-permute-done = bf16[2048,128]{1,0:T(8,128)(2,1)S(1)} collective-permute-done((bf16[2048,128]{1,0:T(8,128)(2,1)S(1)}, bf16[2048,128]{1,0:T(8,128)(2,1)S(1)}, u32[]{:S(2)}, u32[]{:S(2)}) %collective-permute-start) | collective-permute-done | bytes 524320 | tf_op jit(solution)/shard_map/while/body/eval_jaxpr/ppermute | solution.py:14
  266.6 0.8 convert_reduce_fusion.4
  267.6 0.9 fusion.72
  268.6 16.0 %collective-permute-done = bf16[2048,128]{1,0:T(8,128)(2,1)S(1)} collective-permute-done((bf16[2048,128]{1,0:T(8,128)(2,1)S(1)}, bf16[2048,128]{1,0:T(8,128)(2,1)S(1)}, u32[]{:S(2)}, u32[]{:S(2)}) %collective-permute-start) | collective-permute-done | bytes 524320 | tf_op jit(solution)/shard_map/while/body/eval_jaxpr/ppermute | solution.py:14
  285.4 0.8 convert_reduce_fusion.4
  286.4 0.9 fusion.72
  289.0 60.5 %all-gather.2.cloned.1.call-done = bf16[1024,1024]{1,0:T(8,128)(2,1)} async-done(((bf16[64,1024]{1,0:T(8,128)(2,1)}), bf16[1024,1024]{1,0:T(8,128)(2,1)}) %all-gather.2.cloned.1.call-update) | async-done | bytes 2097168 | tf_op jit(solution)/shard_map/all_gather | solution.py:82
  349.5 4.2 %fusion.58 = f32[1024,512]{1,0:T(8,128)} fusion(bf16[1024,1024]{1,0:T(8,128)(2,1)} %all-gather.2.cloned.1.call-done, bf16[1024,512]{1,0:T(8,128)(2,1)S(1)} %copy-done), kind=kOutput, calls=%fused_computation.69 | convolution fusion | flops 1073741824 | bytes 5242880 | tf_op jit(solution)/shard_map/dot_general | solution.py:81
  353.7 50.8 %reduce-scatter.2.cloned.1.call-done = f32[128,512]{1,0:T(8,128)} async-done(((f32[1024,512]{1,0:T(8,128)}), f32[128,512]{1,0:T(8,128)}) %reduce-scatter.2.cloned.1.call-update) | async-done | bytes 262160 | tf_op jit(solution)/shard_map/reduce_scatter | solution.py:86
  404.5 1.6 convert_element_type.29
  (152 shorter events, 17.7 us)
Async XLA Ops:
  6.5 343.0 %copy-start = (bf16[1024,512]{1,0:T(8,128)(2,1)S(1)}, bf16[1024,512]{1,0:T(8,128)(2,1)}, u32[]{:S(2)}) copy-start(bf16[1024,512]{1,0:T(8,128)(2,1)} %param.17) | copy-start | bytes 3145732
  6.5 342.9 %all-gather.2.cloned.1.call-start = ((), (), s32[]{:S(2)}) async-start(), calls=%async_computation.1 | async-start | bytes 2228224 | tf_op jit(solution)/shard_map/all_gather | solution.py:82
  7.7 3.6 copy-start.2
  7.7 3.6 copy-start.3
  11.3 1.9 copy-start.1
  11.3 2.9 copy-start.4
  17.5 9.2 %collective-permute-start = (bf16[2048,128]{1,0:T(8,128)(2,1)S(1)}, bf16[2048,128]{1,0:T(8,128)(2,1)S(1)}, u32[]{:S(2)}, u32[]{:S(2)}) collective-permute-start(bf16[2048,128]{1,0:T(8,128)(2,1)S(1)} %get-tuple-element.144), channel_id=1, source_target_pairs={{0,8},{8,16},{16,24},{24,32},{32,40},{40,48},{48,56},{56,64},{64,7... | collective-permute-start | bytes 1572872 | tf_op jit(solution)/shard_map/while/body/eval_jaxpr/ppermute | solution.py:14
  20.6 11.7 %collective-permute-start.1 = (bf16[2048,128]{1,0:T(8,128)(2,1)S(1)}, bf16[2048,128]{1,0:T(8,128)(2,1)S(1)}, u32[]{:S(2)}, u32[]{:S(2)}) collective-permute-start(bf16[2048,128]{1,0:T(8,128)(2,1)S(1)} %get-tuple-element.145), channel_id=1, source_target_pairs={{0,8},{8,16},{16,24},{24,32},{32,40},{40,48},{48,56},{56,64},{64,7... | collective-permute-start | bytes 1572872 | tf_op jit(solution)/shard_map/while/body/eval_jaxpr/ppermute | solution.py:14
  33.2 8.7 %collective-permute-start = (bf16[2048,128]{1,0:T(8,128)(2,1)S(1)}, bf16[2048,128]{1,0:T(8,128)(2,1)S(1)}, u32[]{:S(2)}, u32[]{:S(2)}) collective-permute-start(bf16[2048,128]{1,0:T(8,128)(2,1)S(1)} %get-tuple-element.144), channel_id=1, source_target_pairs={{0,8},{8,16},{16,24},{24,32},{32,40},{40,48},{48,56},{56,64},{64,7... | collective-permute-start | bytes 1572872 | tf_op jit(solution)/shard_map/while/body/eval_jaxpr/ppermute | solution.py:14
  35.8 11.7 %collective-permute-start.1 = (bf16[2048,128]{1,0:T(8,128)(2,1)S(1)}, bf16[2048,128]{1,0:T(8,128)(2,1)S(1)}, u32[]{:S(2)}, u32[]{:S(2)}) collective-permute-start(bf16[2048,128]{1,0:T(8,128)(2,1)S(1)} %get-tuple-element.145), channel_id=1, source_target_pairs={{0,8},{8,16},{16,24},{24,32},{32,40},{40,48},{48,56},{56,64},{64,7... | collective-permute-start | bytes 1572872 | tf_op jit(solution)/shard_map/while/body/eval_jaxpr/ppermute | solution.py:14
  48.4 10.2 %collective-permute-start = (bf16[2048,128]{1,0:T(8,128)(2,1)S(1)}, bf16[2048,128]{1,0:T(8,128)(2,1)S(1)}, u32[]{:S(2)}, u32[]{:S(2)}) collective-permute-start(bf16[2048,128]{1,0:T(8,128)(2,1)S(1)} %get-tuple-element.144), channel_id=1, source_target_pairs={{0,8},{8,16},{16,24},{24,32},{32,40},{40,48},{48,56},{56,64},{64,7... | collective-permute-start | bytes 1572872 | tf_op jit(solution)/shard_map/while/body/eval_jaxpr/ppermute | solution.py:14
  51.0 11.7 %collective-permute-start.1 = (bf16[2048,128]{1,0:T(8,128)(2,1)S(1)}, bf16[2048,128]{1,0:T(8,128)(2,1)S(1)}, u32[]{:S(2)}, u32[]{:S(2)}) collective-permute-start(bf16[2048,128]{1,0:T(8,128)(2,1)S(1)} %get-tuple-element.145), channel_id=1, source_target_pairs={{0,8},{8,16},{16,24},{24,32},{32,40},{40,48},{48,56},{56,64},{64,7... | collective-permute-start | bytes 1572872 | tf_op jit(solution)/shard_map/while/body/eval_jaxpr/ppermute | solution.py:14
  63.7 13.9 %collective-permute-start = (bf16[2048,128]{1,0:T(8,128)(2,1)S(1)}, bf16[2048,128]{1,0:T(8,128)(2,1)S(1)}, u32[]{:S(2)}, u32[]{:S(2)}) collective-permute-start(bf16[2048,128]{1,0:T(8,128)(2,1)S(1)} %get-tuple-element.144), channel_id=1, source_target_pairs={{0,8},{8,16},{16,24},{24,32},{32,40},{40,48},{48,56},{56,64},{64,7... | collective-permute-start | bytes 1572872 | tf_op jit(solution)/shard_map/while/body/eval_jaxpr/ppermute | solution.py:14
  66.2 13.0 %collective-permute-start.1 = (bf16[2048,128]{1,0:T(8,128)(2,1)S(1)}, bf16[2048,128]{1,0:T(8,128)(2,1)S(1)}, u32[]{:S(2)}, u32[]{:S(2)}) collective-permute-start(bf16[2048,128]{1,0:T(8,128)(2,1)S(1)} %get-tuple-element.145), channel_id=1, source_target_pairs={{0,8},{8,16},{16,24},{24,32},{32,40},{40,48},{48,56},{56,64},{64,7... | collective-permute-start | bytes 1572872 | tf_op jit(solution)/shard_map/while/body/eval_jaxpr/ppermute | solution.py:14
  80.2 16.2 %collective-permute-start = (bf16[2048,128]{1,0:T(8,128)(2,1)S(1)}, bf16[2048,128]{1,0:T(8,128)(2,1)S(1)}, u32[]{:S(2)}, u32[]{:S(2)}) collective-permute-start(bf16[2048,128]{1,0:T(8,128)(2,1)S(1)} %get-tuple-element.144), channel_id=1, source_target_pairs={{0,8},{8,16},{16,24},{24,32},{32,40},{40,48},{48,56},{56,64},{64,7... | collective-permute-start | bytes 1572872 | tf_op jit(solution)/shard_map/while/body/eval_jaxpr/ppermute | solution.py:14
  81.4 16.6 %collective-permute-start.1 = (bf16[2048,128]{1,0:T(8,128)(2,1)S(1)}, bf16[2048,128]{1,0:T(8,128)(2,1)S(1)}, u32[]{:S(2)}, u32[]{:S(2)}) collective-permute-start(bf16[2048,128]{1,0:T(8,128)(2,1)S(1)} %get-tuple-element.145), channel_id=1, source_target_pairs={{0,8},{8,16},{16,24},{24,32},{32,40},{40,48},{48,56},{56,64},{64,7... | collective-permute-start | bytes 1572872 | tf_op jit(solution)/shard_map/while/body/eval_jaxpr/ppermute | solution.py:14
  99.0 16.2 %collective-permute-start = (bf16[2048,128]{1,0:T(8,128)(2,1)S(1)}, bf16[2048,128]{1,0:T(8,128)(2,1)S(1)}, u32[]{:S(2)}, u32[]{:S(2)}) collective-permute-start(bf16[2048,128]{1,0:T(8,128)(2,1)S(1)} %get-tuple-element.144), channel_id=1, source_target_pairs={{0,8},{8,16},{16,24},{24,32},{32,40},{40,48},{48,56},{56,64},{64,7... | collective-permute-start | bytes 1572872 | tf_op jit(solution)/shard_map/while/body/eval_jaxpr/ppermute | solution.py:14
  99.1 17.8 %collective-permute-start.1 = (bf16[2048,128]{1,0:T(8,128)(2,1)S(1)}, bf16[2048,128]{1,0:T(8,128)(2,1)S(1)}, u32[]{:S(2)}, u32[]{:S(2)}) collective-permute-start(bf16[2048,128]{1,0:T(8,128)(2,1)S(1)} %get-tuple-element.145), channel_id=1, source_target_pairs={{0,8},{8,16},{16,24},{24,32},{32,40},{40,48},{48,56},{56,64},{64,7... | collective-permute-start | bytes 1572872 | tf_op jit(solution)/shard_map/while/body/eval_jaxpr/ppermute | solution.py:14
  117.8 16.2 %collective-permute-start = (bf16[2048,128]{1,0:T(8,128)(2,1)S(1)}, bf16[2048,128]{1,0:T(8,128)(2,1)S(1)}, u32[]{:S(2)}, u32[]{:S(2)}) collective-permute-start(bf16[2048,128]{1,0:T(8,128)(2,1)S(1)} %get-tuple-element.144), channel_id=1, source_target_pairs={{0,8},{8,16},{16,24},{24,32},{32,40},{40,48},{48,56},{56,64},{64,7... | collective-permute-start | bytes 1572872 | tf_op jit(solution)/shard_map/while/body/eval_jaxpr/ppermute | solution.py:14
  117.9 17.8 %collective-permute-start.1 = (bf16[2048,128]{1,0:T(8,128)(2,1)S(1)}, bf16[2048,128]{1,0:T(8,128)(2,1)S(1)}, u32[]{:S(2)}, u32[]{:S(2)}) collective-permute-start(bf16[2048,128]{1,0:T(8,128)(2,1)S(1)} %get-tuple-element.145), channel_id=1, source_target_pairs={{0,8},{8,16},{16,24},{24,32},{32,40},{40,48},{48,56},{56,64},{64,7... | collective-permute-start | bytes 1572872 | tf_op jit(solution)/shard_map/while/body/eval_jaxpr/ppermute | solution.py:14
  136.6 16.2 %collective-permute-start = (bf16[2048,128]{1,0:T(8,128)(2,1)S(1)}, bf16[2048,128]{1,0:T(8,128)(2,1)S(1)}, u32[]{:S(2)}, u32[]{:S(2)}) collective-permute-start(bf16[2048,128]{1,0:T(8,128)(2,1)S(1)} %get-tuple-element.144), channel_id=1, source_target_pairs={{0,8},{8,16},{16,24},{24,32},{32,40},{40,48},{48,56},{56,64},{64,7... | collective-permute-start | bytes 1572872 | tf_op jit(solution)/shard_map/while/body/eval_jaxpr/ppermute | solution.py:14
  136.7 17.8 %collective-permute-start.1 = (bf16[2048,128]{1,0:T(8,128)(2,1)S(1)}, bf16[2048,128]{1,0:T(8,128)(2,1)S(1)}, u32[]{:S(2)}, u32[]{:S(2)}) collective-permute-start(bf16[2048,128]{1,0:T(8,128)(2,1)S(1)} %get-tuple-element.145), channel_id=1, source_target_pairs={{0,8},{8,16},{16,24},{24,32},{32,40},{40,48},{48,56},{56,64},{64,7... | collective-permute-start | bytes 1572872 | tf_op jit(solution)/shard_map/while/body/eval_jaxpr/ppermute | solution.py:14
  155.5 16.2 %collective-permute-start = (bf16[2048,128]{1,0:T(8,128)(2,1)S(1)}, bf16[2048,128]{1,0:T(8,128)(2,1)S(1)}, u32[]{:S(2)}, u32[]{:S(2)}) collective-permute-start(bf16[2048,128]{1,0:T(8,128)(2,1)S(1)} %get-tuple-element.144), channel_id=1, source_target_pairs={{0,8},{8,16},{16,24},{24,32},{32,40},{40,48},{48,56},{56,64},{64,7... | collective-permute-start | bytes 1572872 | tf_op jit(solution)/shard_map/while/body/eval_jaxpr/ppermute | solution.py:14
  155.6 17.8 %collective-permute-start.1 = (bf16[2048,128]{1,0:T(8,128)(2,1)S(1)}, bf16[2048,128]{1,0:T(8,128)(2,1)S(1)}, u32[]{:S(2)}, u32[]{:S(2)}) collective-permute-start(bf16[2048,128]{1,0:T(8,128)(2,1)S(1)} %get-tuple-element.145), channel_id=1, source_target_pairs={{0,8},{8,16},{16,24},{24,32},{32,40},{40,48},{48,56},{56,64},{64,7... | collective-permute-start | bytes 1572872 | tf_op jit(solution)/shard_map/while/body/eval_jaxpr/ppermute | solution.py:14
  174.3 16.2 %collective-permute-start = (bf16[2048,128]{1,0:T(8,128)(2,1)S(1)}, bf16[2048,128]{1,0:T(8,128)(2,1)S(1)}, u32[]{:S(2)}, u32[]{:S(2)}) collective-permute-start(bf16[2048,128]{1,0:T(8,128)(2,1)S(1)} %get-tuple-element.144), channel_id=1, source_target_pairs={{0,8},{8,16},{16,24},{24,32},{32,40},{40,48},{48,56},{56,64},{64,7... | collective-permute-start | bytes 1572872 | tf_op jit(solution)/shard_map/while/body/eval_jaxpr/ppermute | solution.py:14
  174.4 17.8 %collective-permute-start.1 = (bf16[2048,128]{1,0:T(8,128)(2,1)S(1)}, bf16[2048,128]{1,0:T(8,128)(2,1)S(1)}, u32[]{:S(2)}, u32[]{:S(2)}) collective-permute-start(bf16[2048,128]{1,0:T(8,128)(2,1)S(1)} %get-tuple-element.145), channel_id=1, source_target_pairs={{0,8},{8,16},{16,24},{24,32},{32,40},{40,48},{48,56},{56,64},{64,7... | collective-permute-start | bytes 1572872 | tf_op jit(solution)/shard_map/while/body/eval_jaxpr/ppermute | solution.py:14
  193.1 16.2 %collective-permute-start = (bf16[2048,128]{1,0:T(8,128)(2,1)S(1)}, bf16[2048,128]{1,0:T(8,128)(2,1)S(1)}, u32[]{:S(2)}, u32[]{:S(2)}) collective-permute-start(bf16[2048,128]{1,0:T(8,128)(2,1)S(1)} %get-tuple-element.144), channel_id=1, source_target_pairs={{0,8},{8,16},{16,24},{24,32},{32,40},{40,48},{48,56},{56,64},{64,7... | collective-permute-start | bytes 1572872 | tf_op jit(solution)/shard_map/while/body/eval_jaxpr/ppermute | solution.py:14
  193.2 17.8 %collective-permute-start.1 = (bf16[2048,128]{1,0:T(8,128)(2,1)S(1)}, bf16[2048,128]{1,0:T(8,128)(2,1)S(1)}, u32[]{:S(2)}, u32[]{:S(2)}) collective-permute-start(bf16[2048,128]{1,0:T(8,128)(2,1)S(1)} %get-tuple-element.145), channel_id=1, source_target_pairs={{0,8},{8,16},{16,24},{24,32},{32,40},{40,48},{48,56},{56,64},{64,7... | collective-permute-start | bytes 1572872 | tf_op jit(solution)/shard_map/while/body/eval_jaxpr/ppermute | solution.py:14
  212.0 16.2 %collective-permute-start = (bf16[2048,128]{1,0:T(8,128)(2,1)S(1)}, bf16[2048,128]{1,0:T(8,128)(2,1)S(1)}, u32[]{:S(2)}, u32[]{:S(2)}) collective-permute-start(bf16[2048,128]{1,0:T(8,128)(2,1)S(1)} %get-tuple-element.144), channel_id=1, source_target_pairs={{0,8},{8,16},{16,24},{24,32},{32,40},{40,48},{48,56},{56,64},{64,7... | collective-permute-start | bytes 1572872 | tf_op jit(solution)/shard_map/while/body/eval_jaxpr/ppermute | solution.py:14
  212.0 17.8 %collective-permute-start.1 = (bf16[2048,128]{1,0:T(8,128)(2,1)S(1)}, bf16[2048,128]{1,0:T(8,128)(2,1)S(1)}, u32[]{:S(2)}, u32[]{:S(2)}) collective-permute-start(bf16[2048,128]{1,0:T(8,128)(2,1)S(1)} %get-tuple-element.145), channel_id=1, source_target_pairs={{0,8},{8,16},{16,24},{24,32},{32,40},{40,48},{48,56},{56,64},{64,7... | collective-permute-start | bytes 1572872 | tf_op jit(solution)/shard_map/while/body/eval_jaxpr/ppermute | solution.py:14
  230.8 16.2 %collective-permute-start = (bf16[2048,128]{1,0:T(8,128)(2,1)S(1)}, bf16[2048,128]{1,0:T(8,128)(2,1)S(1)}, u32[]{:S(2)}, u32[]{:S(2)}) collective-permute-start(bf16[2048,128]{1,0:T(8,128)(2,1)S(1)} %get-tuple-element.144), channel_id=1, source_target_pairs={{0,8},{8,16},{16,24},{24,32},{32,40},{40,48},{48,56},{56,64},{64,7... | collective-permute-start | bytes 1572872 | tf_op jit(solution)/shard_map/while/body/eval_jaxpr/ppermute | solution.py:14
  230.9 17.8 %collective-permute-start.1 = (bf16[2048,128]{1,0:T(8,128)(2,1)S(1)}, bf16[2048,128]{1,0:T(8,128)(2,1)S(1)}, u32[]{:S(2)}, u32[]{:S(2)}) collective-permute-start(bf16[2048,128]{1,0:T(8,128)(2,1)S(1)} %get-tuple-element.145), channel_id=1, source_target_pairs={{0,8},{8,16},{16,24},{24,32},{32,40},{40,48},{48,56},{56,64},{64,7... | collective-permute-start | bytes 1572872 | tf_op jit(solution)/shard_map/while/body/eval_jaxpr/ppermute | solution.py:14
  249.6 16.2 %collective-permute-start = (bf16[2048,128]{1,0:T(8,128)(2,1)S(1)}, bf16[2048,128]{1,0:T(8,128)(2,1)S(1)}, u32[]{:S(2)}, u32[]{:S(2)}) collective-permute-start(bf16[2048,128]{1,0:T(8,128)(2,1)S(1)} %get-tuple-element.144), channel_id=1, source_target_pairs={{0,8},{8,16},{16,24},{24,32},{32,40},{40,48},{48,56},{56,64},{64,7... | collective-permute-start | bytes 1572872 | tf_op jit(solution)/shard_map/while/body/eval_jaxpr/ppermute | solution.py:14
  249.7 17.8 %collective-permute-start.1 = (bf16[2048,128]{1,0:T(8,128)(2,1)S(1)}, bf16[2048,128]{1,0:T(8,128)(2,1)S(1)}, u32[]{:S(2)}, u32[]{:S(2)}) collective-permute-start(bf16[2048,128]{1,0:T(8,128)(2,1)S(1)} %get-tuple-element.145), channel_id=1, source_target_pairs={{0,8},{8,16},{16,24},{24,32},{32,40},{40,48},{48,56},{56,64},{64,7... | collective-permute-start | bytes 1572872 | tf_op jit(solution)/shard_map/while/body/eval_jaxpr/ppermute | solution.py:14
  268.5 16.2 %collective-permute-start = (bf16[2048,128]{1,0:T(8,128)(2,1)S(1)}, bf16[2048,128]{1,0:T(8,128)(2,1)S(1)}, u32[]{:S(2)}, u32[]{:S(2)}) collective-permute-start(bf16[2048,128]{1,0:T(8,128)(2,1)S(1)} %get-tuple-element.144), channel_id=1, source_target_pairs={{0,8},{8,16},{16,24},{24,32},{32,40},{40,48},{48,56},{56,64},{64,7... | collective-permute-start | bytes 1572872 | tf_op jit(solution)/shard_map/while/body/eval_jaxpr/ppermute | solution.py:14
  268.5 17.8 %collective-permute-start.1 = (bf16[2048,128]{1,0:T(8,128)(2,1)S(1)}, bf16[2048,128]{1,0:T(8,128)(2,1)S(1)}, u32[]{:S(2)}, u32[]{:S(2)}) collective-permute-start(bf16[2048,128]{1,0:T(8,128)(2,1)S(1)} %get-tuple-element.145), channel_id=1, source_target_pairs={{0,8},{8,16},{16,24},{24,32},{32,40},{40,48},{48,56},{56,64},{64,7... | collective-permute-start | bytes 1572872 | tf_op jit(solution)/shard_map/while/body/eval_jaxpr/ppermute | solution.py:14
  289.0 115.5 %reduce-scatter.2.cloned.1.call-start = ((), (), s32[]{:S(2)}) async-start(), calls=%async_computation.2 | async-start | bytes 2359296 | tf_op jit(solution)/shard_map/reduce_scatter | solution.py:86
Sparse Core Ops, SparseCore 0:
  289.1 60.3 all-gather.1
  353.8 50.6 reduce-scatter.1
where the time goes:
time: 413 us
  waiting for transfers between devices  327 us (79%)
  matrix products  34 us (8%)
  other arithmetic  17 us (4%)
  between operations  14.2 us (3%)
  starting transfers between devices  13.9 us (3%)
  local copies, waits for them, and re-layouts  5.1 us (1%)
    ppermute x30, waiting for transfers between devices, shifted(): lax.ppermute(array, axis, [(i, (i + by) % peers) for i in range(peers)])  216 us
    all_gather x1, waiting for transfers between devices, shards(): lax.all_gather(attention, 'blk', axis=0, tiled=True)  60.5 us
    reduce_scatter x1, waiting for transfers between devices, shards(): lax.psum_scatter(terms, 'head', scatter_dimension=0, tiled=True)  50.8 us
    dot_general x17, matrix products, block_partial(): jnp.einsum('kgqp,pkd->kgqd', weights, value_heads, preferred_element_type...  16.2 us
    ppermute x30, starting transfers between devices, shifted(): lax.ppermute(array, axis, [(i, (i + by) % peers) for i in range(peers)])  13.9 us
    dot_general x17, matrix products, block_partial(): jnp.einsum('qkgd,pkd->kgqp', query_rows, key_heads, preferred_element_typ...  13.7 us
    reduce_sum x17, other arithmetic, block_partial(): totals = jnp.sum(weights, axis=-1, dtype=jnp.float32)  13.2 us
  transfers between devices with their start and end apart: 32, of which 20 were waited for; matrix products, arithmetic and copies ran while one was open for 6% of the time, Pallas kernels for 0%

commit v1 on v0

v1 whole, which is shorter than its diff:
```python
import functools

import jax
import jax.numpy as jnp
from jax import lax
from jax.experimental import pallas as pl
from jax.experimental.pallas import tpu as pltpu
from jax.sharding import PartitionSpec as P

DH = 128
GROUP = 8
ROWS = 64
LANES = GROUP * ROWS
EXTRA = 16
SCALE = DH**-0.5 * 1.4426950408889634
FLOOR = -1e30
CHUNK = 512
XH, Z, CORE = 2, 4, 2
VMEM_LIMIT = 50 << 20


def moved(array, xh=0, z=0, c=0):
    pairs = []
    for i in range(XH * Z * CORE):
        a, b, d = i // (Z * CORE), (i // CORE) % Z, i % CORE
        to = (((a + xh) % XH) * Z + (b + z) % Z) * CORE + (d + c) % CORE
        pairs.append((i, to))
    return lax.ppermute(array, "blk", pairs)


def scores_of(keys, queries):
    return lax.dot_general(
        keys, queries, (((1,), (1,)), ((), ())), preferred_element_type=jnp.float32
    )


def with_ones(values):
    return jnp.concatenate(
        [values.T, jnp.ones((EXTRA, values.shape[0]), values.dtype)], axis=0
    )


def add_block(top, total, scores, values):
    best = jnp.maximum(top, jnp.max(scores, axis=0, keepdims=True) * SCALE)
    weights = jnp.exp2(scores * SCALE - best).astype(jnp.bfloat16)
    part = jnp.dot(values, weights, preferred_element_type=jnp.float32)
    return best, total * jnp.exp2(top - best) + part


def add_keys(queries, top, total, key_refs, value_scratch):
    chunks = []
    for block, key_ref in enumerate(key_refs):
        for at in range(0, key_ref.shape[0], CHUNK):
            chunks.append((block, key_ref, at))

    def scores_at(i):
        _, key_ref, at = chunks[i]
        return scores_of(key_ref[at : at + CHUNK, :], queries)

    ahead = scores_at(0)
    for i, (block, _, at) in enumerate(chunks):
        scores = ahead
        if i + 1 < len(chunks):
            ahead = scores_at(i + 1)
        top, total = add_block(top, total, scores, value_scratch[block, :, at : at + CHUNK])
    return top, total


def first_kernel(q0, q1, q2, q3, qk, qv, bias, ka, va, kb, vb, rows_ref, top_ref, total_ref, vt):
    for owner, ref in enumerate((q0, q1, q2, q3)):
        for head in range(GROUP):
            rows_ref[owner, head * ROWS : (head + 1) * ROWS, :] = ref[:, head * DH : (head + 1) * DH]
    vt[0] = with_ones(va[...])
    vt[1] = with_ones(vb[...])
    own = scores_of(qk[...], rows_ref[0]) + bias[...]
    top, total = add_block(
        jnp.full((1, LANES), FLOOR, jnp.float32),
        jnp.zeros((DH + EXTRA, LANES), jnp.float32),
        own,
        with_ones(qv[...]),
    )
    top_ref[...] = jnp.full(top_ref.shape, FLOOR, jnp.float32)
    total_ref[...] = jnp.zeros(total_ref.shape, jnp.float32)
    top_ref[0] = jnp.broadcast_to(top, (8, LANES))
    total_ref[0] = total

    def owner_step(owner, _):
        top, total = add_keys(rows_ref[owner], top_ref[owner, :1], total_ref[owner], (ka, kb), vt)
        top_ref[owner] = jnp.broadcast_to(top, (8, LANES))
        total_ref[owner] = total
        return 0

    lax.fori_loop(0, 4, owner_step, 0)


def second_kernel(rows, top_in, total_in, ka, va, kb, vb, own_top, own_total, p1, p2, p3, vt, out):
    vt[0] = with_ones(va[...])
    vt[1] = with_ones(vb[...])

    def owner_step(owner, _):
        top, total = add_keys(rows[owner], top_in[owner, :1], total_in[owner], (ka, kb), vt)

        @pl.when(owner == 0)
        def _():
            own_top[...] = jnp.broadcast_to(top, (8, LANES))
            own_total[...] = total

        denominator = total[DH : DH + 1]
        out[owner, :DH, :] = (total[:DH] * (1.0 / denominator)).astype(jnp.bfloat16)
        level = top + jnp.log2(denominator)
        high = level.astype(jnp.bfloat16)
        rest = level - high.astype(jnp.float32)
        mid = rest.astype(jnp.bfloat16)
        low = (rest - mid.astype(jnp.float32)).astype(jnp.bfloat16)
        row = lax.broadcasted_iota(jnp.int32, (EXTRA, LANES), 0)
        pieces = jnp.where(
            row == 0,
            high.astype(jnp.float32),
            jnp.where(row == 1, mid.astype(jnp.float32), low.astype(jnp.float32)),
        )
        out[owner, DH:, :] = pieces.astype(jnp.bfloat16)
        return 0

    lax.fori_loop(0, 4, owner_step, 0)
    p1[...] = out[1]
    p2[...] = out[2]
    p3[...] = out[3]


def merge_kernel(top, total, r1, r2, r3, live, att):
    parts = []
    best = top[:1]
    for ref in (r1, r2, r3):
        pieces = ref[DH:, :].astype(jnp.float32)
        level = (pieces[0:1] + pieces[1:2]) + pieces[2:3]
        parts.append((level, ref))
        best = jnp.maximum(best, level)
    own = jnp.exp2(top[:1] - best)
    numerator = total[:DH] * own
    denominator = total[DH : DH + 1] * own
    for level, ref in parts:
        share = jnp.exp2(level - best)
        numerator = numerator + ref[:DH, :].astype(jnp.float32) * share
        denominator = denominator + share
    result = jnp.where(live[:1] > 0.0, numerator / denominator, 0.0)
    result = result.T.astype(jnp.bfloat16)
    for head in range(GROUP):
        att[:, head * DH : (head + 1) * DH] = result[head * ROWS : (head + 1) * ROWS, :]


def project_kernel(slots, a0, a1, a2, a3, a4, a5, a6, a7, wa, wb, out, rows):
    for i, ref in enumerate((a0, a1, a2, a3, a4, a5, a6, a7)):
        rows[i * ROWS : (i + 1) * ROWS, :] = ref[...]
    width = wa.shape[1]
    for side, w in enumerate((wa, wb)):
        terms = jnp.dot(rows[...], w[...], preferred_element_type=jnp.float32).astype(jnp.bfloat16)
        for i in range(8):
            out[slots[i], :, side * width : (side + 1) * width] = terms[i * ROWS : (i + 1) * ROWS, :]


def sum_kernel(terms, mine, other, *, width):
    acc = terms[0].astype(jnp.float32)
    for i in range(1, terms.shape[0]):
        acc = acc + terms[i].astype(jnp.float32)
    acc = acc.astype(jnp.bfloat16)
    mine[...] = acc[:, :width]
    other[...] = acc[:, width:]


def call(kernel, outs, scratch=(), **kwargs):
    return pl.pallas_call(
        kernel,
        out_shape=tuple(jax.ShapeDtypeStruct(s, d) for s, d in outs),
        scratch_shapes=list(scratch),
        compiler_params=pltpu.CompilerParams(vmem_limit_bytes=VMEM_LIMIT),
        **kwargs,
    )


def shards(
    queries,
    question_keys,
    question_values,
    question_ids,
    live_rows,
    prefix_keys,
    prefix_values,
    out_weight,
):
    f32, bf16 = jnp.float32, jnp.bfloat16
    index = lax.axis_index("blk")
    core = index % CORE
    positions = prefix_keys.shape[0]

    keys_c = moved(prefix_keys, c=1)
    values_c = moved(prefix_values, c=1)
    q_up = moved(queries, z=1)
    q_down = moved(queries, z=-1)
    q_far = moved(queries, z=2)
    keys_x = moved(prefix_keys, xh=1)
    values_x = moved(prefix_values, xh=1)
    weight_c = moved(out_weight, c=1)

    row = jnp.arange(ROWS, dtype=jnp.int32)
    allowed = (question_ids[:, None] == question_ids[None, :]) & (row[:, None] <= row[None, :])
    bias = jnp.tile(jnp.where(allowed, 0.0, FLOOR).astype(f32), (1, GROUP))
    live = jnp.tile((row < live_rows[0]).astype(f32)[None, :], (8, GROUP))

    state = (DH + EXTRA, LANES)
    vt = pltpu.VMEM((2, DH + EXTRA, positions), bf16)
    rows, top, total = call(
        first_kernel,
        [((4, LANES, DH), bf16), ((4, 8, LANES), f32), ((4,) + state, f32)],
        [vt],
    )(
        queries, q_up, q_down, q_far, question_keys, question_values, bias,
        prefix_keys, prefix_values, keys_c, values_c,
    )
    keys_xc = moved(keys_x, c=1)
    values_xc = moved(values_x, c=1)
    own_top, own_total, p_up, p_down, p_far = call(
        second_kernel,
        [((8, LANES), f32), (state, f32), (state, bf16), (state, bf16), (state, bf16)],
        [vt, pltpu.VMEM((4,) + state, bf16)],
    )(rows, top, total, keys_x, values_x, keys_xc, values_xc)
    r_down = moved(p_up, z=-1)
    r_up = moved(p_down, z=1)
    r_far = moved(p_far, z=2)
    (att,) = call(merge_kernel, [((ROWS, GROUP * DH), bf16)])(
        own_top, own_total, r_down, r_up, r_far, live
    )

    att_x = moved(att, xh=1)
    held = {(0, 0): att, (1, 0): att_x}
    for z in (1, 3, 2):
        held[(0, z)] = moved(att, z=z)
    for z in (1, 3, 2):
        held[(1, z)] = moved(att_x, z=z)
    xh_at, z_at = index // (Z * CORE), (index // CORE) % Z
    order = [(dx, dz) for dx in range(XH) for dz in range(Z)]
    width = out_weight.shape[1]
    slots = jnp.stack([((xh_at - dx) % XH) * Z + (z_at - dz) % Z for dx, dz in order])
    vmem = pl.BlockSpec(memory_space=pltpu.VMEM)
    (terms,) = call(
        project_kernel,
        [((8, ROWS, CORE * width), bf16)],
        [pltpu.VMEM((8 * ROWS, GROUP * DH), bf16)],
        in_specs=[pl.BlockSpec(memory_space=pltpu.SMEM)] + [vmem] * 10,
    )(slots, *[held[o] for o in order], out_weight, weight_c)
    gathered = lax.all_to_all(terms, "head", 0, 0, tiled=True)
    mine, other = call(
        functools.partial(sum_kernel, width=width),
        [((ROWS, width), bf16), ((ROWS, width), bf16)],
    )(gathered)
    theirs = moved(other, c=1)
    return jnp.where(
        core == 0,
        jnp.concatenate([mine, theirs], axis=0),
        jnp.concatenate([theirs, mine], axis=0),
    )


def solution(mesh):
    return jax.shard_map(
        shards,
        mesh=mesh,
        in_specs=(
            P("blk", "head"),
            P("blk", "head"),
            P("blk", "head"),
            P("blk"),
            P("blk"),
            P("blk", "head"),
            P("blk", "head"),
            P("head", "blk"),
        ),
        out_specs=P("head", "blk"),
        check_vma=False,
    )
```

time: 413 us -> 123 us (0.30)
  waiting for transfers between devices: 327 us -> 25.2 us
  matrix products: 34 us -> 0 us
  Pallas kernels: 0 us -> 32.3 us
  starting transfers between devices: 13.9 us -> 35.2 us
  blocking collectives: 0 us -> 17.5 us
  other arithmetic: 17 us -> 1.49 us
  between operations: 14.2 us -> 0.74 us
  local copies, waits for them, and re-layouts: 5.1 us -> 9.58 us
    ppermute x30 -> x21, waiting for transfers between devices: 216 us -> 25.2 us  [moved(): return lax.ppermute(array, 'blk', pairs)]
    all_gather x1 -> x0, waiting for transfers between devices: 60.5 us -> none  [shards(): lax.all_gather(attention, 'blk', axis=0, tiled=True)]
    reduce_scatter x1 -> x0, waiting for transfers between devices: 50.8 us -> none  [shards(): lax.psum_scatter(terms, 'head', scatter_dimension=0, tiled=True)]
    dot_general x35 -> x0, matrix products: 34 us -> none  [the longest x17 16.2 us: block_partial(): jnp.einsum('kgqp,pkd->kgqd', weights, value_heads, preferred_element_type...]
    pallas_call x0 -> x5, Pallas kernels: none -> 32.3 us  [the longest x1 15.3 us: shards(): call(second_kernel, [((8, LANES), f32), (state, f32), (state, bf16), (sta...]
    ppermute x30 -> x21, starting transfers between devices: 13.9 us -> 35.2 us  [moved(): return lax.ppermute(array, 'blk', pairs)]
    all_to_all x0 -> x1, blocking collectives: none -> 17.5 us  [shards(): gathered = lax.all_to_all(terms, 'head', 0, 0, tiled=True)]
    reduce_sum x17 -> x0, other arithmetic: 13.2 us -> none  [block_partial(): totals = jnp.sum(weights, axis=-1, dtype=jnp.float32)]
  transfers between devices with their start and end apart: 32 -> 21, of which waited for: 20 -> 10; matrix products, arithmetic and copies ran while one was open for 6% -> 2% of each run, Pallas kernels for 0% -> 24%
where the time goes in v1:
time: 123 us; the launch traced here: 122 us
  starting transfers between devices  35.2 us (29%)
  Pallas kernels  32.3 us (26%)
  waiting for transfers between devices  25.2 us (20%)
  blocking collectives  17.5 us (14%)
  local copies, waits for them, and re-layouts  9.58 us (8%)
  other arithmetic  1.49 us (1%)
    ppermute x21, starting transfers between devices, moved(): return lax.ppermute(array, 'blk', pairs)  35.2 us
    ppermute x21, waiting for transfers between devices, moved(): return lax.ppermute(array, 'blk', pairs)  25.2 us
    all_to_all x1, blocking collectives, shards(): gathered = lax.all_to_all(terms, 'head', 0, 0, tiled=True)  17.5 us
    pallas_call x1, Pallas kernels, shards(): call(second_kernel, [((8, LANES), f32), (state, f32), (state, bf16), (sta...  15.3 us
    pallas_call x1, Pallas kernels, shards(): call(first_kernel, [((4, LANES, DH), bf16), ((4, 8, LANES), f32), ((4,) +...  14.2 us
    unnamed x20, local copies, waits for them, and re-layouts  7.64 us
    pallas_call x1, Pallas kernels, shards(): call(project_kernel, [((8, ROWS, CORE * width), bf16)], [pltpu.VMEM((8 *...  2.48 us
  transfers between devices with their start and end apart: 21, of which 10 were waited for; matrix products, arithmetic and copies ran while one was open for 2% of the time, Pallas kernels for 24%

profile of v1, /device:TPU:1, one launch (start us, length us, event | category | flops | bytes accessed | tf_op | source)
XLA Modules:
  0.0 122.0 jit_solution(16887657748673411491)
XLA Ops:
  0.0 3.6 %collective-permute-start.5 = (bf16[2048,128]{1,0:T(8,128)(2,1)}, bf16[2048,128]{1,0:T(8,128)(2,1)S(1)}, u32[]{:S(2)}, u32[]{:S(2)}) collective-permute-start(bf16[2048,128]{1,0:T(8,128)(2,1)} %ka.1), channel_id=1, source_target_pairs={{0,64},{8,72},{16,80},{24,88},{32,96},{40,104},{48,112},{56,120},{... | collective-permute-start | bytes 1572872 | tf_op jit(solution)/shard_map/ppermute | solution.py:28
  3.6 0.0 collective-permute-start.6
  3.6 1.8 %collective-permute-start = (bf16[64,1024]{1,0:T(8,128)(2,1)}, bf16[64,1024]{1,0:T(8,128)(2,1)S(1)}, u32[]{:S(2)}, u32[]{:S(2)}) collective-permute-start(bf16[64,1024]{1,0:T(8,128)(2,1)} %q0.1), channel_id=1, source_target_pairs={{0,16},{8,24},{16,32},{24,40},{32,48},{40,56},{48,0},{56,8},{64,80... | collective-permute-start | bytes 393224 | tf_op jit(solution)/shard_map/ppermute | solution.py:28
  5.4 1.5 %collective-permute-start.19 = (bf16[1024,512]{1,0:T(8,128)(2,1)}, bf16[1024,512]{1,0:T(8,128)(2,1)}, u32[]{:S(2)}, u32[]{:S(2)}) collective-permute-start(bf16[1024,512]{1,0:T(8,128)(2,1)} %wa.1), channel_id=1, source_target_pairs={{0,8},{8,0},{16,24},{24,16},{32,40},{40,32},{48,56},{56,48},{64,72... | collective-permute-start | bytes 3145736 | tf_op jit(solution)/shard_map/ppermute | solution.py:28
  7.0 1.8 %collective-permute-start.1 = (bf16[64,1024]{1,0:T(8,128)(2,1)}, bf16[64,1024]{1,0:T(8,128)(2,1)S(1)}, u32[]{:S(2)}, u32[]{:S(2)}) collective-permute-start(bf16[64,1024]{1,0:T(8,128)(2,1)} %q0.1), channel_id=1, source_target_pairs={{0,48},{8,56},{16,0},{24,8},{32,16},{40,24},{48,32},{56,40},{64,11... | collective-permute-start | bytes 393224 | tf_op jit(solution)/shard_map/ppermute | solution.py:28
  8.8 1.6 %collective-permute-done.q1 = bf16[64,1024]{1,0:T(8,128)(2,1)S(1)} collective-permute-done((bf16[64,1024]{1,0:T(8,128)(2,1)}, bf16[64,1024]{1,0:T(8,128)(2,1)S(1)}, u32[]{:S(2)}, u32[]{:S(2)}) %collective-permute-start) | collective-permute-done | bytes 131104 | tf_op jit(solution)/shard_map/ppermute | solution.py:28
  10.4 1.3 %collective-permute-start.2 = (bf16[64,1024]{1,0:T(8,128)(2,1)}, bf16[64,1024]{1,0:T(8,128)(2,1)S(1)}, u32[]{:S(2)}, u32[]{:S(2)}) collective-permute-start(bf16[64,1024]{1,0:T(8,128)(2,1)} %q0.1), channel_id=1, source_target_pairs={{0,32},{8,40},{16,48},{24,56},{32,0},{40,8},{48,16},{56,24},{64,96... | collective-permute-start | bytes 393224 | tf_op jit(solution)/shard_map/ppermute | solution.py:28
  11.7 0.8 collective-permute-done.1.q2
  12.6 1.5 %collective-permute-start.3 = (bf16[2048,128]{1,0:T(8,128)(2,1)}, bf16[2048,128]{1,0:T(8,128)(2,1)S(1)}, u32[]{:S(2)}, u32[]{:S(2)}) collective-permute-start(bf16[2048,128]{1,0:T(8,128)(2,1)} %ka.1), channel_id=1, source_target_pairs={{0,8},{8,0},{16,24},{24,16},{32,40},{40,32},{48,56},{56,48},{64,72... | collective-permute-start | bytes 1572872 | tf_op jit(solution)/shard_map/ppermute | solution.py:28
  14.1 2.2 %collective-permute-done.2.q3 = bf16[64,1024]{1,0:T(8,128)(2,1)S(1)} collective-permute-done((bf16[64,1024]{1,0:T(8,128)(2,1)}, bf16[64,1024]{1,0:T(8,128)(2,1)S(1)}, u32[]{:S(2)}, u32[]{:S(2)}) %collective-permute-start.2) | collective-permute-done | bytes 131104 | tf_op jit(solution)/shard_map/ppermute | solution.py:28
  16.2 0.7 copy-done.6
  16.9 2.7 %collective-permute-start.4 = (bf16[2048,128]{1,0:T(8,128)(2,1)}, bf16[2048,128]{1,0:T(8,128)(2,1)S(1)}, u32[]{:S(2)}, u32[]{:S(2)}) collective-permute-start(bf16[2048,128]{1,0:T(8,128)(2,1)} %va.1), channel_id=1, source_target_pairs={{0,8},{8,0},{16,24},{24,16},{32,40},{40,32},{48,56},{56,48},{64,72... | collective-permute-start | bytes 1572872 | tf_op jit(solution)/shard_map/ppermute | solution.py:28
  19.6 0.0 collective-permute-done.5.ka
  19.6 0.0 collective-permute-start.7
  19.6 6.6 %collective-permute-done.6.va = bf16[2048,128]{1,0:T(8,128)(2,1)S(1)} collective-permute-done((bf16[2048,128]{1,0:T(8,128)(2,1)}, bf16[2048,128]{1,0:T(8,128)(2,1)S(1)}, u32[]{:S(2)}, u32[]{:S(2)}) %collective-permute-start.6) | collective-permute-done | bytes 524320 | tf_op jit(solution)/shard_map/ppermute | solution.py:28
  26.2 1.7 %collective-permute-start.8 = (bf16[2048,128]{1,0:T(8,128)(2,1)S(1)}, bf16[2048,128]{1,0:T(8,128)(2,1)S(1)}, u32[]{:S(2)}, u32[]{:S(2)}) collective-permute-start(bf16[2048,128]{1,0:T(8,128)(2,1)S(1)} %collective-permute-done.6.va), channel_id=1, source_target_pairs={{0,8},{8,0},{16,24},{24,16},{32,40},{40,32},{48,56},{56,48},{64,72... | collective-permute-start | bytes 1572872 | tf_op jit(solution)/shard_map/ppermute | solution.py:28
  27.9 0.8 fusion.1
  28.7 0.7 tile.19
  29.4 1.1 tile.20.bias
  30.5 0.0 collective-permute-done.3.kb
  30.5 0.0 collective-permute-done.4.vb
  30.5 0.0 copy-start.1
  30.5 1.0 copy-done.1
  31.5 1.0 copy-done.2
  32.6 0.9 copy-done.5
  33.5 0.9 copy-done.7
  34.4 0.7 copy-done.8
  35.1 0.7 copy-done.9
  35.8 14.2 %shard_map.82 = (bf16[4,512,128]{2,1,0:T(8,128)(2,1)S(1)}, f32[4,8,512]{2,1,0:T(8,128)S(1)}, f32[4,144,512]{2,1,0:T(8,128)}) custom-call(bf16[64,1024]{1,0:T(8,128)(2,1)S(1)} %copy-done.5, bf16[64,1024]{1,0:T(8,128)(2,1)S(1)} %collective-permute-done.q1, bf16[64,1024]{1,0:T(8,128)(2,1)S(1)} %collective-permute-done.1.q2, bf16[64,1024]{1,0:T(8,128)(2,1)S(1)} %copy-done.7, ...), custom_call_target="tpu_custom_call" | custom-call | tf_op jit(solution)/shard_map/pallas_call | solution.py:211
  50.0 0.0 collective-permute-done.7.kb
  50.0 0.0 collective-permute-done.8.vb
  50.0 15.3 %shard_map.83 = (f32[8,512]{1,0:T(8,128)S(1)}, f32[144,512]{1,0:T(8,128)S(1)}, bf16[144,512]{1,0:T(8,128)(2,1)S(1)}, bf16[144,512]{1,0:T(8,128)(2,1)}, bf16[144,512]{1,0:T(8,128)(2,1)}) custom-call(bf16[4,512,128]{2,1,0:T(8,128)(2,1)S(1)} %get-tuple-element.15.rows, f32[4,8,512]{2,1,0:T(8,128)S(1)} %get-tuple-element.16.top_in, ...), custom_call_target="tpu_custom_call" | custom-call | tf_op jit(solution)/shard_map/pallas_call | solution.py:221
  65.3 0.7 copy-done.3
  66.1 1.9 %collective-permute-start.10 = (bf16[144,512]{1,0:T(8,128)(2,1)}, bf16[144,512]{1,0:T(8,128)(2,1)S(1)}, u32[]{:S(2)}, u32[]{:S(2)}) collective-permute-start(bf16[144,512]{1,0:T(8,128)(2,1)} %get-tuple-element.21), channel_id=1, source_target_pairs={{0,16},{8,24},{16,32},{24,40},{32,48},{40,56},{48,0},{56,8},{64,80... | collective-permute-start | bytes 442376 | tf_op jit(solution)/shard_map/ppermute | solution.py:28
  67.9 3.3 %collective-permute-start.11 = (bf16[144,512]{1,0:T(8,128)(2,1)}, bf16[144,512]{1,0:T(8,128)(2,1)S(1)}, u32[]{:S(2)}, u32[]{:S(2)}) collective-permute-start(bf16[144,512]{1,0:T(8,128)(2,1)} %get-tuple-element.22), channel_id=1, source_target_pairs={{0,32},{8,40},{16,48},{24,56},{32,0},{40,8},{48,16},{56,24},{64,96... | collective-permute-start | bytes 442376 | tf_op jit(solution)/shard_map/ppermute | solution.py:28
  71.2 0.7 collective-permute-start.9
  72.6 0.1 tile.22
  72.7 1.8 %collective-permute-done.10.r2 = bf16[144,512]{1,0:T(8,128)(2,1)S(1)} collective-permute-done((bf16[144,512]{1,0:T(8,128)(2,1)}, bf16[144,512]{1,0:T(8,128)(2,1)S(1)}, u32[]{:S(2)}, u32[]{:S(2)}) %collective-permute-start.10) | collective-permute-done | bytes 147488 | tf_op jit(solution)/shard_map/ppermute | solution.py:28
  74.5 4.1 %collective-permute-done.11.r3 = bf16[144,512]{1,0:T(8,128)(2,1)S(1)} collective-permute-done((bf16[144,512]{1,0:T(8,128)(2,1)}, bf16[144,512]{1,0:T(8,128)(2,1)S(1)}, u32[]{:S(2)}, u32[]{:S(2)}) %collective-permute-start.11) | collective-permute-done | bytes 147488 | tf_op jit(solution)/shard_map/ppermute | solution.py:28
  78.6 0.0 collective-permute-done.9.r1
  78.6 1.0 copy-done.4
  79.6 0.2 shard_map.84.a0
  79.8 2.8 %collective-permute-start.15 = (bf16[64,1024]{1,0:T(8,128)(2,1)S(1)}, bf16[64,1024]{1,0:T(8,128)(2,1)S(1)}, u32[]{:S(2)}, u32[]{:S(2)}) collective-permute-start(bf16[64,1024]{1,0:T(8,128)(2,1)S(1)} %shard_map.84.a0), channel_id=1, source_target_pairs={{0,64},{8,72},{16,80},{24,88},{32,96},{40,104},{48,112},{56,120},{... | collective-permute-start | bytes 393224 | tf_op jit(solution)/shard_map/ppermute | solution.py:28
  82.6 0.3 collective-permute-start.12
  83.0 2.9 %collective-permute-start.13 = (bf16[64,1024]{1,0:T(8,128)(2,1)S(1)}, bf16[64,1024]{1,0:T(8,128)(2,1)S(1)}, u32[]{:S(2)}, u32[]{:S(2)}) collective-permute-start(bf16[64,1024]{1,0:T(8,128)(2,1)S(1)} %shard_map.84.a0), channel_id=1, source_target_pairs={{0,32},{8,40},{16,48},{24,56},{32,0},{40,8},{48,16},{56,24},{64,96... | collective-permute-start | bytes 393224 | tf_op jit(solution)/shard_map/ppermute | solution.py:28
  85.9 0.4 collective-permute-start.14
  86.3 0.0 collective-permute-done.15.a4
  86.3 1.0 collective-permute-start.16
  87.3 0.0 collective-permute-done.19.wb
  87.3 1.9 %collective-permute-start.17 = (bf16[64,1024]{1,0:T(8,128)(2,1)S(1)}, bf16[64,1024]{1,0:T(8,128)(2,1)S(1)}, u32[]{:S(2)}, u32[]{:S(2)}) collective-permute-start(bf16[64,1024]{1,0:T(8,128)(2,1)S(1)} %collective-permute-done.15.a4), channel_id=1, source_target_pairs={{0,32},{8,40},{16,48},{24,56},{32,0},{40,8},{48,16},{56,24},{64,96... | collective-permute-start | bytes 393224 | tf_op jit(solution)/shard_map/ppermute | solution.py:28
  89.2 0.0 collective-permute-done.12.a1
  89.2 0.6 collective-permute-start.18
  89.8 0.1 stack.35.slots
  89.9 1.6 %collective-permute-done.13.a2 = bf16[64,1024]{1,0:T(8,128)(2,1)S(1)} collective-permute-done((bf16[64,1024]{1,0:T(8,128)(2,1)S(1)}, bf16[64,1024]{1,0:T(8,128)(2,1)S(1)}, u32[]{:S(2)}, u32[]{:S(2)}) %collective-permute-start.13) | collective-permute-done | bytes 131104 | tf_op jit(solution)/shard_map/ppermute | solution.py:28
  91.5 0.0 collective-permute-done.14.a3
  91.5 2.2 %collective-permute-done.16.a5 = bf16[64,1024]{1,0:T(8,128)(2,1)S(1)} collective-permute-done((bf16[64,1024]{1,0:T(8,128)(2,1)S(1)}, bf16[64,1024]{1,0:T(8,128)(2,1)S(1)}, u32[]{:S(2)}, u32[]{:S(2)}) %collective-permute-start.16) | collective-permute-done | bytes 131104 | tf_op jit(solution)/shard_map/ppermute | solution.py:28
  93.6 3.5 %collective-permute-done.17.a6 = bf16[64,1024]{1,0:T(8,128)(2,1)S(1)} collective-permute-done((bf16[64,1024]{1,0:T(8,128)(2,1)S(1)}, bf16[64,1024]{1,0:T(8,128)(2,1)S(1)}, u32[]{:S(2)}, u32[]{:S(2)}) %collective-permute-start.17) | collective-permute-done | bytes 131104 | tf_op jit(solution)/shard_map/ppermute | solution.py:28
  97.1 0.0 collective-permute-done.18.a7
  97.1 2.5 %shard_map.85 = bf16[8,64,1024]{2,1,0:T(8,128)(2,1)S(1)} custom-call(s32[8]{0:T(128)S(1)} %stack.35.slots, bf16[64,1024]{1,0:T(8,128)(2,1)S(1)} %shard_map.84.a0, bf16[64,1024]{1,0:T(8,128)(2,1)S(1)} %collective-permute-done.12.a1, bf16[64,1024]{1,0:T(8,128)(2,1)S(1)} %collective-permute-done.13.a2, bf16[64,1024]{1,0:T(8,128)(2,1)S(1)} %collective-permute-done.14.a3, ...), custom_call_target="tpu_custom_call" | custom-call | tf_op jit(solution)/shard_map/pallas_call | solution.py:244
  99.6 17.5 %all_to_all.5.terms = bf16[8,64,1024]{2,1,0:T(8,128)(2,1)S(1)} all-to-all(bf16[8,64,1024]{2,1,0:T(8,128)(2,1)S(1)} %shard_map.85), channel_id=1, replica_groups=mesh['blk'=16,'head'=8] {'head'}, dimensions={0} | all-to-all | bytes 2097152 | tf_op jit(solution)/shard_map/all_to_all | solution.py:250
  117.0 0.1 shard_map.86
  117.2 3.3 %collective-permute-start.20 = (bf16[64,512]{1,0:T(8,128)(2,1)S(1)}, bf16[64,512]{1,0:T(8,128)(2,1)S(1)}, u32[]{:S(2)}, u32[]{:S(2)}) collective-permute-start(bf16[64,512]{1,0:T(8,128)(2,1)S(1)} %get-tuple-element.24), channel_id=1, source_target_pairs={{0,8},{8,0},{16,24},{24,16},{32,40},{40,32},{48,56},{56,48},{64,72... | collective-permute-start | bytes 196616 | tf_op jit(solution)/shard_map/ppermute | solution.py:28
  120.5 0.9 collective-permute-done.20
  121.4 0.7 maximum_select_fusion
  (13 shorter events, 0.0 us)
Async XLA Ops:
  0.0 19.6 %collective-permute-start.5 = (bf16[2048,128]{1,0:T(8,128)(2,1)}, bf16[2048,128]{1,0:T(8,128)(2,1)S(1)}, u32[]{:S(2)}, u32[]{:S(2)}) collective-permute-start(bf16[2048,128]{1,0:T(8,128)(2,1)} %ka.1), channel_id=1, source_target_pairs={{0,64},{8,72},{16,80},{24,88},{32,96},{40,104},{48,112},{56,120},{... | collective-permute-start | bytes 1572872 | tf_op jit(solution)/shard_map/ppermute | solution.py:28
  3.6 22.6 %collective-permute-start.6 = (bf16[2048,128]{1,0:T(8,128)(2,1)}, bf16[2048,128]{1,0:T(8,128)(2,1)S(1)}, u32[]{:S(2)}, u32[]{:S(2)}) collective-permute-start(bf16[2048,128]{1,0:T(8,128)(2,1)} %va.1), channel_id=1, source_target_pairs={{0,64},{8,72},{16,80},{24,88},{32,96},{40,104},{48,112},{56,120},{... | collective-permute-start | bytes 1572872 | tf_op jit(solution)/shard_map/ppermute | solution.py:28
  3.6 6.8 %collective-permute-start = (bf16[64,1024]{1,0:T(8,128)(2,1)}, bf16[64,1024]{1,0:T(8,128)(2,1)S(1)}, u32[]{:S(2)}, u32[]{:S(2)}) collective-permute-start(bf16[64,1024]{1,0:T(8,128)(2,1)} %q0.1), channel_id=1, source_target_pairs={{0,16},{8,24},{16,32},{24,40},{32,48},{40,56},{48,0},{56,8},{64,80... | collective-permute-start | bytes 393224 | tf_op jit(solution)/shard_map/ppermute | solution.py:28
  5.4 81.9 %collective-permute-start.19 = (bf16[1024,512]{1,0:T(8,128)(2,1)}, bf16[1024,512]{1,0:T(8,128)(2,1)}, u32[]{:S(2)}, u32[]{:S(2)}) collective-permute-start(bf16[1024,512]{1,0:T(8,128)(2,1)} %wa.1), channel_id=1, source_target_pairs={{0,8},{8,0},{16,24},{24,16},{32,40},{40,32},{48,56},{56,48},{64,72... | collective-permute-start | bytes 3145736 | tf_op jit(solution)/shard_map/ppermute | solution.py:28
  7.0 5.6 %collective-permute-start.1 = (bf16[64,1024]{1,0:T(8,128)(2,1)}, bf16[64,1024]{1,0:T(8,128)(2,1)S(1)}, u32[]{:S(2)}, u32[]{:S(2)}) collective-permute-start(bf16[64,1024]{1,0:T(8,128)(2,1)} %q0.1), channel_id=1, source_target_pairs={{0,48},{8,56},{16,0},{24,8},{32,16},{40,24},{48,32},{56,40},{64,11... | collective-permute-start | bytes 393224 | tf_op jit(solution)/shard_map/ppermute | solution.py:28
  10.4 5.8 %collective-permute-start.2 = (bf16[64,1024]{1,0:T(8,128)(2,1)}, bf16[64,1024]{1,0:T(8,128)(2,1)S(1)}, u32[]{:S(2)}, u32[]{:S(2)}) collective-permute-start(bf16[64,1024]{1,0:T(8,128)(2,1)} %q0.1), channel_id=1, source_target_pairs={{0,32},{8,40},{16,48},{24,56},{32,0},{40,8},{48,16},{56,24},{64,96... | collective-permute-start | bytes 393224 | tf_op jit(solution)/shard_map/ppermute | solution.py:28
  12.6 17.9 %collective-permute-start.3 = (bf16[2048,128]{1,0:T(8,128)(2,1)}, bf16[2048,128]{1,0:T(8,128)(2,1)S(1)}, u32[]{:S(2)}, u32[]{:S(2)}) collective-permute-start(bf16[2048,128]{1,0:T(8,128)(2,1)} %ka.1), channel_id=1, source_target_pairs={{0,8},{8,0},{16,24},{24,16},{32,40},{40,32},{48,56},{56,48},{64,72... | collective-permute-start | bytes 1572872 | tf_op jit(solution)/shard_map/ppermute | solution.py:28
  16.2 0.7 copy-start.6
  16.9 13.6 %collective-permute-start.4 = (bf16[2048,128]{1,0:T(8,128)(2,1)}, bf16[2048,128]{1,0:T(8,128)(2,1)S(1)}, u32[]{:S(2)}, u32[]{:S(2)}) collective-permute-start(bf16[2048,128]{1,0:T(8,128)(2,1)} %va.1), channel_id=1, source_target_pairs={{0,8},{8,0},{16,24},{24,16},{32,40},{40,32},{48,56},{56,48},{64,72... | collective-permute-start | bytes 1572872 | tf_op jit(solution)/shard_map/ppermute | solution.py:28
  19.6 30.5 %collective-permute-start.7 = (bf16[2048,128]{1,0:T(8,128)(2,1)S(1)}, bf16[2048,128]{1,0:T(8,128)(2,1)S(1)}, u32[]{:S(2)}, u32[]{:S(2)}) collective-permute-start(bf16[2048,128]{1,0:T(8,128)(2,1)S(1)} %collective-permute-done.5.ka), channel_id=1, source_target_pairs={{0,8},{8,0},{16,24},{24,16},{32,40},{40,32},{48,56},{56,48},{64,72... | collective-permute-start | bytes 1572872 | tf_op jit(solution)/shard_map/ppermute | solution.py:28
  26.2 23.9 %collective-permute-start.8 = (bf16[2048,128]{1,0:T(8,128)(2,1)S(1)}, bf16[2048,128]{1,0:T(8,128)(2,1)S(1)}, u32[]{:S(2)}, u32[]{:S(2)}) collective-permute-start(bf16[2048,128]{1,0:T(8,128)(2,1)S(1)} %collective-permute-done.6.va), channel_id=1, source_target_pairs={{0,8},{8,0},{16,24},{24,16},{32,40},{40,32},{48,56},{56,48},{64,72... | collective-permute-start | bytes 1572872 | tf_op jit(solution)/shard_map/ppermute | solution.py:28
  30.5 1.0 copy-start.1
  31.5 1.0 copy-start.2
  32.6 0.9 copy-start.5
  33.5 0.9 copy-start.7
  34.4 0.7 copy-start.8
  35.1 0.7 copy-start.9
  65.3 0.7 copy-start.3
  66.1 31.0 %copy-start = (bf16[1024,512]{1,0:T(8,128)(2,1)S(1)}, bf16[1024,512]{1,0:T(8,128)(2,1)}, u32[]{:S(2)}) copy-start(bf16[1024,512]{1,0:T(8,128)(2,1)} %wa.1) | copy-start | bytes 3145732
  66.1 8.4 %collective-permute-start.10 = (bf16[144,512]{1,0:T(8,128)(2,1)}, bf16[144,512]{1,0:T(8,128)(2,1)S(1)}, u32[]{:S(2)}, u32[]{:S(2)}) collective-permute-start(bf16[144,512]{1,0:T(8,128)(2,1)} %get-tuple-element.21), channel_id=1, source_target_pairs={{0,16},{8,24},{16,32},{24,40},{32,48},{40,56},{48,0},{56,8},{64,80... | collective-permute-start | bytes 442376 | tf_op jit(solution)/shard_map/ppermute | solution.py:28
  67.9 10.7 %collective-permute-start.11 = (bf16[144,512]{1,0:T(8,128)(2,1)}, bf16[144,512]{1,0:T(8,128)(2,1)S(1)}, u32[]{:S(2)}, u32[]{:S(2)}) collective-permute-start(bf16[144,512]{1,0:T(8,128)(2,1)} %get-tuple-element.22), channel_id=1, source_target_pairs={{0,32},{8,40},{16,48},{24,56},{32,0},{40,8},{48,16},{56,24},{64,96... | collective-permute-start | bytes 442376 | tf_op jit(solution)/shard_map/ppermute | solution.py:28
  71.2 7.4 %collective-permute-start.9 = (bf16[144,512]{1,0:T(8,128)(2,1)S(1)}, bf16[144,512]{1,0:T(8,128)(2,1)S(1)}, u32[]{:S(2)}, u32[]{:S(2)}) collective-permute-start(bf16[144,512]{1,0:T(8,128)(2,1)S(1)} %get-tuple-element.20), channel_id=1, source_target_pairs={{0,48},{8,56},{16,0},{24,8},{32,16},{40,24},{48,32},{56,40},{64,11... | collective-permute-start | bytes 442376 | tf_op jit(solution)/shard_map/ppermute | solution.py:28
  78.6 1.0 copy-start.4
  79.8 6.5 %collective-permute-start.15 = (bf16[64,1024]{1,0:T(8,128)(2,1)S(1)}, bf16[64,1024]{1,0:T(8,128)(2,1)S(1)}, u32[]{:S(2)}, u32[]{:S(2)}) collective-permute-start(bf16[64,1024]{1,0:T(8,128)(2,1)S(1)} %shard_map.84.a0), channel_id=1, source_target_pairs={{0,64},{8,72},{16,80},{24,88},{32,96},{40,104},{48,112},{56,120},{... | collective-permute-start | bytes 393224 | tf_op jit(solution)/shard_map/ppermute | solution.py:28
  82.6 6.6 %collective-permute-start.12 = (bf16[64,1024]{1,0:T(8,128)(2,1)S(1)}, bf16[64,1024]{1,0:T(8,128)(2,1)S(1)}, u32[]{:S(2)}, u32[]{:S(2)}) collective-permute-start(bf16[64,1024]{1,0:T(8,128)(2,1)S(1)} %shard_map.84.a0), channel_id=1, source_target_pairs={{0,16},{8,24},{16,32},{24,40},{32,48},{40,56},{48,0},{56,8},{64,80... | collective-permute-start | bytes 393224 | tf_op jit(solution)/shard_map/ppermute | solution.py:28
  83.0 8.5 %collective-permute-start.13 = (bf16[64,1024]{1,0:T(8,128)(2,1)S(1)}, bf16[64,1024]{1,0:T(8,128)(2,1)S(1)}, u32[]{:S(2)}, u32[]{:S(2)}) collective-permute-start(bf16[64,1024]{1,0:T(8,128)(2,1)S(1)} %shard_map.84.a0), channel_id=1, source_target_pairs={{0,32},{8,40},{16,48},{24,56},{32,0},{40,8},{48,16},{56,24},{64,96... | collective-permute-start | bytes 393224 | tf_op jit(solution)/shard_map/ppermute | solution.py:28
  85.9 5.6 %collective-permute-start.14 = (bf16[64,1024]{1,0:T(8,128)(2,1)S(1)}, bf16[64,1024]{1,0:T(8,128)(2,1)S(1)}, u32[]{:S(2)}, u32[]{:S(2)}) collective-permute-start(bf16[64,1024]{1,0:T(8,128)(2,1)S(1)} %shard_map.84.a0), channel_id=1, source_target_pairs={{0,48},{8,56},{16,0},{24,8},{32,16},{40,24},{48,32},{56,40},{64,11... | collective-permute-start | bytes 393224 | tf_op jit(solution)/shard_map/ppermute | solution.py:28
  86.3 7.3 %collective-permute-start.16 = (bf16[64,1024]{1,0:T(8,128)(2,1)S(1)}, bf16[64,1024]{1,0:T(8,128)(2,1)S(1)}, u32[]{:S(2)}, u32[]{:S(2)}) collective-permute-start(bf16[64,1024]{1,0:T(8,128)(2,1)S(1)} %collective-permute-done.15.a4), channel_id=1, source_target_pairs={{0,16},{8,24},{16,32},{24,40},{32,48},{40,56},{48,0},{56,8},{64,80... | collective-permute-start | bytes 393224 | tf_op jit(solution)/shard_map/ppermute | solution.py:28
  87.3 9.7 %collective-permute-start.17 = (bf16[64,1024]{1,0:T(8,128)(2,1)S(1)}, bf16[64,1024]{1,0:T(8,128)(2,1)S(1)}, u32[]{:S(2)}, u32[]{:S(2)}) collective-permute-start(bf16[64,1024]{1,0:T(8,128)(2,1)S(1)} %collective-permute-done.15.a4), channel_id=1, source_target_pairs={{0,32},{8,40},{16,48},{24,56},{32,0},{40,8},{48,16},{56,24},{64,96... | collective-permute-start | bytes 393224 | tf_op jit(solution)/shard_map/ppermute | solution.py:28
  89.2 7.9 %collective-permute-start.18 = (bf16[64,1024]{1,0:T(8,128)(2,1)S(1)}, bf16[64,1024]{1,0:T(8,128)(2,1)S(1)}, u32[]{:S(2)}, u32[]{:S(2)}) collective-permute-start(bf16[64,1024]{1,0:T(8,128)(2,1)S(1)} %collective-permute-done.15.a4), channel_id=1, source_target_pairs={{0,48},{8,56},{16,0},{24,8},{32,16},{40,24},{48,32},{56,40},{64,11... | collective-permute-start | bytes 393224 | tf_op jit(solution)/shard_map/ppermute | solution.py:28
  117.2 4.2 %collective-permute-start.20 = (bf16[64,512]{1,0:T(8,128)(2,1)S(1)}, bf16[64,512]{1,0:T(8,128)(2,1)S(1)}, u32[]{:S(2)}, u32[]{:S(2)}) collective-permute-start(bf16[64,512]{1,0:T(8,128)(2,1)S(1)} %get-tuple-element.24), channel_id=1, source_target_pairs={{0,8},{8,0},{16,24},{24,16},{32,40},{40,32},{48,56},{56,48},{64,72... | collective-permute-start | bytes 196616 | tf_op jit(solution)/shard_map/ppermute | solution.py:28

commit v2 on v0

v2 whole, which is shorter than its diff:
```python
import functools

import jax
import jax.numpy as jnp
from jax import lax
from jax.experimental import pallas as pl
from jax.experimental.pallas import tpu as pltpu
from jax.sharding import PartitionSpec as P

DH = 128
GROUP = 8
ROWS = 64
LANES = GROUP * ROWS
EXTRA = 16
SCALE = DH**-0.5 * 1.4426950408889634
FLOOR = -1e30
DEAD = 1e30
XH, Z, CORE = 2, 4, 2
VMEM_LIMIT = 50 << 20
FAR = (1, 3, 2)


def moved(array, xh=0, z=0, c=0):
    pairs = []
    for i in range(XH * Z * CORE):
        a, b, d = i // (Z * CORE), (i // CORE) % Z, i % CORE
        to = (((a + xh) % XH) * Z + (b + z) % Z) * CORE + (d + c) % CORE
        pairs.append((i, to))
    return lax.ppermute(array, "blk", pairs)


def after(array, *others):
    return lax.optimization_barrier((array, *others))[0]


def scores_of(queries, keys):
    return lax.dot_general(
        queries, keys, (((1,), (1,)), ((), ())), preferred_element_type=jnp.float32
    )


def wide(column, width):
    return jnp.concatenate([column] * (width // column.shape[1]), axis=1)


def add_block(top, total, scores, values):
    best = jnp.maximum(top, jnp.max(scores, axis=1, keepdims=True) * SCALE)
    keys = scores.shape[1]
    at = wide(best, keys) if keys >= DH else best[:, :keys]
    weights = jnp.exp2(scores * SCALE - at).astype(jnp.bfloat16)
    part = jnp.dot(weights, values, preferred_element_type=jnp.float32)
    return best, total * wide(jnp.exp2(top - best), 2 * DH) + part


def stacked(ref):
    return jnp.concatenate([ref[:, h * DH : (h + 1) * DH] for h in range(GROUP)], axis=0)


def fetch(refs, scratch, sems):
    keys, values = scratch
    copies = []
    for i, (key_ref, value_ref) in enumerate(refs):
        copies.append(pltpu.make_async_copy(key_ref, keys.at[i], sems.at[2 * i]))
        copies.append(
            pltpu.make_async_copy(value_ref, values.at[i, :, pl.ds(0, DH)], sems.at[2 * i + 1])
        )
    for copy in copies:
        copy.start()
    values[:, :, DH:] = jnp.ones(values.shape[:2] + (DH,), values.dtype)
    return copies


def finish(top, total):
    denominator = total[:, DH:]
    result = (total[:, :DH] / denominator).T
    level = (top + jnp.log2(denominator)).T[:1]
    return result, level


def packed(result, level):
    high = level.astype(jnp.bfloat16).astype(jnp.float32)
    mid = (level - high).astype(jnp.bfloat16).astype(jnp.float32)
    low = level - high - mid
    row = lax.broadcasted_iota(jnp.int32, (EXTRA, LANES), 0)
    pieces = jnp.where(row == 0, high, jnp.where(row == 1, mid, low))
    return jnp.concatenate([result, pieces], axis=0).astype(jnp.bfloat16)


def unpacked(block):
    pieces = block[DH:, :].astype(jnp.float32)
    return block[:DH, :].astype(jnp.float32), (pieces[0:1] + pieces[1:2]) + pieces[2:3]


def merged(parts):
    best = functools.reduce(jnp.maximum, [level for _, level in parts])
    numerator, denominator = 0.0, 0.0
    for result, level in parts:
        share = jnp.exp2(level - best)
        numerator = numerator + result * share
        denominator = denominator + share
    return numerator / denominator, best + jnp.log2(denominator)


def own_kernel(q, qk, qv, bias, k, v, top_ref, total_ref, keys, values, sems):
    copies = fetch([(k, v)], (keys, values), sems)
    rows = stacked(q)
    scores = scores_of(rows, qk[...]) + jnp.concatenate([bias[...]] * GROUP, axis=0)
    top, total = add_block(
        jnp.full((LANES, DH), FLOOR, jnp.float32),
        jnp.zeros((LANES, 2 * DH), jnp.float32),
        scores,
        jnp.concatenate([qv[...], jnp.ones((ROWS, DH), jnp.bfloat16)], axis=1),
    )
    for copy in copies:
        copy.wait()
    top, total = add_block(top, total, scores_of(rows, keys[0]), values[0])
    top_ref[...] = top
    total_ref[...] = total


def others_kernel(q0, q1, q2, ka, va, kb, vb, out, keys, values, rows, sems):
    copies = fetch([(ka, va), (kb, vb)], (keys, values), sems)
    for i, ref in enumerate((q0, q1, q2)):
        rows[i] = stacked(ref)
    for copy in copies:
        copy.wait()

    def step(i, _):
        top = jnp.full((LANES, DH), FLOOR, jnp.float32)
        total = jnp.zeros((LANES, 2 * DH), jnp.float32)
        for block in range(2):
            top, total = add_block(top, total, scores_of(rows[i], keys[block]), values[block])
        out[i] = packed(*finish(top, total))
        return 0

    lax.fori_loop(0, 3, step, 0)


def pair_kernel(q0, q1, q2, first, ka, va, kb, vb, p0, p1, p2, keys, values, rows, out, sems):
    others_kernel(q0, q1, q2, ka, va, kb, vb, out, keys, values, rows, sems)
    for i, ref in enumerate((p0, p1, p2)):
        ref[0] = first[i]
        ref[1] = out[i]


def near_kernel(live, q, qx, top_in, total_in, ka, va, kb, vb, result_ref, level_ref, keys, values, sems):
    copies = fetch([(ka, va), (kb, vb)], (keys, values), sems)
    own, far = stacked(q), stacked(qx)
    for copy in copies:
        copy.wait()
    top, total = add_block(top_in[...], total_in[...], scores_of(own, keys[1]), values[1])
    result, level = finish(top, total)
    slot = lax.broadcasted_iota(jnp.int32, (1, LANES), 1) % ROWS
    alive = slot < live[0]
    result_ref[0] = jnp.where(alive, result, 0.0)
    level_ref[0] = jnp.broadcast_to(jnp.where(alive, level, DEAD), (8, LANES))
    top = jnp.full((LANES, DH), FLOOR, jnp.float32)
    total = jnp.zeros((LANES, 2 * DH), jnp.float32)
    for block in range(2):
        top, total = add_block(top, total, scores_of(far, keys[block]), values[block])
    result, level = finish(top, total)
    result_ref[1] = result
    level_ref[1] = jnp.broadcast_to(level, (8, LANES))


def merge_z_kernel(result, level, r0, r1, r2, result_ref, level_ref, out):
    for i in range(2):
        parts = [(result[i], level[i, :1])] + [unpacked(r[i]) for r in (r0, r1, r2)]
        whole, height = merged(parts)
        result_ref[i] = whole
        level_ref[i] = jnp.broadcast_to(height, (8, LANES))
        out[i] = packed(whole, height)


def merge_x_kernel(result, level, other, att):
    for i in range(2):
        whole, _ = merged([(result[i], level[i, :1]), unpacked(other[1 - i])])
        rows = whole.T.astype(jnp.bfloat16)
        for head in range(GROUP):
            att[i, :, head * DH : (head + 1) * DH] = rows[head * ROWS : (head + 1) * ROWS, :]


def project_kernel(index, a0, a1, a2, a3, wa, wb, out, rows):
    for i, ref in enumerate((a0, a1, a2, a3)):
        for j in range(2):
            rows[(2 * i + j) * ROWS : (2 * i + j + 1) * ROWS, :] = ref[j]
    width = wa.shape[1]
    xh, z = index[0] // (Z * CORE), (index[0] // CORE) % Z
    slots = [((xh + dx) % XH) * Z + (z + Z - dz) % Z for dz in (0,) + FAR for dx in range(XH)]
    for side, w in enumerate((wa, wb)):
        terms = jnp.dot(rows[...], w[...], preferred_element_type=jnp.float32).astype(jnp.bfloat16)
        for i in range(8):
            out[slots[i], :, side * width : (side + 1) * width] = terms[i * ROWS : (i + 1) * ROWS, :]


def sum_kernel(terms, mine, other, *, width):
    acc = terms[0].astype(jnp.float32)
    for i in range(1, terms.shape[0]):
        acc = acc + terms[i].astype(jnp.float32)
    acc = acc.astype(jnp.bfloat16)
    mine[...] = acc[:, :width]
    other[...] = acc[:, width:]


def call(kernel, outs, scratch=(), flops=0, **kwargs):
    return pl.pallas_call(
        kernel,
        out_shape=tuple(jax.ShapeDtypeStruct(s, d) for s, d in outs),
        scratch_shapes=list(scratch),
        compiler_params=pltpu.CompilerParams(vmem_limit_bytes=VMEM_LIMIT),
        cost_estimate=pl.CostEstimate(flops=flops, bytes_accessed=1 << 20, transcendentals=0),
        **kwargs,
    )


def shards(
    queries,
    question_keys,
    question_values,
    question_ids,
    live_rows,
    prefix_keys,
    prefix_values,
    out_weight,
):
    f32, bf16 = jnp.float32, jnp.bfloat16
    index = lax.axis_index("blk")
    core = index % CORE
    positions = prefix_keys.shape[0]
    vmem = pl.BlockSpec(memory_space=pltpu.VMEM)
    smem = pl.BlockSpec(memory_space=pltpu.SMEM)
    hbm = pl.BlockSpec(memory_space=pl.ANY)
    owner_flops = 8 * LANES * positions * DH

    def kv_scratch(blocks):
        return [
            pltpu.VMEM((blocks, positions, DH), bf16),
            pltpu.VMEM((blocks, positions, 2 * DH), bf16),
        ]

    q_x = moved(queries, xh=1)
    q_z = [moved(queries, z=z) for z in FAR]
    keys_c = moved(prefix_keys, c=1)
    values_c = moved(prefix_values, c=1)

    row = jnp.arange(ROWS, dtype=jnp.int32)
    allowed = (question_ids[:, None] == question_ids[None, :]) & (row[None, :] <= row[:, None])
    bias = jnp.where(allowed, 0.0, FLOOR).astype(f32)
    top, total = call(
        own_kernel,
        [((LANES, DH), f32), ((LANES, 2 * DH), f32)],
        kv_scratch(1) + [pltpu.SemaphoreType.DMA((2,))],
        flops=owner_flops,
        in_specs=[vmem] * 4 + [hbm] * 2,
    )(queries, question_keys, question_values, bias, prefix_keys, prefix_values)

    q_xz = [moved(q_x, z=z) for z in FAR]
    part = (DH + EXTRA, LANES)
    rows = pltpu.VMEM((3, LANES, DH), bf16)
    sems = pltpu.SemaphoreType.DMA((4,))
    kv = (prefix_keys, prefix_values, keys_c, values_c)
    q_z[0] = after(q_z[0], q_x)
    (first,) = call(
        others_kernel,
        [((3,) + part, bf16)],
        kv_scratch(2) + [rows, sems],
        flops=6 * owner_flops,
        in_specs=[vmem] * 3 + [hbm] * 4,
    )(*q_z, *kv)
    pairs = call(
        pair_kernel,
        [((2,) + part, bf16)] * 3,
        kv_scratch(2) + [rows, pltpu.VMEM((3,) + part, bf16), sems],
        flops=6 * owner_flops,
        in_specs=[vmem] * 4 + [hbm] * 4,
    )(*q_xz, first, *kv)
    back = [moved(pair, z=-z) for pair, z in zip(pairs, FAR)]
    result, level = call(
        near_kernel,
        [((2, DH, LANES), f32), ((2, 8, LANES), f32)],
        kv_scratch(2) + [sems],
        flops=3 * owner_flops,
        in_specs=[smem] + [vmem] * 4 + [hbm] * 4,
    )(live_rows, queries, after(q_x, *pairs), top, total, *kv)
    result, level, pair = call(
        merge_z_kernel,
        [((2, DH, LANES), f32), ((2, 8, LANES), f32), ((2,) + part, bf16)],
    )(result, level, *back)
    (att,) = call(merge_x_kernel, [((2, ROWS, GROUP * DH), bf16)])(
        result, level, moved(pair, xh=1)
    )

    weight_c = moved(after(out_weight, top), c=1)
    held = [att] + [moved(att, z=z) for z in FAR]
    width = out_weight.shape[1]
    (terms,) = call(
        project_kernel,
        [((8, ROWS, CORE * width), bf16)],
        [pltpu.VMEM((8 * ROWS, GROUP * DH), bf16)],
        in_specs=[smem] + [vmem] * 6,
    )(index.reshape(1), *held, out_weight, weight_c)
    gathered = lax.all_to_all(terms, "head", 0, 0, tiled=True)
    mine, other = call(
        functools.partial(sum_kernel, width=width),
        [((ROWS, width), bf16), ((ROWS, width), bf16)],
    )(gathered)
    theirs = moved(other, c=1)
    return jnp.where(
        core == 0,
        jnp.concatenate([mine, theirs], axis=0),
        jnp.concatenate([theirs, mine], axis=0),
    )


def solution(mesh):
    return jax.shard_map(
        shards,
        mesh=mesh,
        in_specs=(
            P("blk", "head"),
            P("blk", "head"),
            P("blk", "head"),
            P("blk"),
            P("blk"),
            P("blk", "head"),
            P("blk", "head"),
            P("head", "blk"),
        ),
        out_specs=P("head", "blk"),
        check_vma=False,
    )
```

time: 413 us -> 114 us (0.28)
  waiting for transfers between devices: 327 us -> 22.9 us
  Pallas kernels: 0 us -> 34.3 us
  matrix products: 34 us -> 0 us
  starting transfers between devices: 13.9 us -> 33.1 us
  blocking collectives: 0 us -> 18.1 us
  other arithmetic: 17 us -> 1.48 us
  between operations: 14.2 us -> 0.82 us
    ppermute x30 -> x18, waiting for transfers between devices: 216 us -> 22.9 us  [moved(): return lax.ppermute(array, 'blk', pairs)]
    all_gather x1 -> x0, waiting for transfers between devices: 60.5 us -> none  [shards(): lax.all_gather(attention, 'blk', axis=0, tiled=True)]
    reduce_scatter x1 -> x0, waiting for transfers between devices: 50.8 us -> none  [shards(): lax.psum_scatter(terms, 'head', scatter_dimension=0, tiled=True)]
    pallas_call x0 -> x8, Pallas kernels: none -> 34.3 us  [the longest x1 11.5 us: shards(): call(pair_kernel, [((2,) + part, bf16)] * 3, kv_scratch(2) + [rows, pltpu...]
    dot_general x35 -> x0, matrix products: 34 us -> none  [the longest x17 16.2 us: block_partial(): jnp.einsum('kgqp,pkd->kgqd', weights, value_heads, preferred_element_type...]
    ppermute x30 -> x18, starting transfers between devices: 13.9 us -> 33.1 us  [moved(): return lax.ppermute(array, 'blk', pairs)]
    all_to_all x0 -> x1, blocking collectives: none -> 18.1 us  [shards(): gathered = lax.all_to_all(terms, 'head', 0, 0, tiled=True)]
    reduce_sum x17 -> x0, other arithmetic: 13.2 us -> none  [block_partial(): totals = jnp.sum(weights, axis=-1, dtype=jnp.float32)]
  transfers between devices with their start and end apart: 32 -> 18, of which waited for: 20 -> 7; matrix products, arithmetic and copies ran while one was open for 6% -> 1% of each run, Pallas kernels for 0% -> 28%
where the time goes in v2:
time: 114 us
  Pallas kernels  34.3 us (30%)
  starting transfers between devices  33.1 us (29%)
  waiting for transfers between devices  22.9 us (20%)
  blocking collectives  18.1 us (16%)
  local copies, waits for them, and re-layouts  3 us (3%)
  other arithmetic  1.48 us (1%)
    ppermute x18, starting transfers between devices, moved(): return lax.ppermute(array, 'blk', pairs)  33.1 us
    ppermute x18, waiting for transfers between devices, moved(): return lax.ppermute(array, 'blk', pairs)  22.9 us
    all_to_all x1, blocking collectives, shards(): gathered = lax.all_to_all(terms, 'head', 0, 0, tiled=True)  18.1 us
    pallas_call x1, Pallas kernels, shards(): call(pair_kernel, [((2,) + part, bf16)] * 3, kv_scratch(2) + [rows, pltpu...  11.5 us
    pallas_call x1, Pallas kernels, shards(): call(others_kernel, [((3,) + part, bf16)], kv_scratch(2) + [rows, sems],...  11.5 us
    pallas_call x1, Pallas kernels, shards(): call(near_kernel, [((2, DH, LANES), f32), ((2, 8, LANES), f32)], kv_scrat...  5.29 us
    unnamed x18, local copies, waits for them, and re-layouts  3 us
    pallas_call x1, Pallas kernels, shards(): call(own_kernel, [((LANES, DH), f32), ((LANES, 2 * DH), f32)], kv_scratch...  2.84 us
  transfers between devices with their start and end apart: 18, of which 7 were waited for; matrix products, arithmetic and copies ran while one was open for 1% of the time, Pallas kernels for 28%

profile of v2, /device:TPU:1, one launch (start us, length us, event | category | flops | bytes accessed | tf_op | source)
XLA Modules:
  0.0 113.7 jit_solution(2764837480992133511)
XLA Ops:
  0.0 0.0 copy-start.7
  0.0 0.0 copy-start.6
  0.0 1.4 %collective-permute-start.7 = (bf16[2048,128]{1,0:T(8,128)(2,1)}, bf16[2048,128]{1,0:T(8,128)(2,1)S(1)}, u32[]{:S(2)}, u32[]{:S(2)}) collective-permute-start(bf16[2048,128]{1,0:T(8,128)(2,1)} %ka.5), channel_id=1, source_target_pairs={{0,8},{8,0},{16,24},{24,16},{32,40},{40,32},{48,56},{56,48},{64,72... | collective-permute-start | bytes 1572872 | tf_op jit(solution)/shard_map/ppermute | solution.py:29
  1.4 0.0 collective-permute-start.8
  1.4 2.9 %collective-permute-start = (bf16[64,1024]{1,0:T(8,128)(2,1)}, bf16[64,1024]{1,0:T(8,128)(2,1)S(1)}, u32[]{:S(2)}, u32[]{:S(2)}) collective-permute-start(bf16[64,1024]{1,0:T(8,128)(2,1)} %q.3), channel_id=1, source_target_pairs={{0,64},{8,72},{16,80},{24,88},{32,96},{40,104},{48,112},{56,120},{... | collective-permute-start | bytes 393224 | tf_op jit(solution)/shard_map/ppermute | solution.py:29
  4.3 1.6 %collective-permute-start.4 = (bf16[64,1024]{1,0:T(8,128)(2,1)}, bf16[64,1024]{1,0:T(8,128)(2,1)S(1)}, u32[]{:S(2)}, u32[]{:S(2)}) collective-permute-start(bf16[64,1024]{1,0:T(8,128)(2,1)} %q.3), channel_id=1, source_target_pairs={{0,16},{8,24},{16,32},{24,40},{32,48},{40,56},{48,0},{56,8},{64,80... | collective-permute-start | bytes 393224 | tf_op jit(solution)/shard_map/ppermute | solution.py:29
  6.0 2.1 %collective-permute-start.5 = (bf16[64,1024]{1,0:T(8,128)(2,1)}, bf16[64,1024]{1,0:T(8,128)(2,1)S(1)}, u32[]{:S(2)}, u32[]{:S(2)}) collective-permute-start(bf16[64,1024]{1,0:T(8,128)(2,1)} %q.3), channel_id=1, source_target_pairs={{0,48},{8,56},{16,0},{24,8},{32,16},{40,24},{48,32},{56,40},{64,11... | collective-permute-start | bytes 393224 | tf_op jit(solution)/shard_map/ppermute | solution.py:29
  8.1 0.0 collective-permute-done.qx
  8.1 3.5 %collective-permute-start.6 = (bf16[64,1024]{1,0:T(8,128)(2,1)}, bf16[64,1024]{1,0:T(8,128)(2,1)S(1)}, u32[]{:S(2)}, u32[]{:S(2)}) collective-permute-start(bf16[64,1024]{1,0:T(8,128)(2,1)} %q.3), channel_id=1, source_target_pairs={{0,32},{8,40},{16,48},{24,56},{32,0},{40,8},{48,16},{56,24},{64,96... | collective-permute-start | bytes 393224 | tf_op jit(solution)/shard_map/ppermute | solution.py:29
  11.6 0.8 fusion.1.bias
  13.0 0.0 copy-done.7
  13.0 0.0 copy-done.6
  13.0 0.0 copy-start.1
  13.1 1.0 copy-done.1
  14.1 0.0 copy-start.3
  14.1 1.0 copy-done.3
  15.1 0.9 copy-done.5
  16.0 0.0 copy-start
  16.0 0.0 copy-start.2
  16.0 0.0 copy-start.4
  16.0 2.8 %shard_map.84 = (f32[512,128]{1,0:T(8,128)S(1)}, f32[512,256]{1,0:T(8,128)S(1)}) custom-call(bf16[64,1024]{1,0:T(8,128)(2,1)S(1)} %copy-done.5, bf16[64,128]{1,0:T(8,128)(2,1)S(1)} %copy-done.6, bf16[64,128]{1,0:T(8,128)(2,1)S(1)} %copy-done.7, f32[64,64]{1,0:T(8,128)S(1)} %fusion.1.bias, bf16[2048,128]{1,0:T(8,128)(2,1)S(1)} %copy-done.1, ...), custom_call_target="tpu_custom_call" | custom-call | flops 1073741824 | bytes 1048576 | tf_op jit(solution)/shard_map/pallas_call | solution.py:249
  18.9 0.0 collective-permute-done.4.q0
  18.9 0.0 copy-done
  18.9 1.6 %collective-permute-start.16 = (bf16[1024,512]{1,0:T(8,128)(2,1)S(1)}, bf16[1024,512]{1,0:T(8,128)(2,1)S(1)}, u32[]{:S(2)}, u32[]{:S(2)}) collective-permute-start(bf16[1024,512]{1,0:T(8,128)(2,1)S(1)} %copy-done), channel_id=1, source_target_pairs={{0,8},{8,0},{16,24},{24,16},{32,40},{40,32},{48,56},{56,48},{64,72... | collective-permute-start | bytes 3145736 | tf_op jit(solution)/shard_map/ppermute | solution.py:29
  20.5 0.0 collective-permute-done.5.q1
  20.5 0.7 collective-permute-start.1
  21.3 0.0 collective-permute-done.6.q2
  21.3 1.9 %collective-permute-start.2 = (bf16[64,1024]{1,0:T(8,128)(2,1)S(1)}, bf16[64,1024]{1,0:T(8,128)(2,1)S(1)}, u32[]{:S(2)}, u32[]{:S(2)}) collective-permute-start(bf16[64,1024]{1,0:T(8,128)(2,1)S(1)} %collective-permute-done.qx), channel_id=1, source_target_pairs={{0,48},{8,56},{16,0},{24,8},{32,16},{40,24},{48,32},{56,40},{64,11... | collective-permute-start | bytes 393224 | tf_op jit(solution)/shard_map/ppermute | solution.py:29
  23.2 0.0 collective-permute-done.7.kb
  23.2 0.0 collective-permute-start.3
  23.2 0.0 collective-permute-done.8.vb
  23.2 0.0 copy-done.2
  23.3 0.0 copy-done.4
  23.3 11.5 %shard_map.82.first = bf16[3,144,512]{2,1,0:T(8,128)(2,1)S(1)} custom-call(bf16[64,1024]{1,0:T(8,128)(2,1)S(1)} %collective-permute-done.4.q0, bf16[64,1024]{1,0:T(8,128)(2,1)S(1)} %collective-permute-done.5.q1, bf16[64,1024]{1,0:T(8,128)(2,1)S(1)} %collective-permute-done.6.q2, bf16[2048,128]{1,0:T(8,128)(2,1)S(1)} %copy-done.2, ...), custom_call_target="tpu_custom_call" | custom-call | flops 6442450944 | bytes 1048576 | tf_op jit(solution)/shard_map/pallas_call | solution.py:263
  34.8 0.0 collective-permute-done.1.q0
  34.8 0.0 collective-permute-done.2.q1
  34.8 0.0 collective-permute-done.3.q2
  34.8 11.5 %shard_map.83 = (bf16[2,144,512]{2,1,0:T(8,128)(2,1)S(1)}, bf16[2,144,512]{2,1,0:T(8,128)(2,1)S(1)}, bf16[2,144,512]{2,1,0:T(8,128)(2,1)S(1)}) custom-call(bf16[64,1024]{1,0:T(8,128)(2,1)S(1)} %collective-permute-done.1.q0, bf16[64,1024]{1,0:T(8,128)(2,1)S(1)} %collective-permute-done.2.q1, bf16[64,1024]{1,0:T(8,128)(2,1)S(1)} %collective-permute-done.3.q2, ...), custom_call_target="tpu_custom_call" | custom-call | flops 6442450944 | bytes 1048576 | tf_op jit(solution)/shard_map/pallas_call | solution.py:270
  46.4 0.9 collective-permute-start.10
  47.3 2.3 %collective-permute-start.11 = (bf16[2,144,512]{2,1,0:T(8,128)(2,1)S(1)}, bf16[2,144,512]{2,1,0:T(8,128)(2,1)S(1)}, u32[]{:S(2)}, u32[]{:S(2)}) collective-permute-start(bf16[2,144,512]{2,1,0:T(8,128)(2,1)S(1)} %get-tuple-element.23), channel_id=1, source_target_pairs={{0,32},{8,40},{16,48},{24,56},{32,0},{40,8},{48,16},{56,24},{64,96... | collective-permute-start | bytes 884744 | tf_op jit(solution)/shard_map/ppermute | solution.py:29
  49.5 1.9 %collective-permute-start.9 = (bf16[2,144,512]{2,1,0:T(8,128)(2,1)S(1)}, bf16[2,144,512]{2,1,0:T(8,128)(2,1)S(1)}, u32[]{:S(2)}, u32[]{:S(2)}) collective-permute-start(bf16[2,144,512]{2,1,0:T(8,128)(2,1)S(1)} %get-tuple-element.21), channel_id=1, source_target_pairs={{0,48},{8,56},{16,0},{24,8},{32,16},{40,24},{48,32},{56,40},{64,11... | collective-permute-start | bytes 884744 | tf_op jit(solution)/shard_map/ppermute | solution.py:29
  51.4 5.3 %shard_map.85 = (f32[2,128,512]{2,1,0:T(8,128)S(1)}, f32[2,8,512]{2,1,0:T(8,128)S(1)}) custom-call(s32[1]{0:T(128)S(6)} %copy.9.live, bf16[64,1024]{1,0:T(8,128)(2,1)S(1)} %copy-done.5, bf16[64,1024]{1,0:T(8,128)(2,1)S(1)} %collective-permute-done.qx, f32[512,128]{1,0:T(8,128)S(1)} %get-tuple-element.25.top_in, f32[512,256]{1,0:T(8,128)S(1)} %get-tuple-element.26.total_in, ...), custom_call_target="tpu_custom_call" | custom-call | flops 3221225472 | bytes 1048576 | tf_op jit(solution)/shard_map/pallas_call | solution.py:278
  56.8 0.0 collective-permute-done.10.r1
  56.8 5.2 %collective-permute-done.11.r2 = bf16[2,144,512]{2,1,0:T(8,128)(2,1)S(1)} collective-permute-done((bf16[2,144,512]{2,1,0:T(8,128)(2,1)S(1)}, bf16[2,144,512]{2,1,0:T(8,128)(2,1)S(1)}, u32[]{:S(2)}, u32[]{:S(2)}) %collective-permute-start.11) | collective-permute-done | bytes 294944 | tf_op jit(solution)/shard_map/ppermute | solution.py:29
  62.0 0.5 collective-permute-done.9.r0
  62.4 0.3 shard_map.86
  62.7 2.8 %collective-permute-start.12 = (bf16[2,144,512]{2,1,0:T(8,128)(2,1)S(1)}, bf16[2,144,512]{2,1,0:T(8,128)(2,1)S(1)}, u32[]{:S(2)}, u32[]{:S(2)}) collective-permute-start(bf16[2,144,512]{2,1,0:T(8,128)(2,1)S(1)} %get-tuple-element.31), channel_id=1, source_target_pairs={{0,64},{8,72},{16,80},{24,88},{32,96},{40,104},{48,112},{56,120},{... | collective-permute-start | bytes 884744 | tf_op jit(solution)/shard_map/ppermute | solution.py:29
  65.6 5.7 %collective-permute-done.12.other = bf16[2,144,512]{2,1,0:T(8,128)(2,1)S(1)} collective-permute-done((bf16[2,144,512]{2,1,0:T(8,128)(2,1)S(1)}, bf16[2,144,512]{2,1,0:T(8,128)(2,1)S(1)}, u32[]{:S(2)}, u32[]{:S(2)}) %collective-permute-start.12) | collective-permute-done | bytes 294944 | tf_op jit(solution)/shard_map/ppermute | solution.py:29
  71.3 0.2 shard_map.87.a0
  71.5 1.7 %collective-permute-start.13 = (bf16[2,64,1024]{2,1,0:T(8,128)(2,1)S(1)}, bf16[2,64,1024]{2,1,0:T(8,128)(2,1)S(1)}, u32[]{:S(2)}, u32[]{:S(2)}) collective-permute-start(bf16[2,64,1024]{2,1,0:T(8,128)(2,1)S(1)} %shard_map.87.a0), channel_id=1, source_target_pairs={{0,16},{8,24},{16,32},{24,40},{32,48},{40,56},{48,0},{56,8},{64,80... | collective-permute-start | bytes 786440 | tf_op jit(solution)/shard_map/ppermute | solution.py:29
  73.2 3.0 %collective-permute-start.14 = (bf16[2,64,1024]{2,1,0:T(8,128)(2,1)S(1)}, bf16[2,64,1024]{2,1,0:T(8,128)(2,1)S(1)}, u32[]{:S(2)}, u32[]{:S(2)}) collective-permute-start(bf16[2,64,1024]{2,1,0:T(8,128)(2,1)S(1)} %shard_map.87.a0), channel_id=1, source_target_pairs={{0,48},{8,56},{16,0},{24,8},{32,16},{40,24},{48,32},{56,40},{64,11... | collective-permute-start | bytes 786440 | tf_op jit(solution)/shard_map/ppermute | solution.py:29
  76.2 1.1 collective-permute-start.15
  77.3 0.0 collective-permute-done.16.wb
  77.3 0.0 copy-start.8
  77.3 4.1 %collective-permute-done.13.a1 = bf16[2,64,1024]{2,1,0:T(8,128)(2,1)S(1)} collective-permute-done((bf16[2,64,1024]{2,1,0:T(8,128)(2,1)S(1)}, bf16[2,64,1024]{2,1,0:T(8,128)(2,1)S(1)}, u32[]{:S(2)}, u32[]{:S(2)}) %collective-permute-start.13) | collective-permute-done | bytes 262176 | tf_op jit(solution)/shard_map/ppermute | solution.py:29
  81.4 0.8 collective-permute-done.14.a2
  82.1 5.8 %collective-permute-done.15.a3 = bf16[2,64,1024]{2,1,0:T(8,128)(2,1)S(1)} collective-permute-done((bf16[2,64,1024]{2,1,0:T(8,128)(2,1)S(1)}, bf16[2,64,1024]{2,1,0:T(8,128)(2,1)S(1)}, u32[]{:S(2)}, u32[]{:S(2)}) %collective-permute-start.15) | collective-permute-done | bytes 262176 | tf_op jit(solution)/shard_map/ppermute | solution.py:29
  87.9 0.0 copy-done.8
  87.9 2.5 %shard_map.88 = bf16[8,64,1024]{2,1,0:T(8,128)(2,1)S(1)} custom-call(s32[1]{0:T(128)} %bitcast.index, bf16[2,64,1024]{2,1,0:T(8,128)(2,1)S(1)} %shard_map.87.a0, bf16[2,64,1024]{2,1,0:T(8,128)(2,1)S(1)} %collective-permute-done.13.a1, bf16[2,64,1024]{2,1,0:T(8,128)(2,1)S(1)} %collective-permute-done.14.a2, ...), custom_call_target="tpu_custom_call" | custom-call | bytes 1048576 | tf_op jit(solution)/shard_map/pallas_call | solution.py:296
  90.4 18.1 %all_to_all.5.terms = bf16[8,64,1024]{2,1,0:T(8,128)(2,1)S(1)} all-to-all(bf16[8,64,1024]{2,1,0:T(8,128)(2,1)S(1)} %shard_map.88), channel_id=1, replica_groups=mesh['blk'=16,'head'=8] {'head'}, dimensions={0} | all-to-all | bytes 2097152 | tf_op jit(solution)/shard_map/all_to_all | solution.py:302
  108.5 0.1 shard_map.89
  108.6 3.5 %collective-permute-start.17 = (bf16[64,512]{1,0:T(8,128)(2,1)S(1)}, bf16[64,512]{1,0:T(8,128)(2,1)S(1)}, u32[]{:S(2)}, u32[]{:S(2)}) collective-permute-start(bf16[64,512]{1,0:T(8,128)(2,1)S(1)} %get-tuple-element.34), channel_id=1, source_target_pairs={{0,8},{8,0},{16,24},{24,16},{32,40},{40,32},{48,56},{56,48},{64,72... | collective-permute-start | bytes 196616 | tf_op jit(solution)/shard_map/ppermute | solution.py:29
  112.2 0.9 collective-permute-done.17
  113.1 0.7 maximum_select_fusion
  (1 shorter events, 0.0 us)
Async XLA Ops:
  0.0 13.0 %copy-start.7 = (bf16[64,128]{1,0:T(8,128)(2,1)S(1)}, bf16[64,128]{1,0:T(8,128)(2,1)}, u32[]{:S(2)}) copy-start(bf16[64,128]{1,0:T(8,128)(2,1)} %qv.1) | copy-start | bytes 49156
  0.0 13.0 %copy-start.6 = (bf16[64,128]{1,0:T(8,128)(2,1)S(1)}, bf16[64,128]{1,0:T(8,128)(2,1)}, u32[]{:S(2)}) copy-start(bf16[64,128]{1,0:T(8,128)(2,1)} %qk.1) | copy-start | bytes 49156
  0.0 23.2 %collective-permute-start.7 = (bf16[2048,128]{1,0:T(8,128)(2,1)}, bf16[2048,128]{1,0:T(8,128)(2,1)S(1)}, u32[]{:S(2)}, u32[]{:S(2)}) collective-permute-start(bf16[2048,128]{1,0:T(8,128)(2,1)} %ka.5), channel_id=1, source_target_pairs={{0,8},{8,0},{16,24},{24,16},{32,40},{40,32},{48,56},{56,48},{64,72... | collective-permute-start | bytes 1572872 | tf_op jit(solution)/shard_map/ppermute | solution.py:29
  1.4 21.8 %collective-permute-start.8 = (bf16[2048,128]{1,0:T(8,128)(2,1)}, bf16[2048,128]{1,0:T(8,128)(2,1)S(1)}, u32[]{:S(2)}, u32[]{:S(2)}) collective-permute-start(bf16[2048,128]{1,0:T(8,128)(2,1)} %va.5), channel_id=1, source_target_pairs={{0,8},{8,0},{16,24},{24,16},{32,40},{40,32},{48,56},{56,48},{64,72... | collective-permute-start | bytes 1572872 | tf_op jit(solution)/shard_map/ppermute | solution.py:29
  1.4 6.7 %collective-permute-start = (bf16[64,1024]{1,0:T(8,128)(2,1)}, bf16[64,1024]{1,0:T(8,128)(2,1)S(1)}, u32[]{:S(2)}, u32[]{:S(2)}) collective-permute-start(bf16[64,1024]{1,0:T(8,128)(2,1)} %q.3), channel_id=1, source_target_pairs={{0,64},{8,72},{16,80},{24,88},{32,96},{40,104},{48,112},{56,120},{... | collective-permute-start | bytes 393224 | tf_op jit(solution)/shard_map/ppermute | solution.py:29
  4.3 14.6 %collective-permute-start.4 = (bf16[64,1024]{1,0:T(8,128)(2,1)}, bf16[64,1024]{1,0:T(8,128)(2,1)S(1)}, u32[]{:S(2)}, u32[]{:S(2)}) collective-permute-start(bf16[64,1024]{1,0:T(8,128)(2,1)} %q.3), channel_id=1, source_target_pairs={{0,16},{8,24},{16,32},{24,40},{32,48},{40,56},{48,0},{56,8},{64,80... | collective-permute-start | bytes 393224 | tf_op jit(solution)/shard_map/ppermute | solution.py:29
  6.0 14.6 %collective-permute-start.5 = (bf16[64,1024]{1,0:T(8,128)(2,1)}, bf16[64,1024]{1,0:T(8,128)(2,1)S(1)}, u32[]{:S(2)}, u32[]{:S(2)}) collective-permute-start(bf16[64,1024]{1,0:T(8,128)(2,1)} %q.3), channel_id=1, source_target_pairs={{0,48},{8,56},{16,0},{24,8},{32,16},{40,24},{48,32},{56,40},{64,11... | collective-permute-start | bytes 393224 | tf_op jit(solution)/shard_map/ppermute | solution.py:29
  8.1 13.2 %collective-permute-start.6 = (bf16[64,1024]{1,0:T(8,128)(2,1)}, bf16[64,1024]{1,0:T(8,128)(2,1)S(1)}, u32[]{:S(2)}, u32[]{:S(2)}) collective-permute-start(bf16[64,1024]{1,0:T(8,128)(2,1)} %q.3), channel_id=1, source_target_pairs={{0,32},{8,40},{16,48},{24,56},{32,0},{40,8},{48,16},{56,24},{64,96... | collective-permute-start | bytes 393224 | tf_op jit(solution)/shard_map/ppermute | solution.py:29
  13.0 1.0 copy-start.1
  14.1 1.0 copy-start.3
  15.1 0.9 copy-start.5
  16.0 2.9 %copy-start = (bf16[1024,512]{1,0:T(8,128)(2,1)S(1)}, bf16[1024,512]{1,0:T(8,128)(2,1)}, u32[]{:S(2)}) copy-start(bf16[1024,512]{1,0:T(8,128)(2,1)} %wa.1) | copy-start | bytes 3145732
  16.0 7.2 %copy-start.2 = (bf16[2048,128]{1,0:T(8,128)(2,1)S(1)}, bf16[2048,128]{1,0:T(8,128)(2,1)}, u32[]{:S(2)}) copy-start(bf16[2048,128]{1,0:T(8,128)(2,1)} %ka.5) | copy-start | bytes 1572868
  16.0 7.2 %copy-start.4 = (bf16[2048,128]{1,0:T(8,128)(2,1)S(1)}, bf16[2048,128]{1,0:T(8,128)(2,1)}, u32[]{:S(2)}) copy-start(bf16[2048,128]{1,0:T(8,128)(2,1)} %va.5) | copy-start | bytes 1572868
  18.9 58.4 %collective-permute-start.16 = (bf16[1024,512]{1,0:T(8,128)(2,1)S(1)}, bf16[1024,512]{1,0:T(8,128)(2,1)S(1)}, u32[]{:S(2)}, u32[]{:S(2)}) collective-permute-start(bf16[1024,512]{1,0:T(8,128)(2,1)S(1)} %copy-done), channel_id=1, source_target_pairs={{0,8},{8,0},{16,24},{24,16},{32,40},{40,32},{48,56},{56,48},{64,72... | collective-permute-start | bytes 3145736 | tf_op jit(solution)/shard_map/ppermute | solution.py:29
  20.5 14.2 %collective-permute-start.1 = (bf16[64,1024]{1,0:T(8,128)(2,1)S(1)}, bf16[64,1024]{1,0:T(8,128)(2,1)S(1)}, u32[]{:S(2)}, u32[]{:S(2)}) collective-permute-start(bf16[64,1024]{1,0:T(8,128)(2,1)S(1)} %collective-permute-done.qx), channel_id=1, source_target_pairs={{0,16},{8,24},{16,32},{24,40},{32,48},{40,56},{48,0},{56,8},{64,80... | collective-permute-start | bytes 393224 | tf_op jit(solution)/shard_map/ppermute | solution.py:29
  21.3 13.5 %collective-permute-start.2 = (bf16[64,1024]{1,0:T(8,128)(2,1)S(1)}, bf16[64,1024]{1,0:T(8,128)(2,1)S(1)}, u32[]{:S(2)}, u32[]{:S(2)}) collective-permute-start(bf16[64,1024]{1,0:T(8,128)(2,1)S(1)} %collective-permute-done.qx), channel_id=1, source_target_pairs={{0,48},{8,56},{16,0},{24,8},{32,16},{40,24},{48,32},{56,40},{64,11... | collective-permute-start | bytes 393224 | tf_op jit(solution)/shard_map/ppermute | solution.py:29
  23.2 11.6 %collective-permute-start.3 = (bf16[64,1024]{1,0:T(8,128)(2,1)S(1)}, bf16[64,1024]{1,0:T(8,128)(2,1)S(1)}, u32[]{:S(2)}, u32[]{:S(2)}) collective-permute-start(bf16[64,1024]{1,0:T(8,128)(2,1)S(1)} %collective-permute-done.qx), channel_id=1, source_target_pairs={{0,32},{8,40},{16,48},{24,56},{32,0},{40,8},{48,16},{56,24},{64,96... | collective-permute-start | bytes 393224 | tf_op jit(solution)/shard_map/ppermute | solution.py:29
  46.4 10.4 %collective-permute-start.10 = (bf16[2,144,512]{2,1,0:T(8,128)(2,1)S(1)}, bf16[2,144,512]{2,1,0:T(8,128)(2,1)S(1)}, u32[]{:S(2)}, u32[]{:S(2)}) collective-permute-start(bf16[2,144,512]{2,1,0:T(8,128)(2,1)S(1)} %get-tuple-element.22), channel_id=1, source_target_pairs={{0,16},{8,24},{16,32},{24,40},{32,48},{40,56},{48,0},{56,8},{64,80... | collective-permute-start | bytes 884744 | tf_op jit(solution)/shard_map/ppermute | solution.py:29
  47.3 14.7 %collective-permute-start.11 = (bf16[2,144,512]{2,1,0:T(8,128)(2,1)S(1)}, bf16[2,144,512]{2,1,0:T(8,128)(2,1)S(1)}, u32[]{:S(2)}, u32[]{:S(2)}) collective-permute-start(bf16[2,144,512]{2,1,0:T(8,128)(2,1)S(1)} %get-tuple-element.23), channel_id=1, source_target_pairs={{0,32},{8,40},{16,48},{24,56},{32,0},{40,8},{48,16},{56,24},{64,96... | collective-permute-start | bytes 884744 | tf_op jit(solution)/shard_map/ppermute | solution.py:29
  49.5 12.9 %collective-permute-start.9 = (bf16[2,144,512]{2,1,0:T(8,128)(2,1)S(1)}, bf16[2,144,512]{2,1,0:T(8,128)(2,1)S(1)}, u32[]{:S(2)}, u32[]{:S(2)}) collective-permute-start(bf16[2,144,512]{2,1,0:T(8,128)(2,1)S(1)} %get-tuple-element.21), channel_id=1, source_target_pairs={{0,48},{8,56},{16,0},{24,8},{32,16},{40,24},{48,32},{56,40},{64,11... | collective-permute-start | bytes 884744 | tf_op jit(solution)/shard_map/ppermute | solution.py:29
  62.7 8.5 %collective-permute-start.12 = (bf16[2,144,512]{2,1,0:T(8,128)(2,1)S(1)}, bf16[2,144,512]{2,1,0:T(8,128)(2,1)S(1)}, u32[]{:S(2)}, u32[]{:S(2)}) collective-permute-start(bf16[2,144,512]{2,1,0:T(8,128)(2,1)S(1)} %get-tuple-element.31), channel_id=1, source_target_pairs={{0,64},{8,72},{16,80},{24,88},{32,96},{40,104},{48,112},{56,120},{... | collective-permute-start | bytes 884744 | tf_op jit(solution)/shard_map/ppermute | solution.py:29
  71.5 9.9 %collective-permute-start.13 = (bf16[2,64,1024]{2,1,0:T(8,128)(2,1)S(1)}, bf16[2,64,1024]{2,1,0:T(8,128)(2,1)S(1)}, u32[]{:S(2)}, u32[]{:S(2)}) collective-permute-start(bf16[2,64,1024]{2,1,0:T(8,128)(2,1)S(1)} %shard_map.87.a0), channel_id=1, source_target_pairs={{0,16},{8,24},{16,32},{24,40},{32,48},{40,56},{48,0},{56,8},{64,80... | collective-permute-start | bytes 786440 | tf_op jit(solution)/shard_map/ppermute | solution.py:29
  73.2 8.9 %collective-permute-start.14 = (bf16[2,64,1024]{2,1,0:T(8,128)(2,1)S(1)}, bf16[2,64,1024]{2,1,0:T(8,128)(2,1)S(1)}, u32[]{:S(2)}, u32[]{:S(2)}) collective-permute-start(bf16[2,64,1024]{2,1,0:T(8,128)(2,1)S(1)} %shard_map.87.a0), channel_id=1, source_target_pairs={{0,48},{8,56},{16,0},{24,8},{32,16},{40,24},{48,32},{56,40},{64,11... | collective-permute-start | bytes 786440 | tf_op jit(solution)/shard_map/ppermute | solution.py:29
  76.2 11.7 %collective-permute-start.15 = (bf16[2,64,1024]{2,1,0:T(8,128)(2,1)S(1)}, bf16[2,64,1024]{2,1,0:T(8,128)(2,1)S(1)}, u32[]{:S(2)}, u32[]{:S(2)}) collective-permute-start(bf16[2,64,1024]{2,1,0:T(8,128)(2,1)S(1)} %shard_map.87.a0), channel_id=1, source_target_pairs={{0,32},{8,40},{16,48},{24,56},{32,0},{40,8},{48,16},{56,24},{64,96... | collective-permute-start | bytes 786440 | tf_op jit(solution)/shard_map/ppermute | solution.py:29
  77.3 10.6 %copy-start.8 = (bf16[1024,512]{1,0:T(8,128)(2,1)}, bf16[1024,512]{1,0:T(8,128)(2,1)S(1)}, u32[]{:S(2)}) copy-start(bf16[1024,512]{1,0:T(8,128)(2,1)S(1)} %collective-permute-done.16.wb) | copy-start | bytes 3145732
  108.6 4.4 %collective-permute-start.17 = (bf16[64,512]{1,0:T(8,128)(2,1)S(1)}, bf16[64,512]{1,0:T(8,128)(2,1)S(1)}, u32[]{:S(2)}, u32[]{:S(2)}) collective-permute-start(bf16[64,512]{1,0:T(8,128)(2,1)S(1)} %get-tuple-element.34), channel_id=1, source_target_pairs={{0,8},{8,0},{16,24},{24,16},{32,40},{40,32},{48,56},{56,48},{64,72... | collective-permute-start | bytes 196616 | tf_op jit(solution)/shard_map/ppermute | solution.py:29

commit v3 on v2

v3 whole, which is shorter than its diff:
```python
import functools

import jax
import jax.numpy as jnp
from jax import lax
from jax.experimental import pallas as pl
from jax.experimental.pallas import tpu as pltpu
from jax.sharding import PartitionSpec as P

DH = 128
GROUP = 8
ROWS = 64
LANES = GROUP * ROWS
EXTRA = 16
SCALE = DH**-0.5 * 1.4426950408889634
FLOOR = -1e30
XH, Z, CORE = 2, 4, 2
VMEM_LIMIT = 30 << 20
FAR = (1, 3, 2)


def moved(array, xh=0, z=0, c=0):
    pairs = []
    for i in range(XH * Z * CORE):
        a, b, d = i // (Z * CORE), (i // CORE) % Z, i % CORE
        to = (((a + xh) % XH) * Z + (b + z) % Z) * CORE + (d + c) % CORE
        pairs.append((i, to))
    return lax.ppermute(array, "blk", pairs)


def after(array, *others):
    return lax.optimization_barrier((array, *others))[0]


def scores_of(queries, keys):
    return lax.dot_general(
        queries, keys, (((1,), (1,)), ((), ())), preferred_element_type=jnp.float32
    )


def wide(column, width):
    return jnp.concatenate([column] * (width // column.shape[1]), axis=1)


def add_block(top, total, scores, values):
    best = jnp.maximum(top, jnp.max(scores, axis=1, keepdims=True) * SCALE)
    keys = scores.shape[1]
    at = wide(best, keys) if keys >= DH else best[:, :keys]
    weights = jnp.exp2(scores * SCALE - at).astype(jnp.bfloat16)
    part = jnp.dot(weights, values, preferred_element_type=jnp.float32)
    return best, total * wide(jnp.exp2(top - best), 2 * DH) + part


def stacked(ref):
    return jnp.concatenate([ref[:, h * DH : (h + 1) * DH] for h in range(GROUP)], axis=0)


def with_ones(values, scratch):
    scratch[:, :DH] = values[...]
    scratch[:, DH:] = jnp.ones(values.shape, values.dtype)


def finish(top, total):
    denominator = total[:, DH:]
    result = (total[:, :DH] / denominator).T
    level = (top + jnp.log2(denominator)).T[:1]
    return result, level


def packed(result, level):
    high = level.astype(jnp.bfloat16).astype(jnp.float32)
    mid = (level - high).astype(jnp.bfloat16).astype(jnp.float32)
    low = level - high - mid
    row = lax.broadcasted_iota(jnp.int32, (EXTRA, LANES), 0)
    pieces = jnp.where(row == 0, high, jnp.where(row == 1, mid, low))
    return jnp.concatenate([result, pieces], axis=0).astype(jnp.bfloat16)


def unpacked(block):
    pieces = block[DH:, :].astype(jnp.float32)
    return block[:DH, :].astype(jnp.float32), (pieces[0:1] + pieces[1:2]) + pieces[2:3]


def merged(parts):
    best = functools.reduce(jnp.maximum, [level for _, level in parts])
    numerator, denominator = 0.0, 0.0
    for result, level in parts:
        share = jnp.exp2(level - best)
        numerator = numerator + result * share
        denominator = denominator + share
    return numerator / denominator, best + jnp.log2(denominator)


def near_kernel(
    q0, q1, q2, q, qk, qv, bias, ka, va, kb, vb,
    top_out, total_out, rows, own_q, own_k, own_v, keys, values, sems,
):
    moves = [(q, own_q), (qk, own_k), (qv, own_v), (ka, keys), (va, values.at[0, :, pl.ds(0, DH)])]
    copies = [pltpu.make_async_copy(a, b, sems.at[i]) for i, (a, b) in enumerate(moves)]
    for copy in copies:
        copy.start()
    values[0, :, DH:] = jnp.ones(vb.shape, vb.dtype)
    with_ones(vb, values.at[1])
    for i, ref in enumerate((q0, q1, q2)):
        rows[i] = stacked(ref)
    for copy in copies:
        copy.wait()
    rows[3] = stacked(own_q)
    top_out[...] = jnp.full(top_out.shape, FLOOR, jnp.float32)
    total_out[...] = jnp.zeros(total_out.shape, jnp.float32)
    scores = scores_of(rows[3], own_k[...]) + jnp.concatenate([bias[...]] * GROUP, axis=0)
    top_out[3], total_out[3] = add_block(
        top_out[3],
        total_out[3],
        scores,
        jnp.concatenate([own_v[...], jnp.ones((ROWS, DH), jnp.bfloat16)], axis=1),
    )

    def step(i, _):
        first, second = scores_of(rows[i], keys[...]), scores_of(rows[i], kb[...])
        top, total = add_block(top_out[i], total_out[i], first, values[0])
        top_out[i], total_out[i] = add_block(top, total, second, values[1])
        return 0

    lax.fori_loop(0, 4, step, 0)


def far_kernel(rows, top_in, total_in, k, v, top_out, total_out, values):
    with_ones(v, values)

    def step(i, _):
        top, total = add_block(top_in[i], total_in[i], scores_of(rows[i], k[...]), values[...])
        top_out[i] = top
        total_out[i] = total
        return 0

    lax.fori_loop(0, 3, step, 0)


def last_kernel(rows, top_in, total_in, k, v, p0, p1, p2, values, out):
    with_ones(v, values)

    def step(i, _):
        top, total = add_block(top_in[i], total_in[i], scores_of(rows[i], k[...]), values[...])
        out[i] = packed(*finish(top, total))
        return 0

    lax.fori_loop(0, 3, step, 0)
    for i, ref in enumerate((p0, p1, p2)):
        ref[...] = out[i]


def own_last_kernel(rows, top, total, ka, va, kb, vb, result_ref, level_ref, values):
    with_ones(va, values.at[0])
    with_ones(vb, values.at[1])
    first, second = scores_of(rows[3], ka[...]), scores_of(rows[3], kb[...])
    top, total = add_block(top[3], total[3], first, values[0])
    top, total = add_block(top, total, second, values[1])
    result, level = finish(top, total)
    result_ref[...] = result
    level_ref[...] = jnp.broadcast_to(level, (8, LANES))


def merge_kernel(live, result, level, r0, r1, r2, att):
    parts = [(result[...], level[:1])] + [unpacked(r) for r in (r0, r1, r2)]
    whole, _ = merged(parts)
    slot = lax.broadcasted_iota(jnp.int32, (1, LANES), 1) % ROWS
    rows = jnp.where(slot < live[0], whole, 0.0).T.astype(jnp.bfloat16)
    for head in range(GROUP):
        att[:, head * DH : (head + 1) * DH] = rows[head * ROWS : (head + 1) * ROWS, :]


def project_kernel(index, a0, a1, a2, a3, a4, a5, a6, a7, wa, wb, out, rows):
    for i, ref in enumerate((a0, a1, a2, a3, a4, a5, a6, a7)):
        rows[i * ROWS : (i + 1) * ROWS, :] = ref[...]
    width = wa.shape[1]
    xh, z = index[0] // (Z * CORE), (index[0] // CORE) % Z
    slots = [((xh + dx) % XH) * Z + (z + Z - dz) % Z for dx in range(XH) for dz in (0,) + FAR]
    for side, w in enumerate((wa, wb)):
        terms = jnp.dot(rows[...], w[...], preferred_element_type=jnp.float32).astype(jnp.bfloat16)
        for i in range(8):
            out[slots[i], :, side * width : (side + 1) * width] = terms[i * ROWS : (i + 1) * ROWS, :]


def sum_kernel(terms, mine, other, *, width):
    acc = terms[0].astype(jnp.float32)
    for i in range(1, terms.shape[0]):
        acc = acc + terms[i].astype(jnp.float32)
    acc = acc.astype(jnp.bfloat16)
    mine[...] = acc[:, :width]
    other[...] = acc[:, width:]


def call(kernel, outs, scratch=(), flops=0, **kwargs):
    return pl.pallas_call(
        kernel,
        out_shape=tuple(jax.ShapeDtypeStruct(s, d) for s, d in outs),
        scratch_shapes=list(scratch),
        compiler_params=pltpu.CompilerParams(vmem_limit_bytes=VMEM_LIMIT),
        cost_estimate=pl.CostEstimate(flops=flops, bytes_accessed=1 << 20, transcendentals=0),
        **kwargs,
    )


def shards(
    queries,
    question_keys,
    question_values,
    question_ids,
    live_rows,
    prefix_keys,
    prefix_values,
    out_weight,
):
    f32, bf16 = jnp.float32, jnp.bfloat16
    index = lax.axis_index("blk")
    core = index % CORE
    positions = prefix_keys.shape[0]
    vmem = pl.BlockSpec(memory_space=pltpu.VMEM)
    smem = pl.BlockSpec(memory_space=pltpu.SMEM)
    hbm = pl.BlockSpec(memory_space=pltpu.HBM)
    block_flops = 8 * LANES * positions * DH
    part = ((DH + EXTRA, LANES), bf16)
    ones_shape = (positions, 2 * DH)

    def state(owners):
        return [((owners, LANES, DH), f32), ((owners, LANES, 2 * DH), f32)]

    keys_x = moved(prefix_keys, xh=1)
    values_x = moved(prefix_values, xh=1)
    keys_c = moved(prefix_keys, c=1)
    values_c = moved(prefix_values, c=1)
    q_z = [moved(queries, z=z) for z in FAR]
    row = jnp.arange(ROWS, dtype=jnp.int32)
    allowed = (question_ids[:, None] == question_ids[None, :]) & (row[None, :] <= row[:, None])
    bias = jnp.where(allowed, 0.0, FLOOR).astype(f32)
    top, total, rows = call(
        near_kernel,
        state(4) + [((4, LANES, DH), bf16)],
        [
            pltpu.VMEM(queries.shape, bf16),
            pltpu.VMEM(question_keys.shape, bf16),
            pltpu.VMEM(question_keys.shape, bf16),
            pltpu.VMEM((positions, DH), bf16),
            pltpu.VMEM((2,) + ones_shape, bf16),
            pltpu.SemaphoreType.DMA((5,)),
        ],
        flops=block_flops,
        in_specs=[vmem] * 3 + [hbm] * 3 + [vmem] + [hbm] * 2 + [vmem] * 2,
    )(
        *q_z, queries, question_keys, question_values, bias,
        prefix_keys, prefix_values, keys_c, values_c,
    )

    keys_x, values_x, weight, top, total = lax.optimization_barrier(
        (keys_x, values_x, out_weight, top, total)
    )
    keys_xc = moved(keys_x, c=1)
    values_xc = moved(values_x, c=1)
    weight_c = moved(weight, c=1)
    far_top, far_total = call(
        far_kernel, state(3), [pltpu.VMEM(ones_shape, bf16)], flops=3 * block_flops
    )(rows, top, total, keys_x, values_x)
    parts = call(
        last_kernel,
        [part] * 3,
        [pltpu.VMEM(ones_shape, bf16), pltpu.VMEM((3,) + part[0], bf16)],
        flops=3 * block_flops,
    )(rows, far_top, far_total, keys_xc, values_xc)
    back = [moved(p, z=-z) for p, z in zip(parts, FAR)]
    result, level = call(
        own_last_kernel,
        [((DH, LANES), f32), ((8, LANES), f32)],
        [pltpu.VMEM((2,) + ones_shape, bf16)],
        flops=2 * block_flops,
    )(after(rows, *parts), top, total, keys_x, values_x, keys_xc, values_xc)
    (att,) = call(
        merge_kernel, [((ROWS, GROUP * DH), bf16)], in_specs=[smem] + [vmem] * 5
    )(live_rows, result, level, *back)

    att_x = moved(att, xh=1)
    held = [att] + [moved(att, z=z) for z in FAR] + [att_x] + [moved(att_x, z=z) for z in FAR]
    width = out_weight.shape[1]
    (terms,) = call(
        project_kernel,
        [((8, ROWS, CORE * width), bf16)],
        [pltpu.VMEM((8 * ROWS, GROUP * DH), bf16)],
        in_specs=[smem] + [vmem] * 10,
    )(index.reshape(1), *held, out_weight, weight_c)
    gathered = lax.all_to_all(terms, "head", 0, 0, tiled=True)
    mine, other = call(
        functools.partial(sum_kernel, width=width),
        [((ROWS, width), bf16), ((ROWS, width), bf16)],
    )(gathered)
    theirs = moved(other, c=1)
    return jnp.where(
        core == 0,
        jnp.concatenate([mine, theirs], axis=0),
        jnp.concatenate([theirs, mine], axis=0),
    )


def solution(mesh):
    return jax.shard_map(
        shards,
        mesh=mesh,
        in_specs=(
            P("blk", "head"),
            P("blk", "head"),
            P("blk", "head"),
            P("blk"),
            P("blk"),
            P("blk", "head"),
            P("blk", "head"),
            P("head", "blk"),
        ),
        out_specs=P("head", "blk"),
        check_vma=False,
    )
```

time: 114 us -> 106 us (0.930)
  starting transfers between devices: 33.1 us -> 29.3 us
  Pallas kernels: 34.3 us -> 30.5 us
  blocking collectives: 18.1 us -> 16.6 us
  local copies, waits for them, and re-layouts: 3 us -> 4.42 us
    ppermute x18 -> x21, starting transfers between devices: 33.1 us -> 29.3 us  [moved(): return lax.ppermute(array, 'blk', pairs)]
    pallas_call x6 -> x5, Pallas kernels: 31.7 us -> 29.1 us  [the longest x1 11.1 us: shards(): call(near_kernel, state(4) + [((4, LANES, DH), bf16)], [pltpu.VMEM(querie...]
    all_to_all x1, blocking collectives: 18.1 us -> 16.6 us  [shards(): gathered = lax.all_to_all(terms, 'head', 0, 0, tiled=True)]
    unnamed x18 -> x12, local copies, waits for them, and re-layouts: 3 us -> 4.42 us
    pallas_call x1, Pallas kernels: 2.47 us -> 1.25 us  [shards(): call(project_kernel, [((8, ROWS, CORE * width), bf16)], [pltpu.VMEM((8 *...]
    ppermute x18 -> x21, waiting for transfers between devices: 22.9 us -> 22.7 us  [moved(): return lax.ppermute(array, 'blk', pairs)]
  transfers between devices with their start and end apart: 18 -> 21, of which waited for: 7 -> 9; matrix products, arithmetic and copies ran while one was open for 1% -> 1% of each run, Pallas kernels for 28% -> 28%
where the time goes in v3:
time: 106 us
  Pallas kernels  30.5 us (29%)
  starting transfers between devices  29.3 us (28%)
  waiting for transfers between devices  22.7 us (21%)
  blocking collectives  16.6 us (16%)
  local copies, waits for them, and re-layouts  4.42 us (4%)
  other arithmetic  1.48 us (1%)
    ppermute x21, starting transfers between devices, moved(): return lax.ppermute(array, 'blk', pairs)  29.3 us
    ppermute x21, waiting for transfers between devices, moved(): return lax.ppermute(array, 'blk', pairs)  22.7 us
    all_to_all x1, blocking collectives, shards(): gathered = lax.all_to_all(terms, 'head', 0, 0, tiled=True)  16.6 us
    pallas_call x1, Pallas kernels, shards(): call(near_kernel, state(4) + [((4, LANES, DH), bf16)], [pltpu.VMEM(querie...  11.1 us
    pallas_call x1, Pallas kernels, shards(): call(last_kernel, [part] * 3, [pltpu.VMEM(ones_shape, bf16), pltpu.VMEM((...  7.63 us
    pallas_call x1, Pallas kernels, shards(): call(far_kernel, state(3), [pltpu.VMEM(ones_shape, bf16)], flops=3 * bloc...  7.33 us
    unnamed x12, local copies, waits for them, and re-layouts  4.42 us
    pallas_call x1, Pallas kernels, shards(): call(own_last_kernel, [((DH, LANES), f32), ((8, LANES), f32)], [pltpu.VME...  2.83 us
  transfers between devices with their start and end apart: 21, of which 9 were waited for; matrix products, arithmetic and copies ran while one was open for 1% of the time, Pallas kernels for 28%

profile of v3, /device:TPU:1, one launch (start us, length us, event | category | flops | bytes accessed | tf_op | source)
XLA Modules:
  0.0 105.7 jit_solution(18164026104949639918)
XLA Ops:
  0.0 0.0 copy-start
  0.0 1.4 %collective-permute-start.3 = (bf16[2048,128]{1,0:T(8,128)(2,1)}, bf16[2048,128]{1,0:T(8,128)(2,1)S(1)}, u32[]{:S(2)}, u32[]{:S(2)}) collective-permute-start(bf16[2048,128]{1,0:T(8,128)(2,1)} %ka.1), channel_id=1, source_target_pairs={{0,8},{8,0},{16,24},{24,16},{32,40},{40,32},{48,56},{56,48},{64,72... | collective-permute-start | bytes 1572872 | tf_op jit(solution)/shard_map/ppermute | solution.py:28
  1.4 0.0 collective-permute-start.4
  1.4 1.8 %collective-permute-start = (bf16[64,1024]{1,0:T(8,128)(2,1)}, bf16[64,1024]{1,0:T(8,128)(2,1)S(1)}, u32[]{:S(2)}, u32[]{:S(2)}) collective-permute-start(bf16[64,1024]{1,0:T(8,128)(2,1)} %q.1), channel_id=1, source_target_pairs={{0,16},{8,24},{16,32},{24,40},{32,48},{40,56},{48,0},{56,8},{64,80... | collective-permute-start | bytes 393224 | tf_op jit(solution)/shard_map/ppermute | solution.py:28
  3.2 2.7 %collective-permute-start.5 = (bf16[2048,128]{1,0:T(8,128)(2,1)}, bf16[2048,128]{1,0:T(8,128)(2,1)S(1)}, u32[]{:S(2)}, u32[]{:S(2)}) collective-permute-start(bf16[2048,128]{1,0:T(8,128)(2,1)} %ka.1), channel_id=1, source_target_pairs={{0,64},{8,72},{16,80},{24,88},{32,96},{40,104},{48,112},{56,120},{... | collective-permute-start | bytes 1572872 | tf_op jit(solution)/shard_map/ppermute | solution.py:28
  6.0 0.2 collective-permute-start.6
  6.2 2.9 %collective-permute-done.q0 = bf16[64,1024]{1,0:T(8,128)(2,1)S(1)} collective-permute-done((bf16[64,1024]{1,0:T(8,128)(2,1)}, bf16[64,1024]{1,0:T(8,128)(2,1)S(1)}, u32[]{:S(2)}, u32[]{:S(2)}) %collective-permute-start) | collective-permute-done | bytes 131104 | tf_op jit(solution)/shard_map/ppermute | solution.py:28
  9.0 1.1 %collective-permute-start.1 = (bf16[64,1024]{1,0:T(8,128)(2,1)}, bf16[64,1024]{1,0:T(8,128)(2,1)S(1)}, u32[]{:S(2)}, u32[]{:S(2)}) collective-permute-start(bf16[64,1024]{1,0:T(8,128)(2,1)} %q.1), channel_id=1, source_target_pairs={{0,48},{8,56},{16,0},{24,8},{32,16},{40,24},{48,32},{56,40},{64,11... | collective-permute-start | bytes 393224 | tf_op jit(solution)/shard_map/ppermute | solution.py:28
  10.2 3.2 %collective-permute-done.1.q1 = bf16[64,1024]{1,0:T(8,128)(2,1)S(1)} collective-permute-done((bf16[64,1024]{1,0:T(8,128)(2,1)}, bf16[64,1024]{1,0:T(8,128)(2,1)S(1)}, u32[]{:S(2)}, u32[]{:S(2)}) %collective-permute-start.1) | collective-permute-done | bytes 131104 | tf_op jit(solution)/shard_map/ppermute | solution.py:28
  13.4 1.0 collective-permute-start.2
  14.4 0.8 fusion.1.bias
  15.2 4.0 %collective-permute-done.2.q2 = bf16[64,1024]{1,0:T(8,128)(2,1)S(1)} collective-permute-done((bf16[64,1024]{1,0:T(8,128)(2,1)}, bf16[64,1024]{1,0:T(8,128)(2,1)S(1)}, u32[]{:S(2)}, u32[]{:S(2)}) %collective-permute-start.2) | collective-permute-done | bytes 131104 | tf_op jit(solution)/shard_map/ppermute | solution.py:28
  19.2 0.0 collective-permute-done.3.kb
  19.2 0.0 collective-permute-done.4.vb
  19.2 0.0 copy-start.1
  19.2 1.0 copy-done.1
  20.3 0.0 copy-start.2
  20.3 1.0 copy-done.2
  21.3 0.0 copy-start.3
  21.3 0.9 copy-done.3
  22.2 0.0 copy-start.4
  22.2 0.7 copy-done.4
  22.9 0.0 copy-start.5
  22.9 0.7 copy-done.5
  23.6 11.1 %shard_map.82 = (f32[4,512,128]{2,1,0:T(8,128)S(1)}, f32[4,512,256]{2,1,0:T(8,128)S(1)}, bf16[4,512,128]{2,1,0:T(8,128)(2,1)S(1)}) custom-call(bf16[64,1024]{1,0:T(8,128)(2,1)S(1)} %collective-permute-done.q0, bf16[64,1024]{1,0:T(8,128)(2,1)S(1)} %collective-permute-done.1.q1, bf16[64,1024]{1,0:T(8,128)(2,1)S(1)} %collective-permute-done.2.q2, ...), custom_call_target="tpu_custom_call" | custom-call | flops 1073741824 | bytes 1048576 | tf_op jit(solution)/shard_map/pallas_call | solution.py:237
  34.8 0.0 collective-permute-done.5.k.ka
  34.8 0.0 collective-permute-done.6.v.va
  34.8 2.7 %collective-permute-start.7 = (bf16[2048,128]{1,0:T(8,128)(2,1)S(1)}, bf16[2048,128]{1,0:T(8,128)(2,1)S(1)}, u32[]{:S(2)}, u32[]{:S(2)}) collective-permute-start(bf16[2048,128]{1,0:T(8,128)(2,1)S(1)} %collective-permute-done.5.k.ka), channel_id=1, source_target_pairs={{0,8},{8,0},{16,24},{24,16},{32,40},{40,32},{48,56},{56,48},{64,72... | collective-permute-start | bytes 1572872 | tf_op jit(solution)/shard_map/ppermute | solution.py:28
  37.5 0.1 collective-permute-start.8
  38.3 0.0 copy-done
  38.3 0.5 collective-permute-start.19
  38.8 7.3 %shard_map.83 = (f32[3,512,128]{2,1,0:T(8,128)S(1)}, f32[3,512,256]{2,1,0:T(8,128)S(1)}) custom-call(bf16[4,512,128]{2,1,0:T(8,128)(2,1)S(1)} %get-tuple-element.35.rows, f32[4,512,128]{2,1,0:T(8,128)S(1)} %get-tuple-element.26.top_in.top, f32[4,512,256]{2,1,0:T(8,128)S(1)} %get-tuple-element.27.total_in.total, ...), custom_call_target="tpu_custom_call" | custom-call | flops 3221225472 | bytes 1048576 | tf_op jit(solution)/shard_map/pallas_call | solution.py:261
  46.1 0.0 collective-permute-done.7.k.kb
  46.1 0.0 collective-permute-done.8.v.vb
  46.1 7.6 %shard_map.84 = (bf16[144,512]{1,0:T(8,128)(2,1)S(1)}, bf16[144,512]{1,0:T(8,128)(2,1)S(1)}, bf16[144,512]{1,0:T(8,128)(2,1)S(1)}) custom-call(bf16[4,512,128]{2,1,0:T(8,128)(2,1)S(1)} %get-tuple-element.35.rows, f32[3,512,128]{2,1,0:T(8,128)S(1)} %get-tuple-element.30.top_in, f32[3,512,256]{2,1,0:T(8,128)S(1)} %get-tuple-element.31.total_in, ...), custom_call_target="tpu_custom_call" | custom-call | flops 3221225472 | bytes 1048576 | tf_op jit(solution)/shard_map/pallas_call | solution.py:264
  53.8 0.1 collective-permute-start.10
  53.9 3.9 %collective-permute-start.11 = (bf16[144,512]{1,0:T(8,128)(2,1)S(1)}, bf16[144,512]{1,0:T(8,128)(2,1)S(1)}, u32[]{:S(2)}, u32[]{:S(2)}) collective-permute-start(bf16[144,512]{1,0:T(8,128)(2,1)S(1)} %get-tuple-element.34), channel_id=1, source_target_pairs={{0,32},{8,40},{16,48},{24,56},{32,0},{40,8},{48,16},{56,24},{64,96... | collective-permute-start | bytes 442376 | tf_op jit(solution)/shard_map/ppermute | solution.py:28
  57.7 0.0 collective-permute-start.9
  57.7 2.8 %shard_map.85 = (f32[128,512]{1,0:T(8,128)S(1)}, f32[8,512]{1,0:T(8,128)S(1)}) custom-call(bf16[4,512,128]{2,1,0:T(8,128)(2,1)S(1)} %get-tuple-element.35.rows, f32[4,512,128]{2,1,0:T(8,128)S(1)} %get-tuple-element.26.top_in.top, f32[4,512,256]{2,1,0:T(8,128)S(1)} %get-tuple-element.27.total_in.total, bf16[2048,128]{1,0:T(8,128)(2,1)S(1)} %collective-permute-done.5.k.ka, ...), custom_call_target="tpu_custom_call" | custom-call | flops 2147483648 | bytes 1048576 | tf_op jit(solution)/shard_map/pallas_call | solution.py:271
  60.6 0.0 collective-permute-done.10.r1
  60.6 4.2 %collective-permute-done.11.r2 = bf16[144,512]{1,0:T(8,128)(2,1)S(1)} collective-permute-done((bf16[144,512]{1,0:T(8,128)(2,1)S(1)}, bf16[144,512]{1,0:T(8,128)(2,1)S(1)}, u32[]{:S(2)}, u32[]{:S(2)}) %collective-permute-start.11) | collective-permute-done | bytes 147488 | tf_op jit(solution)/shard_map/ppermute | solution.py:28
  64.8 0.0 collective-permute-done.9.r0
  64.8 0.2 shard_map.86.a0
  65.0 2.8 %collective-permute-start.15 = (bf16[64,1024]{1,0:T(8,128)(2,1)S(1)}, bf16[64,1024]{1,0:T(8,128)(2,1)S(1)}, u32[]{:S(2)}, u32[]{:S(2)}) collective-permute-start(bf16[64,1024]{1,0:T(8,128)(2,1)S(1)} %shard_map.86.a0), channel_id=1, source_target_pairs={{0,64},{8,72},{16,80},{24,88},{32,96},{40,104},{48,112},{56,120},{... | collective-permute-start | bytes 393224 | tf_op jit(solution)/shard_map/ppermute | solution.py:28
  67.8 0.5 collective-permute-start.12
  68.3 2.2 %collective-permute-start.13 = (bf16[64,1024]{1,0:T(8,128)(2,1)S(1)}, bf16[64,1024]{1,0:T(8,128)(2,1)S(1)}, u32[]{:S(2)}, u32[]{:S(2)}) collective-permute-start(bf16[64,1024]{1,0:T(8,128)(2,1)S(1)} %shard_map.86.a0), channel_id=1, source_target_pairs={{0,48},{8,56},{16,0},{24,8},{32,16},{40,24},{48,32},{56,40},{64,11... | collective-permute-start | bytes 393224 | tf_op jit(solution)/shard_map/ppermute | solution.py:28
  70.5 0.8 collective-permute-start.14
  71.3 0.0 collective-permute-done.15.a4
  71.3 0.9 collective-permute-start.16
  72.2 0.7 collective-permute-done.12.a1
  72.9 1.5 %collective-permute-start.17 = (bf16[64,1024]{1,0:T(8,128)(2,1)S(1)}, bf16[64,1024]{1,0:T(8,128)(2,1)S(1)}, u32[]{:S(2)}, u32[]{:S(2)}) collective-permute-start(bf16[64,1024]{1,0:T(8,128)(2,1)S(1)} %collective-permute-done.15.a4), channel_id=1, source_target_pairs={{0,48},{8,56},{16,0},{24,8},{32,16},{40,24},{48,32},{56,40},{64,11... | collective-permute-start | bytes 393224 | tf_op jit(solution)/shard_map/ppermute | solution.py:28
  74.4 0.0 collective-permute-done.13.a2
  74.4 0.7 collective-permute-start.18
  75.1 1.4 %collective-permute-done.14.a3 = bf16[64,1024]{1,0:T(8,128)(2,1)S(1)} collective-permute-done((bf16[64,1024]{1,0:T(8,128)(2,1)S(1)}, bf16[64,1024]{1,0:T(8,128)(2,1)S(1)}, u32[]{:S(2)}, u32[]{:S(2)}) %collective-permute-start.14) | collective-permute-done | bytes 131104 | tf_op jit(solution)/shard_map/ppermute | solution.py:28
  76.5 4.0 %collective-permute-done.16.a5 = bf16[64,1024]{1,0:T(8,128)(2,1)S(1)} collective-permute-done((bf16[64,1024]{1,0:T(8,128)(2,1)S(1)}, bf16[64,1024]{1,0:T(8,128)(2,1)S(1)}, u32[]{:S(2)}, u32[]{:S(2)}) %collective-permute-start.16) | collective-permute-done | bytes 131104 | tf_op jit(solution)/shard_map/ppermute | solution.py:28
  80.5 0.0 collective-permute-done.17.a6
  80.5 1.3 %collective-permute-done.18.a7 = bf16[64,1024]{1,0:T(8,128)(2,1)S(1)} collective-permute-done((bf16[64,1024]{1,0:T(8,128)(2,1)S(1)}, bf16[64,1024]{1,0:T(8,128)(2,1)S(1)}, u32[]{:S(2)}, u32[]{:S(2)}) %collective-permute-start.18) | collective-permute-done | bytes 131104 | tf_op jit(solution)/shard_map/ppermute | solution.py:28
  81.8 0.0 collective-permute-done.19.wb
  81.8 1.2 %shard_map.87 = bf16[8,64,1024]{2,1,0:T(8,128)(2,1)S(1)} custom-call(s32[1]{0:T(128)} %bitcast.index, bf16[64,1024]{1,0:T(8,128)(2,1)S(1)} %shard_map.86.a0, bf16[64,1024]{1,0:T(8,128)(2,1)S(1)} %collective-permute-done.12.a1, bf16[64,1024]{1,0:T(8,128)(2,1)S(1)} %collective-permute-done.13.a2, bf16[64,1024]{1,0:T(8,128)(2,1)S(1)} %collective-permute-done.14.a3, ...), custom_call_target="tpu_custom_call" | custom-call | bytes 1048576 | tf_op jit(solution)/shard_map/pallas_call | solution.py:284
  83.1 16.6 %all_to_all.5.terms = bf16[8,64,1024]{2,1,0:T(8,128)(2,1)S(1)} all-to-all(bf16[8,64,1024]{2,1,0:T(8,128)(2,1)S(1)} %shard_map.87), channel_id=1, replica_groups=mesh['blk'=16,'head'=8] {'head'}, dimensions={0} | all-to-all | bytes 2097152 | tf_op jit(solution)/shard_map/all_to_all | solution.py:290
  99.7 0.1 shard_map.88
  99.8 4.3 %collective-permute-start.20 = (bf16[64,512]{1,0:T(8,128)(2,1)S(1)}, bf16[64,512]{1,0:T(8,128)(2,1)S(1)}, u32[]{:S(2)}, u32[]{:S(2)}) collective-permute-start(bf16[64,512]{1,0:T(8,128)(2,1)S(1)} %get-tuple-element.40), channel_id=1, source_target_pairs={{0,8},{8,0},{16,24},{24,16},{32,40},{40,32},{48,56},{56,48},{64,72... | collective-permute-start | bytes 196616 | tf_op jit(solution)/shard_map/ppermute | solution.py:28
  104.1 0.9 collective-permute-done.20
  105.0 0.7 maximum_select_fusion
Async XLA Ops:
  0.0 38.3 %copy-start = (bf16[1024,512]{1,0:T(8,128)(2,1)S(1)}, bf16[1024,512]{1,0:T(8,128)(2,1)}, u32[]{:S(2)}) copy-start(bf16[1024,512]{1,0:T(8,128)(2,1)} %wa.1) | copy-start | bytes 3145732
  0.0 19.2 %collective-permute-start.3 = (bf16[2048,128]{1,0:T(8,128)(2,1)}, bf16[2048,128]{1,0:T(8,128)(2,1)S(1)}, u32[]{:S(2)}, u32[]{:S(2)}) collective-permute-start(bf16[2048,128]{1,0:T(8,128)(2,1)} %ka.1), channel_id=1, source_target_pairs={{0,8},{8,0},{16,24},{24,16},{32,40},{40,32},{48,56},{56,48},{64,72... | collective-permute-start | bytes 1572872 | tf_op jit(solution)/shard_map/ppermute | solution.py:28
  1.4 17.8 %collective-permute-start.4 = (bf16[2048,128]{1,0:T(8,128)(2,1)}, bf16[2048,128]{1,0:T(8,128)(2,1)S(1)}, u32[]{:S(2)}, u32[]{:S(2)}) collective-permute-start(bf16[2048,128]{1,0:T(8,128)(2,1)} %va.1), channel_id=1, source_target_pairs={{0,8},{8,0},{16,24},{24,16},{32,40},{40,32},{48,56},{56,48},{64,72... | collective-permute-start | bytes 1572872 | tf_op jit(solution)/shard_map/ppermute | solution.py:28
  1.4 7.6 %collective-permute-start = (bf16[64,1024]{1,0:T(8,128)(2,1)}, bf16[64,1024]{1,0:T(8,128)(2,1)S(1)}, u32[]{:S(2)}, u32[]{:S(2)}) collective-permute-start(bf16[64,1024]{1,0:T(8,128)(2,1)} %q.1), channel_id=1, source_target_pairs={{0,16},{8,24},{16,32},{24,40},{32,48},{40,56},{48,0},{56,8},{64,80... | collective-permute-start | bytes 393224 | tf_op jit(solution)/shard_map/ppermute | solution.py:28
  3.2 31.5 %collective-permute-start.5 = (bf16[2048,128]{1,0:T(8,128)(2,1)}, bf16[2048,128]{1,0:T(8,128)(2,1)S(1)}, u32[]{:S(2)}, u32[]{:S(2)}) collective-permute-start(bf16[2048,128]{1,0:T(8,128)(2,1)} %ka.1), channel_id=1, source_target_pairs={{0,64},{8,72},{16,80},{24,88},{32,96},{40,104},{48,112},{56,120},{... | collective-permute-start | bytes 1572872 | tf_op jit(solution)/shard_map/ppermute | solution.py:28
  6.0 28.8 %collective-permute-start.6 = (bf16[2048,128]{1,0:T(8,128)(2,1)}, bf16[2048,128]{1,0:T(8,128)(2,1)S(1)}, u32[]{:S(2)}, u32[]{:S(2)}) collective-permute-start(bf16[2048,128]{1,0:T(8,128)(2,1)} %va.1), channel_id=1, source_target_pairs={{0,64},{8,72},{16,80},{24,88},{32,96},{40,104},{48,112},{56,120},{... | collective-permute-start | bytes 1572872 | tf_op jit(solution)/shard_map/ppermute | solution.py:28
  9.0 4.3 %collective-permute-start.1 = (bf16[64,1024]{1,0:T(8,128)(2,1)}, bf16[64,1024]{1,0:T(8,128)(2,1)S(1)}, u32[]{:S(2)}, u32[]{:S(2)}) collective-permute-start(bf16[64,1024]{1,0:T(8,128)(2,1)} %q.1), channel_id=1, source_target_pairs={{0,48},{8,56},{16,0},{24,8},{32,16},{40,24},{48,32},{56,40},{64,11... | collective-permute-start | bytes 393224 | tf_op jit(solution)/shard_map/ppermute | solution.py:28
  13.4 5.8 %collective-permute-start.2 = (bf16[64,1024]{1,0:T(8,128)(2,1)}, bf16[64,1024]{1,0:T(8,128)(2,1)S(1)}, u32[]{:S(2)}, u32[]{:S(2)}) collective-permute-start(bf16[64,1024]{1,0:T(8,128)(2,1)} %q.1), channel_id=1, source_target_pairs={{0,32},{8,40},{16,48},{24,56},{32,0},{40,8},{48,16},{56,24},{64,96... | collective-permute-start | bytes 393224 | tf_op jit(solution)/shard_map/ppermute | solution.py:28
  19.2 1.0 copy-start.1
  20.3 1.0 copy-start.2
  21.3 0.9 copy-start.3
  22.2 0.7 copy-start.4
  22.9 0.7 copy-start.5
  34.8 11.3 %collective-permute-start.7 = (bf16[2048,128]{1,0:T(8,128)(2,1)S(1)}, bf16[2048,128]{1,0:T(8,128)(2,1)S(1)}, u32[]{:S(2)}, u32[]{:S(2)}) collective-permute-start(bf16[2048,128]{1,0:T(8,128)(2,1)S(1)} %collective-permute-done.5.k.ka), channel_id=1, source_target_pairs={{0,8},{8,0},{16,24},{24,16},{32,40},{40,32},{48,56},{56,48},{64,72... | collective-permute-start | bytes 1572872 | tf_op jit(solution)/shard_map/ppermute | solution.py:28
  37.5 8.6 %collective-permute-start.8 = (bf16[2048,128]{1,0:T(8,128)(2,1)S(1)}, bf16[2048,128]{1,0:T(8,128)(2,1)S(1)}, u32[]{:S(2)}, u32[]{:S(2)}) collective-permute-start(bf16[2048,128]{1,0:T(8,128)(2,1)S(1)} %collective-permute-done.6.v.va), channel_id=1, source_target_pairs={{0,8},{8,0},{16,24},{24,16},{32,40},{40,32},{48,56},{56,48},{64,72... | collective-permute-start | bytes 1572872 | tf_op jit(solution)/shard_map/ppermute | solution.py:28
  38.3 43.6 %collective-permute-start.19 = (bf16[1024,512]{1,0:T(8,128)(2,1)S(1)}, bf16[1024,512]{1,0:T(8,128)(2,1)S(1)}, u32[]{:S(2)}, u32[]{:S(2)}) collective-permute-start(bf16[1024,512]{1,0:T(8,128)(2,1)S(1)} %copy-done), channel_id=1, source_target_pairs={{0,8},{8,0},{16,24},{24,16},{32,40},{40,32},{48,56},{56,48},{64,72... | collective-permute-start | bytes 3145736 | tf_op jit(solution)/shard_map/ppermute | solution.py:28
  53.8 6.8 %collective-permute-start.10 = (bf16[144,512]{1,0:T(8,128)(2,1)S(1)}, bf16[144,512]{1,0:T(8,128)(2,1)S(1)}, u32[]{:S(2)}, u32[]{:S(2)}) collective-permute-start(bf16[144,512]{1,0:T(8,128)(2,1)S(1)} %get-tuple-element.33), channel_id=1, source_target_pairs={{0,16},{8,24},{16,32},{24,40},{32,48},{40,56},{48,0},{56,8},{64,80... | collective-permute-start | bytes 442376 | tf_op jit(solution)/shard_map/ppermute | solution.py:28
  53.9 10.9 %collective-permute-start.11 = (bf16[144,512]{1,0:T(8,128)(2,1)S(1)}, bf16[144,512]{1,0:T(8,128)(2,1)S(1)}, u32[]{:S(2)}, u32[]{:S(2)}) collective-permute-start(bf16[144,512]{1,0:T(8,128)(2,1)S(1)} %get-tuple-element.34), channel_id=1, source_target_pairs={{0,32},{8,40},{16,48},{24,56},{32,0},{40,8},{48,16},{56,24},{64,96... | collective-permute-start | bytes 442376 | tf_op jit(solution)/shard_map/ppermute | solution.py:28
  57.7 7.1 %collective-permute-start.9 = (bf16[144,512]{1,0:T(8,128)(2,1)S(1)}, bf16[144,512]{1,0:T(8,128)(2,1)S(1)}, u32[]{:S(2)}, u32[]{:S(2)}) collective-permute-start(bf16[144,512]{1,0:T(8,128)(2,1)S(1)} %get-tuple-element.32), channel_id=1, source_target_pairs={{0,48},{8,56},{16,0},{24,8},{32,16},{40,24},{48,32},{56,40},{64,11... | collective-permute-start | bytes 442376 | tf_op jit(solution)/shard_map/ppermute | solution.py:28
  65.0 6.3 %collective-permute-start.15 = (bf16[64,1024]{1,0:T(8,128)(2,1)S(1)}, bf16[64,1024]{1,0:T(8,128)(2,1)S(1)}, u32[]{:S(2)}, u32[]{:S(2)}) collective-permute-start(bf16[64,1024]{1,0:T(8,128)(2,1)S(1)} %shard_map.86.a0), channel_id=1, source_target_pairs={{0,64},{8,72},{16,80},{24,88},{32,96},{40,104},{48,112},{56,120},{... | collective-permute-start | bytes 393224 | tf_op jit(solution)/shard_map/ppermute | solution.py:28
  67.8 5.0 %collective-permute-start.12 = (bf16[64,1024]{1,0:T(8,128)(2,1)S(1)}, bf16[64,1024]{1,0:T(8,128)(2,1)S(1)}, u32[]{:S(2)}, u32[]{:S(2)}) collective-permute-start(bf16[64,1024]{1,0:T(8,128)(2,1)S(1)} %shard_map.86.a0), channel_id=1, source_target_pairs={{0,16},{8,24},{16,32},{24,40},{32,48},{40,56},{48,0},{56,8},{64,80... | collective-permute-start | bytes 393224 | tf_op jit(solution)/shard_map/ppermute | solution.py:28
  68.3 6.1 %collective-permute-start.13 = (bf16[64,1024]{1,0:T(8,128)(2,1)S(1)}, bf16[64,1024]{1,0:T(8,128)(2,1)S(1)}, u32[]{:S(2)}, u32[]{:S(2)}) collective-permute-start(bf16[64,1024]{1,0:T(8,128)(2,1)S(1)} %shard_map.86.a0), channel_id=1, source_target_pairs={{0,48},{8,56},{16,0},{24,8},{32,16},{40,24},{48,32},{56,40},{64,11... | collective-permute-start | bytes 393224 | tf_op jit(solution)/shard_map/ppermute | solution.py:28
  70.5 6.0 %collective-permute-start.14 = (bf16[64,1024]{1,0:T(8,128)(2,1)S(1)}, bf16[64,1024]{1,0:T(8,128)(2,1)S(1)}, u32[]{:S(2)}, u32[]{:S(2)}) collective-permute-start(bf16[64,1024]{1,0:T(8,128)(2,1)S(1)} %shard_map.86.a0), channel_id=1, source_target_pairs={{0,32},{8,40},{16,48},{24,56},{32,0},{40,8},{48,16},{56,24},{64,96... | collective-permute-start | bytes 393224 | tf_op jit(solution)/shard_map/ppermute | solution.py:28
  71.3 9.2 %collective-permute-start.16 = (bf16[64,1024]{1,0:T(8,128)(2,1)S(1)}, bf16[64,1024]{1,0:T(8,128)(2,1)S(1)}, u32[]{:S(2)}, u32[]{:S(2)}) collective-permute-start(bf16[64,1024]{1,0:T(8,128)(2,1)S(1)} %collective-permute-done.15.a4), channel_id=1, source_target_pairs={{0,16},{8,24},{16,32},{24,40},{32,48},{40,56},{48,0},{56,8},{64,80... | collective-permute-start | bytes 393224 | tf_op jit(solution)/shard_map/ppermute | solution.py:28
  72.9 7.6 %collective-permute-start.17 = (bf16[64,1024]{1,0:T(8,128)(2,1)S(1)}, bf16[64,1024]{1,0:T(8,128)(2,1)S(1)}, u32[]{:S(2)}, u32[]{:S(2)}) collective-permute-start(bf16[64,1024]{1,0:T(8,128)(2,1)S(1)} %collective-permute-done.15.a4), channel_id=1, source_target_pairs={{0,48},{8,56},{16,0},{24,8},{32,16},{40,24},{48,32},{56,40},{64,11... | collective-permute-start | bytes 393224 | tf_op jit(solution)/shard_map/ppermute | solution.py:28
  74.4 7.4 %collective-permute-start.18 = (bf16[64,1024]{1,0:T(8,128)(2,1)S(1)}, bf16[64,1024]{1,0:T(8,128)(2,1)S(1)}, u32[]{:S(2)}, u32[]{:S(2)}) collective-permute-start(bf16[64,1024]{1,0:T(8,128)(2,1)S(1)} %collective-permute-done.15.a4), channel_id=1, source_target_pairs={{0,32},{8,40},{16,48},{24,56},{32,0},{40,8},{48,16},{56,24},{64,96... | collective-permute-start | bytes 393224 | tf_op jit(solution)/shard_map/ppermute | solution.py:28
  99.8 5.2 %collective-permute-start.20 = (bf16[64,512]{1,0:T(8,128)(2,1)S(1)}, bf16[64,512]{1,0:T(8,128)(2,1)S(1)}, u32[]{:S(2)}, u32[]{:S(2)}) collective-permute-start(bf16[64,512]{1,0:T(8,128)(2,1)S(1)} %get-tuple-element.40), channel_id=1, source_target_pairs={{0,8},{8,0},{16,24},{24,16},{32,40},{40,32},{48,56},{56,48},{64,72... | collective-permute-start | bytes 196616 | tf_op jit(solution)/shard_map/ppermute | solution.py:28

commit v4 on v3

--- a/solution.py
+++ b/solution.py
@@ -55,9 +55,30 @@
     return jnp.concatenate([ref[:, h * DH : (h + 1) * DH] for h in range(GROUP)], axis=0)
 
 
-def with_ones(values, scratch):
-    scratch[:, :DH] = values[...]
-    scratch[:, DH:] = jnp.ones(values.shape, values.dtype)
+def join_kernel(k, v, kv, sems):
+    half = k.shape[0]
+    part = half // 2
+    copies = []
+    for i, ref in enumerate((k, v)):
+        for j in range(2):
+            copies.append(
+                pltpu.make_async_copy(
+                    ref.at[pl.ds(j * part, part)],
+                    kv.at[pl.ds(i * half + j * part, part)],
+                    sems.at[2 * i + j],
+                )
+            )
+    for copy in copies:
+        copy.start()
+    for copy in copies:
+        copy.wait()
+
+
+def split(kv, scratch):
+    half = kv.shape[0] // 2
+    scratch[:, :DH] = kv[half:, :]
+    scratch[:, DH:] = jnp.ones((half, DH), kv.dtype)
+    return kv.at[pl.ds(0, half)]
 
 
 def finish(top, total):
@@ -91,72 +112,70 @@
     return numerator / denominator, best + jnp.log2(denominator)
 
 
-def near_kernel(
-    q0, q1, q2, q, qk, qv, bias, ka, va, kb, vb,
-    top_out, total_out, rows, own_q, own_k, own_v, keys, values, sems,
-):
-    moves = [(q, own_q), (qk, own_k), (qv, own_v), (ka, keys), (va, values.at[0, :, pl.ds(0, DH)])]
-    copies = [pltpu.make_async_copy(a, b, sems.at[i]) for i, (a, b) in enumerate(moves)]
-    for copy in copies:
-        copy.start()
-    values[0, :, DH:] = jnp.ones(vb.shape, vb.dtype)
-    with_ones(vb, values.at[1])
-    for i, ref in enumerate((q0, q1, q2)):
+def run(tasks, states):
+    def scores_at(i):
+        _, rows, keys, _ = tasks[i]
+        return scores_of(rows[...], keys[...])
+
+    ahead = scores_at(0)
+    for i, (owner, _, _, values) in enumerate(tasks):
+        scores = ahead
+        if i + 1 < len(tasks):
+            ahead = scores_at(i + 1)
+        states[owner] = add_block(*states[owner], scores, values[...])
+    return states
+
+
+def empty():
+    return (
+        jnp.full((LANES, DH), FLOOR, jnp.float32),
+        jnp.zeros((LANES, 2 * DH), jnp.float32),
+    )
+
+
+def own_kernel(q, qk, qv, bias, kv, top_out, total_out, values):
+    k = split(kv, values)
+    rows = stacked(q)
+    scores = scores_of(rows, qk[...]) + jnp.concatenate([bias[...]] * GROUP, axis=0)
+    far = scores_of(rows, k[...])
+    top, total = add_block(
+        *empty(),
+        scores,
+        jnp.concatenate([qv[...], jnp.ones((ROWS, DH), jnp.bfloat16)], axis=1),
+    )
+    top_out[...], total_out[...] = add_block(top, total, far, values[...])
+
+
+def near_kernel(q0, q1, q2, q, own_top, own_total, kv, top_out, total_out, rows, values):
+    k = split(kv, values)
+    for i, ref in enumerate((q0, q1, q2, q)):
         rows[i] = stacked(ref)
-    for copy in copies:
-        copy.wait()
-    rows[3] = stacked(own_q)
-    top_out[...] = jnp.full(top_out.shape, FLOOR, jnp.float32)
-    total_out[...] = jnp.zeros(total_out.shape, jnp.float32)
-    scores = scores_of(rows[3], own_k[...]) + jnp.concatenate([bias[...]] * GROUP, axis=0)
-    top_out[3], total_out[3] = add_block(
-        top_out[3],
-        total_out[3],
-        scores,
-        jnp.concatenate([own_v[...], jnp.ones((ROWS, DH), jnp.bfloat16)], axis=1),
-    )
-
-    def step(i, _):
-        first, second = scores_of(rows[i], keys[...]), scores_of(rows[i], kb[...])
-        top, total = add_block(top_out[i], total_out[i], first, values[0])
-        top_out[i], total_out[i] = add_block(top, total, second, values[1])
-        return 0
-
-    lax.fori_loop(0, 4, step, 0)
-
-
-def far_kernel(rows, top_in, total_in, k, v, top_out, total_out, values):
-    with_ones(v, values)
-
-    def step(i, _):
-        top, total = add_block(top_in[i], total_in[i], scores_of(rows[i], k[...]), values[...])
-        top_out[i] = top
-        total_out[i] = total
-        return 0
-
-    lax.fori_loop(0, 3, step, 0)
-
-
-def last_kernel(rows, top_in, total_in, k, v, p0, p1, p2, values, out):
-    with_ones(v, values)
-
-    def step(i, _):
-        top, total = add_block(top_in[i], total_in[i], scores_of(rows[i], k[...]), values[...])
-        out[i] = packed(*finish(top, total))
-        return 0
-
-    lax.fori_loop(0, 3, step, 0)
-    for i, ref in enumerate((p0, p1, p2)):
-        ref[...] = out[i]
-
-
-def own_last_kernel(rows, top, total, ka, va, kb, vb, result_ref, level_ref, values):
-    with_ones(va, values.at[0])
-    with_ones(vb, values.at[1])
-    first, second = scores_of(rows[3], ka[...]), scores_of(rows[3], kb[...])
-    top, total = add_block(top[3], total[3], first, values[0])
-    top, total = add_block(top, total, second, values[1])
-    result, level = finish(top, total)
+    states = run([(i, rows.at[i], k, values) for i in range(3)], [empty() for _ in range(3)])
+    for i, (top, total) in enumerate(states):
+        top_out[i], total_out[i] = top, total
+    top_out[3], total_out[3] = own_top[...], own_total[...]
+
+
+def block_kernel(rows, top_in, total_in, kv, top_out, total_out, values):
+    k = split(kv, values)
+    states = [(top_in[i], total_in[i]) for i in range(4)]
+    states = run([(i, rows.at[i], k, values) for i in range(4)], states)
+    for i, (top, total) in enumerate(states):
+        top_out[i], total_out[i] = top, total
+
+
+def last_kernel(rows, top_in, total_in, kv, p0, p1, p2, values):
+    k = split(kv, values)
+    states = [(top_in[i], total_in[i]) for i in range(3)]
+    states = run([(i, rows.at[i], k, values) for i in range(3)], states)
+    for state, ref in zip(states, (p0, p1, p2)):
+        ref[...] = packed(*finish(*state))
+
+
+def own_last_kernel(rows, top, total, kv, result_ref, level_ref, values):
+    k = split(kv, values)
+    states = run([(0, rows.at[3], k, values)], [(top[3], total[3])])
+    result, level = finish(*states[0])
     result_ref[...] = result
     level_ref[...] = jnp.broadcast_to(level, (8, LANES))
 
@@ -191,13 +210,15 @@
     other[...] = acc[:, width:]
 
 
-def call(kernel, outs, scratch=(), flops=0, **kwargs):
+def call(kernel, outs, scratch=(), flops=0, limit=VMEM_LIMIT, **kwargs):
     return pl.pallas_call(
         kernel,
         out_shape=tuple(jax.ShapeDtypeStruct(s, d) for s, d in outs),
         scratch_shapes=list(scratch),
-        compiler_params=pltpu.CompilerParams(vmem_limit_bytes=VMEM_LIMIT),
-        cost_estimate=pl.CostEstimate(flops=flops, bytes_accessed=1 << 20, transcendentals=0),
+        compiler_params=pltpu.CompilerParams(vmem_limit_bytes=limit),
+        cost_estimate=(
+            pl.CostEstimate(flops=flops, bytes_accessed=0, transcendentals=0) if flops else None
+        ),
         **kwargs,
     )
 
@@ -218,62 +239,49 @@
     positions = prefix_keys.shape[0]
     vmem = pl.BlockSpec(memory_space=pltpu.VMEM)
     smem = pl.BlockSpec(memory_space=pltpu.SMEM)
-    hbm = pl.BlockSpec(memory_space=pltpu.HBM)
     block_flops = 8 * LANES * positions * DH
     part = ((DH + EXTRA, LANES), bf16)
     ones_shape = (positions, 2 * DH)
 
-    def state(owners):
-        return [((owners, LANES, DH), f32), ((owners, LANES, 2 * DH), f32)]
-
-    keys_x = moved(prefix_keys, xh=1)
-    values_x = moved(prefix_values, xh=1)
-    keys_c = moved(prefix_keys, c=1)
-    values_c = moved(prefix_values, c=1)
+    own_state = [((LANES, DH), f32), ((LANES, 2 * DH), f32)]
+    state = [((4, LANES, DH), f32), ((4, LANES, 2 * DH), f32)]
+
+    hbm = pl.BlockSpec(memory_space=pltpu.HBM)
+    (kv,) = call(
+        join_kernel,
+        [((2 * positions, DH), bf16)],
+        [pltpu.SemaphoreType.DMA((4,))],
+        limit=62 << 20,
+        in_specs=[hbm, hbm],
+        out_specs=(hbm,),
+    )(prefix_keys, prefix_values)
+    kv_x = moved(kv, xh=1)
+    kv_c = moved(kv, c=1)
     q_z = [moved(queries, z=z) for z in FAR]
     row = jnp.arange(ROWS, dtype=jnp.int32)
     allowed = (question_ids[:, None] == question_ids[None, :]) & (row[None, :] <= row[:, None])
     bias = jnp.where(allowed, 0.0, FLOOR).astype(f32)
-    top, total, rows = call(
-        near_kernel,
-        state(4) + [((4, LANES, DH), bf16)],
-        [
-            pltpu.VMEM(queries.shape, bf16),
-            pltpu.VMEM(question_keys.shape, bf16),
-            pltpu.VMEM(question_keys.shape, bf16),
-            pltpu.VMEM((positions, DH), bf16),
-            pltpu.VMEM((2,) + ones_shape, bf16),
-            pltpu.SemaphoreType.DMA((5,)),
-        ],
-        flops=block_flops,
-        in_specs=[vmem] * 3 + [hbm] * 3 + [vmem] + [hbm] * 2 + [vmem] * 2,
-    )(
-        *q_z, queries, question_keys, question_values, bias,
-        prefix_keys, prefix_values, keys_c, values_c,
-    )
-
-    keys_x, values_x, weight, top, total = lax.optimization_barrier(
-        (keys_x, values_x, out_weight, top, total)
-    )
-    keys_xc = moved(keys_x, c=1)
-    values_xc = moved(values_x, c=1)
+    scratch = [pltpu.VMEM(ones_shape, bf16)]
+    own_top, own_total = call(own_kernel, own_state, scratch)(
+        after(queries, q_z[0]), question_keys, question_values, bias, kv
+    )
+    top, total, rows = call(near_kernel, state + [((4, LANES, DH), bf16)], scratch)(
+        *q_z, queries, own_top, own_total, kv
+    )
+    top, total = call(block_kernel, state, scratch)(rows, top, total, kv_c)
+
+    kv_x, weight, top, total = lax.optimization_barrier((kv_x, out_weight, top, total))
+    kv_xc = moved(kv_x, c=1)
     weight_c = moved(weight, c=1)
-    far_top, far_total = call(
-        far_kernel, state(3), [pltpu.VMEM(ones_shape, bf16)], flops=3 * block_flops
-    )(rows, top, total, keys_x, values_x)
-    parts = call(
-        last_kernel,
-        [part] * 3,
-        [pltpu.VMEM(ones_shape, bf16), pltpu.VMEM((3,) + part[0], bf16)],
-        flops=3 * block_flops,
-    )(rows, far_top, far_total, keys_xc, values_xc)
+    top, total = call(block_kernel, state, scratch, flops=4 * block_flops)(rows, top, total, kv_x)
+    parts = call(last_kernel, [part] * 3, scratch, flops=3 * block_flops)(rows, top, total, kv_xc)
     back = [moved(p, z=-z) for p, z in zip(parts, FAR)]
     result, level = call(
         own_last_kernel,
         [((DH, LANES), f32), ((8, LANES), f32)],
-        [pltpu.VMEM((2,) + ones_shape, bf16)],
-        flops=2 * block_flops,
-    )(after(rows, *parts), top, total, keys_x, values_x, keys_xc, values_xc)
+        [pltpu.VMEM(ones_shape, bf16)],
+        flops=block_flops,
+    )(after(rows, *parts), top, total, kv_xc)
     (att,) = call(
         merge_kernel, [((ROWS, GROUP * DH), bf16)], in_specs=[smem] + [vmem] * 5
     )(live_rows, result, level, *back)

time: 106 us -> 125 us (1.18)
  Pallas kernels: 30.5 us -> 57.9 us
  waiting for transfers between devices: 22.7 us -> 18.7 us
  local copies, waits for them, and re-layouts: 4.42 us -> 2.47 us
  starting transfers between devices: 29.3 us -> 27.4 us
    pallas_call x3 -> x6, Pallas kernels: 26.1 us -> 53.7 us  [the longest x1 32.9 us: shards(): call(join_kernel, [((2 * positions, DH), bf16)], [pltpu.SemaphoreType.DMA...]
    ppermute x21 -> x18, waiting for transfers between devices: 22.7 us -> 18.7 us  [moved(): return lax.ppermute(array, 'blk', pairs)]
    unnamed x12 -> x14, local copies, waits for them, and re-layouts: 4.42 us -> 2.47 us
    ppermute x21 -> x18, starting transfers between devices: 29.3 us -> 27.4 us  [moved(): return lax.ppermute(array, 'blk', pairs)]
  transfers between devices with their start and end apart: 21 -> 18, of which waited for: 9 -> 8; matrix products, arithmetic and copies ran while one was open for 1% -> 0% of each run, Pallas kernels for 28% -> 19%
where the time goes in v4:
time: 125 us
  Pallas kernels  57.9 us (46%)
  starting transfers between devices  27.4 us (22%)
  waiting for transfers between devices  18.7 us (15%)
  blocking collectives  17 us (14%)
  local copies, waits for them, and re-layouts  2.47 us (2%)
    pallas_call x1, Pallas kernels, shards(): call(join_kernel, [((2 * positions, DH), bf16)], [pltpu.SemaphoreType.DMA...  32.9 us
    ppermute x18, starting transfers between devices, moved(): return lax.ppermute(array, 'blk', pairs)  27.4 us
    ppermute x18, waiting for transfers between devices, moved(): return lax.ppermute(array, 'blk', pairs)  18.7 us
    all_to_all x1, blocking collectives, shards(): gathered = lax.all_to_all(terms, 'head', 0, 0, tiled=True)  17 us
    pallas_call x1, Pallas kernels, shards(): top, total = call(block_kernel, state, scratch)(rows, top, total, kv_c)  5.13 us
    pallas_call x1, Pallas kernels, shards(): call(block_kernel, state, scratch, flops=4 * block_flops)  5.13 us
    pallas_call x1, Pallas kernels, shards(): call(last_kernel, [part] * 3, scratch, flops=3 * block_flops)  4.12 us
    pallas_call x1, Pallas kernels, shards(): call(near_kernel, state + [((4, LANES, DH), bf16)], scratch)  3.9 us
  transfers between devices with their start and end apart: 18, of which 8 were waited for; matrix products, arithmetic and copies ran while one was open for 0% of the time, Pallas kernels for 19%

profile of v4, /device:TPU:1, one launch (start us, length us, event | category | flops | bytes accessed | tf_op | source)
XLA Modules:
  0.0 125.2 jit_solution(5018512360498915145)
XLA Ops:
  0.0 0.0 copy-start.3
  0.0 0.0 copy-start.6
  0.0 0.0 copy-start.5
  0.0 0.0 copy-start.4
  0.0 32.9 %shard_map.82.kv = bf16[4096,128]{1,0:T(8,128)(2,1)} custom-call(bf16[2048,128]{1,0:T(8,128)(2,1)} %k.1, bf16[2048,128]{1,0:T(8,128)(2,1)} %v.1), custom_call_target="tpu_custom_call" | custom-call | tf_op jit(solution)/shard_map/pallas_call | solution.py:250
  32.9 1.5 %collective-permute-start.4 = (bf16[4096,128]{1,0:T(8,128)(2,1)}, bf16[4096,128]{1,0:T(8,128)(2,1)S(1)}, u32[]{:S(2)}, u32[]{:S(2)}) collective-permute-start(bf16[4096,128]{1,0:T(8,128)(2,1)} %shard_map.82.kv), channel_id=1, source_target_pairs={{0,8},{8,0},{16,24},{24,16},{32,40},{40,32},{48,56},{56,48},{64,72... | collective-permute-start | bytes 3145736 | tf_op jit(solution)/shard_map/ppermute | solution.py:28
  34.4 2.9 %collective-permute-start.3 = (bf16[4096,128]{1,0:T(8,128)(2,1)}, bf16[4096,128]{1,0:T(8,128)(2,1)S(1)}, u32[]{:S(2)}, u32[]{:S(2)}) collective-permute-start(bf16[4096,128]{1,0:T(8,128)(2,1)} %shard_map.82.kv), channel_id=1, source_target_pairs={{0,64},{8,72},{16,80},{24,88},{32,96},{40,104},{48,112},{56,120},{... | collective-permute-start | bytes 3145736 | tf_op jit(solution)/shard_map/ppermute | solution.py:28
  37.3 0.0 copy-done.3
  37.3 1.6 %collective-permute-start = (bf16[64,1024]{1,0:T(8,128)(2,1)S(1)}, bf16[64,1024]{1,0:T(8,128)(2,1)S(1)}, u32[]{:S(2)}, u32[]{:S(2)}) collective-permute-start(bf16[64,1024]{1,0:T(8,128)(2,1)S(1)} %copy-done.3), channel_id=1, source_target_pairs={{0,16},{8,24},{16,32},{24,40},{32,48},{40,56},{48,0},{56,8},{64,80... | collective-permute-start | bytes 393224 | tf_op jit(solution)/shard_map/ppermute | solution.py:28
  38.9 2.1 %collective-permute-start.1 = (bf16[64,1024]{1,0:T(8,128)(2,1)S(1)}, bf16[64,1024]{1,0:T(8,128)(2,1)S(1)}, u32[]{:S(2)}, u32[]{:S(2)}) collective-permute-start(bf16[64,1024]{1,0:T(8,128)(2,1)S(1)} %copy-done.3), channel_id=1, source_target_pairs={{0,48},{8,56},{16,0},{24,8},{32,16},{40,24},{48,32},{56,40},{64,11... | collective-permute-start | bytes 393224 | tf_op jit(solution)/shard_map/ppermute | solution.py:28
  41.0 1.3 %collective-permute-start.2 = (bf16[64,1024]{1,0:T(8,128)(2,1)S(1)}, bf16[64,1024]{1,0:T(8,128)(2,1)S(1)}, u32[]{:S(2)}, u32[]{:S(2)}) collective-permute-start(bf16[64,1024]{1,0:T(8,128)(2,1)S(1)} %copy-done.3), channel_id=1, source_target_pairs={{0,32},{8,40},{16,48},{24,56},{32,0},{40,8},{48,16},{56,24},{64,96... | collective-permute-start | bytes 393224 | tf_op jit(solution)/shard_map/ppermute | solution.py:28
  42.3 0.0 copy-done.6
  42.3 0.1 fusion.1.bias
  42.4 2.2 %collective-permute-done.q0 = bf16[64,1024]{1,0:T(8,128)(2,1)S(1)} collective-permute-done((bf16[64,1024]{1,0:T(8,128)(2,1)S(1)}, bf16[64,1024]{1,0:T(8,128)(2,1)S(1)}, u32[]{:S(2)}, u32[]{:S(2)}) %collective-permute-start) | collective-permute-done | bytes 131104 | tf_op jit(solution)/shard_map/ppermute | solution.py:28
  44.6 0.0 copy-done.5
  44.6 0.0 copy-done.4
  44.6 0.0 copy-start
  44.6 1.2 copy-done
  45.8 2.5 %shard_map.83 = (f32[512,128]{1,0:T(8,128)S(1)}, f32[512,256]{1,0:T(8,128)S(1)}) custom-call(bf16[64,1024]{1,0:T(8,128)(2,1)S(1)} %copy-done.3, bf16[64,128]{1,0:T(8,128)(2,1)S(1)} %copy-done.4, bf16[64,128]{1,0:T(8,128)(2,1)S(1)} %copy-done.5, f32[64,64]{1,0:T(8,128)S(1)} %fusion.1.bias, bf16[4096,128]{1,0:T(8,128)(2,1)S(1)} %copy-done), custom_call_target="tpu_custom_call" | custom-call | tf_op jit(solution)/shard_map/pallas_call | solution.py:265
  48.4 0.0 collective-permute-done.1.q1
  48.4 0.0 collective-permute-done.2.q2
  48.4 0.0 copy-start.1
  48.4 1.2 copy-done.1
  49.6 3.9 %shard_map.84 = (f32[4,512,128]{2,1,0:T(8,128)S(1)}, f32[4,512,256]{2,1,0:T(8,128)S(1)}, bf16[4,512,128]{2,1,0:T(8,128)(2,1)S(1)}) custom-call(bf16[64,1024]{1,0:T(8,128)(2,1)S(1)} %collective-permute-done.q0, bf16[64,1024]{1,0:T(8,128)(2,1)S(1)} %collective-permute-done.1.q1, bf16[64,1024]{1,0:T(8,128)(2,1)S(1)} %collective-permute-done.2.q2, ...), custom_call_target="tpu_custom_call" | custom-call | tf_op jit(solution)/shard_map/pallas_call | solution.py:268
  53.5 0.0 collective-permute-done.4.kv
  53.6 0.0 copy-start.2
  53.6 5.1 %shard_map.85 = (f32[4,512,128]{2,1,0:T(8,128)S(1)}, f32[4,512,256]{2,1,0:T(8,128)S(1)}) custom-call(bf16[4,512,128]{2,1,0:T(8,128)(2,1)S(1)} %get-tuple-element.43.rows, f32[4,512,128]{2,1,0:T(8,128)S(1)} %get-tuple-element.31.top_in, f32[4,512,256]{2,1,0:T(8,128)S(1)} %get-tuple-element.32.total_in, bf16[4096,128]{1,0:T(8,128)(2,1)S(1)} %collective-permute-done.4.kv), custom_call_target="tpu_custom_call" | custom-call | tf_op jit(solution)/shard_map/pallas_call | solution.py:271
  58.7 2.1 %collective-permute-done.3.kv = bf16[4096,128]{1,0:T(8,128)(2,1)S(1)} collective-permute-done((bf16[4096,128]{1,0:T(8,128)(2,1)}, bf16[4096,128]{1,0:T(8,128)(2,1)S(1)}, u32[]{:S(2)}, u32[]{:S(2)}) %collective-permute-start.3) | collective-permute-done | bytes 1048608 | tf_op jit(solution)/shard_map/ppermute | solution.py:28
  60.8 0.9 collective-permute-start.5
  61.7 0.0 copy-done.2
  61.7 0.0 collective-permute-start.16
  61.7 5.1 %shard_map.86 = (f32[4,512,128]{2,1,0:T(8,128)S(1)}, f32[4,512,256]{2,1,0:T(8,128)S(1)}) custom-call(bf16[4,512,128]{2,1,0:T(8,128)(2,1)S(1)} %get-tuple-element.43.rows, f32[4,512,128]{2,1,0:T(8,128)S(1)} %get-tuple-element.35.top_in, f32[4,512,256]{2,1,0:T(8,128)S(1)} %get-tuple-element.36.total_in, bf16[4096,128]{1,0:T(8,128)(2,1)S(1)} %collective-permute-done.3.kv), custom_call_target="tpu_custom_call" | custom-call | flops 4294967296 | tf_op jit(solution)/shard_map/pallas_call | solution.py:276
  66.9 0.0 collective-permute-done.5.kv
  66.9 4.1 %shard_map.87 = (bf16[144,512]{1,0:T(8,128)(2,1)S(1)}, bf16[144,512]{1,0:T(8,128)(2,1)S(1)}, bf16[144,512]{1,0:T(8,128)(2,1)S(1)}) custom-call(bf16[4,512,128]{2,1,0:T(8,128)(2,1)S(1)} %get-tuple-element.43.rows, f32[4,512,128]{2,1,0:T(8,128)S(1)} %get-tuple-element.38.top_in.top, f32[4,512,256]{2,1,0:T(8,128)S(1)} %get-tuple-element.39.total_in.total, ...), custom_call_target="tpu_custom_call" | custom-call | flops 3221225472 | tf_op jit(solution)/shard_map/pallas_call | solution.py:277
  71.0 3.9 %collective-permute-start.6 = (bf16[144,512]{1,0:T(8,128)(2,1)S(1)}, bf16[144,512]{1,0:T(8,128)(2,1)S(1)}, u32[]{:S(2)}, u32[]{:S(2)}) collective-permute-start(bf16[144,512]{1,0:T(8,128)(2,1)S(1)} %get-tuple-element.40), channel_id=1, source_target_pairs={{0,48},{8,56},{16,0},{24,8},{32,16},{40,24},{48,32},{56,40},{64,11... | collective-permute-start | bytes 442376 | tf_op jit(solution)/shard_map/ppermute | solution.py:28
  74.9 0.0 collective-permute-start.7
  74.9 1.3 %collective-permute-start.8 = (bf16[144,512]{1,0:T(8,128)(2,1)S(1)}, bf16[144,512]{1,0:T(8,128)(2,1)S(1)}, u32[]{:S(2)}, u32[]{:S(2)}) collective-permute-start(bf16[144,512]{1,0:T(8,128)(2,1)S(1)} %get-tuple-element.42), channel_id=1, source_target_pairs={{0,32},{8,40},{16,48},{24,56},{32,0},{40,8},{48,16},{56,24},{64,96... | collective-permute-start | bytes 442376 | tf_op jit(solution)/shard_map/ppermute | solution.py:28
  76.9 2.6 %shard_map.88 = (f32[128,512]{1,0:T(8,128)S(1)}, f32[8,512]{1,0:T(8,128)S(1)}) custom-call(bf16[4,512,128]{2,1,0:T(8,128)(2,1)S(1)} %get-tuple-element.43.rows, f32[4,512,128]{2,1,0:T(8,128)S(1)} %get-tuple-element.38.top_in.top, f32[4,512,256]{2,1,0:T(8,128)S(1)} %get-tuple-element.39.total_in.total, bf16[4096,128]{1,0:T(8,128)(2,1)S(1)} %collective-permute-done.5.kv), custom_call_target="tpu_custom_call" | custom-call | flops 1073741824 | tf_op jit(solution)/shard_map/pallas_call | solution.py:279
  79.5 0.0 collective-permute-done.6.r0
  79.5 4.8 %collective-permute-done.7.r1 = bf16[144,512]{1,0:T(8,128)(2,1)S(1)} collective-permute-done((bf16[144,512]{1,0:T(8,128)(2,1)S(1)}, bf16[144,512]{1,0:T(8,128)(2,1)S(1)}, u32[]{:S(2)}, u32[]{:S(2)}) %collective-permute-start.7) | collective-permute-done | bytes 147488 | tf_op jit(solution)/shard_map/ppermute | solution.py:28
  84.3 0.0 collective-permute-done.8.r2
  84.3 0.2 shard_map.89.a0
  84.5 2.8 %collective-permute-start.12 = (bf16[64,1024]{1,0:T(8,128)(2,1)S(1)}, bf16[64,1024]{1,0:T(8,128)(2,1)S(1)}, u32[]{:S(2)}, u32[]{:S(2)}) collective-permute-start(bf16[64,1024]{1,0:T(8,128)(2,1)S(1)} %shard_map.89.a0), channel_id=1, source_target_pairs={{0,64},{8,72},{16,80},{24,88},{32,96},{40,104},{48,112},{56,120},{... | collective-permute-start | bytes 393224 | tf_op jit(solution)/shard_map/ppermute | solution.py:28
  87.3 0.0 collective-permute-start.10
  87.3 0.2 collective-permute-start.11
  87.5 1.2 collective-permute-start.9
  88.8 1.1 collective-permute-done.12.a4
  89.9 0.1 collective-permute-start.13
  89.9 0.0 collective-permute-done.16.wb
  89.9 2.6 %collective-permute-start.14 = (bf16[64,1024]{1,0:T(8,128)(2,1)S(1)}, bf16[64,1024]{1,0:T(8,128)(2,1)S(1)}, u32[]{:S(2)}, u32[]{:S(2)}) collective-permute-start(bf16[64,1024]{1,0:T(8,128)(2,1)S(1)} %collective-permute-done.12.a4), channel_id=1, source_target_pairs={{0,48},{8,56},{16,0},{24,8},{32,16},{40,24},{48,32},{56,40},{64,11... | collective-permute-start | bytes 393224 | tf_op jit(solution)/shard_map/ppermute | solution.py:28
  92.6 0.0 collective-permute-done.10.a2
  92.6 1.3 %collective-permute-start.15 = (bf16[64,1024]{1,0:T(8,128)(2,1)S(1)}, bf16[64,1024]{1,0:T(8,128)(2,1)S(1)}, u32[]{:S(2)}, u32[]{:S(2)}) collective-permute-start(bf16[64,1024]{1,0:T(8,128)(2,1)S(1)} %collective-permute-done.12.a4), channel_id=1, source_target_pairs={{0,32},{8,40},{16,48},{24,56},{32,0},{40,8},{48,16},{56,24},{64,96... | collective-permute-start | bytes 393224 | tf_op jit(solution)/shard_map/ppermute | solution.py:28
  93.8 0.0 collective-permute-done.11.a3
  93.8 1.0 collective-permute-done.9.a1
  94.8 3.7 %collective-permute-done.13.a5 = bf16[64,1024]{1,0:T(8,128)(2,1)S(1)} collective-permute-done((bf16[64,1024]{1,0:T(8,128)(2,1)S(1)}, bf16[64,1024]{1,0:T(8,128)(2,1)S(1)}, u32[]{:S(2)}, u32[]{:S(2)}) %collective-permute-start.13) | collective-permute-done | bytes 131104 | tf_op jit(solution)/shard_map/ppermute | solution.py:28
  98.5 0.0 collective-permute-done.14.a6
  98.5 2.9 %collective-permute-done.15.a7 = bf16[64,1024]{1,0:T(8,128)(2,1)S(1)} collective-permute-done((bf16[64,1024]{1,0:T(8,128)(2,1)S(1)}, bf16[64,1024]{1,0:T(8,128)(2,1)S(1)}, u32[]{:S(2)}, u32[]{:S(2)}) %collective-permute-start.15) | collective-permute-done | bytes 131104 | tf_op jit(solution)/shard_map/ppermute | solution.py:28
  101.4 1.2 shard_map.90
  102.7 17.0 %all_to_all.5.terms = bf16[8,64,1024]{2,1,0:T(8,128)(2,1)S(1)} all-to-all(bf16[8,64,1024]{2,1,0:T(8,128)(2,1)S(1)} %shard_map.90), channel_id=1, replica_groups=mesh['blk'=16,'head'=8] {'head'}, dimensions={0} | all-to-all | bytes 2097152 | tf_op jit(solution)/shard_map/all_to_all | solution.py:298
  119.7 0.1 shard_map.91
  119.8 3.7 %collective-permute-start.17 = (bf16[64,512]{1,0:T(8,128)(2,1)S(1)}, bf16[64,512]{1,0:T(8,128)(2,1)S(1)}, u32[]{:S(2)}, u32[]{:S(2)}) collective-permute-start(bf16[64,512]{1,0:T(8,128)(2,1)S(1)} %get-tuple-element.48), channel_id=1, source_target_pairs={{0,8},{8,0},{16,24},{24,16},{32,40},{40,32},{48,56},{56,48},{64,72... | collective-permute-start | bytes 196616 | tf_op jit(solution)/shard_map/ppermute | solution.py:28
  123.6 0.9 collective-permute-done.17
  124.5 0.7 maximum_select_fusion
Async XLA Ops:
  0.0 37.3 %copy-start.3 = (bf16[64,1024]{1,0:T(8,128)(2,1)S(1)}, bf16[64,1024]{1,0:T(8,128)(2,1)}, u32[]{:S(2)}) copy-start(bf16[64,1024]{1,0:T(8,128)(2,1)} %q.2) | copy-start | bytes 393220
  0.0 42.3 %copy-start.6 = (s32[64]{0:T(128)S(1)}, s32[64]{0:T(128)}, u32[]{:S(2)}) copy-start(s32[64]{0:T(128)} %param.11) | copy-start | bytes 772
  0.0 44.6 %copy-start.5 = (bf16[64,128]{1,0:T(8,128)(2,1)S(1)}, bf16[64,128]{1,0:T(8,128)(2,1)}, u32[]{:S(2)}) copy-start(bf16[64,128]{1,0:T(8,128)(2,1)} %qv.1) | copy-start | bytes 49156
  0.0 44.6 %copy-start.4 = (bf16[64,128]{1,0:T(8,128)(2,1)S(1)}, bf16[64,128]{1,0:T(8,128)(2,1)}, u32[]{:S(2)}) copy-start(bf16[64,128]{1,0:T(8,128)(2,1)} %qk.1) | copy-start | bytes 49156
  32.9 20.6 %collective-permute-start.4 = (bf16[4096,128]{1,0:T(8,128)(2,1)}, bf16[4096,128]{1,0:T(8,128)(2,1)S(1)}, u32[]{:S(2)}, u32[]{:S(2)}) collective-permute-start(bf16[4096,128]{1,0:T(8,128)(2,1)} %shard_map.82.kv), channel_id=1, source_target_pairs={{0,8},{8,0},{16,24},{24,16},{32,40},{40,32},{48,56},{56,48},{64,72... | collective-permute-start | bytes 3145736 | tf_op jit(solution)/shard_map/ppermute | solution.py:28
  34.4 26.4 %collective-permute-start.3 = (bf16[4096,128]{1,0:T(8,128)(2,1)}, bf16[4096,128]{1,0:T(8,128)(2,1)S(1)}, u32[]{:S(2)}, u32[]{:S(2)}) collective-permute-start(bf16[4096,128]{1,0:T(8,128)(2,1)} %shard_map.82.kv), channel_id=1, source_target_pairs={{0,64},{8,72},{16,80},{24,88},{32,96},{40,104},{48,112},{56,120},{... | collective-permute-start | bytes 3145736 | tf_op jit(solution)/shard_map/ppermute | solution.py:28
  37.3 7.3 %collective-permute-start = (bf16[64,1024]{1,0:T(8,128)(2,1)S(1)}, bf16[64,1024]{1,0:T(8,128)(2,1)S(1)}, u32[]{:S(2)}, u32[]{:S(2)}) collective-permute-start(bf16[64,1024]{1,0:T(8,128)(2,1)S(1)} %copy-done.3), channel_id=1, source_target_pairs={{0,16},{8,24},{16,32},{24,40},{32,48},{40,56},{48,0},{56,8},{64,80... | collective-permute-start | bytes 393224 | tf_op jit(solution)/shard_map/ppermute | solution.py:28
  38.9 9.5 %collective-permute-start.1 = (bf16[64,1024]{1,0:T(8,128)(2,1)S(1)}, bf16[64,1024]{1,0:T(8,128)(2,1)S(1)}, u32[]{:S(2)}, u32[]{:S(2)}) collective-permute-start(bf16[64,1024]{1,0:T(8,128)(2,1)S(1)} %copy-done.3), channel_id=1, source_target_pairs={{0,48},{8,56},{16,0},{24,8},{32,16},{40,24},{48,32},{56,40},{64,11... | collective-permute-start | bytes 393224 | tf_op jit(solution)/shard_map/ppermute | solution.py:28
  41.0 7.4 %collective-permute-start.2 = (bf16[64,1024]{1,0:T(8,128)(2,1)S(1)}, bf16[64,1024]{1,0:T(8,128)(2,1)S(1)}, u32[]{:S(2)}, u32[]{:S(2)}) collective-permute-start(bf16[64,1024]{1,0:T(8,128)(2,1)S(1)} %copy-done.3), channel_id=1, source_target_pairs={{0,32},{8,40},{16,48},{24,56},{32,0},{40,8},{48,16},{56,24},{64,96... | collective-permute-start | bytes 393224 | tf_op jit(solution)/shard_map/ppermute | solution.py:28
  44.6 1.2 copy-start
  48.4 1.2 copy-start.1
  53.6 8.2 %copy-start.2 = (bf16[1024,512]{1,0:T(8,128)(2,1)S(1)}, bf16[1024,512]{1,0:T(8,128)(2,1)}, u32[]{:S(2)}) copy-start(bf16[1024,512]{1,0:T(8,128)(2,1)} %wa.1) | copy-start | bytes 3145732
  60.8 6.0 %collective-permute-start.5 = (bf16[4096,128]{1,0:T(8,128)(2,1)S(1)}, bf16[4096,128]{1,0:T(8,128)(2,1)S(1)}, u32[]{:S(2)}, u32[]{:S(2)}) collective-permute-start(bf16[4096,128]{1,0:T(8,128)(2,1)S(1)} %collective-permute-done.3.kv), channel_id=1, source_target_pairs={{0,8},{8,0},{16,24},{24,16},{32,40},{40,32},{48,56},{56,48},{64,72... | collective-permute-start | bytes 3145736 | tf_op jit(solution)/shard_map/ppermute | solution.py:28
  61.7 28.2 %collective-permute-start.16 = (bf16[1024,512]{1,0:T(8,128)(2,1)S(1)}, bf16[1024,512]{1,0:T(8,128)(2,1)S(1)}, u32[]{:S(2)}, u32[]{:S(2)}) collective-permute-start(bf16[1024,512]{1,0:T(8,128)(2,1)S(1)} %copy-done.2), channel_id=1, source_target_pairs={{0,8},{8,0},{16,24},{24,16},{32,40},{40,32},{48,56},{56,48},{64,72... | collective-permute-start | bytes 3145736 | tf_op jit(solution)/shard_map/ppermute | solution.py:28
  71.0 8.5 %collective-permute-start.6 = (bf16[144,512]{1,0:T(8,128)(2,1)S(1)}, bf16[144,512]{1,0:T(8,128)(2,1)S(1)}, u32[]{:S(2)}, u32[]{:S(2)}) collective-permute-start(bf16[144,512]{1,0:T(8,128)(2,1)S(1)} %get-tuple-element.40), channel_id=1, source_target_pairs={{0,48},{8,56},{16,0},{24,8},{32,16},{40,24},{48,32},{56,40},{64,11... | collective-permute-start | bytes 442376 | tf_op jit(solution)/shard_map/ppermute | solution.py:28
  74.9 9.3 %collective-permute-start.7 = (bf16[144,512]{1,0:T(8,128)(2,1)S(1)}, bf16[144,512]{1,0:T(8,128)(2,1)S(1)}, u32[]{:S(2)}, u32[]{:S(2)}) collective-permute-start(bf16[144,512]{1,0:T(8,128)(2,1)S(1)} %get-tuple-element.41), channel_id=1, source_target_pairs={{0,16},{8,24},{16,32},{24,40},{32,48},{40,56},{48,0},{56,8},{64,80... | collective-permute-start | bytes 442376 | tf_op jit(solution)/shard_map/ppermute | solution.py:28
  74.9 9.3 %collective-permute-start.8 = (bf16[144,512]{1,0:T(8,128)(2,1)S(1)}, bf16[144,512]{1,0:T(8,128)(2,1)S(1)}, u32[]{:S(2)}, u32[]{:S(2)}) collective-permute-start(bf16[144,512]{1,0:T(8,128)(2,1)S(1)} %get-tuple-element.42), channel_id=1, source_target_pairs={{0,32},{8,40},{16,48},{24,56},{32,0},{40,8},{48,16},{56,24},{64,96... | collective-permute-start | bytes 442376 | tf_op jit(solution)/shard_map/ppermute | solution.py:28
  84.5 5.4 %collective-permute-start.12 = (bf16[64,1024]{1,0:T(8,128)(2,1)S(1)}, bf16[64,1024]{1,0:T(8,128)(2,1)S(1)}, u32[]{:S(2)}, u32[]{:S(2)}) collective-permute-start(bf16[64,1024]{1,0:T(8,128)(2,1)S(1)} %shard_map.89.a0), channel_id=1, source_target_pairs={{0,64},{8,72},{16,80},{24,88},{32,96},{40,104},{48,112},{56,120},{... | collective-permute-start | bytes 393224 | tf_op jit(solution)/shard_map/ppermute | solution.py:28
  87.3 5.3 %collective-permute-start.10 = (bf16[64,1024]{1,0:T(8,128)(2,1)S(1)}, bf16[64,1024]{1,0:T(8,128)(2,1)S(1)}, u32[]{:S(2)}, u32[]{:S(2)}) collective-permute-start(bf16[64,1024]{1,0:T(8,128)(2,1)S(1)} %shard_map.89.a0), channel_id=1, source_target_pairs={{0,48},{8,56},{16,0},{24,8},{32,16},{40,24},{48,32},{56,40},{64,11... | collective-permute-start | bytes 393224 | tf_op jit(solution)/shard_map/ppermute | solution.py:28
  87.3 6.5 %collective-permute-start.11 = (bf16[64,1024]{1,0:T(8,128)(2,1)S(1)}, bf16[64,1024]{1,0:T(8,128)(2,1)S(1)}, u32[]{:S(2)}, u32[]{:S(2)}) collective-permute-start(bf16[64,1024]{1,0:T(8,128)(2,1)S(1)} %shard_map.89.a0), channel_id=1, source_target_pairs={{0,32},{8,40},{16,48},{24,56},{32,0},{40,8},{48,16},{56,24},{64,96... | collective-permute-start | bytes 393224 | tf_op jit(solution)/shard_map/ppermute | solution.py:28
  87.5 7.2 %collective-permute-start.9 = (bf16[64,1024]{1,0:T(8,128)(2,1)S(1)}, bf16[64,1024]{1,0:T(8,128)(2,1)S(1)}, u32[]{:S(2)}, u32[]{:S(2)}) collective-permute-start(bf16[64,1024]{1,0:T(8,128)(2,1)S(1)} %shard_map.89.a0), channel_id=1, source_target_pairs={{0,16},{8,24},{16,32},{24,40},{32,48},{40,56},{48,0},{56,8},{64,80... | collective-permute-start | bytes 393224 | tf_op jit(solution)/shard_map/ppermute | solution.py:28
  89.9 8.6 %collective-permute-start.13 = (bf16[64,1024]{1,0:T(8,128)(2,1)S(1)}, bf16[64,1024]{1,0:T(8,128)(2,1)S(1)}, u32[]{:S(2)}, u32[]{:S(2)}) collective-permute-start(bf16[64,1024]{1,0:T(8,128)(2,1)S(1)} %collective-permute-done.12.a4), channel_id=1, source_target_pairs={{0,16},{8,24},{16,32},{24,40},{32,48},{40,56},{48,0},{56,8},{64,80... | collective-permute-start | bytes 393224 | tf_op jit(solution)/shard_map/ppermute | solution.py:28
  89.9 8.5 %collective-permute-start.14 = (bf16[64,1024]{1,0:T(8,128)(2,1)S(1)}, bf16[64,1024]{1,0:T(8,128)(2,1)S(1)}, u32[]{:S(2)}, u32[]{:S(2)}) collective-permute-start(bf16[64,1024]{1,0:T(8,128)(2,1)S(1)} %collective-permute-done.12.a4), channel_id=1, source_target_pairs={{0,48},{8,56},{16,0},{24,8},{32,16},{40,24},{48,32},{56,40},{64,11... | collective-permute-start | bytes 393224 | tf_op jit(solution)/shard_map/ppermute | solution.py:28
  92.6 8.9 %collective-permute-start.15 = (bf16[64,1024]{1,0:T(8,128)(2,1)S(1)}, bf16[64,1024]{1,0:T(8,128)(2,1)S(1)}, u32[]{:S(2)}, u32[]{:S(2)}) collective-permute-start(bf16[64,1024]{1,0:T(8,128)(2,1)S(1)} %collective-permute-done.12.a4), channel_id=1, source_target_pairs={{0,32},{8,40},{16,48},{24,56},{32,0},{40,8},{48,16},{56,24},{64,96... | collective-permute-start | bytes 393224 | tf_op jit(solution)/shard_map/ppermute | solution.py:28
  119.8 4.6 %collective-permute-start.17 = (bf16[64,512]{1,0:T(8,128)(2,1)S(1)}, bf16[64,512]{1,0:T(8,128)(2,1)S(1)}, u32[]{:S(2)}, u32[]{:S(2)}) collective-permute-start(bf16[64,512]{1,0:T(8,128)(2,1)S(1)} %get-tuple-element.48), channel_id=1, source_target_pairs={{0,8},{8,0},{16,24},{24,16},{32,40},{40,32},{48,56},{56,48},{64,72... | collective-permute-start | bytes 196616 | tf_op jit(solution)/shard_map/ppermute | solution.py:28

commit v5 on v4

--- a/solution.py
+++ b/solution.py
@@ -55,23 +55,10 @@
     return jnp.concatenate([ref[:, h * DH : (h + 1) * DH] for h in range(GROUP)], axis=0)
 
 
-def join_kernel(k, v, kv, sems):
+def join_kernel(k, v, kv):
     half = k.shape[0]
-    part = half // 2
-    copies = []
-    for i, ref in enumerate((k, v)):
-        for j in range(2):
-            copies.append(
-                pltpu.make_async_copy(
-                    ref.at[pl.ds(j * part, part)],
-                    kv.at[pl.ds(i * half + j * part, part)],
-                    sems.at[2 * i + j],
-                )
-            )
-    for copy in copies:
-        copy.start()
-    for copy in copies:
-        copy.wait()
+    kv[:half, :] = k[...]
+    kv[half:, :] = v[...]
 
 
 def split(kv, scratch):
@@ -210,12 +197,12 @@
     other[...] = acc[:, width:]
 
 
-def call(kernel, outs, scratch=(), flops=0, limit=VMEM_LIMIT, **kwargs):
+def call(kernel, outs, scratch=(), flops=0, **kwargs):
     return pl.pallas_call(
         kernel,
         out_shape=tuple(jax.ShapeDtypeStruct(s, d) for s, d in outs),
         scratch_shapes=list(scratch),
-        compiler_params=pltpu.CompilerParams(vmem_limit_bytes=limit),
+        compiler_params=pltpu.CompilerParams(vmem_limit_bytes=VMEM_LIMIT),
         cost_estimate=(
             pl.CostEstimate(flops=flops, bytes_accessed=0, transcendentals=0) if flops else None
         ),
@@ -246,15 +233,7 @@
     own_state = [((LANES, DH), f32), ((LANES, 2 * DH), f32)]
     state = [((4, LANES, DH), f32), ((4, LANES, 2 * DH), f32)]
 
-    hbm = pl.BlockSpec(memory_space=pltpu.HBM)
-    (kv,) = call(
-        join_kernel,
-        [((2 * positions, DH), bf16)],
-        [pltpu.SemaphoreType.DMA((4,))],
-        limit=62 << 20,
-        in_specs=[hbm, hbm],
-        out_specs=(hbm,),
-    )(prefix_keys, prefix_values)
+    (kv,) = call(join_kernel, [((2 * positions, DH), bf16)])(prefix_keys, prefix_values)
     kv_x = moved(kv, xh=1)
     kv_c = moved(kv, c=1)
     q_z = [moved(queries, z=z) for z in FAR]

time: 125 us -> 94.4 us (0.76)
  Pallas kernels: 57.9 us -> 25.1 us
  waiting for transfers between devices: 18.7 us -> 21 us
    pallas_call x1, Pallas kernels: 32.9 us -> 0.07 us  [shards(): call(join_kernel, [((2 * positions, DH), bf16)])(prefix_keys, prefix_values)]
    ppermute x18, waiting for transfers between devices: 18.7 us -> 21 us  [moved(): return lax.ppermute(array, 'blk', pairs)]
  transfers between devices with their start and end apart: 18 -> 18, of which waited for: 8 -> 9; matrix products, arithmetic and copies ran while one was open for 0% -> 0% of each run, Pallas kernels for 19% -> 25%
where the time goes in v5:
time: 94.4 us; the launch traced here: 94.2 us
  starting transfers between devices  27.4 us (29%)
  Pallas kernels  25.1 us (27%)
  waiting for transfers between devices  21 us (22%)
  blocking collectives  17 us (18%)
  local copies, waits for them, and re-layouts  2.14 us (2%)
    ppermute x18, starting transfers between devices, moved(): return lax.ppermute(array, 'blk', pairs)  27.4 us
    ppermute x18, waiting for transfers between devices, moved(): return lax.ppermute(array, 'blk', pairs)  21 us
    all_to_all x1, blocking collectives, shards(): gathered = lax.all_to_all(terms, 'head', 0, 0, tiled=True)  17 us
    pallas_call x1, Pallas kernels, shards(): top, total = call(block_kernel, state, scratch)(rows, top, total, kv_c)  5.13 us
    pallas_call x1, Pallas kernels, shards(): call(block_kernel, state, scratch, flops=4 * block_flops)  5.13 us
    pallas_call x1, Pallas kernels, shards(): call(last_kernel, [part] * 3, scratch, flops=3 * block_flops)  4.12 us
    pallas_call x1, Pallas kernels, shards(): call(near_kernel, state + [((4, LANES, DH), bf16)], scratch)  3.9 us
    pallas_call x1, Pallas kernels, shards(): call(own_last_kernel, [((DH, LANES), f32), ((8, LANES), f32)], [pltpu.VME...  2.6 us
  transfers between devices with their start and end apart: 18, of which 9 were waited for; matrix products, arithmetic and copies ran while one was open for 0% of the time, Pallas kernels for 25%

profile of v5, /device:TPU:1, one launch (start us, length us, event | category | flops | bytes accessed | tf_op | source)
XLA Modules:
  0.0 94.2 jit_solution(16068578851823500675)
XLA Ops:
  0.0 0.0 copy-start.1
  0.0 0.0 copy-start.2
  0.0 1.1 %copy-done.2 = bf16[2048,128]{1,0:T(8,128)(2,1)S(1)} copy-done((bf16[2048,128]{1,0:T(8,128)(2,1)S(1)}, bf16[2048,128]{1,0:T(8,128)(2,1)}, u32[]{:S(2)}) %copy-start.2) | copy-done | bytes 524312
  1.1 0.0 copy-start.3
  1.1 1.0 %copy-done.3 = bf16[2048,128]{1,0:T(8,128)(2,1)S(1)} copy-done((bf16[2048,128]{1,0:T(8,128)(2,1)S(1)}, bf16[2048,128]{1,0:T(8,128)(2,1)}, u32[]{:S(2)}) %copy-start.3) | copy-done | bytes 524312
  2.1 0.0 copy-start.6
  2.1 0.0 copy-start.4
  2.1 0.0 copy-start.5
  2.1 0.1 shard_map.82.kv
  2.2 1.5 %collective-permute-start.4 = (bf16[4096,128]{1,0:T(8,128)(2,1)S(1)}, bf16[4096,128]{1,0:T(8,128)(2,1)S(1)}, u32[]{:S(2)}, u32[]{:S(2)}) collective-permute-start(bf16[4096,128]{1,0:T(8,128)(2,1)S(1)} %shard_map.82.kv), channel_id=1, source_target_pairs={{0,8},{8,0},{16,24},{24,16},{32,40},{40,32},{48,56},{56,48},{64,72... | collective-permute-start | bytes 3145736 | tf_op jit(solution)/shard_map/ppermute | solution.py:28
  3.7 2.8 %collective-permute-start.3 = (bf16[4096,128]{1,0:T(8,128)(2,1)S(1)}, bf16[4096,128]{1,0:T(8,128)(2,1)S(1)}, u32[]{:S(2)}, u32[]{:S(2)}) collective-permute-start(bf16[4096,128]{1,0:T(8,128)(2,1)S(1)} %shard_map.82.kv), channel_id=1, source_target_pairs={{0,64},{8,72},{16,80},{24,88},{32,96},{40,104},{48,112},{56,120},{... | collective-permute-start | bytes 3145736 | tf_op jit(solution)/shard_map/ppermute | solution.py:28
  6.5 0.0 copy-done.1
  6.5 1.6 %collective-permute-start = (bf16[64,1024]{1,0:T(8,128)(2,1)S(1)}, bf16[64,1024]{1,0:T(8,128)(2,1)S(1)}, u32[]{:S(2)}, u32[]{:S(2)}) collective-permute-start(bf16[64,1024]{1,0:T(8,128)(2,1)S(1)} %copy-done.1), channel_id=1, source_target_pairs={{0,16},{8,24},{16,32},{24,40},{32,48},{40,56},{48,0},{56,8},{64,80... | collective-permute-start | bytes 393224 | tf_op jit(solution)/shard_map/ppermute | solution.py:28
  8.2 2.1 %collective-permute-start.1 = (bf16[64,1024]{1,0:T(8,128)(2,1)S(1)}, bf16[64,1024]{1,0:T(8,128)(2,1)S(1)}, u32[]{:S(2)}, u32[]{:S(2)}) collective-permute-start(bf16[64,1024]{1,0:T(8,128)(2,1)S(1)} %copy-done.1), channel_id=1, source_target_pairs={{0,48},{8,56},{16,0},{24,8},{32,16},{40,24},{48,32},{56,40},{64,11... | collective-permute-start | bytes 393224 | tf_op jit(solution)/shard_map/ppermute | solution.py:28
  10.3 1.3 %collective-permute-start.2 = (bf16[64,1024]{1,0:T(8,128)(2,1)S(1)}, bf16[64,1024]{1,0:T(8,128)(2,1)S(1)}, u32[]{:S(2)}, u32[]{:S(2)}) collective-permute-start(bf16[64,1024]{1,0:T(8,128)(2,1)S(1)} %copy-done.1), channel_id=1, source_target_pairs={{0,32},{8,40},{16,48},{24,56},{32,0},{40,8},{48,16},{56,24},{64,96... | collective-permute-start | bytes 393224 | tf_op jit(solution)/shard_map/ppermute | solution.py:28
  11.6 0.0 copy-done.6
  11.6 0.1 fusion.1.bias
  11.7 2.2 %collective-permute-done.q0 = bf16[64,1024]{1,0:T(8,128)(2,1)S(1)} collective-permute-done((bf16[64,1024]{1,0:T(8,128)(2,1)S(1)}, bf16[64,1024]{1,0:T(8,128)(2,1)S(1)}, u32[]{:S(2)}, u32[]{:S(2)}) %collective-permute-start) | collective-permute-done | bytes 131104 | tf_op jit(solution)/shard_map/ppermute | solution.py:28
  13.9 0.0 copy-done.4
  13.9 0.0 copy-done.5
  13.9 2.5 %shard_map.83 = (f32[512,128]{1,0:T(8,128)S(1)}, f32[512,256]{1,0:T(8,128)S(1)}) custom-call(bf16[64,1024]{1,0:T(8,128)(2,1)S(1)} %copy-done.1, bf16[64,128]{1,0:T(8,128)(2,1)S(1)} %copy-done.4, bf16[64,128]{1,0:T(8,128)(2,1)S(1)} %copy-done.5, f32[64,64]{1,0:T(8,128)S(1)} %fusion.1.bias, bf16[4096,128]{1,0:T(8,128)(2,1)S(1)} %shard_map.82.kv), custom_call_target="tpu_custom_call" | custom-call | tf_op jit(solution)/shard_map/pallas_call | solution.py:244
  16.4 0.0 collective-permute-done.1.q1
  16.5 1.1 %collective-permute-done.2.q2 = bf16[64,1024]{1,0:T(8,128)(2,1)S(1)} collective-permute-done((bf16[64,1024]{1,0:T(8,128)(2,1)S(1)}, bf16[64,1024]{1,0:T(8,128)(2,1)S(1)}, u32[]{:S(2)}, u32[]{:S(2)}) %collective-permute-start.2) | collective-permute-done | bytes 131104 | tf_op jit(solution)/shard_map/ppermute | solution.py:28
  17.6 3.9 %shard_map.84 = (f32[4,512,128]{2,1,0:T(8,128)S(1)}, f32[4,512,256]{2,1,0:T(8,128)S(1)}, bf16[4,512,128]{2,1,0:T(8,128)(2,1)S(1)}) custom-call(bf16[64,1024]{1,0:T(8,128)(2,1)S(1)} %collective-permute-done.q0, bf16[64,1024]{1,0:T(8,128)(2,1)S(1)} %collective-permute-done.1.q1, bf16[64,1024]{1,0:T(8,128)(2,1)S(1)} %collective-permute-done.2.q2, ...), custom_call_target="tpu_custom_call" | custom-call | tf_op jit(solution)/shard_map/pallas_call | solution.py:247
  21.5 0.0 collective-permute-done.4.kv
  21.5 0.0 copy-start
  21.5 5.1 %shard_map.85 = (f32[4,512,128]{2,1,0:T(8,128)S(1)}, f32[4,512,256]{2,1,0:T(8,128)S(1)}) custom-call(bf16[4,512,128]{2,1,0:T(8,128)(2,1)S(1)} %get-tuple-element.43.rows, f32[4,512,128]{2,1,0:T(8,128)S(1)} %get-tuple-element.31.top_in, f32[4,512,256]{2,1,0:T(8,128)S(1)} %get-tuple-element.32.total_in, bf16[4096,128]{1,0:T(8,128)(2,1)S(1)} %collective-permute-done.4.kv), custom_call_target="tpu_custom_call" | custom-call | tf_op jit(solution)/shard_map/pallas_call | solution.py:250
  26.6 3.3 %collective-permute-done.3.kv = bf16[4096,128]{1,0:T(8,128)(2,1)S(1)} collective-permute-done((bf16[4096,128]{1,0:T(8,128)(2,1)S(1)}, bf16[4096,128]{1,0:T(8,128)(2,1)S(1)}, u32[]{:S(2)}, u32[]{:S(2)}) %collective-permute-start.3) | collective-permute-done | bytes 1048608 | tf_op jit(solution)/shard_map/ppermute | solution.py:28
  29.9 0.9 collective-permute-start.5
  30.8 0.0 copy-done
  30.8 0.0 collective-permute-start.16
  30.8 5.1 %shard_map.86 = (f32[4,512,128]{2,1,0:T(8,128)S(1)}, f32[4,512,256]{2,1,0:T(8,128)S(1)}) custom-call(bf16[4,512,128]{2,1,0:T(8,128)(2,1)S(1)} %get-tuple-element.43.rows, f32[4,512,128]{2,1,0:T(8,128)S(1)} %get-tuple-element.35.top_in, f32[4,512,256]{2,1,0:T(8,128)S(1)} %get-tuple-element.36.total_in, bf16[4096,128]{1,0:T(8,128)(2,1)S(1)} %collective-permute-done.3.kv), custom_call_target="tpu_custom_call" | custom-call | flops 4294967296 | tf_op jit(solution)/shard_map/pallas_call | solution.py:255
  35.9 0.0 collective-permute-done.5.kv
  36.0 4.1 %shard_map.87 = (bf16[144,512]{1,0:T(8,128)(2,1)S(1)}, bf16[144,512]{1,0:T(8,128)(2,1)S(1)}, bf16[144,512]{1,0:T(8,128)(2,1)S(1)}) custom-call(bf16[4,512,128]{2,1,0:T(8,128)(2,1)S(1)} %get-tuple-element.43.rows, f32[4,512,128]{2,1,0:T(8,128)S(1)} %get-tuple-element.38.top_in.top, f32[4,512,256]{2,1,0:T(8,128)S(1)} %get-tuple-element.39.total_in.total, ...), custom_call_target="tpu_custom_call" | custom-call | flops 3221225472 | tf_op jit(solution)/shard_map/pallas_call | solution.py:256
  40.1 3.9 %collective-permute-start.6 = (bf16[144,512]{1,0:T(8,128)(2,1)S(1)}, bf16[144,512]{1,0:T(8,128)(2,1)S(1)}, u32[]{:S(2)}, u32[]{:S(2)}) collective-permute-start(bf16[144,512]{1,0:T(8,128)(2,1)S(1)} %get-tuple-element.40), channel_id=1, source_target_pairs={{0,48},{8,56},{16,0},{24,8},{32,16},{40,24},{48,32},{56,40},{64,11... | collective-permute-start | bytes 442376 | tf_op jit(solution)/shard_map/ppermute | solution.py:28
  44.0 0.0 collective-permute-start.7
  44.0 1.3 %collective-permute-start.8 = (bf16[144,512]{1,0:T(8,128)(2,1)S(1)}, bf16[144,512]{1,0:T(8,128)(2,1)S(1)}, u32[]{:S(2)}, u32[]{:S(2)}) collective-permute-start(bf16[144,512]{1,0:T(8,128)(2,1)S(1)} %get-tuple-element.42), channel_id=1, source_target_pairs={{0,32},{8,40},{16,48},{24,56},{32,0},{40,8},{48,16},{56,24},{64,96... | collective-permute-start | bytes 442376 | tf_op jit(solution)/shard_map/ppermute | solution.py:28
  45.9 2.6 %shard_map.88 = (f32[128,512]{1,0:T(8,128)S(1)}, f32[8,512]{1,0:T(8,128)S(1)}) custom-call(bf16[4,512,128]{2,1,0:T(8,128)(2,1)S(1)} %get-tuple-element.43.rows, f32[4,512,128]{2,1,0:T(8,128)S(1)} %get-tuple-element.38.top_in.top, f32[4,512,256]{2,1,0:T(8,128)S(1)} %get-tuple-element.39.total_in.total, bf16[4096,128]{1,0:T(8,128)(2,1)S(1)} %collective-permute-done.5.kv), custom_call_target="tpu_custom_call" | custom-call | flops 1073741824 | tf_op jit(solution)/shard_map/pallas_call | solution.py:258
  48.6 0.0 collective-permute-done.6.r0
  48.6 4.7 %collective-permute-done.7.r1 = bf16[144,512]{1,0:T(8,128)(2,1)S(1)} collective-permute-done((bf16[144,512]{1,0:T(8,128)(2,1)S(1)}, bf16[144,512]{1,0:T(8,128)(2,1)S(1)}, u32[]{:S(2)}, u32[]{:S(2)}) %collective-permute-start.7) | collective-permute-done | bytes 147488 | tf_op jit(solution)/shard_map/ppermute | solution.py:28
  53.3 0.0 collective-permute-done.8.r2
  53.3 0.2 shard_map.89.a0
  53.5 2.8 %collective-permute-start.12 = (bf16[64,1024]{1,0:T(8,128)(2,1)S(1)}, bf16[64,1024]{1,0:T(8,128)(2,1)S(1)}, u32[]{:S(2)}, u32[]{:S(2)}) collective-permute-start(bf16[64,1024]{1,0:T(8,128)(2,1)S(1)} %shard_map.89.a0), channel_id=1, source_target_pairs={{0,64},{8,72},{16,80},{24,88},{32,96},{40,104},{48,112},{56,120},{... | collective-permute-start | bytes 393224 | tf_op jit(solution)/shard_map/ppermute | solution.py:28
  56.3 0.0 collective-permute-start.10
  56.3 0.2 collective-permute-start.11
  56.6 1.2 %collective-permute-start.9 = (bf16[64,1024]{1,0:T(8,128)(2,1)S(1)}, bf16[64,1024]{1,0:T(8,128)(2,1)S(1)}, u32[]{:S(2)}, u32[]{:S(2)}) collective-permute-start(bf16[64,1024]{1,0:T(8,128)(2,1)S(1)} %shard_map.89.a0), channel_id=1, source_target_pairs={{0,16},{8,24},{16,32},{24,40},{32,48},{40,56},{48,0},{56,8},{64,80... | collective-permute-start | bytes 393224 | tf_op jit(solution)/shard_map/ppermute | solution.py:28
  57.8 1.1 %collective-permute-done.12.a4 = bf16[64,1024]{1,0:T(8,128)(2,1)S(1)} collective-permute-done((bf16[64,1024]{1,0:T(8,128)(2,1)S(1)}, bf16[64,1024]{1,0:T(8,128)(2,1)S(1)}, u32[]{:S(2)}, u32[]{:S(2)}) %collective-permute-start.12) | collective-permute-done | bytes 131104 | tf_op jit(solution)/shard_map/ppermute | solution.py:28
  58.9 0.1 collective-permute-start.13
  59.0 0.0 collective-permute-done.16.wb
  59.0 2.6 %collective-permute-start.14 = (bf16[64,1024]{1,0:T(8,128)(2,1)S(1)}, bf16[64,1024]{1,0:T(8,128)(2,1)S(1)}, u32[]{:S(2)}, u32[]{:S(2)}) collective-permute-start(bf16[64,1024]{1,0:T(8,128)(2,1)S(1)} %collective-permute-done.12.a4), channel_id=1, source_target_pairs={{0,48},{8,56},{16,0},{24,8},{32,16},{40,24},{48,32},{56,40},{64,11... | collective-permute-start | bytes 393224 | tf_op jit(solution)/shard_map/ppermute | solution.py:28
  61.6 0.0 collective-permute-done.10.a2
  61.6 1.3 %collective-permute-start.15 = (bf16[64,1024]{1,0:T(8,128)(2,1)S(1)}, bf16[64,1024]{1,0:T(8,128)(2,1)S(1)}, u32[]{:S(2)}, u32[]{:S(2)}) collective-permute-start(bf16[64,1024]{1,0:T(8,128)(2,1)S(1)} %collective-permute-done.12.a4), channel_id=1, source_target_pairs={{0,32},{8,40},{16,48},{24,56},{32,0},{40,8},{48,16},{56,24},{64,96... | collective-permute-start | bytes 393224 | tf_op jit(solution)/shard_map/ppermute | solution.py:28
  62.9 0.0 collective-permute-done.11.a3
  62.9 1.0 %collective-permute-done.9.a1 = bf16[64,1024]{1,0:T(8,128)(2,1)S(1)} collective-permute-done((bf16[64,1024]{1,0:T(8,128)(2,1)S(1)}, bf16[64,1024]{1,0:T(8,128)(2,1)S(1)}, u32[]{:S(2)}, u32[]{:S(2)}) %collective-permute-start.9) | collective-permute-done | bytes 131104 | tf_op jit(solution)/shard_map/ppermute | solution.py:28
  63.8 3.7 %collective-permute-done.13.a5 = bf16[64,1024]{1,0:T(8,128)(2,1)S(1)} collective-permute-done((bf16[64,1024]{1,0:T(8,128)(2,1)S(1)}, bf16[64,1024]{1,0:T(8,128)(2,1)S(1)}, u32[]{:S(2)}, u32[]{:S(2)}) %collective-permute-start.13) | collective-permute-done | bytes 131104 | tf_op jit(solution)/shard_map/ppermute | solution.py:28
  67.5 0.0 collective-permute-done.14.a6
  67.5 2.9 %collective-permute-done.15.a7 = bf16[64,1024]{1,0:T(8,128)(2,1)S(1)} collective-permute-done((bf16[64,1024]{1,0:T(8,128)(2,1)S(1)}, bf16[64,1024]{1,0:T(8,128)(2,1)S(1)}, u32[]{:S(2)}, u32[]{:S(2)}) %collective-permute-start.15) | collective-permute-done | bytes 131104 | tf_op jit(solution)/shard_map/ppermute | solution.py:28
  70.5 1.2 %shard_map.90 = bf16[8,64,1024]{2,1,0:T(8,128)(2,1)S(1)} custom-call(s32[1]{0:T(128)} %bitcast.index, bf16[64,1024]{1,0:T(8,128)(2,1)S(1)} %shard_map.89.a0, bf16[64,1024]{1,0:T(8,128)(2,1)S(1)} %collective-permute-done.9.a1, bf16[64,1024]{1,0:T(8,128)(2,1)S(1)} %collective-permute-done.10.a2, bf16[64,1024]{1,0:T(8,128)(2,1)S(1)} %collective-permute-done.11.a3, ...), custom_call_target="tpu_custom_call" | custom-call | tf_op jit(solution)/shard_map/pallas_call | solution.py:271
  71.7 17.0 %all_to_all.5.terms = bf16[8,64,1024]{2,1,0:T(8,128)(2,1)S(1)} all-to-all(bf16[8,64,1024]{2,1,0:T(8,128)(2,1)S(1)} %shard_map.90), channel_id=1, replica_groups=mesh['blk'=16,'head'=8] {'head'}, dimensions={0} | all-to-all | bytes 2097152 | tf_op jit(solution)/shard_map/all_to_all | solution.py:277
  88.8 0.1 shard_map.91
  88.9 3.7 %collective-permute-start.17 = (bf16[64,512]{1,0:T(8,128)(2,1)S(1)}, bf16[64,512]{1,0:T(8,128)(2,1)S(1)}, u32[]{:S(2)}, u32[]{:S(2)}) collective-permute-start(bf16[64,512]{1,0:T(8,128)(2,1)S(1)} %get-tuple-element.48), channel_id=1, source_target_pairs={{0,8},{8,0},{16,24},{24,16},{32,40},{40,32},{48,56},{56,48},{64,72... | collective-permute-start | bytes 196616 | tf_op jit(solution)/shard_map/ppermute | solution.py:28
  92.7 0.9 collective-permute-done.17
  93.6 0.7 maximum_select_fusion
Async XLA Ops:
  0.0 6.5 %copy-start.1 = (bf16[64,1024]{1,0:T(8,128)(2,1)S(1)}, bf16[64,1024]{1,0:T(8,128)(2,1)}, u32[]{:S(2)}) copy-start(bf16[64,1024]{1,0:T(8,128)(2,1)} %q.2) | copy-start | bytes 393220
  0.0 1.1 %copy-start.2 = (bf16[2048,128]{1,0:T(8,128)(2,1)S(1)}, bf16[2048,128]{1,0:T(8,128)(2,1)}, u32[]{:S(2)}) copy-start(bf16[2048,128]{1,0:T(8,128)(2,1)} %k.1) | copy-start | bytes 1572868
  1.1 1.0 %copy-start.3 = (bf16[2048,128]{1,0:T(8,128)(2,1)S(1)}, bf16[2048,128]{1,0:T(8,128)(2,1)}, u32[]{:S(2)}) copy-start(bf16[2048,128]{1,0:T(8,128)(2,1)} %v.1) | copy-start | bytes 1572868
  2.1 9.5 %copy-start.6 = (s32[64]{0:T(128)S(1)}, s32[64]{0:T(128)}, u32[]{:S(2)}) copy-start(s32[64]{0:T(128)} %param.11) | copy-start | bytes 772
  2.1 11.8 %copy-start.4 = (bf16[64,128]{1,0:T(8,128)(2,1)S(1)}, bf16[64,128]{1,0:T(8,128)(2,1)}, u32[]{:S(2)}) copy-start(bf16[64,128]{1,0:T(8,128)(2,1)} %qk.1) | copy-start | bytes 49156
  2.1 11.8 %copy-start.5 = (bf16[64,128]{1,0:T(8,128)(2,1)S(1)}, bf16[64,128]{1,0:T(8,128)(2,1)}, u32[]{:S(2)}) copy-start(bf16[64,128]{1,0:T(8,128)(2,1)} %qv.1) | copy-start | bytes 49156
  2.2 19.3 %collective-permute-start.4 = (bf16[4096,128]{1,0:T(8,128)(2,1)S(1)}, bf16[4096,128]{1,0:T(8,128)(2,1)S(1)}, u32[]{:S(2)}, u32[]{:S(2)}) collective-permute-start(bf16[4096,128]{1,0:T(8,128)(2,1)S(1)} %shard_map.82.kv), channel_id=1, source_target_pairs={{0,8},{8,0},{16,24},{24,16},{32,40},{40,32},{48,56},{56,48},{64,72... | collective-permute-start | bytes 3145736 | tf_op jit(solution)/shard_map/ppermute | solution.py:28
  3.7 26.2 %collective-permute-start.3 = (bf16[4096,128]{1,0:T(8,128)(2,1)S(1)}, bf16[4096,128]{1,0:T(8,128)(2,1)S(1)}, u32[]{:S(2)}, u32[]{:S(2)}) collective-permute-start(bf16[4096,128]{1,0:T(8,128)(2,1)S(1)} %shard_map.82.kv), channel_id=1, source_target_pairs={{0,64},{8,72},{16,80},{24,88},{32,96},{40,104},{48,112},{56,120},{... | collective-permute-start | bytes 3145736 | tf_op jit(solution)/shard_map/ppermute | solution.py:28
  6.5 7.3 %collective-permute-start = (bf16[64,1024]{1,0:T(8,128)(2,1)S(1)}, bf16[64,1024]{1,0:T(8,128)(2,1)S(1)}, u32[]{:S(2)}, u32[]{:S(2)}) collective-permute-start(bf16[64,1024]{1,0:T(8,128)(2,1)S(1)} %copy-done.1), channel_id=1, source_target_pairs={{0,16},{8,24},{16,32},{24,40},{32,48},{40,56},{48,0},{56,8},{64,80... | collective-permute-start | bytes 393224 | tf_op jit(solution)/shard_map/ppermute | solution.py:28
  8.2 8.3 %collective-permute-start.1 = (bf16[64,1024]{1,0:T(8,128)(2,1)S(1)}, bf16[64,1024]{1,0:T(8,128)(2,1)S(1)}, u32[]{:S(2)}, u32[]{:S(2)}) collective-permute-start(bf16[64,1024]{1,0:T(8,128)(2,1)S(1)} %copy-done.1), channel_id=1, source_target_pairs={{0,48},{8,56},{16,0},{24,8},{32,16},{40,24},{48,32},{56,40},{64,11... | collective-permute-start | bytes 393224 | tf_op jit(solution)/shard_map/ppermute | solution.py:28
  10.3 7.2 %collective-permute-start.2 = (bf16[64,1024]{1,0:T(8,128)(2,1)S(1)}, bf16[64,1024]{1,0:T(8,128)(2,1)S(1)}, u32[]{:S(2)}, u32[]{:S(2)}) collective-permute-start(bf16[64,1024]{1,0:T(8,128)(2,1)S(1)} %copy-done.1), channel_id=1, source_target_pairs={{0,32},{8,40},{16,48},{24,56},{32,0},{40,8},{48,16},{56,24},{64,96... | collective-permute-start | bytes 393224 | tf_op jit(solution)/shard_map/ppermute | solution.py:28
  21.5 9.3 %copy-start = (bf16[1024,512]{1,0:T(8,128)(2,1)S(1)}, bf16[1024,512]{1,0:T(8,128)(2,1)}, u32[]{:S(2)}) copy-start(bf16[1024,512]{1,0:T(8,128)(2,1)} %wa.1) | copy-start | bytes 3145732
  29.9 6.0 %collective-permute-start.5 = (bf16[4096,128]{1,0:T(8,128)(2,1)S(1)}, bf16[4096,128]{1,0:T(8,128)(2,1)S(1)}, u32[]{:S(2)}, u32[]{:S(2)}) collective-permute-start(bf16[4096,128]{1,0:T(8,128)(2,1)S(1)} %collective-permute-done.3.kv), channel_id=1, source_target_pairs={{0,8},{8,0},{16,24},{24,16},{32,40},{40,32},{48,56},{56,48},{64,72... | collective-permute-start | bytes 3145736 | tf_op jit(solution)/shard_map/ppermute | solution.py:28
  30.8 28.2 %collective-permute-start.16 = (bf16[1024,512]{1,0:T(8,128)(2,1)S(1)}, bf16[1024,512]{1,0:T(8,128)(2,1)S(1)}, u32[]{:S(2)}, u32[]{:S(2)}) collective-permute-start(bf16[1024,512]{1,0:T(8,128)(2,1)S(1)} %copy-done), channel_id=1, source_target_pairs={{0,8},{8,0},{16,24},{24,16},{32,40},{40,32},{48,56},{56,48},{64,72... | collective-permute-start | bytes 3145736 | tf_op jit(solution)/shard_map/ppermute | solution.py:28
  40.1 8.5 %collective-permute-start.6 = (bf16[144,512]{1,0:T(8,128)(2,1)S(1)}, bf16[144,512]{1,0:T(8,128)(2,1)S(1)}, u32[]{:S(2)}, u32[]{:S(2)}) collective-permute-start(bf16[144,512]{1,0:T(8,128)(2,1)S(1)} %get-tuple-element.40), channel_id=1, source_target_pairs={{0,48},{8,56},{16,0},{24,8},{32,16},{40,24},{48,32},{56,40},{64,11... | collective-permute-start | bytes 442376 | tf_op jit(solution)/shard_map/ppermute | solution.py:28
  44.0 9.3 %collective-permute-start.7 = (bf16[144,512]{1,0:T(8,128)(2,1)S(1)}, bf16[144,512]{1,0:T(8,128)(2,1)S(1)}, u32[]{:S(2)}, u32[]{:S(2)}) collective-permute-start(bf16[144,512]{1,0:T(8,128)(2,1)S(1)} %get-tuple-element.41), channel_id=1, source_target_pairs={{0,16},{8,24},{16,32},{24,40},{32,48},{40,56},{48,0},{56,8},{64,80... | collective-permute-start | bytes 442376 | tf_op jit(solution)/shard_map/ppermute | solution.py:28
  44.0 9.3 %collective-permute-start.8 = (bf16[144,512]{1,0:T(8,128)(2,1)S(1)}, bf16[144,512]{1,0:T(8,128)(2,1)S(1)}, u32[]{:S(2)}, u32[]{:S(2)}) collective-permute-start(bf16[144,512]{1,0:T(8,128)(2,1)S(1)} %get-tuple-element.42), channel_id=1, source_target_pairs={{0,32},{8,40},{16,48},{24,56},{32,0},{40,8},{48,16},{56,24},{64,96... | collective-permute-start | bytes 442376 | tf_op jit(solution)/shard_map/ppermute | solution.py:28
  53.5 5.4 %collective-permute-start.12 = (bf16[64,1024]{1,0:T(8,128)(2,1)S(1)}, bf16[64,1024]{1,0:T(8,128)(2,1)S(1)}, u32[]{:S(2)}, u32[]{:S(2)}) collective-permute-start(bf16[64,1024]{1,0:T(8,128)(2,1)S(1)} %shard_map.89.a0), channel_id=1, source_target_pairs={{0,64},{8,72},{16,80},{24,88},{32,96},{40,104},{48,112},{56,120},{... | collective-permute-start | bytes 393224 | tf_op jit(solution)/shard_map/ppermute | solution.py:28
  56.3 5.3 %collective-permute-start.10 = (bf16[64,1024]{1,0:T(8,128)(2,1)S(1)}, bf16[64,1024]{1,0:T(8,128)(2,1)S(1)}, u32[]{:S(2)}, u32[]{:S(2)}) collective-permute-start(bf16[64,1024]{1,0:T(8,128)(2,1)S(1)} %shard_map.89.a0), channel_id=1, source_target_pairs={{0,48},{8,56},{16,0},{24,8},{32,16},{40,24},{48,32},{56,40},{64,11... | collective-permute-start | bytes 393224 | tf_op jit(solution)/shard_map/ppermute | solution.py:28
  56.3 6.5 %collective-permute-start.11 = (bf16[64,1024]{1,0:T(8,128)(2,1)S(1)}, bf16[64,1024]{1,0:T(8,128)(2,1)S(1)}, u32[]{:S(2)}, u32[]{:S(2)}) collective-permute-start(bf16[64,1024]{1,0:T(8,128)(2,1)S(1)} %shard_map.89.a0), channel_id=1, source_target_pairs={{0,32},{8,40},{16,48},{24,56},{32,0},{40,8},{48,16},{56,24},{64,96... | collective-permute-start | bytes 393224 | tf_op jit(solution)/shard_map/ppermute | solution.py:28
  56.6 7.2 %collective-permute-start.9 = (bf16[64,1024]{1,0:T(8,128)(2,1)S(1)}, bf16[64,1024]{1,0:T(8,128)(2,1)S(1)}, u32[]{:S(2)}, u32[]{:S(2)}) collective-permute-start(bf16[64,1024]{1,0:T(8,128)(2,1)S(1)} %shard_map.89.a0), channel_id=1, source_target_pairs={{0,16},{8,24},{16,32},{24,40},{32,48},{40,56},{48,0},{56,8},{64,80... | collective-permute-start | bytes 393224 | tf_op jit(solution)/shard_map/ppermute | solution.py:28
  58.9 8.6 %collective-permute-start.13 = (bf16[64,1024]{1,0:T(8,128)(2,1)S(1)}, bf16[64,1024]{1,0:T(8,128)(2,1)S(1)}, u32[]{:S(2)}, u32[]{:S(2)}) collective-permute-start(bf16[64,1024]{1,0:T(8,128)(2,1)S(1)} %collective-permute-done.12.a4), channel_id=1, source_target_pairs={{0,16},{8,24},{16,32},{24,40},{32,48},{40,56},{48,0},{56,8},{64,80... | collective-permute-start | bytes 393224 | tf_op jit(solution)/shard_map/ppermute | solution.py:28
  59.0 8.5 %collective-permute-start.14 = (bf16[64,1024]{1,0:T(8,128)(2,1)S(1)}, bf16[64,1024]{1,0:T(8,128)(2,1)S(1)}, u32[]{:S(2)}, u32[]{:S(2)}) collective-permute-start(bf16[64,1024]{1,0:T(8,128)(2,1)S(1)} %collective-permute-done.12.a4), channel_id=1, source_target_pairs={{0,48},{8,56},{16,0},{24,8},{32,16},{40,24},{48,32},{56,40},{64,11... | collective-permute-start | bytes 393224 | tf_op jit(solution)/shard_map/ppermute | solution.py:28
  61.6 8.9 %collective-permute-start.15 = (bf16[64,1024]{1,0:T(8,128)(2,1)S(1)}, bf16[64,1024]{1,0:T(8,128)(2,1)S(1)}, u32[]{:S(2)}, u32[]{:S(2)}) collective-permute-start(bf16[64,1024]{1,0:T(8,128)(2,1)S(1)} %collective-permute-done.12.a4), channel_id=1, source_target_pairs={{0,32},{8,40},{16,48},{24,56},{32,0},{40,8},{48,16},{56,24},{64,96... | collective-permute-start | bytes 393224 | tf_op jit(solution)/shard_map/ppermute | solution.py:28
  88.9 4.6 %collective-permute-start.17 = (bf16[64,512]{1,0:T(8,128)(2,1)S(1)}, bf16[64,512]{1,0:T(8,128)(2,1)S(1)}, u32[]{:S(2)}, u32[]{:S(2)}) collective-permute-start(bf16[64,512]{1,0:T(8,128)(2,1)S(1)} %get-tuple-element.48), channel_id=1, source_target_pairs={{0,8},{8,0},{16,24},{24,16},{32,40},{40,32},{48,56},{56,48},{64,72... | collective-permute-start | bytes 196616 | tf_op jit(solution)/shard_map/ppermute | solution.py:28

commit v6 on v5

--- a/solution.py
+++ b/solution.py
@@ -1,4 +1,5 @@
 import functools
+import itertools
 
 import jax
 import jax.numpy as jnp
@@ -14,7 +15,8 @@
 EXTRA = 16
 SCALE = DH**-0.5 * 1.4426950408889634
 FLOOR = -1e30
-XH, Z, CORE = 2, 4, 2
+XH, Z, CORE, Y, XL = 2, 4, 2, 4, 2
+PIECES = tuple(itertools.product(range(2), range(2), range(2)))
 VMEM_LIMIT = 30 << 20
 FAR = (1, 3, 2)
 
@@ -26,6 +28,18 @@
         to = (((a + xh) % XH) * Z + (b + z) % Z) * CORE + (d + c) % CORE
         pairs.append((i, to))
     return lax.ppermute(array, "blk", pairs)
+
+
+def routed(array, source_of):
+    pairs = []
+    for to in itertools.product(range(XH), range(Z), range(CORE), range(Y), range(XL)):
+        pairs.append((place(source_of(*to)), place(to)))
+    return lax.ppermute(array, ("blk", "head"), sorted(pairs))
+
+
+def place(at):
+    xh, z, c, y, xl = at
+    return (((xh * Z + z) * CORE + c) * Y + y) * XL + xl
 
 
 def after(array, *others):
@@ -176,23 +190,33 @@
         att[:, head * DH : (head + 1) * DH] = rows[head * ROWS : (head + 1) * ROWS, :]
 
 
-def project_kernel(index, a0, a1, a2, a3, a4, a5, a6, a7, wa, wb, out, rows):
-    for i, ref in enumerate((a0, a1, a2, a3, a4, a5, a6, a7)):
-        rows[i * ROWS : (i + 1) * ROWS, :] = ref[...]
+def project_kernel(index, a0, a1, a2, a3, a4, a5, a6, a7, wa, wb, xa, xb, t0, t1, t2, t3, rows, terms):
+    blk, head = index[0], index[1]
+    xh, z = blk // (Z * CORE), (blk // CORE) % Z
+    y, xl = head // XL, head % XL
+    swap = (z % 2 + xl) % 2
+    for (dx, dz, e), ref in zip(PIECES, (a0, a1, a2, a3, a4, a5, a6, a7)):
+        at = (2 * dx + dz) * ROWS
+        rows[(swap + e) % 2, at : at + ROWS, :] = ref[...]
     width = wa.shape[1]
-    xh, z = index[0] // (Z * CORE), (index[0] // CORE) % Z
-    slots = [((xh + dx) % XH) * Z + (z + Z - dz) % Z for dx in range(XH) for dz in (0,) + FAR]
-    for side, w in enumerate((wa, wb)):
-        terms = jnp.dot(rows[...], w[...], preferred_element_type=jnp.float32).astype(jnp.bfloat16)
-        for i in range(8):
-            out[slots[i], :, side * width : (side + 1) * width] = terms[i * ROWS : (i + 1) * ROWS, :]
-
-
-def sum_kernel(terms, mine, other, *, width):
-    acc = terms[0].astype(jnp.float32)
-    for i in range(1, terms.shape[0]):
-        acc = acc + terms[i].astype(jnp.float32)
+    for side, (mine, other) in enumerate(((wa, xa), (wb, xb))):
+        part = jnp.dot(rows[0], mine[...], preferred_element_type=jnp.float32) + jnp.dot(
+            rows[1], other[...], preferred_element_type=jnp.float32
+        )
+        for i in range(4):
+            terms[i, :, side * width : (side + 1) * width] = part[i * ROWS : (i + 1) * ROWS, :]
+    for s, out in enumerate((t0, t1, t2, t3)):
+        to = (y + s) % Y
+        i = 2 * ((to // 2 + xh) % 2) + (to % 2 + z // 2) % 2
+        out[...] = terms[i].astype(out.dtype)
+
+
+def sum_kernel(own, r1, r2, r3, mine, other):
+    acc = own[...]
+    for ref in (r1, r2, r3):
+        acc = acc + ref[...].astype(jnp.float32)
     acc = acc.astype(jnp.bfloat16)
+    width = mine.shape[1]
     mine[...] = acc[:, :width]
     other[...] = acc[:, width:]
 
@@ -252,6 +276,7 @@
     kv_x, weight, top, total = lax.optimization_barrier((kv_x, out_weight, top, total))
     kv_xc = moved(kv_x, c=1)
     weight_c = moved(weight, c=1)
+    weight_x = routed(weight, lambda xh, z, c, y, xl: (xh, z, c, y, 1 - xl))
     top, total = call(block_kernel, state, scratch, flops=4 * block_flops)(rows, top, total, kv_x)
     parts = call(last_kernel, [part] * 3, scratch, flops=3 * block_flops)(rows, top, total, kv_xc)
     back = [moved(p, z=-z) for p, z in zip(parts, FAR)]
@@ -265,20 +290,33 @@
         merge_kernel, [((ROWS, GROUP * DH), bf16)], in_specs=[smem] + [vmem] * 5
     )(live_rows, result, level, *back)
 
-    att_x = moved(att, xh=1)
-    held = [att] + [moved(att, z=z) for z in FAR] + [att_x] + [moved(att_x, z=z) for z in FAR]
+    att, weight_x, weight_c = lax.optimization_barrier((att, weight_x, weight_c))
+    weight_xc = moved(weight_x, c=1)
+    held = [
+        routed(
+            att,
+            lambda xh, z, c, y, xl, dx=dx, dz=dz, e=e: (
+                xh ^ dx, 2 * ((z // 2) ^ dz) + xl, c, y, (z % 2) ^ e,
+            ),
+        )
+        for dx, dz, e in PIECES
+    ]
     width = out_weight.shape[1]
-    (terms,) = call(
+    shape = (ROWS, CORE * width)
+    own, *terms = call(
         project_kernel,
-        [((8, ROWS, CORE * width), bf16)],
-        [pltpu.VMEM((8 * ROWS, GROUP * DH), bf16)],
-        in_specs=[smem] + [vmem] * 10,
-    )(index.reshape(1), *held, out_weight, weight_c)
-    gathered = lax.all_to_all(terms, "head", 0, 0, tiled=True)
-    mine, other = call(
-        functools.partial(sum_kernel, width=width),
-        [((ROWS, width), bf16), ((ROWS, width), bf16)],
-    )(gathered)
+        [(shape, f32)] + [(shape, bf16)] * 3,
+        [pltpu.VMEM((2, 4 * ROWS, GROUP * DH), bf16), pltpu.VMEM((4,) + shape, f32)],
+        in_specs=[smem] + [vmem] * 12,
+    )(
+        jnp.stack([index, lax.axis_index("head")]), *held,
+        out_weight, weight_c, weight_x, weight_xc,
+    )
+    back = [
+        routed(t, lambda xh, z, c, y, xl, s=s: (xh, z, c, (y - s) % Y, xl))
+        for s, t in zip((1, 2, 3), terms)
+    ]
+    mine, other = call(sum_kernel, [((ROWS, width), bf16)] * 2)(own, *back)
     theirs = moved(other, c=1)
     return jnp.where(
         core == 0,

time: 94.4 us -> 115 us (1.22)
  waiting for transfers between devices: 21 us -> 42.2 us
  blocking collectives: 17 us -> 0 us
  starting transfers between devices: 27.4 us -> 39.6 us
  Pallas kernels: 25.1 us -> 27.3 us
  local copies, waits for them, and re-layouts: 2.14 us -> 3.7 us
    ppermute x0 -> x12, waiting for transfers between devices: none -> 30 us  [routed(): return lax.ppermute(array, ('blk', 'head'), sorted(pairs))]
    ppermute x0 -> x12, starting transfers between devices: none -> 21.4 us  [routed(): return lax.ppermute(array, ('blk', 'head'), sorted(pairs))]
    all_to_all x1 -> x0, blocking collectives: 17 us -> none  [shards(): gathered = lax.all_to_all(terms, 'head', 0, 0, tiled=True)]
    ppermute x18 -> x12, starting transfers between devices: 27.4 us -> 18.2 us  [moved(): return lax.ppermute(array, 'blk', pairs)]
    ppermute x18 -> x12, waiting for transfers between devices: 21 us -> 12.2 us  [moved(): return lax.ppermute(array, 'blk', pairs)]
    pallas_call x2, Pallas kernels: 1.38 us -> 2.95 us  [the longest x1 2.87 us: shards(): call(project_kernel, [(shape, f32)] + [(shape, bf16)] * 3, [pltpu.VMEM((2...]
    unnamed x14 -> x18, local copies, waits for them, and re-layouts: 2.14 us -> 3.7 us
  transfers between devices with their start and end apart: 18 -> 24, of which waited for: 9 -> 11; matrix products, arithmetic and copies ran while one was open for 0% -> 0% of each run, Pallas kernels for 25% -> 21%
where the time goes in v6:
time: 115 us; the launch traced here: 114 us
  waiting for transfers between devices  42.2 us (37%)
  starting transfers between devices  39.6 us (34%)
  Pallas kernels  27.3 us (24%)
  local copies, waits for them, and re-layouts  3.7 us (3%)
    ppermute x12, waiting for transfers between devices, routed(): return lax.ppermute(array, ('blk', 'head'), sorted(pairs))  30 us
    ppermute x12, starting transfers between devices, routed(): return lax.ppermute(array, ('blk', 'head'), sorted(pairs))  21.4 us
    ppermute x12, starting transfers between devices, moved(): return lax.ppermute(array, 'blk', pairs)  18.2 us
    ppermute x12, waiting for transfers between devices, moved(): return lax.ppermute(array, 'blk', pairs)  12.2 us
    pallas_call x1, Pallas kernels, shards(): top, total = call(block_kernel, state, scratch)(rows, top, total, kv_c)  5.13 us
    pallas_call x1, Pallas kernels, shards(): call(block_kernel, state, scratch, flops=4 * block_flops)  5.13 us
    pallas_call x1, Pallas kernels, shards(): call(last_kernel, [part] * 3, scratch, flops=3 * block_flops)  4.12 us
    pallas_call x1, Pallas kernels, shards(): call(near_kernel, state + [((4, LANES, DH), bf16)], scratch)  3.9 us
  transfers between devices with their start and end apart: 24, of which 11 were waited for; matrix products, arithmetic and copies ran while one was open for 0% of the time, Pallas kernels for 21%

profile of v6, /device:TPU:1, one launch (start us, length us, event | category | flops | bytes accessed | tf_op | source)
XLA Modules:
  0.0 114.4 jit_solution(3533351101317076542)
XLA Ops:
  0.0 1.1 copy-done.2
  1.1 1.0 copy-done.3
  2.1 0.1 shard_map.82.kv
  2.2 1.5 %collective-permute-start.4 = (bf16[4096,128]{1,0:T(8,128)(2,1)S(1)}, bf16[4096,128]{1,0:T(8,128)(2,1)S(1)}, u32[]{:S(2)}, u32[]{:S(2)}) collective-permute-start(bf16[4096,128]{1,0:T(8,128)(2,1)S(1)} %shard_map.82.kv), channel_id=1, source_target_pairs={{0,8},{8,0},{16,24},{24,16},{32,40},{40,32},{48,56},{56,48},{64,72... | collective-permute-start | bytes 3145736 | tf_op jit(solution)/shard_map/ppermute | solution.py:30
  3.7 2.8 %collective-permute-start.3 = (bf16[4096,128]{1,0:T(8,128)(2,1)S(1)}, bf16[4096,128]{1,0:T(8,128)(2,1)S(1)}, u32[]{:S(2)}, u32[]{:S(2)}) collective-permute-start(bf16[4096,128]{1,0:T(8,128)(2,1)S(1)} %shard_map.82.kv), channel_id=1, source_target_pairs={{0,64},{8,72},{16,80},{24,88},{32,96},{40,104},{48,112},{56,120},{... | collective-permute-start | bytes 3145736 | tf_op jit(solution)/shard_map/ppermute | solution.py:30
  6.5 1.6 %collective-permute-start = (bf16[64,1024]{1,0:T(8,128)(2,1)S(1)}, bf16[64,1024]{1,0:T(8,128)(2,1)S(1)}, u32[]{:S(2)}, u32[]{:S(2)}) collective-permute-start(bf16[64,1024]{1,0:T(8,128)(2,1)S(1)} %copy-done.1), channel_id=1, source_target_pairs={{0,16},{8,24},{16,32},{24,40},{32,48},{40,56},{48,0},{56,8},{64,80... | collective-permute-start | bytes 393224 | tf_op jit(solution)/shard_map/ppermute | solution.py:30
  8.2 2.1 %collective-permute-start.1 = (bf16[64,1024]{1,0:T(8,128)(2,1)S(1)}, bf16[64,1024]{1,0:T(8,128)(2,1)S(1)}, u32[]{:S(2)}, u32[]{:S(2)}) collective-permute-start(bf16[64,1024]{1,0:T(8,128)(2,1)S(1)} %copy-done.1), channel_id=1, source_target_pairs={{0,48},{8,56},{16,0},{24,8},{32,16},{40,24},{48,32},{56,40},{64,11... | collective-permute-start | bytes 393224 | tf_op jit(solution)/shard_map/ppermute | solution.py:30
  10.3 1.3 %collective-permute-start.2 = (bf16[64,1024]{1,0:T(8,128)(2,1)S(1)}, bf16[64,1024]{1,0:T(8,128)(2,1)S(1)}, u32[]{:S(2)}, u32[]{:S(2)}) collective-permute-start(bf16[64,1024]{1,0:T(8,128)(2,1)S(1)} %copy-done.1), channel_id=1, source_target_pairs={{0,32},{8,40},{16,48},{24,56},{32,0},{40,8},{48,16},{56,24},{64,96... | collective-permute-start | bytes 393224 | tf_op jit(solution)/shard_map/ppermute | solution.py:30
  11.6 0.1 fusion.1.bias
  11.7 2.2 %collective-permute-done.q0 = bf16[64,1024]{1,0:T(8,128)(2,1)S(1)} collective-permute-done((bf16[64,1024]{1,0:T(8,128)(2,1)S(1)}, bf16[64,1024]{1,0:T(8,128)(2,1)S(1)}, u32[]{:S(2)}, u32[]{:S(2)}) %collective-permute-start) | collective-permute-done | bytes 131104 | tf_op jit(solution)/shard_map/ppermute | solution.py:30
  13.9 2.5 %shard_map.83 = (f32[512,128]{1,0:T(8,128)S(1)}, f32[512,256]{1,0:T(8,128)S(1)}) custom-call(bf16[64,1024]{1,0:T(8,128)(2,1)S(1)} %copy-done.1, bf16[64,128]{1,0:T(8,128)(2,1)S(1)} %copy-done.6, bf16[64,128]{1,0:T(8,128)(2,1)S(1)} %copy-done.7, f32[64,64]{1,0:T(8,128)S(1)} %fusion.1.bias, bf16[4096,128]{1,0:T(8,128)(2,1)S(1)} %shard_map.82.kv), custom_call_target="tpu_custom_call" | custom-call | tf_op jit(solution)/shard_map/pallas_call | solution.py:268
  16.4 0.0 collective-permute-done.1.q1
  16.5 1.1 collective-permute-done.2.q2
  17.6 3.9 %shard_map.84 = (f32[4,512,128]{2,1,0:T(8,128)S(1)}, f32[4,512,256]{2,1,0:T(8,128)S(1)}, bf16[4,512,128]{2,1,0:T(8,128)(2,1)S(1)}) custom-call(bf16[64,1024]{1,0:T(8,128)(2,1)S(1)} %collective-permute-done.q0, bf16[64,1024]{1,0:T(8,128)(2,1)S(1)} %collective-permute-done.1.q1, bf16[64,1024]{1,0:T(8,128)(2,1)S(1)} %collective-permute-done.2.q2, ...), custom_call_target="tpu_custom_call" | custom-call | tf_op jit(solution)/shard_map/pallas_call | solution.py:271
  21.5 0.0 collective-permute-done.4.kv
  21.5 0.0 copy-start
  21.5 5.1 %shard_map.85 = (f32[4,512,128]{2,1,0:T(8,128)S(1)}, f32[4,512,256]{2,1,0:T(8,128)S(1)}) custom-call(bf16[4,512,128]{2,1,0:T(8,128)(2,1)S(1)} %get-tuple-element.50.rows, f32[4,512,128]{2,1,0:T(8,128)S(1)} %get-tuple-element.38.top_in, f32[4,512,256]{2,1,0:T(8,128)S(1)} %get-tuple-element.39.total_in, bf16[4096,128]{1,0:T(8,128)(2,1)S(1)} %collective-permute-done.4.kv), custom_call_target="tpu_custom_call" | custom-call | tf_op jit(solution)/shard_map/pallas_call | solution.py:274
  26.6 3.3 %collective-permute-done.3.kv = bf16[4096,128]{1,0:T(8,128)(2,1)S(1)} collective-permute-done((bf16[4096,128]{1,0:T(8,128)(2,1)S(1)}, bf16[4096,128]{1,0:T(8,128)(2,1)S(1)}, u32[]{:S(2)}, u32[]{:S(2)}) %collective-permute-start.3) | collective-permute-done | bytes 1048608 | tf_op jit(solution)/shard_map/ppermute | solution.py:30
  29.9 0.9 collective-permute-start.5
  30.8 0.0 collective-permute-start.10
  30.8 1.3 %collective-permute-start.9 = (bf16[1024,512]{1,0:T(8,128)(2,1)S(1)}, bf16[1024,512]{1,0:T(8,128)(2,1)S(1)}, u32[]{:S(2)}, u32[]{:S(2)}) collective-permute-start(bf16[1024,512]{1,0:T(8,128)(2,1)S(1)} %copy-done), channel_id=1, source_target_pairs={{0,1},{1,0},{2,3},{3,2},{4,5},{5,4},{6,7},{7,6},{8,9},{9,8},{10,11... | collective-permute-start | bytes 3145736 | tf_op jit(solution)/shard_map/ppermute | solution.py:37
  32.1 5.1 %shard_map.86 = (f32[4,512,128]{2,1,0:T(8,128)S(1)}, f32[4,512,256]{2,1,0:T(8,128)S(1)}) custom-call(bf16[4,512,128]{2,1,0:T(8,128)(2,1)S(1)} %get-tuple-element.50.rows, f32[4,512,128]{2,1,0:T(8,128)S(1)} %get-tuple-element.42.top_in, f32[4,512,256]{2,1,0:T(8,128)S(1)} %get-tuple-element.43.total_in, bf16[4096,128]{1,0:T(8,128)(2,1)S(1)} %collective-permute-done.3.kv), custom_call_target="tpu_custom_call" | custom-call | flops 4294967296 | tf_op jit(solution)/shard_map/pallas_call | solution.py:280
  37.2 0.0 collective-permute-done.5.kv
  37.2 4.1 %shard_map.87 = (bf16[144,512]{1,0:T(8,128)(2,1)S(1)}, bf16[144,512]{1,0:T(8,128)(2,1)S(1)}, bf16[144,512]{1,0:T(8,128)(2,1)S(1)}) custom-call(bf16[4,512,128]{2,1,0:T(8,128)(2,1)S(1)} %get-tuple-element.50.rows, f32[4,512,128]{2,1,0:T(8,128)S(1)} %get-tuple-element.45.top_in.top, f32[4,512,256]{2,1,0:T(8,128)S(1)} %get-tuple-element.46.total_in.total, ...), custom_call_target="tpu_custom_call" | custom-call | flops 3221225472 | tf_op jit(solution)/shard_map/pallas_call | solution.py:281
  41.4 3.8 %collective-permute-start.6 = (bf16[144,512]{1,0:T(8,128)(2,1)S(1)}, bf16[144,512]{1,0:T(8,128)(2,1)S(1)}, u32[]{:S(2)}, u32[]{:S(2)}) collective-permute-start(bf16[144,512]{1,0:T(8,128)(2,1)S(1)} %get-tuple-element.47), channel_id=1, source_target_pairs={{0,48},{8,56},{16,0},{24,8},{32,16},{40,24},{48,32},{56,40},{64,11... | collective-permute-start | bytes 442376 | tf_op jit(solution)/shard_map/ppermute | solution.py:30
  45.2 0.0 collective-permute-start.7
  45.2 1.3 %collective-permute-start.8 = (bf16[144,512]{1,0:T(8,128)(2,1)S(1)}, bf16[144,512]{1,0:T(8,128)(2,1)S(1)}, u32[]{:S(2)}, u32[]{:S(2)}) collective-permute-start(bf16[144,512]{1,0:T(8,128)(2,1)S(1)} %get-tuple-element.49), channel_id=1, source_target_pairs={{0,32},{8,40},{16,48},{24,56},{32,0},{40,8},{48,16},{56,24},{64,96... | collective-permute-start | bytes 442376 | tf_op jit(solution)/shard_map/ppermute | solution.py:30
  47.2 2.6 %shard_map.88 = (f32[128,512]{1,0:T(8,128)S(1)}, f32[8,512]{1,0:T(8,128)S(1)}) custom-call(bf16[4,512,128]{2,1,0:T(8,128)(2,1)S(1)} %get-tuple-element.50.rows, f32[4,512,128]{2,1,0:T(8,128)S(1)} %get-tuple-element.45.top_in.top, f32[4,512,256]{2,1,0:T(8,128)S(1)} %get-tuple-element.46.total_in.total, bf16[4096,128]{1,0:T(8,128)(2,1)S(1)} %collective-permute-done.5.kv), custom_call_target="tpu_custom_call" | custom-call | flops 1073741824 | tf_op jit(solution)/shard_map/pallas_call | solution.py:283
  49.8 0.0 collective-permute-done.6.r0
  49.8 4.7 %collective-permute-done.7.r1 = bf16[144,512]{1,0:T(8,128)(2,1)S(1)} collective-permute-done((bf16[144,512]{1,0:T(8,128)(2,1)S(1)}, bf16[144,512]{1,0:T(8,128)(2,1)S(1)}, u32[]{:S(2)}, u32[]{:S(2)}) %collective-permute-start.7) | collective-permute-done | bytes 147488 | tf_op jit(solution)/shard_map/ppermute | solution.py:30
  54.5 0.0 collective-permute-done.8.r2
  54.5 0.9 shard_map.89
  55.3 0.0 collective-permute-done.10.wb
  55.3 0.0 collective-permute-done.9.xa
  55.3 1.4 %collective-permute-start.19 = (bf16[1024,512]{1,0:T(8,128)(2,1)S(1)}, bf16[1024,512]{1,0:T(8,128)(2,1)}, u32[]{:S(2)}, u32[]{:S(2)}) collective-permute-start(bf16[1024,512]{1,0:T(8,128)(2,1)S(1)} %collective-permute-done.9.xa), channel_id=1, source_target_pairs={{0,8},{8,0},{16,24},{24,16},{32,40},{40,32},{48,56},{56,48},{64,72... | collective-permute-start | bytes 3145736 | tf_op jit(solution)/shard_map/ppermute | solution.py:30
  56.7 1.6 %collective-permute-start.11 = (bf16[64,1024]{1,0:T(8,128)(2,1)}, bf16[64,1024]{1,0:T(8,128)(2,1)S(1)}, u32[]{:S(2)}, u32[]{:S(2)}) collective-permute-start(bf16[64,1024]{1,0:T(8,128)(2,1)} %shard_map.89), channel_id=1, source_target_pairs={{0,0},{1,16},{2,2},{3,18},{4,4},{5,20},{6,6},{7,22},{8,8},{9,24},{... | collective-permute-start | bytes 393224 | tf_op jit(solution)/shard_map/ppermute | solution.py:37
  58.3 2.6 %collective-permute-start.12 = (bf16[64,1024]{1,0:T(8,128)(2,1)}, bf16[64,1024]{1,0:T(8,128)(2,1)S(1)}, u32[]{:S(2)}, u32[]{:S(2)}) collective-permute-start(bf16[64,1024]{1,0:T(8,128)(2,1)} %shard_map.89), channel_id=1, source_target_pairs={{0,16},{1,0},{2,18},{3,2},{4,20},{5,4},{6,22},{7,6},{8,24},{9,8},{... | collective-permute-start | bytes 393224 | tf_op jit(solution)/shard_map/ppermute | solution.py:37
  60.8 3.6 %collective-permute-start.13 = (bf16[64,1024]{1,0:T(8,128)(2,1)}, bf16[64,1024]{1,0:T(8,128)(2,1)S(1)}, u32[]{:S(2)}, u32[]{:S(2)}) collective-permute-start(bf16[64,1024]{1,0:T(8,128)(2,1)} %shard_map.89), channel_id=1, source_target_pairs={{0,32},{1,48},{2,34},{3,50},{4,36},{5,52},{6,38},{7,54},{8,40},{9,... | collective-permute-start | bytes 393224 | tf_op jit(solution)/shard_map/ppermute | solution.py:37
  64.4 0.0 collective-permute-start.14
  64.4 0.0 collective-permute-done.11.a0
  64.4 2.5 %collective-permute-start.15 = (bf16[64,1024]{1,0:T(8,128)(2,1)}, bf16[64,1024]{1,0:T(8,128)(2,1)}, u32[]{:S(2)}, u32[]{:S(2)}) collective-permute-start(bf16[64,1024]{1,0:T(8,128)(2,1)} %shard_map.89), channel_id=1, source_target_pairs={{0,64},{1,80},{2,66},{3,82},{4,68},{5,84},{6,70},{7,86},{8,72},{9,... | collective-permute-start | bytes 393224 | tf_op jit(solution)/shard_map/ppermute | solution.py:37
  66.9 1.0 collective-permute-done.12.a1
  67.9 3.2 %collective-permute-start.16 = (bf16[64,1024]{1,0:T(8,128)(2,1)}, bf16[64,1024]{1,0:T(8,128)(2,1)}, u32[]{:S(2)}, u32[]{:S(2)}) collective-permute-start(bf16[64,1024]{1,0:T(8,128)(2,1)} %shard_map.89), channel_id=1, source_target_pairs={{0,80},{1,64},{2,82},{3,66},{4,84},{5,68},{6,86},{7,70},{8,88},{9,... | collective-permute-start | bytes 393224 | tf_op jit(solution)/shard_map/ppermute | solution.py:37
  71.1 11.3 %collective-permute-done.13.a2 = bf16[64,1024]{1,0:T(8,128)(2,1)S(1)} collective-permute-done((bf16[64,1024]{1,0:T(8,128)(2,1)}, bf16[64,1024]{1,0:T(8,128)(2,1)S(1)}, u32[]{:S(2)}, u32[]{:S(2)}) %collective-permute-start.13) | collective-permute-done | bytes 131104 | tf_op jit(solution)/shard_map/ppermute | solution.py:37
  82.4 1.7 %collective-permute-start.17 = (bf16[64,1024]{1,0:T(8,128)(2,1)}, bf16[64,1024]{1,0:T(8,128)(2,1)}, u32[]{:S(2)}, u32[]{:S(2)}) collective-permute-start(bf16[64,1024]{1,0:T(8,128)(2,1)} %shard_map.89), channel_id=1, source_target_pairs={{0,96},{1,112},{2,98},{3,114},{4,100},{5,116},{6,102},{7,118},{8,1... | collective-permute-start | bytes 393224 | tf_op jit(solution)/shard_map/ppermute | solution.py:37
  84.1 0.0 collective-permute-done.14.a3
  84.1 0.7 copy-done.4
  84.8 0.0 collective-permute-start.18
  84.8 0.1 pad_add_fusion.index
  84.9 6.4 %collective-permute-done.17.a6 = bf16[64,1024]{1,0:T(8,128)(2,1)} collective-permute-done((bf16[64,1024]{1,0:T(8,128)(2,1)}, bf16[64,1024]{1,0:T(8,128)(2,1)}, u32[]{:S(2)}, u32[]{:S(2)}) %collective-permute-start.17) | collective-permute-done | bytes 131104 | tf_op jit(solution)/shard_map/ppermute | solution.py:37
  91.2 6.4 %collective-permute-done.18.a7 = bf16[64,1024]{1,0:T(8,128)(2,1)} collective-permute-done((bf16[64,1024]{1,0:T(8,128)(2,1)}, bf16[64,1024]{1,0:T(8,128)(2,1)}, u32[]{:S(2)}, u32[]{:S(2)}) %collective-permute-start.18) | collective-permute-done | bytes 131104 | tf_op jit(solution)/shard_map/ppermute | solution.py:37
  97.7 0.0 collective-permute-done.19.xb
  97.7 0.9 copy-done.5
  98.6 2.9 %shard_map.90 = (f32[64,1024]{1,0:T(8,128)S(1)}, bf16[64,1024]{1,0:T(8,128)(2,1)S(1)}, bf16[64,1024]{1,0:T(8,128)(2,1)S(1)}, bf16[64,1024]{1,0:T(8,128)(2,1)S(1)}) custom-call(s32[2]{0:T(128)S(1)} %pad_add_fusion.index, bf16[64,1024]{1,0:T(8,128)(2,1)S(1)} %collective-permute-done.11.a0, bf16[64,1024]{1,0:T(8,128)(2,1)S(1)} %collective-permute-done.12.a1, ...), custom_call_target="tpu_custom_call" | custom-call | tf_op jit(solution)/shard_map/pallas_call | solution.py:306
  101.5 1.4 %collective-permute-start.20 = (bf16[64,1024]{1,0:T(8,128)(2,1)S(1)}, bf16[64,1024]{1,0:T(8,128)(2,1)S(1)}, u32[]{:S(2)}, u32[]{:S(2)}) collective-permute-start(bf16[64,1024]{1,0:T(8,128)(2,1)S(1)} %get-tuple-element.58), channel_id=1, source_target_pairs={{0,2},{1,3},{2,4},{3,5},{4,6},{5,7},{6,0},{7,1},{8,10},{9,11},{10,... | collective-permute-start | bytes 393224 | tf_op jit(solution)/shard_map/ppermute | solution.py:37
  102.8 2.6 %collective-permute-start.21 = (bf16[64,1024]{1,0:T(8,128)(2,1)S(1)}, bf16[64,1024]{1,0:T(8,128)(2,1)S(1)}, u32[]{:S(2)}, u32[]{:S(2)}) collective-permute-start(bf16[64,1024]{1,0:T(8,128)(2,1)S(1)} %get-tuple-element.59), channel_id=1, source_target_pairs={{0,4},{1,5},{2,6},{3,7},{4,0},{5,1},{6,2},{7,3},{8,12},{9,13},{10,... | collective-permute-start | bytes 393224 | tf_op jit(solution)/shard_map/ppermute | solution.py:37
  105.4 1.1 collective-permute-start.22
  106.5 0.9 collective-permute-done.20.r1
  107.4 3.9 %collective-permute-done.21.r2 = bf16[64,1024]{1,0:T(8,128)(2,1)S(1)} collective-permute-done((bf16[64,1024]{1,0:T(8,128)(2,1)S(1)}, bf16[64,1024]{1,0:T(8,128)(2,1)S(1)}, u32[]{:S(2)}, u32[]{:S(2)}) %collective-permute-start.21) | collective-permute-done | bytes 131104 | tf_op jit(solution)/shard_map/ppermute | solution.py:37
  111.4 0.0 collective-permute-done.22.r3
  111.4 0.1 shard_map.91
  111.4 1.4 %collective-permute-start.23 = (bf16[64,512]{1,0:T(8,128)(2,1)S(1)}, bf16[64,512]{1,0:T(8,128)(2,1)S(1)}, u32[]{:S(2)}, u32[]{:S(2)}) collective-permute-start(bf16[64,512]{1,0:T(8,128)(2,1)S(1)} %get-tuple-element.62), channel_id=1, source_target_pairs={{0,8},{8,0},{16,24},{24,16},{32,40},{40,32},{48,56},{56,48},{64,72... | collective-permute-start | bytes 196616 | tf_op jit(solution)/shard_map/ppermute | solution.py:30
  112.9 0.9 collective-permute-done.23
  113.8 0.7 maximum_select_fusion
  (15 shorter events, 0.0 us)
Async XLA Ops:
  0.0 6.5 %copy-start.1 = (bf16[64,1024]{1,0:T(8,128)(2,1)S(1)}, bf16[64,1024]{1,0:T(8,128)(2,1)}, u32[]{:S(2)}) copy-start(bf16[64,1024]{1,0:T(8,128)(2,1)} %q.2) | copy-start | bytes 393220
  0.0 1.1 copy-start.2
  1.1 1.0 copy-start.3
  2.1 9.5 %copy-start.8 = (s32[64]{0:T(128)S(1)}, s32[64]{0:T(128)}, u32[]{:S(2)}) copy-start(s32[64]{0:T(128)} %param.11) | copy-start | bytes 772
  2.1 11.8 %copy-start.6 = (bf16[64,128]{1,0:T(8,128)(2,1)S(1)}, bf16[64,128]{1,0:T(8,128)(2,1)}, u32[]{:S(2)}) copy-start(bf16[64,128]{1,0:T(8,128)(2,1)} %qk.1) | copy-start | bytes 49156
  2.1 11.8 %copy-start.7 = (bf16[64,128]{1,0:T(8,128)(2,1)S(1)}, bf16[64,128]{1,0:T(8,128)(2,1)}, u32[]{:S(2)}) copy-start(bf16[64,128]{1,0:T(8,128)(2,1)} %qv.1) | copy-start | bytes 49156
  2.2 19.3 %collective-permute-start.4 = (bf16[4096,128]{1,0:T(8,128)(2,1)S(1)}, bf16[4096,128]{1,0:T(8,128)(2,1)S(1)}, u32[]{:S(2)}, u32[]{:S(2)}) collective-permute-start(bf16[4096,128]{1,0:T(8,128)(2,1)S(1)} %shard_map.82.kv), channel_id=1, source_target_pairs={{0,8},{8,0},{16,24},{24,16},{32,40},{40,32},{48,56},{56,48},{64,72... | collective-permute-start | bytes 3145736 | tf_op jit(solution)/shard_map/ppermute | solution.py:30
  3.7 26.2 %collective-permute-start.3 = (bf16[4096,128]{1,0:T(8,128)(2,1)S(1)}, bf16[4096,128]{1,0:T(8,128)(2,1)S(1)}, u32[]{:S(2)}, u32[]{:S(2)}) collective-permute-start(bf16[4096,128]{1,0:T(8,128)(2,1)S(1)} %shard_map.82.kv), channel_id=1, source_target_pairs={{0,64},{8,72},{16,80},{24,88},{32,96},{40,104},{48,112},{56,120},{... | collective-permute-start | bytes 3145736 | tf_op jit(solution)/shard_map/ppermute | solution.py:30
  6.5 7.3 %collective-permute-start = (bf16[64,1024]{1,0:T(8,128)(2,1)S(1)}, bf16[64,1024]{1,0:T(8,128)(2,1)S(1)}, u32[]{:S(2)}, u32[]{:S(2)}) collective-permute-start(bf16[64,1024]{1,0:T(8,128)(2,1)S(1)} %copy-done.1), channel_id=1, source_target_pairs={{0,16},{8,24},{16,32},{24,40},{32,48},{40,56},{48,0},{56,8},{64,80... | collective-permute-start | bytes 393224 | tf_op jit(solution)/shard_map/ppermute | solution.py:30
  8.2 8.3 %collective-permute-start.1 = (bf16[64,1024]{1,0:T(8,128)(2,1)S(1)}, bf16[64,1024]{1,0:T(8,128)(2,1)S(1)}, u32[]{:S(2)}, u32[]{:S(2)}) collective-permute-start(bf16[64,1024]{1,0:T(8,128)(2,1)S(1)} %copy-done.1), channel_id=1, source_target_pairs={{0,48},{8,56},{16,0},{24,8},{32,16},{40,24},{48,32},{56,40},{64,11... | collective-permute-start | bytes 393224 | tf_op jit(solution)/shard_map/ppermute | solution.py:30
  10.3 7.2 %collective-permute-start.2 = (bf16[64,1024]{1,0:T(8,128)(2,1)S(1)}, bf16[64,1024]{1,0:T(8,128)(2,1)S(1)}, u32[]{:S(2)}, u32[]{:S(2)}) collective-permute-start(bf16[64,1024]{1,0:T(8,128)(2,1)S(1)} %copy-done.1), channel_id=1, source_target_pairs={{0,32},{8,40},{16,48},{24,56},{32,0},{40,8},{48,16},{56,24},{64,96... | collective-permute-start | bytes 393224 | tf_op jit(solution)/shard_map/ppermute | solution.py:30
  21.5 9.3 %copy-start = (bf16[1024,512]{1,0:T(8,128)(2,1)S(1)}, bf16[1024,512]{1,0:T(8,128)(2,1)}, u32[]{:S(2)}) copy-start(bf16[1024,512]{1,0:T(8,128)(2,1)} %wa.1) | copy-start | bytes 3145732
  29.9 7.3 %collective-permute-start.5 = (bf16[4096,128]{1,0:T(8,128)(2,1)S(1)}, bf16[4096,128]{1,0:T(8,128)(2,1)S(1)}, u32[]{:S(2)}, u32[]{:S(2)}) collective-permute-start(bf16[4096,128]{1,0:T(8,128)(2,1)S(1)} %collective-permute-done.3.kv), channel_id=1, source_target_pairs={{0,8},{8,0},{16,24},{24,16},{32,40},{40,32},{48,56},{56,48},{64,72... | collective-permute-start | bytes 3145736 | tf_op jit(solution)/shard_map/ppermute | solution.py:30
  30.8 24.5 %collective-permute-start.10 = (bf16[1024,512]{1,0:T(8,128)(2,1)S(1)}, bf16[1024,512]{1,0:T(8,128)(2,1)S(1)}, u32[]{:S(2)}, u32[]{:S(2)}) collective-permute-start(bf16[1024,512]{1,0:T(8,128)(2,1)S(1)} %copy-done), channel_id=1, source_target_pairs={{0,8},{8,0},{16,24},{24,16},{32,40},{40,32},{48,56},{56,48},{64,72... | collective-permute-start | bytes 3145736 | tf_op jit(solution)/shard_map/ppermute | solution.py:30
  30.8 24.5 %collective-permute-start.9 = (bf16[1024,512]{1,0:T(8,128)(2,1)S(1)}, bf16[1024,512]{1,0:T(8,128)(2,1)S(1)}, u32[]{:S(2)}, u32[]{:S(2)}) collective-permute-start(bf16[1024,512]{1,0:T(8,128)(2,1)S(1)} %copy-done), channel_id=1, source_target_pairs={{0,1},{1,0},{2,3},{3,2},{4,5},{5,4},{6,7},{7,6},{8,9},{9,8},{10,11... | collective-permute-start | bytes 3145736 | tf_op jit(solution)/shard_map/ppermute | solution.py:37
  41.4 8.4 %collective-permute-start.6 = (bf16[144,512]{1,0:T(8,128)(2,1)S(1)}, bf16[144,512]{1,0:T(8,128)(2,1)S(1)}, u32[]{:S(2)}, u32[]{:S(2)}) collective-permute-start(bf16[144,512]{1,0:T(8,128)(2,1)S(1)} %get-tuple-element.47), channel_id=1, source_target_pairs={{0,48},{8,56},{16,0},{24,8},{32,16},{40,24},{48,32},{56,40},{64,11... | collective-permute-start | bytes 442376 | tf_op jit(solution)/shard_map/ppermute | solution.py:30
  45.2 9.3 %collective-permute-start.7 = (bf16[144,512]{1,0:T(8,128)(2,1)S(1)}, bf16[144,512]{1,0:T(8,128)(2,1)S(1)}, u32[]{:S(2)}, u32[]{:S(2)}) collective-permute-start(bf16[144,512]{1,0:T(8,128)(2,1)S(1)} %get-tuple-element.48), channel_id=1, source_target_pairs={{0,16},{8,24},{16,32},{24,40},{32,48},{40,56},{48,0},{56,8},{64,80... | collective-permute-start | bytes 442376 | tf_op jit(solution)/shard_map/ppermute | solution.py:30
  45.2 9.3 %collective-permute-start.8 = (bf16[144,512]{1,0:T(8,128)(2,1)S(1)}, bf16[144,512]{1,0:T(8,128)(2,1)S(1)}, u32[]{:S(2)}, u32[]{:S(2)}) collective-permute-start(bf16[144,512]{1,0:T(8,128)(2,1)S(1)} %get-tuple-element.49), channel_id=1, source_target_pairs={{0,32},{8,40},{16,48},{24,56},{32,0},{40,8},{48,16},{56,24},{64,96... | collective-permute-start | bytes 442376 | tf_op jit(solution)/shard_map/ppermute | solution.py:30
  55.3 42.3 %collective-permute-start.19 = (bf16[1024,512]{1,0:T(8,128)(2,1)S(1)}, bf16[1024,512]{1,0:T(8,128)(2,1)}, u32[]{:S(2)}, u32[]{:S(2)}) collective-permute-start(bf16[1024,512]{1,0:T(8,128)(2,1)S(1)} %collective-permute-done.9.xa), channel_id=1, source_target_pairs={{0,8},{8,0},{16,24},{24,16},{32,40},{40,32},{48,56},{56,48},{64,72... | collective-permute-start | bytes 3145736 | tf_op jit(solution)/shard_map/ppermute | solution.py:30
  56.7 7.7 %collective-permute-start.11 = (bf16[64,1024]{1,0:T(8,128)(2,1)}, bf16[64,1024]{1,0:T(8,128)(2,1)S(1)}, u32[]{:S(2)}, u32[]{:S(2)}) collective-permute-start(bf16[64,1024]{1,0:T(8,128)(2,1)} %shard_map.89), channel_id=1, source_target_pairs={{0,0},{1,16},{2,2},{3,18},{4,4},{5,20},{6,6},{7,22},{8,8},{9,24},{... | collective-permute-start | bytes 393224 | tf_op jit(solution)/shard_map/ppermute | solution.py:37
  58.3 9.6 %collective-permute-start.12 = (bf16[64,1024]{1,0:T(8,128)(2,1)}, bf16[64,1024]{1,0:T(8,128)(2,1)S(1)}, u32[]{:S(2)}, u32[]{:S(2)}) collective-permute-start(bf16[64,1024]{1,0:T(8,128)(2,1)} %shard_map.89), channel_id=1, source_target_pairs={{0,16},{1,0},{2,18},{3,2},{4,20},{5,4},{6,22},{7,6},{8,24},{9,8},{... | collective-permute-start | bytes 393224 | tf_op jit(solution)/shard_map/ppermute | solution.py:37
  60.8 21.6 %collective-permute-start.13 = (bf16[64,1024]{1,0:T(8,128)(2,1)}, bf16[64,1024]{1,0:T(8,128)(2,1)S(1)}, u32[]{:S(2)}, u32[]{:S(2)}) collective-permute-start(bf16[64,1024]{1,0:T(8,128)(2,1)} %shard_map.89), channel_id=1, source_target_pairs={{0,32},{1,48},{2,34},{3,50},{4,36},{5,52},{6,38},{7,54},{8,40},{9,... | collective-permute-start | bytes 393224 | tf_op jit(solution)/shard_map/ppermute | solution.py:37
  64.4 19.7 %collective-permute-start.14 = (bf16[64,1024]{1,0:T(8,128)(2,1)}, bf16[64,1024]{1,0:T(8,128)(2,1)S(1)}, u32[]{:S(2)}, u32[]{:S(2)}) collective-permute-start(bf16[64,1024]{1,0:T(8,128)(2,1)} %shard_map.89), channel_id=1, source_target_pairs={{0,48},{1,32},{2,50},{3,34},{4,52},{5,36},{6,54},{7,38},{8,56},{9,... | collective-permute-start | bytes 393224 | tf_op jit(solution)/shard_map/ppermute | solution.py:37
  64.4 20.4 %collective-permute-start.15 = (bf16[64,1024]{1,0:T(8,128)(2,1)}, bf16[64,1024]{1,0:T(8,128)(2,1)}, u32[]{:S(2)}, u32[]{:S(2)}) collective-permute-start(bf16[64,1024]{1,0:T(8,128)(2,1)} %shard_map.89), channel_id=1, source_target_pairs={{0,64},{1,80},{2,66},{3,82},{4,68},{5,84},{6,70},{7,86},{8,72},{9,... | collective-permute-start | bytes 393224 | tf_op jit(solution)/shard_map/ppermute | solution.py:37
  67.9 17.0 %collective-permute-start.16 = (bf16[64,1024]{1,0:T(8,128)(2,1)}, bf16[64,1024]{1,0:T(8,128)(2,1)}, u32[]{:S(2)}, u32[]{:S(2)}) collective-permute-start(bf16[64,1024]{1,0:T(8,128)(2,1)} %shard_map.89), channel_id=1, source_target_pairs={{0,80},{1,64},{2,82},{3,66},{4,84},{5,68},{6,86},{7,70},{8,88},{9,... | collective-permute-start | bytes 393224 | tf_op jit(solution)/shard_map/ppermute | solution.py:37
  82.4 8.8 %collective-permute-start.17 = (bf16[64,1024]{1,0:T(8,128)(2,1)}, bf16[64,1024]{1,0:T(8,128)(2,1)}, u32[]{:S(2)}, u32[]{:S(2)}) collective-permute-start(bf16[64,1024]{1,0:T(8,128)(2,1)} %shard_map.89), channel_id=1, source_target_pairs={{0,96},{1,112},{2,98},{3,114},{4,100},{5,116},{6,102},{7,118},{8,1... | collective-permute-start | bytes 393224 | tf_op jit(solution)/shard_map/ppermute | solution.py:37
  84.1 0.7 copy-start.4
  84.8 12.9 %collective-permute-start.18 = (bf16[64,1024]{1,0:T(8,128)(2,1)}, bf16[64,1024]{1,0:T(8,128)(2,1)}, u32[]{:S(2)}, u32[]{:S(2)}) collective-permute-start(bf16[64,1024]{1,0:T(8,128)(2,1)} %shard_map.89), channel_id=1, source_target_pairs={{0,112},{1,96},{2,114},{3,98},{4,116},{5,100},{6,118},{7,102},{8,1... | collective-permute-start | bytes 393224 | tf_op jit(solution)/shard_map/ppermute | solution.py:37
  97.7 0.9 copy-start.5
  101.5 6.0 %collective-permute-start.20 = (bf16[64,1024]{1,0:T(8,128)(2,1)S(1)}, bf16[64,1024]{1,0:T(8,128)(2,1)S(1)}, u32[]{:S(2)}, u32[]{:S(2)}) collective-permute-start(bf16[64,1024]{1,0:T(8,128)(2,1)S(1)} %get-tuple-element.58), channel_id=1, source_target_pairs={{0,2},{1,3},{2,4},{3,5},{4,6},{5,7},{6,0},{7,1},{8,10},{9,11},{10,... | collective-permute-start | bytes 393224 | tf_op jit(solution)/shard_map/ppermute | solution.py:37
  102.8 8.5 %collective-permute-start.21 = (bf16[64,1024]{1,0:T(8,128)(2,1)S(1)}, bf16[64,1024]{1,0:T(8,128)(2,1)S(1)}, u32[]{:S(2)}, u32[]{:S(2)}) collective-permute-start(bf16[64,1024]{1,0:T(8,128)(2,1)S(1)} %get-tuple-element.59), channel_id=1, source_target_pairs={{0,4},{1,5},{2,6},{3,7},{4,0},{5,1},{6,2},{7,3},{8,12},{9,13},{10,... | collective-permute-start | bytes 393224 | tf_op jit(solution)/shard_map/ppermute | solution.py:37
  105.4 5.9 %collective-permute-start.22 = (bf16[64,1024]{1,0:T(8,128)(2,1)S(1)}, bf16[64,1024]{1,0:T(8,128)(2,1)S(1)}, u32[]{:S(2)}, u32[]{:S(2)}) collective-permute-start(bf16[64,1024]{1,0:T(8,128)(2,1)S(1)} %get-tuple-element.60), channel_id=1, source_target_pairs={{0,6},{1,7},{2,0},{3,1},{4,2},{5,3},{6,4},{7,5},{8,14},{9,15},{10,... | collective-permute-start | bytes 393224 | tf_op jit(solution)/shard_map/ppermute | solution.py:37
  111.4 2.3 %collective-permute-start.23 = (bf16[64,512]{1,0:T(8,128)(2,1)S(1)}, bf16[64,512]{1,0:T(8,128)(2,1)S(1)}, u32[]{:S(2)}, u32[]{:S(2)}) collective-permute-start(bf16[64,512]{1,0:T(8,128)(2,1)S(1)} %get-tuple-element.62), channel_id=1, source_target_pairs={{0,8},{8,0},{16,24},{24,16},{32,40},{40,32},{48,56},{56,48},{64,72... | collective-permute-start | bytes 196616 | tf_op jit(solution)/shard_map/ppermute | solution.py:30

commit v7 on v5

--- a/solution.py
+++ b/solution.py
@@ -133,42 +133,51 @@
     top_out[...], total_out[...] = add_block(top, total, far, values[...])
 
 
-def near_kernel(q0, q1, q2, q, own_top, own_total, kv, top_out, total_out, rows, values):
+def near_kernel(q0, q1, q2, q, kv, top_out, total_out, rows, values):
     k = split(kv, values)
     for i, ref in enumerate((q0, q1, q2, q)):
         rows[i] = stacked(ref)
     states = run([(i, rows.at[i], k, values) for i in range(3)], [empty() for _ in range(3)])
     for i, (top, total) in enumerate(states):
         top_out[i], total_out[i] = top, total
-    top_out[3], total_out[3] = own_top[...], own_total[...]
-
-
-def block_kernel(rows, top_in, total_in, kv, top_out, total_out, values):
-    k = split(kv, values)
-    states = [(top_in[i], total_in[i]) for i in range(4)]
-    states = run([(i, rows.at[i], k, values) for i in range(4)], states)
-    for i, (top, total) in enumerate(states):
-        top_out[i], total_out[i] = top, total
-
-
-def last_kernel(rows, top_in, total_in, kv, p0, p1, p2, values):
+
+
+def core_kernel(rows, top_in, total_in, kv, top_out, total_out, values):
     k = split(kv, values)
     states = [(top_in[i], total_in[i]) for i in range(3)]
     states = run([(i, rows.at[i], k, values) for i in range(3)], states)
-    for state, ref in zip(states, (p0, p1, p2)):
-        ref[...] = packed(*finish(*state))
-
-
-def own_last_kernel(rows, top, total, kv, result_ref, level_ref, values):
+    for i, (top, total) in enumerate(states):
+        top_out[i], total_out[i] = top, total
+
+
+def own_kernel_2(rows, top, total, kv0, kv1, top_out, total_out, values):
+    k0, k1 = split(kv0, values.at[0]), split(kv1, values.at[1])
+    tasks = [(0, rows.at[3], k0, values.at[0]), (0, rows.at[3], k1, values.at[1])]
+    top_out[...], total_out[...] = run(tasks, [(top[...], total[...])])[0]
+
+
+def far_kernel(rows, top, total, kv0, kv1, *refs, owners):
+    *outs, values = refs
+    k0, k1 = split(kv0, values.at[0]), split(kv1, values.at[1])
+    tasks = []
+    for i, owner in enumerate(owners):
+        tasks.append((i, rows.at[owner], k0, values.at[0]))
+        tasks.append((i, rows.at[owner], k1, values.at[1]))
+    states = run(tasks, [(top[owner], total[owner]) for owner in owners])
+    for state, out in zip(states, outs):
+        out[...] = packed(*finish(*state))
+
+
+def own_last_kernel(rows, top, total, kv, r2, result_ref, level_ref, values):
     k = split(kv, values)
-    states = run([(0, rows.at[3], k, values)], [(top[3], total[3])])
-    result, level = finish(*states[0])
+    states = run([(0, rows.at[3], k, values)], [(top[...], total[...])])
+    result, level = merged([finish(*states[0]), unpacked(r2)])
     result_ref[...] = result
     level_ref[...] = jnp.broadcast_to(level, (8, LANES))
 
 
-def merge_kernel(live, result, level, r0, r1, r2, att):
-    parts = [(result[...], level[:1])] + [unpacked(r) for r in (r0, r1, r2)]
+def merge_kernel(live, result, level, r0, r1, att):
+    parts = [(result[...], level[:1])] + [unpacked(r) for r in (r0, r1)]
     whole, _ = merged(parts)
     slot = lax.broadcasted_iota(jnp.int32, (1, LANES), 1) % ROWS
     rows = jnp.where(slot < live[0], whole, 0.0).T.astype(jnp.bfloat16)
@@ -231,7 +240,7 @@
     ones_shape = (positions, 2 * DH)
 
     own_state = [((LANES, DH), f32), ((LANES, 2 * DH), f32)]
-    state = [((4, LANES, DH), f32), ((4, LANES, 2 * DH), f32)]
+    state = [((3, LANES, DH), f32), ((3, LANES, 2 * DH), f32)]
 
     (kv,) = call(join_kernel, [((2 * positions, DH), bf16)])(prefix_keys, prefix_values)
     kv_x = moved(kv, xh=1)
@@ -245,25 +254,31 @@
         after(queries, q_z[0]), question_keys, question_values, bias, kv
     )
     top, total, rows = call(near_kernel, state + [((4, LANES, DH), bf16)], scratch)(
-        *q_z, queries, own_top, own_total, kv
-    )
-    top, total = call(block_kernel, state, scratch)(rows, top, total, kv_c)
-
-    kv_x, weight, top, total = lax.optimization_barrier((kv_x, out_weight, top, total))
+        *q_z, after(queries, own_top), kv
+    )
+    top, total = call(core_kernel, state, scratch)(rows, top, total, kv_c)
+
+    kv_x, weight, top = lax.optimization_barrier((kv_x, out_weight, top))
     kv_xc = moved(kv_x, c=1)
     weight_c = moved(weight, c=1)
-    top, total = call(block_kernel, state, scratch, flops=4 * block_flops)(rows, top, total, kv_x)
-    parts = call(last_kernel, [part] * 3, scratch, flops=3 * block_flops)(rows, top, total, kv_xc)
-    back = [moved(p, z=-z) for p, z in zip(parts, FAR)]
+    pair = [pltpu.VMEM((2,) + ones_shape, bf16)]
+    own_top, own_total = call(own_kernel_2, own_state, pair, flops=2 * block_flops)(
+        rows, own_top, own_total, kv_c, kv_x
+    )
+    top = after(top, own_top)
+    (p_far,) = call(functools.partial(far_kernel, owners=(2,)), [part], pair, flops=1)(
+        rows, top, total, kv_x, kv_xc
+    )
+    p_next = call(functools.partial(far_kernel, owners=(0, 1)), [part] * 2, pair, flops=4 * block_flops)(
+        rows, after(top, p_far), total, kv_x, kv_xc
+    )
+    back = [moved(p, z=-z) for p, z in zip((*p_next, p_far), FAR)]
     result, level = call(
-        own_last_kernel,
-        [((DH, LANES), f32), ((8, LANES), f32)],
-        [pltpu.VMEM(ones_shape, bf16)],
-        flops=block_flops,
-    )(after(rows, *parts), top, total, kv_xc)
+        own_last_kernel, [((DH, LANES), f32), ((8, LANES), f32)], scratch, flops=1
+    )(after(rows, *p_next), own_top, own_total, kv_xc, back[2])
     (att,) = call(
-        merge_kernel, [((ROWS, GROUP * DH), bf16)], in_specs=[smem] + [vmem] * 5
-    )(live_rows, result, level, *back)
+        merge_kernel, [((ROWS, GROUP * DH), bf16)], in_specs=[smem] + [vmem] * 4
+    )(live_rows, result, level, *back[:2])
 
     att_x = moved(att, xh=1)
     held = [att] + [moved(att, z=z) for z in FAR] + [att_x] + [moved(att_x, z=z) for z in FAR]

time: 94.4 us -> 91.8 us (0.972)
  waiting for transfers between devices: 21 us -> 17.2 us
  starting transfers between devices: 27.4 us -> 29.1 us
  blocking collectives: 17 us -> 16 us
    ppermute x18, waiting for transfers between devices: 21 us -> 17.2 us  [moved(): return lax.ppermute(array, 'blk', pairs)]
    ppermute x18, starting transfers between devices: 27.4 us -> 29.1 us  [moved(): return lax.ppermute(array, 'blk', pairs)]
    all_to_all x1, blocking collectives: 17 us -> 16 us  [shards(): gathered = lax.all_to_all(terms, 'head', 0, 0, tiled=True)]
    pallas_call x4 -> x5, Pallas kernels: 17 us -> 17.6 us  [the longest x1 5.49 us: shards(): call(functools.partial(far_kernel, owners=(0, 1)), [part] * 2, pair, flop...]
  transfers between devices with their start and end apart: 18 -> 18, of which waited for: 9 -> 9; matrix products, arithmetic and copies ran while one was open for 0% -> 0% of each run, Pallas kernels for 25% -> 26%
where the time goes in v7:
time: 91.8 us; the launch traced here: 91.6 us
  starting transfers between devices  29.1 us (32%)
  Pallas kernels  25.7 us (28%)
  waiting for transfers between devices  17.2 us (19%)
  blocking collectives  16 us (17%)
  local copies, waits for them, and re-layouts  2.14 us (2%)
    ppermute x18, starting transfers between devices, moved(): return lax.ppermute(array, 'blk', pairs)  29.1 us
    ppermute x18, waiting for transfers between devices, moved(): return lax.ppermute(array, 'blk', pairs)  17.2 us
    all_to_all x1, blocking collectives, shards(): gathered = lax.all_to_all(terms, 'head', 0, 0, tiled=True)  16 us
    pallas_call x1, Pallas kernels, shards(): call(functools.partial(far_kernel, owners=(0, 1)), [part] * 2, pair, flop...  5.49 us
    pallas_call x1, Pallas kernels, shards(): call(near_kernel, state + [((4, LANES, DH), bf16)], scratch)  3.89 us
    pallas_call x1, Pallas kernels, shards(): top, total = call(core_kernel, state, scratch)(rows, top, total, kv_c)  3.86 us
    pallas_call x1, Pallas kernels, shards(): call(functools.partial(far_kernel, owners=(2,)), [part], pair, flops=1)  2.85 us
    pallas_call x1, Pallas kernels, shards(): call(own_kernel_2, own_state, pair, flops=2 * block_flops)  2.76 us
  transfers between devices with their start and end apart: 18, of which 9 were waited for; matrix products, arithmetic and copies ran while one was open for 0% of the time, Pallas kernels for 26%

profile of v7, /device:TPU:1, one launch (start us, length us, event | category | flops | bytes accessed | tf_op | source)
XLA Modules:
  0.0 91.6 jit_solution(5492840828669833185)
XLA Ops:
  0.0 0.0 copy-start.1
  0.0 0.0 copy-start.2
  0.0 1.1 %copy-done.2 = bf16[2048,128]{1,0:T(8,128)(2,1)S(1)} copy-done((bf16[2048,128]{1,0:T(8,128)(2,1)S(1)}, bf16[2048,128]{1,0:T(8,128)(2,1)}, u32[]{:S(2)}) %copy-start.2) | copy-done | bytes 524312
  1.1 0.0 copy-start.3
  1.1 1.0 %copy-done.3 = bf16[2048,128]{1,0:T(8,128)(2,1)S(1)} copy-done((bf16[2048,128]{1,0:T(8,128)(2,1)S(1)}, bf16[2048,128]{1,0:T(8,128)(2,1)}, u32[]{:S(2)}) %copy-start.3) | copy-done | bytes 524312
  2.1 0.0 copy-start.6
  2.1 0.0 copy-start.4
  2.1 0.0 copy-start.5
  2.1 0.1 shard_map.82.kv
  2.2 1.5 %collective-permute-start.4 = (bf16[4096,128]{1,0:T(8,128)(2,1)S(1)}, bf16[4096,128]{1,0:T(8,128)(2,1)S(1)}, u32[]{:S(2)}, u32[]{:S(2)}) collective-permute-start(bf16[4096,128]{1,0:T(8,128)(2,1)S(1)} %shard_map.82.kv), channel_id=1, source_target_pairs={{0,8},{8,0},{16,24},{24,16},{32,40},{40,32},{48,56},{56,48},{64,72... | collective-permute-start | bytes 3145736 | tf_op jit(solution)/shard_map/ppermute | solution.py:28
  3.7 2.8 %collective-permute-start.3 = (bf16[4096,128]{1,0:T(8,128)(2,1)S(1)}, bf16[4096,128]{1,0:T(8,128)(2,1)S(1)}, u32[]{:S(2)}, u32[]{:S(2)}) collective-permute-start(bf16[4096,128]{1,0:T(8,128)(2,1)S(1)} %shard_map.82.kv), channel_id=1, source_target_pairs={{0,64},{8,72},{16,80},{24,88},{32,96},{40,104},{48,112},{56,120},{... | collective-permute-start | bytes 3145736 | tf_op jit(solution)/shard_map/ppermute | solution.py:28
  6.5 0.0 copy-done.1
  6.5 1.6 %collective-permute-start = (bf16[64,1024]{1,0:T(8,128)(2,1)S(1)}, bf16[64,1024]{1,0:T(8,128)(2,1)S(1)}, u32[]{:S(2)}, u32[]{:S(2)}) collective-permute-start(bf16[64,1024]{1,0:T(8,128)(2,1)S(1)} %copy-done.1), channel_id=1, source_target_pairs={{0,16},{8,24},{16,32},{24,40},{32,48},{40,56},{48,0},{56,8},{64,80... | collective-permute-start | bytes 393224 | tf_op jit(solution)/shard_map/ppermute | solution.py:28
  8.2 2.1 %collective-permute-start.1 = (bf16[64,1024]{1,0:T(8,128)(2,1)S(1)}, bf16[64,1024]{1,0:T(8,128)(2,1)S(1)}, u32[]{:S(2)}, u32[]{:S(2)}) collective-permute-start(bf16[64,1024]{1,0:T(8,128)(2,1)S(1)} %copy-done.1), channel_id=1, source_target_pairs={{0,48},{8,56},{16,0},{24,8},{32,16},{40,24},{48,32},{56,40},{64,11... | collective-permute-start | bytes 393224 | tf_op jit(solution)/shard_map/ppermute | solution.py:28
  10.3 1.3 %collective-permute-start.2 = (bf16[64,1024]{1,0:T(8,128)(2,1)S(1)}, bf16[64,1024]{1,0:T(8,128)(2,1)S(1)}, u32[]{:S(2)}, u32[]{:S(2)}) collective-permute-start(bf16[64,1024]{1,0:T(8,128)(2,1)S(1)} %copy-done.1), channel_id=1, source_target_pairs={{0,32},{8,40},{16,48},{24,56},{32,0},{40,8},{48,16},{56,24},{64,96... | collective-permute-start | bytes 393224 | tf_op jit(solution)/shard_map/ppermute | solution.py:28
  11.6 0.0 copy-done.6
  11.6 0.1 fusion.1.bias
  11.7 2.2 %collective-permute-done.q0 = bf16[64,1024]{1,0:T(8,128)(2,1)S(1)} collective-permute-done((bf16[64,1024]{1,0:T(8,128)(2,1)S(1)}, bf16[64,1024]{1,0:T(8,128)(2,1)S(1)}, u32[]{:S(2)}, u32[]{:S(2)}) %collective-permute-start) | collective-permute-done | bytes 131104 | tf_op jit(solution)/shard_map/ppermute | solution.py:28
  13.9 0.0 copy-done.4
  13.9 0.0 copy-done.5
  13.9 2.5 %shard_map.83 = (f32[512,128]{1,0:T(8,128)S(1)}, f32[512,256]{1,0:T(8,128)S(1)}) custom-call(bf16[64,1024]{1,0:T(8,128)(2,1)S(1)} %copy-done.1, bf16[64,128]{1,0:T(8,128)(2,1)S(1)} %copy-done.4, bf16[64,128]{1,0:T(8,128)(2,1)S(1)} %copy-done.5, f32[64,64]{1,0:T(8,128)S(1)} %fusion.1.bias, bf16[4096,128]{1,0:T(8,128)(2,1)S(1)} %shard_map.82.kv), custom_call_target="tpu_custom_call" | custom-call | tf_op jit(solution)/shard_map/pallas_call | solution.py:253
  16.4 0.0 collective-permute-done.1.q1
  16.5 1.1 %collective-permute-done.2.q2 = bf16[64,1024]{1,0:T(8,128)(2,1)S(1)} collective-permute-done((bf16[64,1024]{1,0:T(8,128)(2,1)S(1)}, bf16[64,1024]{1,0:T(8,128)(2,1)S(1)}, u32[]{:S(2)}, u32[]{:S(2)}) %collective-permute-start.2) | collective-permute-done | bytes 131104 | tf_op jit(solution)/shard_map/ppermute | solution.py:28
  17.6 3.9 %shard_map.84 = (f32[3,512,128]{2,1,0:T(8,128)S(1)}, f32[3,512,256]{2,1,0:T(8,128)S(1)}, bf16[4,512,128]{2,1,0:T(8,128)(2,1)S(1)}) custom-call(bf16[64,1024]{1,0:T(8,128)(2,1)S(1)} %collective-permute-done.q0, bf16[64,1024]{1,0:T(8,128)(2,1)S(1)} %collective-permute-done.1.q1, bf16[64,1024]{1,0:T(8,128)(2,1)S(1)} %collective-permute-done.2.q2, ...), custom_call_target="tpu_custom_call" | custom-call | tf_op jit(solution)/shard_map/pallas_call | solution.py:256
  21.5 0.0 collective-permute-done.4.kv.kv0
  21.5 0.0 copy-start
  21.5 3.9 %shard_map.85 = (f32[3,512,128]{2,1,0:T(8,128)S(1)}, f32[3,512,256]{2,1,0:T(8,128)S(1)}) custom-call(bf16[4,512,128]{2,1,0:T(8,128)(2,1)S(1)} %get-tuple-element.44.rows, f32[3,512,128]{2,1,0:T(8,128)S(1)} %get-tuple-element.32.top_in, f32[3,512,256]{2,1,0:T(8,128)S(1)} %get-tuple-element.33.total_in, bf16[4096,128]{1,0:T(8,128)(2,1)S(1)} %collective-permute-done.4.kv.kv0), custom_call_target="tpu_custom_call" | custom-call | tf_op jit(solution)/shard_map/pallas_call | solution.py:259
  25.3 4.6 %collective-permute-done.3.kv1.kv0 = bf16[4096,128]{1,0:T(8,128)(2,1)S(1)} collective-permute-done((bf16[4096,128]{1,0:T(8,128)(2,1)S(1)}, bf16[4096,128]{1,0:T(8,128)(2,1)S(1)}, u32[]{:S(2)}, u32[]{:S(2)}) %collective-permute-start.3) | collective-permute-done | bytes 1048608 | tf_op jit(solution)/shard_map/ppermute | solution.py:28
  29.9 0.9 collective-permute-start.5
  30.8 0.0 copy-done
  30.8 0.0 collective-permute-start.16
  30.8 2.8 %shard_map.86 = (f32[512,128]{1,0:T(8,128)S(1)}, f32[512,256]{1,0:T(8,128)S(1)}) custom-call(bf16[4,512,128]{2,1,0:T(8,128)(2,1)S(1)} %get-tuple-element.44.rows, f32[512,128]{1,0:T(8,128)S(1)} %get-tuple-element.29.top, f32[512,256]{1,0:T(8,128)S(1)} %get-tuple-element.36.total, bf16[4096,128]{1,0:T(8,128)(2,1)S(1)} %collective-permute-done.4.kv.kv0, ...), custom_call_target="tpu_custom_call" | custom-call | flops 2147483648 | tf_op jit(solution)/shard_map/pallas_call | solution.py:265
  33.6 0.0 collective-permute-done.5.kv1.kv
  33.6 2.9 %shard_map.87 = bf16[144,512]{1,0:T(8,128)(2,1)S(1)} custom-call(bf16[4,512,128]{2,1,0:T(8,128)(2,1)S(1)} %get-tuple-element.44.rows, f32[3,512,128]{2,1,0:T(8,128)S(1)} %get-tuple-element.41.top, f32[3,512,256]{2,1,0:T(8,128)S(1)} %get-tuple-element.40.total, bf16[4096,128]{1,0:T(8,128)(2,1)S(1)} %collective-permute-done.3.kv1.kv0, ...), custom_call_target="tpu_custom_call" | custom-call | flops 1 | tf_op jit(solution)/shard_map/pallas_call | solution.py:269
  36.4 3.8 %collective-permute-start.6 = (bf16[144,512]{1,0:T(8,128)(2,1)S(1)}, bf16[144,512]{1,0:T(8,128)(2,1)S(1)}, u32[]{:S(2)}, u32[]{:S(2)}) collective-permute-start(bf16[144,512]{1,0:T(8,128)(2,1)S(1)} %shard_map.87), channel_id=1, source_target_pairs={{0,32},{8,40},{16,48},{24,56},{32,0},{40,8},{48,16},{56,24},{64,96... | collective-permute-start | bytes 442376 | tf_op jit(solution)/shard_map/ppermute | solution.py:28
  40.2 5.5 %shard_map.88 = (bf16[144,512]{1,0:T(8,128)(2,1)S(1)}, bf16[144,512]{1,0:T(8,128)(2,1)S(1)}) custom-call(bf16[4,512,128]{2,1,0:T(8,128)(2,1)S(1)} %get-tuple-element.44.rows, f32[3,512,128]{2,1,0:T(8,128)S(1)} %get-tuple-element.41.top, f32[3,512,256]{2,1,0:T(8,128)S(1)} %get-tuple-element.40.total, bf16[4096,128]{1,0:T(8,128)(2,1)S(1)} %collective-permute-done.3.kv1.kv0, ...), custom_call_target="tpu_custom_call" | custom-call | flops 4294967296 | tf_op jit(solution)/shard_map/pallas_call | solution.py:272
  45.7 0.5 collective-permute-start.7
  46.2 1.0 %collective-permute-start.8 = (bf16[144,512]{1,0:T(8,128)(2,1)S(1)}, bf16[144,512]{1,0:T(8,128)(2,1)S(1)}, u32[]{:S(2)}, u32[]{:S(2)}) collective-permute-start(bf16[144,512]{1,0:T(8,128)(2,1)S(1)} %get-tuple-element.43), channel_id=1, source_target_pairs={{0,16},{8,24},{16,32},{24,40},{32,48},{40,56},{48,0},{56,8},{64,80... | collective-permute-start | bytes 442376 | tf_op jit(solution)/shard_map/ppermute | solution.py:28
  47.9 0.0 collective-permute-done.6.r2
  47.9 2.6 %shard_map.89 = (f32[128,512]{1,0:T(8,128)S(1)}, f32[8,512]{1,0:T(8,128)S(1)}) custom-call(bf16[4,512,128]{2,1,0:T(8,128)(2,1)S(1)} %get-tuple-element.44.rows, f32[512,128]{1,0:T(8,128)S(1)} %get-tuple-element.38.top, f32[512,256]{1,0:T(8,128)S(1)} %get-tuple-element.45.total, bf16[4096,128]{1,0:T(8,128)(2,1)S(1)} %collective-permute-done.5.kv1.kv, ...), custom_call_target="tpu_custom_call" | custom-call | flops 1 | tf_op jit(solution)/shard_map/pallas_call | solution.py:276
  50.6 0.0 collective-permute-done.7.r0
  50.6 0.8 collective-permute-done.8.r1
  51.4 0.2 shard_map.90.a0
  51.6 2.8 %collective-permute-start.12 = (bf16[64,1024]{1,0:T(8,128)(2,1)S(1)}, bf16[64,1024]{1,0:T(8,128)(2,1)S(1)}, u32[]{:S(2)}, u32[]{:S(2)}) collective-permute-start(bf16[64,1024]{1,0:T(8,128)(2,1)S(1)} %shard_map.90.a0), channel_id=1, source_target_pairs={{0,64},{8,72},{16,80},{24,88},{32,96},{40,104},{48,112},{56,120},{... | collective-permute-start | bytes 393224 | tf_op jit(solution)/shard_map/ppermute | solution.py:28
  54.4 0.8 collective-permute-start.10
  55.2 1.1 %collective-permute-start.11 = (bf16[64,1024]{1,0:T(8,128)(2,1)S(1)}, bf16[64,1024]{1,0:T(8,128)(2,1)S(1)}, u32[]{:S(2)}, u32[]{:S(2)}) collective-permute-start(bf16[64,1024]{1,0:T(8,128)(2,1)S(1)} %shard_map.90.a0), channel_id=1, source_target_pairs={{0,32},{8,40},{16,48},{24,56},{32,0},{40,8},{48,16},{56,24},{64,96... | collective-permute-start | bytes 393224 | tf_op jit(solution)/shard_map/ppermute | solution.py:28
  56.3 0.0 collective-permute-start.9
  56.3 0.7 collective-permute-done.12.a4
  57.0 0.9 collective-permute-start.13
  57.9 0.0 collective-permute-done.16.wb
  57.9 1.8 %collective-permute-start.14 = (bf16[64,1024]{1,0:T(8,128)(2,1)S(1)}, bf16[64,1024]{1,0:T(8,128)(2,1)S(1)}, u32[]{:S(2)}, u32[]{:S(2)}) collective-permute-start(bf16[64,1024]{1,0:T(8,128)(2,1)S(1)} %collective-permute-done.12.a4), channel_id=1, source_target_pairs={{0,48},{8,56},{16,0},{24,8},{32,16},{40,24},{48,32},{56,40},{64,11... | collective-permute-start | bytes 393224 | tf_op jit(solution)/shard_map/ppermute | solution.py:28
  59.7 0.0 collective-permute-done.10.a2
  59.7 1.3 %collective-permute-start.15 = (bf16[64,1024]{1,0:T(8,128)(2,1)S(1)}, bf16[64,1024]{1,0:T(8,128)(2,1)S(1)}, u32[]{:S(2)}, u32[]{:S(2)}) collective-permute-start(bf16[64,1024]{1,0:T(8,128)(2,1)S(1)} %collective-permute-done.12.a4), channel_id=1, source_target_pairs={{0,32},{8,40},{16,48},{24,56},{32,0},{40,8},{48,16},{56,24},{64,96... | collective-permute-start | bytes 393224 | tf_op jit(solution)/shard_map/ppermute | solution.py:28
  60.9 0.0 collective-permute-done.11.a3
  60.9 1.6 %collective-permute-done.9.a1 = bf16[64,1024]{1,0:T(8,128)(2,1)S(1)} collective-permute-done((bf16[64,1024]{1,0:T(8,128)(2,1)S(1)}, bf16[64,1024]{1,0:T(8,128)(2,1)S(1)}, u32[]{:S(2)}, u32[]{:S(2)}) %collective-permute-start.9) | collective-permute-done | bytes 131104 | tf_op jit(solution)/shard_map/ppermute | solution.py:28
  62.5 4.0 %collective-permute-done.13.a5 = bf16[64,1024]{1,0:T(8,128)(2,1)S(1)} collective-permute-done((bf16[64,1024]{1,0:T(8,128)(2,1)S(1)}, bf16[64,1024]{1,0:T(8,128)(2,1)S(1)}, u32[]{:S(2)}, u32[]{:S(2)}) %collective-permute-start.13) | collective-permute-done | bytes 131104 | tf_op jit(solution)/shard_map/ppermute | solution.py:28
  66.5 0.0 collective-permute-done.14.a6
  66.5 1.4 %collective-permute-done.15.a7 = bf16[64,1024]{1,0:T(8,128)(2,1)S(1)} collective-permute-done((bf16[64,1024]{1,0:T(8,128)(2,1)S(1)}, bf16[64,1024]{1,0:T(8,128)(2,1)S(1)}, u32[]{:S(2)}, u32[]{:S(2)}) %collective-permute-start.15) | collective-permute-done | bytes 131104 | tf_op jit(solution)/shard_map/ppermute | solution.py:28
  67.8 1.2 %shard_map.91 = bf16[8,64,1024]{2,1,0:T(8,128)(2,1)S(1)} custom-call(s32[1]{0:T(128)} %bitcast.index, bf16[64,1024]{1,0:T(8,128)(2,1)S(1)} %shard_map.90.a0, bf16[64,1024]{1,0:T(8,128)(2,1)S(1)} %collective-permute-done.9.a1, bf16[64,1024]{1,0:T(8,128)(2,1)S(1)} %collective-permute-done.10.a2, bf16[64,1024]{1,0:T(8,128)(2,1)S(1)} %collective-permute-done.11.a3, ...), custom_call_target="tpu_custom_call" | custom-call | tf_op jit(solution)/shard_map/pallas_call | solution.py:286
  69.1 16.0 %all_to_all.5.terms = bf16[8,64,1024]{2,1,0:T(8,128)(2,1)S(1)} all-to-all(bf16[8,64,1024]{2,1,0:T(8,128)(2,1)S(1)} %shard_map.91), channel_id=1, replica_groups=mesh['blk'=16,'head'=8] {'head'}, dimensions={0} | all-to-all | bytes 2097152 | tf_op jit(solution)/shard_map/all_to_all | solution.py:292
  85.1 0.1 shard_map.92
  85.2 4.8 %collective-permute-start.17 = (bf16[64,512]{1,0:T(8,128)(2,1)S(1)}, bf16[64,512]{1,0:T(8,128)(2,1)S(1)}, u32[]{:S(2)}, u32[]{:S(2)}) collective-permute-start(bf16[64,512]{1,0:T(8,128)(2,1)S(1)} %get-tuple-element.50), channel_id=1, source_target_pairs={{0,8},{8,0},{16,24},{24,16},{32,40},{40,32},{48,56},{56,48},{64,72... | collective-permute-start | bytes 196616 | tf_op jit(solution)/shard_map/ppermute | solution.py:28
  90.0 0.9 collective-permute-done.17
  90.9 0.7 maximum_select_fusion
Async XLA Ops:
  0.0 6.5 %copy-start.1 = (bf16[64,1024]{1,0:T(8,128)(2,1)S(1)}, bf16[64,1024]{1,0:T(8,128)(2,1)}, u32[]{:S(2)}) copy-start(bf16[64,1024]{1,0:T(8,128)(2,1)} %q.1) | copy-start | bytes 393220
  0.0 1.1 %copy-start.2 = (bf16[2048,128]{1,0:T(8,128)(2,1)S(1)}, bf16[2048,128]{1,0:T(8,128)(2,1)}, u32[]{:S(2)}) copy-start(bf16[2048,128]{1,0:T(8,128)(2,1)} %k.1) | copy-start | bytes 1572868
  1.1 1.0 %copy-start.3 = (bf16[2048,128]{1,0:T(8,128)(2,1)S(1)}, bf16[2048,128]{1,0:T(8,128)(2,1)}, u32[]{:S(2)}) copy-start(bf16[2048,128]{1,0:T(8,128)(2,1)} %v.1) | copy-start | bytes 1572868
  2.1 9.5 %copy-start.6 = (s32[64]{0:T(128)S(1)}, s32[64]{0:T(128)}, u32[]{:S(2)}) copy-start(s32[64]{0:T(128)} %param.11) | copy-start | bytes 772
  2.1 11.8 %copy-start.4 = (bf16[64,128]{1,0:T(8,128)(2,1)S(1)}, bf16[64,128]{1,0:T(8,128)(2,1)}, u32[]{:S(2)}) copy-start(bf16[64,128]{1,0:T(8,128)(2,1)} %qk.1) | copy-start | bytes 49156
  2.1 11.8 %copy-start.5 = (bf16[64,128]{1,0:T(8,128)(2,1)S(1)}, bf16[64,128]{1,0:T(8,128)(2,1)}, u32[]{:S(2)}) copy-start(bf16[64,128]{1,0:T(8,128)(2,1)} %qv.1) | copy-start | bytes 49156
  2.2 19.3 %collective-permute-start.4 = (bf16[4096,128]{1,0:T(8,128)(2,1)S(1)}, bf16[4096,128]{1,0:T(8,128)(2,1)S(1)}, u32[]{:S(2)}, u32[]{:S(2)}) collective-permute-start(bf16[4096,128]{1,0:T(8,128)(2,1)S(1)} %shard_map.82.kv), channel_id=1, source_target_pairs={{0,8},{8,0},{16,24},{24,16},{32,40},{40,32},{48,56},{56,48},{64,72... | collective-permute-start | bytes 3145736 | tf_op jit(solution)/shard_map/ppermute | solution.py:28
  3.7 26.2 %collective-permute-start.3 = (bf16[4096,128]{1,0:T(8,128)(2,1)S(1)}, bf16[4096,128]{1,0:T(8,128)(2,1)S(1)}, u32[]{:S(2)}, u32[]{:S(2)}) collective-permute-start(bf16[4096,128]{1,0:T(8,128)(2,1)S(1)} %shard_map.82.kv), channel_id=1, source_target_pairs={{0,64},{8,72},{16,80},{24,88},{32,96},{40,104},{48,112},{56,120},{... | collective-permute-start | bytes 3145736 | tf_op jit(solution)/shard_map/ppermute | solution.py:28
  6.5 7.3 %collective-permute-start = (bf16[64,1024]{1,0:T(8,128)(2,1)S(1)}, bf16[64,1024]{1,0:T(8,128)(2,1)S(1)}, u32[]{:S(2)}, u32[]{:S(2)}) collective-permute-start(bf16[64,1024]{1,0:T(8,128)(2,1)S(1)} %copy-done.1), channel_id=1, source_target_pairs={{0,16},{8,24},{16,32},{24,40},{32,48},{40,56},{48,0},{56,8},{64,80... | collective-permute-start | bytes 393224 | tf_op jit(solution)/shard_map/ppermute | solution.py:28
  8.2 8.3 %collective-permute-start.1 = (bf16[64,1024]{1,0:T(8,128)(2,1)S(1)}, bf16[64,1024]{1,0:T(8,128)(2,1)S(1)}, u32[]{:S(2)}, u32[]{:S(2)}) collective-permute-start(bf16[64,1024]{1,0:T(8,128)(2,1)S(1)} %copy-done.1), channel_id=1, source_target_pairs={{0,48},{8,56},{16,0},{24,8},{32,16},{40,24},{48,32},{56,40},{64,11... | collective-permute-start | bytes 393224 | tf_op jit(solution)/shard_map/ppermute | solution.py:28
  10.3 7.2 %collective-permute-start.2 = (bf16[64,1024]{1,0:T(8,128)(2,1)S(1)}, bf16[64,1024]{1,0:T(8,128)(2,1)S(1)}, u32[]{:S(2)}, u32[]{:S(2)}) collective-permute-start(bf16[64,1024]{1,0:T(8,128)(2,1)S(1)} %copy-done.1), channel_id=1, source_target_pairs={{0,32},{8,40},{16,48},{24,56},{32,0},{40,8},{48,16},{56,24},{64,96... | collective-permute-start | bytes 393224 | tf_op jit(solution)/shard_map/ppermute | solution.py:28
  21.5 9.3 %copy-start = (bf16[1024,512]{1,0:T(8,128)(2,1)S(1)}, bf16[1024,512]{1,0:T(8,128)(2,1)}, u32[]{:S(2)}) copy-start(bf16[1024,512]{1,0:T(8,128)(2,1)} %wa.1) | copy-start | bytes 3145732
  29.9 3.7 %collective-permute-start.5 = (bf16[4096,128]{1,0:T(8,128)(2,1)S(1)}, bf16[4096,128]{1,0:T(8,128)(2,1)S(1)}, u32[]{:S(2)}, u32[]{:S(2)}) collective-permute-start(bf16[4096,128]{1,0:T(8,128)(2,1)S(1)} %collective-permute-done.3.kv1.kv0), channel_id=1, source_target_pairs={{0,8},{8,0},{16,24},{24,16},{32,40},{40,32},{48,56},{56,48},{64,72... | collective-permute-start | bytes 3145736 | tf_op jit(solution)/shard_map/ppermute | solution.py:28
  30.8 27.1 %collective-permute-start.16 = (bf16[1024,512]{1,0:T(8,128)(2,1)S(1)}, bf16[1024,512]{1,0:T(8,128)(2,1)S(1)}, u32[]{:S(2)}, u32[]{:S(2)}) collective-permute-start(bf16[1024,512]{1,0:T(8,128)(2,1)S(1)} %copy-done), channel_id=1, source_target_pairs={{0,8},{8,0},{16,24},{24,16},{32,40},{40,32},{48,56},{56,48},{64,72... | collective-permute-start | bytes 3145736 | tf_op jit(solution)/shard_map/ppermute | solution.py:28
  36.4 11.5 %collective-permute-start.6 = (bf16[144,512]{1,0:T(8,128)(2,1)S(1)}, bf16[144,512]{1,0:T(8,128)(2,1)S(1)}, u32[]{:S(2)}, u32[]{:S(2)}) collective-permute-start(bf16[144,512]{1,0:T(8,128)(2,1)S(1)} %shard_map.87), channel_id=1, source_target_pairs={{0,32},{8,40},{16,48},{24,56},{32,0},{40,8},{48,16},{56,24},{64,96... | collective-permute-start | bytes 442376 | tf_op jit(solution)/shard_map/ppermute | solution.py:28
  45.7 4.9 %collective-permute-start.7 = (bf16[144,512]{1,0:T(8,128)(2,1)S(1)}, bf16[144,512]{1,0:T(8,128)(2,1)S(1)}, u32[]{:S(2)}, u32[]{:S(2)}) collective-permute-start(bf16[144,512]{1,0:T(8,128)(2,1)S(1)} %get-tuple-element.42), channel_id=1, source_target_pairs={{0,48},{8,56},{16,0},{24,8},{32,16},{40,24},{48,32},{56,40},{64,11... | collective-permute-start | bytes 442376 | tf_op jit(solution)/shard_map/ppermute | solution.py:28
  46.2 5.2 %collective-permute-start.8 = (bf16[144,512]{1,0:T(8,128)(2,1)S(1)}, bf16[144,512]{1,0:T(8,128)(2,1)S(1)}, u32[]{:S(2)}, u32[]{:S(2)}) collective-permute-start(bf16[144,512]{1,0:T(8,128)(2,1)S(1)} %get-tuple-element.43), channel_id=1, source_target_pairs={{0,16},{8,24},{16,32},{24,40},{32,48},{40,56},{48,0},{56,8},{64,80... | collective-permute-start | bytes 442376 | tf_op jit(solution)/shard_map/ppermute | solution.py:28
  51.6 5.4 %collective-permute-start.12 = (bf16[64,1024]{1,0:T(8,128)(2,1)S(1)}, bf16[64,1024]{1,0:T(8,128)(2,1)S(1)}, u32[]{:S(2)}, u32[]{:S(2)}) collective-permute-start(bf16[64,1024]{1,0:T(8,128)(2,1)S(1)} %shard_map.90.a0), channel_id=1, source_target_pairs={{0,64},{8,72},{16,80},{24,88},{32,96},{40,104},{48,112},{56,120},{... | collective-permute-start | bytes 393224 | tf_op jit(solution)/shard_map/ppermute | solution.py:28
  54.4 5.3 %collective-permute-start.10 = (bf16[64,1024]{1,0:T(8,128)(2,1)S(1)}, bf16[64,1024]{1,0:T(8,128)(2,1)S(1)}, u32[]{:S(2)}, u32[]{:S(2)}) collective-permute-start(bf16[64,1024]{1,0:T(8,128)(2,1)S(1)} %shard_map.90.a0), channel_id=1, source_target_pairs={{0,48},{8,56},{16,0},{24,8},{32,16},{40,24},{48,32},{56,40},{64,11... | collective-permute-start | bytes 393224 | tf_op jit(solution)/shard_map/ppermute | solution.py:28
  55.2 5.7 %collective-permute-start.11 = (bf16[64,1024]{1,0:T(8,128)(2,1)S(1)}, bf16[64,1024]{1,0:T(8,128)(2,1)S(1)}, u32[]{:S(2)}, u32[]{:S(2)}) collective-permute-start(bf16[64,1024]{1,0:T(8,128)(2,1)S(1)} %shard_map.90.a0), channel_id=1, source_target_pairs={{0,32},{8,40},{16,48},{24,56},{32,0},{40,8},{48,16},{56,24},{64,96... | collective-permute-start | bytes 393224 | tf_op jit(solution)/shard_map/ppermute | solution.py:28
  56.3 6.2 %collective-permute-start.9 = (bf16[64,1024]{1,0:T(8,128)(2,1)S(1)}, bf16[64,1024]{1,0:T(8,128)(2,1)S(1)}, u32[]{:S(2)}, u32[]{:S(2)}) collective-permute-start(bf16[64,1024]{1,0:T(8,128)(2,1)S(1)} %shard_map.90.a0), channel_id=1, source_target_pairs={{0,16},{8,24},{16,32},{24,40},{32,48},{40,56},{48,0},{56,8},{64,80... | collective-permute-start | bytes 393224 | tf_op jit(solution)/shard_map/ppermute | solution.py:28
  57.0 9.5 %collective-permute-start.13 = (bf16[64,1024]{1,0:T(8,128)(2,1)S(1)}, bf16[64,1024]{1,0:T(8,128)(2,1)S(1)}, u32[]{:S(2)}, u32[]{:S(2)}) collective-permute-start(bf16[64,1024]{1,0:T(8,128)(2,1)S(1)} %collective-permute-done.12.a4), channel_id=1, source_target_pairs={{0,16},{8,24},{16,32},{24,40},{32,48},{40,56},{48,0},{56,8},{64,80... | collective-permute-start | bytes 393224 | tf_op jit(solution)/shard_map/ppermute | solution.py:28
  57.9 8.6 %collective-permute-start.14 = (bf16[64,1024]{1,0:T(8,128)(2,1)S(1)}, bf16[64,1024]{1,0:T(8,128)(2,1)S(1)}, u32[]{:S(2)}, u32[]{:S(2)}) collective-permute-start(bf16[64,1024]{1,0:T(8,128)(2,1)S(1)} %collective-permute-done.12.a4), channel_id=1, source_target_pairs={{0,48},{8,56},{16,0},{24,8},{32,16},{40,24},{48,32},{56,40},{64,11... | collective-permute-start | bytes 393224 | tf_op jit(solution)/shard_map/ppermute | solution.py:28
  59.7 8.2 %collective-permute-start.15 = (bf16[64,1024]{1,0:T(8,128)(2,1)S(1)}, bf16[64,1024]{1,0:T(8,128)(2,1)S(1)}, u32[]{:S(2)}, u32[]{:S(2)}) collective-permute-start(bf16[64,1024]{1,0:T(8,128)(2,1)S(1)} %collective-permute-done.12.a4), channel_id=1, source_target_pairs={{0,32},{8,40},{16,48},{24,56},{32,0},{40,8},{48,16},{56,24},{64,96... | collective-permute-start | bytes 393224 | tf_op jit(solution)/shard_map/ppermute | solution.py:28
  85.2 5.7 %collective-permute-start.17 = (bf16[64,512]{1,0:T(8,128)(2,1)S(1)}, bf16[64,512]{1,0:T(8,128)(2,1)S(1)}, u32[]{:S(2)}, u32[]{:S(2)}) collective-permute-start(bf16[64,512]{1,0:T(8,128)(2,1)S(1)} %get-tuple-element.50), channel_id=1, source_target_pairs={{0,8},{8,0},{16,24},{24,16},{32,40},{40,32},{48,56},{56,48},{64,72... | collective-permute-start | bytes 196616 | tf_op jit(solution)/shard_map/ppermute | solution.py:28

commit v8 on v7

--- a/solution.py
+++ b/solution.py
@@ -280,8 +280,8 @@
         merge_kernel, [((ROWS, GROUP * DH), bf16)], in_specs=[smem] + [vmem] * 4
     )(live_rows, result, level, *back[:2])
 
-    att_x = moved(att, xh=1)
-    held = [att] + [moved(att, z=z) for z in FAR] + [att_x] + [moved(att_x, z=z) for z in FAR]
+    held = [att] + [moved(att, z=z) for z in FAR]
+    held = held + [moved(rows, xh=1) for rows in held]
     width = out_weight.shape[1]
     (terms,) = call(
         project_kernel,

time: 91.8 us -> 91.6 us (level)
  starting transfers between devices: 29.1 us -> 32.8 us
  waiting for transfers between devices: 17.2 us -> 14.7 us
  blocking collectives: 16 us -> 14.5 us
    ppermute x18, starting transfers between devices: 29.1 us -> 32.8 us  [moved(): return lax.ppermute(array, 'blk', pairs)]
    ppermute x18, waiting for transfers between devices: 17.2 us -> 14.7 us  [moved(): return lax.ppermute(array, 'blk', pairs)]
    all_to_all x1, blocking collectives: 16 us -> 14.5 us  [shards(): gathered = lax.all_to_all(terms, 'head', 0, 0, tiled=True)]
  transfers between devices with their start and end apart: 18 -> 18, of which waited for: 9 -> 8; matrix products, arithmetic and copies ran while one was open for 0% -> 0% of each run, Pallas kernels for 26% -> 27%
where the time goes in v8:
time: 91.6 us; the launch traced here: 91.4 us
  starting transfers between devices  32.8 us (36%)
  Pallas kernels  25.7 us (28%)
  waiting for transfers between devices  14.7 us (16%)
  blocking collectives  14.5 us (16%)
  local copies, waits for them, and re-layouts  2.14 us (2%)
    ppermute x18, starting transfers between devices, moved(): return lax.ppermute(array, 'blk', pairs)  32.8 us
    ppermute x18, waiting for transfers between devices, moved(): return lax.ppermute(array, 'blk', pairs)  14.7 us
    all_to_all x1, blocking collectives, shards(): gathered = lax.all_to_all(terms, 'head', 0, 0, tiled=True)  14.5 us
    pallas_call x1, Pallas kernels, shards(): call(functools.partial(far_kernel, owners=(0, 1)), [part] * 2, pair, flop...  5.49 us
    pallas_call x1, Pallas kernels, shards(): call(near_kernel, state + [((4, LANES, DH), bf16)], scratch)  3.89 us
    pallas_call x1, Pallas kernels, shards(): top, total = call(core_kernel, state, scratch)(rows, top, total, kv_c)  3.86 us
    pallas_call x1, Pallas kernels, shards(): call(functools.partial(far_kernel, owners=(2,)), [part], pair, flops=1)  2.85 us
    pallas_call x1, Pallas kernels, shards(): call(own_kernel_2, own_state, pair, flops=2 * block_flops)  2.76 us
  transfers between devices with their start and end apart: 18, of which 8 were waited for; matrix products, arithmetic and copies ran while one was open for 0% of the time, Pallas kernels for 27%

profile of v8, /device:TPU:1, one launch (start us, length us, event | category | flops | bytes accessed | tf_op | source)
XLA Modules:
  0.0 91.4 jit_solution(16925502911804994908)
XLA Ops:
  0.0 0.0 copy-start.1
  0.0 0.0 copy-start.2
  0.0 1.1 %copy-done.2 = bf16[2048,128]{1,0:T(8,128)(2,1)S(1)} copy-done((bf16[2048,128]{1,0:T(8,128)(2,1)S(1)}, bf16[2048,128]{1,0:T(8,128)(2,1)}, u32[]{:S(2)}) %copy-start.2) | copy-done | bytes 524312
  1.1 0.0 copy-start.3
  1.1 1.0 %copy-done.3 = bf16[2048,128]{1,0:T(8,128)(2,1)S(1)} copy-done((bf16[2048,128]{1,0:T(8,128)(2,1)S(1)}, bf16[2048,128]{1,0:T(8,128)(2,1)}, u32[]{:S(2)}) %copy-start.3) | copy-done | bytes 524312
  2.1 0.0 copy-start.6
  2.1 0.0 copy-start.4
  2.1 0.0 copy-start.5
  2.1 0.1 shard_map.82.kv
  2.2 1.5 %collective-permute-start.4 = (bf16[4096,128]{1,0:T(8,128)(2,1)S(1)}, bf16[4096,128]{1,0:T(8,128)(2,1)S(1)}, u32[]{:S(2)}, u32[]{:S(2)}) collective-permute-start(bf16[4096,128]{1,0:T(8,128)(2,1)S(1)} %shard_map.82.kv), channel_id=1, source_target_pairs={{0,8},{8,0},{16,24},{24,16},{32,40},{40,32},{48,56},{56,48},{64,72... | collective-permute-start | bytes 3145736 | tf_op jit(solution)/shard_map/ppermute | solution.py:28
  3.7 2.8 %collective-permute-start.3 = (bf16[4096,128]{1,0:T(8,128)(2,1)S(1)}, bf16[4096,128]{1,0:T(8,128)(2,1)S(1)}, u32[]{:S(2)}, u32[]{:S(2)}) collective-permute-start(bf16[4096,128]{1,0:T(8,128)(2,1)S(1)} %shard_map.82.kv), channel_id=1, source_target_pairs={{0,64},{8,72},{16,80},{24,88},{32,96},{40,104},{48,112},{56,120},{... | collective-permute-start | bytes 3145736 | tf_op jit(solution)/shard_map/ppermute | solution.py:28
  6.5 0.0 copy-done.1
  6.5 1.6 %collective-permute-start = (bf16[64,1024]{1,0:T(8,128)(2,1)S(1)}, bf16[64,1024]{1,0:T(8,128)(2,1)S(1)}, u32[]{:S(2)}, u32[]{:S(2)}) collective-permute-start(bf16[64,1024]{1,0:T(8,128)(2,1)S(1)} %copy-done.1), channel_id=1, source_target_pairs={{0,16},{8,24},{16,32},{24,40},{32,48},{40,56},{48,0},{56,8},{64,80... | collective-permute-start | bytes 393224 | tf_op jit(solution)/shard_map/ppermute | solution.py:28
  8.2 2.1 %collective-permute-start.1 = (bf16[64,1024]{1,0:T(8,128)(2,1)S(1)}, bf16[64,1024]{1,0:T(8,128)(2,1)S(1)}, u32[]{:S(2)}, u32[]{:S(2)}) collective-permute-start(bf16[64,1024]{1,0:T(8,128)(2,1)S(1)} %copy-done.1), channel_id=1, source_target_pairs={{0,48},{8,56},{16,0},{24,8},{32,16},{40,24},{48,32},{56,40},{64,11... | collective-permute-start | bytes 393224 | tf_op jit(solution)/shard_map/ppermute | solution.py:28
  10.3 1.3 %collective-permute-start.2 = (bf16[64,1024]{1,0:T(8,128)(2,1)S(1)}, bf16[64,1024]{1,0:T(8,128)(2,1)S(1)}, u32[]{:S(2)}, u32[]{:S(2)}) collective-permute-start(bf16[64,1024]{1,0:T(8,128)(2,1)S(1)} %copy-done.1), channel_id=1, source_target_pairs={{0,32},{8,40},{16,48},{24,56},{32,0},{40,8},{48,16},{56,24},{64,96... | collective-permute-start | bytes 393224 | tf_op jit(solution)/shard_map/ppermute | solution.py:28
  11.6 0.0 copy-done.6
  11.6 0.1 fusion.1.bias
  11.7 2.2 %collective-permute-done.q0 = bf16[64,1024]{1,0:T(8,128)(2,1)S(1)} collective-permute-done((bf16[64,1024]{1,0:T(8,128)(2,1)S(1)}, bf16[64,1024]{1,0:T(8,128)(2,1)S(1)}, u32[]{:S(2)}, u32[]{:S(2)}) %collective-permute-start) | collective-permute-done | bytes 131104 | tf_op jit(solution)/shard_map/ppermute | solution.py:28
  13.9 0.0 copy-done.4
  13.9 0.0 copy-done.5
  13.9 2.5 %shard_map.83 = (f32[512,128]{1,0:T(8,128)S(1)}, f32[512,256]{1,0:T(8,128)S(1)}) custom-call(bf16[64,1024]{1,0:T(8,128)(2,1)S(1)} %copy-done.1, bf16[64,128]{1,0:T(8,128)(2,1)S(1)} %copy-done.4, bf16[64,128]{1,0:T(8,128)(2,1)S(1)} %copy-done.5, f32[64,64]{1,0:T(8,128)S(1)} %fusion.1.bias, bf16[4096,128]{1,0:T(8,128)(2,1)S(1)} %shard_map.82.kv), custom_call_target="tpu_custom_call" | custom-call | tf_op jit(solution)/shard_map/pallas_call | solution.py:253
  16.4 0.0 collective-permute-done.1.q1
  16.5 1.1 %collective-permute-done.2.q2 = bf16[64,1024]{1,0:T(8,128)(2,1)S(1)} collective-permute-done((bf16[64,1024]{1,0:T(8,128)(2,1)S(1)}, bf16[64,1024]{1,0:T(8,128)(2,1)S(1)}, u32[]{:S(2)}, u32[]{:S(2)}) %collective-permute-start.2) | collective-permute-done | bytes 131104 | tf_op jit(solution)/shard_map/ppermute | solution.py:28
  17.6 3.9 %shard_map.84 = (f32[3,512,128]{2,1,0:T(8,128)S(1)}, f32[3,512,256]{2,1,0:T(8,128)S(1)}, bf16[4,512,128]{2,1,0:T(8,128)(2,1)S(1)}) custom-call(bf16[64,1024]{1,0:T(8,128)(2,1)S(1)} %collective-permute-done.q0, bf16[64,1024]{1,0:T(8,128)(2,1)S(1)} %collective-permute-done.1.q1, bf16[64,1024]{1,0:T(8,128)(2,1)S(1)} %collective-permute-done.2.q2, ...), custom_call_target="tpu_custom_call" | custom-call | tf_op jit(solution)/shard_map/pallas_call | solution.py:256
  21.5 0.0 collective-permute-done.4.kv.kv0
  21.5 0.0 copy-start
  21.5 3.9 %shard_map.85 = (f32[3,512,128]{2,1,0:T(8,128)S(1)}, f32[3,512,256]{2,1,0:T(8,128)S(1)}) custom-call(bf16[4,512,128]{2,1,0:T(8,128)(2,1)S(1)} %get-tuple-element.44.rows, f32[3,512,128]{2,1,0:T(8,128)S(1)} %get-tuple-element.32.top_in, f32[3,512,256]{2,1,0:T(8,128)S(1)} %get-tuple-element.33.total_in, bf16[4096,128]{1,0:T(8,128)(2,1)S(1)} %collective-permute-done.4.kv.kv0), custom_call_target="tpu_custom_call" | custom-call | tf_op jit(solution)/shard_map/pallas_call | solution.py:259
  25.3 4.6 %collective-permute-done.3.kv1.kv0 = bf16[4096,128]{1,0:T(8,128)(2,1)S(1)} collective-permute-done((bf16[4096,128]{1,0:T(8,128)(2,1)S(1)}, bf16[4096,128]{1,0:T(8,128)(2,1)S(1)}, u32[]{:S(2)}, u32[]{:S(2)}) %collective-permute-start.3) | collective-permute-done | bytes 1048608 | tf_op jit(solution)/shard_map/ppermute | solution.py:28
  29.9 0.9 collective-permute-start.5
  30.8 0.0 copy-done
  30.8 0.0 collective-permute-start.16
  30.8 2.8 %shard_map.86 = (f32[512,128]{1,0:T(8,128)S(1)}, f32[512,256]{1,0:T(8,128)S(1)}) custom-call(bf16[4,512,128]{2,1,0:T(8,128)(2,1)S(1)} %get-tuple-element.44.rows, f32[512,128]{1,0:T(8,128)S(1)} %get-tuple-element.29.top, f32[512,256]{1,0:T(8,128)S(1)} %get-tuple-element.36.total, bf16[4096,128]{1,0:T(8,128)(2,1)S(1)} %collective-permute-done.4.kv.kv0, ...), custom_call_target="tpu_custom_call" | custom-call | flops 2147483648 | tf_op jit(solution)/shard_map/pallas_call | solution.py:265
  33.6 0.0 collective-permute-done.5.kv1.kv
  33.6 2.9 %shard_map.87 = bf16[144,512]{1,0:T(8,128)(2,1)S(1)} custom-call(bf16[4,512,128]{2,1,0:T(8,128)(2,1)S(1)} %get-tuple-element.44.rows, f32[3,512,128]{2,1,0:T(8,128)S(1)} %get-tuple-element.41.top, f32[3,512,256]{2,1,0:T(8,128)S(1)} %get-tuple-element.40.total, bf16[4096,128]{1,0:T(8,128)(2,1)S(1)} %collective-permute-done.3.kv1.kv0, ...), custom_call_target="tpu_custom_call" | custom-call | flops 1 | tf_op jit(solution)/shard_map/pallas_call | solution.py:269
  36.4 3.8 %collective-permute-start.6 = (bf16[144,512]{1,0:T(8,128)(2,1)S(1)}, bf16[144,512]{1,0:T(8,128)(2,1)S(1)}, u32[]{:S(2)}, u32[]{:S(2)}) collective-permute-start(bf16[144,512]{1,0:T(8,128)(2,1)S(1)} %shard_map.87), channel_id=1, source_target_pairs={{0,32},{8,40},{16,48},{24,56},{32,0},{40,8},{48,16},{56,24},{64,96... | collective-permute-start | bytes 442376 | tf_op jit(solution)/shard_map/ppermute | solution.py:28
  40.2 5.5 %shard_map.88 = (bf16[144,512]{1,0:T(8,128)(2,1)S(1)}, bf16[144,512]{1,0:T(8,128)(2,1)S(1)}) custom-call(bf16[4,512,128]{2,1,0:T(8,128)(2,1)S(1)} %get-tuple-element.44.rows, f32[3,512,128]{2,1,0:T(8,128)S(1)} %get-tuple-element.41.top, f32[3,512,256]{2,1,0:T(8,128)S(1)} %get-tuple-element.40.total, bf16[4096,128]{1,0:T(8,128)(2,1)S(1)} %collective-permute-done.3.kv1.kv0, ...), custom_call_target="tpu_custom_call" | custom-call | flops 4294967296 | tf_op jit(solution)/shard_map/pallas_call | solution.py:272
  45.7 0.5 collective-permute-start.7
  46.2 1.0 %collective-permute-start.8 = (bf16[144,512]{1,0:T(8,128)(2,1)S(1)}, bf16[144,512]{1,0:T(8,128)(2,1)S(1)}, u32[]{:S(2)}, u32[]{:S(2)}) collective-permute-start(bf16[144,512]{1,0:T(8,128)(2,1)S(1)} %get-tuple-element.43), channel_id=1, source_target_pairs={{0,16},{8,24},{16,32},{24,40},{32,48},{40,56},{48,0},{56,8},{64,80... | collective-permute-start | bytes 442376 | tf_op jit(solution)/shard_map/ppermute | solution.py:28
  47.9 0.0 collective-permute-done.6.r2
  47.9 2.6 %shard_map.89 = (f32[128,512]{1,0:T(8,128)S(1)}, f32[8,512]{1,0:T(8,128)S(1)}) custom-call(bf16[4,512,128]{2,1,0:T(8,128)(2,1)S(1)} %get-tuple-element.44.rows, f32[512,128]{1,0:T(8,128)S(1)} %get-tuple-element.38.top, f32[512,256]{1,0:T(8,128)S(1)} %get-tuple-element.45.total, bf16[4096,128]{1,0:T(8,128)(2,1)S(1)} %collective-permute-done.5.kv1.kv, ...), custom_call_target="tpu_custom_call" | custom-call | flops 1 | tf_op jit(solution)/shard_map/pallas_call | solution.py:276
  50.6 0.0 collective-permute-done.7.r0
  50.6 0.8 collective-permute-done.8.r1
  51.4 0.2 shard_map.90.a0
  51.6 0.2 collective-permute-start.9
  51.8 2.6 %collective-permute-start.10 = (bf16[64,1024]{1,0:T(8,128)(2,1)S(1)}, bf16[64,1024]{1,0:T(8,128)(2,1)S(1)}, u32[]{:S(2)}, u32[]{:S(2)}) collective-permute-start(bf16[64,1024]{1,0:T(8,128)(2,1)S(1)} %shard_map.90.a0), channel_id=1, source_target_pairs={{0,48},{8,56},{16,0},{24,8},{32,16},{40,24},{48,32},{56,40},{64,11... | collective-permute-start | bytes 393224 | tf_op jit(solution)/shard_map/ppermute | solution.py:28
  54.3 0.0 collective-permute-start.11
  54.3 2.7 %collective-permute-start.12 = (bf16[64,1024]{1,0:T(8,128)(2,1)S(1)}, bf16[64,1024]{1,0:T(8,128)(2,1)S(1)}, u32[]{:S(2)}, u32[]{:S(2)}) collective-permute-start(bf16[64,1024]{1,0:T(8,128)(2,1)S(1)} %shard_map.90.a0), channel_id=1, source_target_pairs={{0,64},{8,72},{16,80},{24,88},{32,96},{40,104},{48,112},{56,120},{... | collective-permute-start | bytes 393224 | tf_op jit(solution)/shard_map/ppermute | solution.py:28
  57.1 0.0 collective-permute-done.9.a1
  57.1 2.3 %collective-permute-start.13 = (bf16[64,1024]{1,0:T(8,128)(2,1)S(1)}, bf16[64,1024]{1,0:T(8,128)(2,1)S(1)}, u32[]{:S(2)}, u32[]{:S(2)}) collective-permute-start(bf16[64,1024]{1,0:T(8,128)(2,1)S(1)} %collective-permute-done.9.a1), channel_id=1, source_target_pairs={{0,64},{8,72},{16,80},{24,88},{32,96},{40,104},{48,112},{56,120},{... | collective-permute-start | bytes 393224 | tf_op jit(solution)/shard_map/ppermute | solution.py:28
  59.4 0.0 collective-permute-done.10.a2
  59.4 1.0 %collective-permute-start.14 = (bf16[64,1024]{1,0:T(8,128)(2,1)S(1)}, bf16[64,1024]{1,0:T(8,128)(2,1)S(1)}, u32[]{:S(2)}, u32[]{:S(2)}) collective-permute-start(bf16[64,1024]{1,0:T(8,128)(2,1)S(1)} %collective-permute-done.10.a2), channel_id=1, source_target_pairs={{0,64},{8,72},{16,80},{24,88},{32,96},{40,104},{48,112},{56,120},{... | collective-permute-start | bytes 393224 | tf_op jit(solution)/shard_map/ppermute | solution.py:28
  60.4 0.0 collective-permute-done.11.a3
  60.4 2.1 %collective-permute-start.15 = (bf16[64,1024]{1,0:T(8,128)(2,1)S(1)}, bf16[64,1024]{1,0:T(8,128)(2,1)S(1)}, u32[]{:S(2)}, u32[]{:S(2)}) collective-permute-start(bf16[64,1024]{1,0:T(8,128)(2,1)S(1)} %collective-permute-done.11.a3), channel_id=1, source_target_pairs={{0,64},{8,72},{16,80},{24,88},{32,96},{40,104},{48,112},{56,120},{... | collective-permute-start | bytes 393224 | tf_op jit(solution)/shard_map/ppermute | solution.py:28
  62.5 0.0 collective-permute-done.16.wb
  62.5 0.0 collective-permute-done.12.a4
  62.5 1.1 %collective-permute-done.13.a5 = bf16[64,1024]{1,0:T(8,128)(2,1)S(1)} collective-permute-done((bf16[64,1024]{1,0:T(8,128)(2,1)S(1)}, bf16[64,1024]{1,0:T(8,128)(2,1)S(1)}, u32[]{:S(2)}, u32[]{:S(2)}) %collective-permute-start.13) | collective-permute-done | bytes 131104 | tf_op jit(solution)/shard_map/ppermute | solution.py:28
  63.7 1.6 %collective-permute-done.14.a6 = bf16[64,1024]{1,0:T(8,128)(2,1)S(1)} collective-permute-done((bf16[64,1024]{1,0:T(8,128)(2,1)S(1)}, bf16[64,1024]{1,0:T(8,128)(2,1)S(1)}, u32[]{:S(2)}, u32[]{:S(2)}) %collective-permute-start.14) | collective-permute-done | bytes 131104 | tf_op jit(solution)/shard_map/ppermute | solution.py:28
  65.2 2.4 %collective-permute-done.15.a7 = bf16[64,1024]{1,0:T(8,128)(2,1)S(1)} collective-permute-done((bf16[64,1024]{1,0:T(8,128)(2,1)S(1)}, bf16[64,1024]{1,0:T(8,128)(2,1)S(1)}, u32[]{:S(2)}, u32[]{:S(2)}) %collective-permute-start.15) | collective-permute-done | bytes 131104 | tf_op jit(solution)/shard_map/ppermute | solution.py:28
  67.6 1.2 %shard_map.91 = bf16[8,64,1024]{2,1,0:T(8,128)(2,1)S(1)} custom-call(s32[1]{0:T(128)} %bitcast.index, bf16[64,1024]{1,0:T(8,128)(2,1)S(1)} %shard_map.90.a0, bf16[64,1024]{1,0:T(8,128)(2,1)S(1)} %collective-permute-done.9.a1, bf16[64,1024]{1,0:T(8,128)(2,1)S(1)} %collective-permute-done.10.a2, bf16[64,1024]{1,0:T(8,128)(2,1)S(1)} %collective-permute-done.11.a3, ...), custom_call_target="tpu_custom_call" | custom-call | tf_op jit(solution)/shard_map/pallas_call | solution.py:286
  68.9 14.5 %all_to_all.5.terms = bf16[8,64,1024]{2,1,0:T(8,128)(2,1)S(1)} all-to-all(bf16[8,64,1024]{2,1,0:T(8,128)(2,1)S(1)} %shard_map.91), channel_id=1, replica_groups=mesh['blk'=16,'head'=8] {'head'}, dimensions={0} | all-to-all | bytes 2097152 | tf_op jit(solution)/shard_map/all_to_all | solution.py:292
  83.4 0.1 shard_map.92
  83.5 6.3 %collective-permute-start.17 = (bf16[64,512]{1,0:T(8,128)(2,1)S(1)}, bf16[64,512]{1,0:T(8,128)(2,1)S(1)}, u32[]{:S(2)}, u32[]{:S(2)}) collective-permute-start(bf16[64,512]{1,0:T(8,128)(2,1)S(1)} %get-tuple-element.50), channel_id=1, source_target_pairs={{0,8},{8,0},{16,24},{24,16},{32,40},{40,32},{48,56},{56,48},{64,72... | collective-permute-start | bytes 196616 | tf_op jit(solution)/shard_map/ppermute | solution.py:28
  89.8 0.9 collective-permute-done.17
  90.7 0.7 maximum_select_fusion
Async XLA Ops:
  0.0 6.5 %copy-start.1 = (bf16[64,1024]{1,0:T(8,128)(2,1)S(1)}, bf16[64,1024]{1,0:T(8,128)(2,1)}, u32[]{:S(2)}) copy-start(bf16[64,1024]{1,0:T(8,128)(2,1)} %q.1) | copy-start | bytes 393220
  0.0 1.1 %copy-start.2 = (bf16[2048,128]{1,0:T(8,128)(2,1)S(1)}, bf16[2048,128]{1,0:T(8,128)(2,1)}, u32[]{:S(2)}) copy-start(bf16[2048,128]{1,0:T(8,128)(2,1)} %k.1) | copy-start | bytes 1572868
  1.1 1.0 %copy-start.3 = (bf16[2048,128]{1,0:T(8,128)(2,1)S(1)}, bf16[2048,128]{1,0:T(8,128)(2,1)}, u32[]{:S(2)}) copy-start(bf16[2048,128]{1,0:T(8,128)(2,1)} %v.1) | copy-start | bytes 1572868
  2.1 9.5 %copy-start.6 = (s32[64]{0:T(128)S(1)}, s32[64]{0:T(128)}, u32[]{:S(2)}) copy-start(s32[64]{0:T(128)} %param.11) | copy-start | bytes 772
  2.1 11.8 %copy-start.4 = (bf16[64,128]{1,0:T(8,128)(2,1)S(1)}, bf16[64,128]{1,0:T(8,128)(2,1)}, u32[]{:S(2)}) copy-start(bf16[64,128]{1,0:T(8,128)(2,1)} %qk.1) | copy-start | bytes 49156
  2.1 11.8 %copy-start.5 = (bf16[64,128]{1,0:T(8,128)(2,1)S(1)}, bf16[64,128]{1,0:T(8,128)(2,1)}, u32[]{:S(2)}) copy-start(bf16[64,128]{1,0:T(8,128)(2,1)} %qv.1) | copy-start | bytes 49156
  2.2 19.3 %collective-permute-start.4 = (bf16[4096,128]{1,0:T(8,128)(2,1)S(1)}, bf16[4096,128]{1,0:T(8,128)(2,1)S(1)}, u32[]{:S(2)}, u32[]{:S(2)}) collective-permute-start(bf16[4096,128]{1,0:T(8,128)(2,1)S(1)} %shard_map.82.kv), channel_id=1, source_target_pairs={{0,8},{8,0},{16,24},{24,16},{32,40},{40,32},{48,56},{56,48},{64,72... | collective-permute-start | bytes 3145736 | tf_op jit(solution)/shard_map/ppermute | solution.py:28
  3.7 26.2 %collective-permute-start.3 = (bf16[4096,128]{1,0:T(8,128)(2,1)S(1)}, bf16[4096,128]{1,0:T(8,128)(2,1)S(1)}, u32[]{:S(2)}, u32[]{:S(2)}) collective-permute-start(bf16[4096,128]{1,0:T(8,128)(2,1)S(1)} %shard_map.82.kv), channel_id=1, source_target_pairs={{0,64},{8,72},{16,80},{24,88},{32,96},{40,104},{48,112},{56,120},{... | collective-permute-start | bytes 3145736 | tf_op jit(solution)/shard_map/ppermute | solution.py:28
  6.5 7.3 %collective-permute-start = (bf16[64,1024]{1,0:T(8,128)(2,1)S(1)}, bf16[64,1024]{1,0:T(8,128)(2,1)S(1)}, u32[]{:S(2)}, u32[]{:S(2)}) collective-permute-start(bf16[64,1024]{1,0:T(8,128)(2,1)S(1)} %copy-done.1), channel_id=1, source_target_pairs={{0,16},{8,24},{16,32},{24,40},{32,48},{40,56},{48,0},{56,8},{64,80... | collective-permute-start | bytes 393224 | tf_op jit(solution)/shard_map/ppermute | solution.py:28
  8.2 8.3 %collective-permute-start.1 = (bf16[64,1024]{1,0:T(8,128)(2,1)S(1)}, bf16[64,1024]{1,0:T(8,128)(2,1)S(1)}, u32[]{:S(2)}, u32[]{:S(2)}) collective-permute-start(bf16[64,1024]{1,0:T(8,128)(2,1)S(1)} %copy-done.1), channel_id=1, source_target_pairs={{0,48},{8,56},{16,0},{24,8},{32,16},{40,24},{48,32},{56,40},{64,11... | collective-permute-start | bytes 393224 | tf_op jit(solution)/shard_map/ppermute | solution.py:28
  10.3 7.2 %collective-permute-start.2 = (bf16[64,1024]{1,0:T(8,128)(2,1)S(1)}, bf16[64,1024]{1,0:T(8,128)(2,1)S(1)}, u32[]{:S(2)}, u32[]{:S(2)}) collective-permute-start(bf16[64,1024]{1,0:T(8,128)(2,1)S(1)} %copy-done.1), channel_id=1, source_target_pairs={{0,32},{8,40},{16,48},{24,56},{32,0},{40,8},{48,16},{56,24},{64,96... | collective-permute-start | bytes 393224 | tf_op jit(solution)/shard_map/ppermute | solution.py:28
  21.5 9.3 %copy-start = (bf16[1024,512]{1,0:T(8,128)(2,1)S(1)}, bf16[1024,512]{1,0:T(8,128)(2,1)}, u32[]{:S(2)}) copy-start(bf16[1024,512]{1,0:T(8,128)(2,1)} %wa.1) | copy-start | bytes 3145732
  29.9 3.7 %collective-permute-start.5 = (bf16[4096,128]{1,0:T(8,128)(2,1)S(1)}, bf16[4096,128]{1,0:T(8,128)(2,1)S(1)}, u32[]{:S(2)}, u32[]{:S(2)}) collective-permute-start(bf16[4096,128]{1,0:T(8,128)(2,1)S(1)} %collective-permute-done.3.kv1.kv0), channel_id=1, source_target_pairs={{0,8},{8,0},{16,24},{24,16},{32,40},{40,32},{48,56},{56,48},{64,72... | collective-permute-start | bytes 3145736 | tf_op jit(solution)/shard_map/ppermute | solution.py:28
  30.8 31.7 %collective-permute-start.16 = (bf16[1024,512]{1,0:T(8,128)(2,1)S(1)}, bf16[1024,512]{1,0:T(8,128)(2,1)S(1)}, u32[]{:S(2)}, u32[]{:S(2)}) collective-permute-start(bf16[1024,512]{1,0:T(8,128)(2,1)S(1)} %copy-done), channel_id=1, source_target_pairs={{0,8},{8,0},{16,24},{24,16},{32,40},{40,32},{48,56},{56,48},{64,72... | collective-permute-start | bytes 3145736 | tf_op jit(solution)/shard_map/ppermute | solution.py:28
  36.4 11.5 %collective-permute-start.6 = (bf16[144,512]{1,0:T(8,128)(2,1)S(1)}, bf16[144,512]{1,0:T(8,128)(2,1)S(1)}, u32[]{:S(2)}, u32[]{:S(2)}) collective-permute-start(bf16[144,512]{1,0:T(8,128)(2,1)S(1)} %shard_map.87), channel_id=1, source_target_pairs={{0,32},{8,40},{16,48},{24,56},{32,0},{40,8},{48,16},{56,24},{64,96... | collective-permute-start | bytes 442376 | tf_op jit(solution)/shard_map/ppermute | solution.py:28
  45.7 4.9 %collective-permute-start.7 = (bf16[144,512]{1,0:T(8,128)(2,1)S(1)}, bf16[144,512]{1,0:T(8,128)(2,1)S(1)}, u32[]{:S(2)}, u32[]{:S(2)}) collective-permute-start(bf16[144,512]{1,0:T(8,128)(2,1)S(1)} %get-tuple-element.42), channel_id=1, source_target_pairs={{0,48},{8,56},{16,0},{24,8},{32,16},{40,24},{48,32},{56,40},{64,11... | collective-permute-start | bytes 442376 | tf_op jit(solution)/shard_map/ppermute | solution.py:28
  46.2 5.2 %collective-permute-start.8 = (bf16[144,512]{1,0:T(8,128)(2,1)S(1)}, bf16[144,512]{1,0:T(8,128)(2,1)S(1)}, u32[]{:S(2)}, u32[]{:S(2)}) collective-permute-start(bf16[144,512]{1,0:T(8,128)(2,1)S(1)} %get-tuple-element.43), channel_id=1, source_target_pairs={{0,16},{8,24},{16,32},{24,40},{32,48},{40,56},{48,0},{56,8},{64,80... | collective-permute-start | bytes 442376 | tf_op jit(solution)/shard_map/ppermute | solution.py:28
  51.6 5.5 %collective-permute-start.9 = (bf16[64,1024]{1,0:T(8,128)(2,1)S(1)}, bf16[64,1024]{1,0:T(8,128)(2,1)S(1)}, u32[]{:S(2)}, u32[]{:S(2)}) collective-permute-start(bf16[64,1024]{1,0:T(8,128)(2,1)S(1)} %shard_map.90.a0), channel_id=1, source_target_pairs={{0,16},{8,24},{16,32},{24,40},{32,48},{40,56},{48,0},{56,8},{64,80... | collective-permute-start | bytes 393224 | tf_op jit(solution)/shard_map/ppermute | solution.py:28
  51.8 7.7 %collective-permute-start.10 = (bf16[64,1024]{1,0:T(8,128)(2,1)S(1)}, bf16[64,1024]{1,0:T(8,128)(2,1)S(1)}, u32[]{:S(2)}, u32[]{:S(2)}) collective-permute-start(bf16[64,1024]{1,0:T(8,128)(2,1)S(1)} %shard_map.90.a0), channel_id=1, source_target_pairs={{0,48},{8,56},{16,0},{24,8},{32,16},{40,24},{48,32},{56,40},{64,11... | collective-permute-start | bytes 393224 | tf_op jit(solution)/shard_map/ppermute | solution.py:28
  54.3 6.1 %collective-permute-start.11 = (bf16[64,1024]{1,0:T(8,128)(2,1)S(1)}, bf16[64,1024]{1,0:T(8,128)(2,1)S(1)}, u32[]{:S(2)}, u32[]{:S(2)}) collective-permute-start(bf16[64,1024]{1,0:T(8,128)(2,1)S(1)} %shard_map.90.a0), channel_id=1, source_target_pairs={{0,32},{8,40},{16,48},{24,56},{32,0},{40,8},{48,16},{56,24},{64,96... | collective-permute-start | bytes 393224 | tf_op jit(solution)/shard_map/ppermute | solution.py:28
  54.3 8.2 %collective-permute-start.12 = (bf16[64,1024]{1,0:T(8,128)(2,1)S(1)}, bf16[64,1024]{1,0:T(8,128)(2,1)S(1)}, u32[]{:S(2)}, u32[]{:S(2)}) collective-permute-start(bf16[64,1024]{1,0:T(8,128)(2,1)S(1)} %shard_map.90.a0), channel_id=1, source_target_pairs={{0,64},{8,72},{16,80},{24,88},{32,96},{40,104},{48,112},{56,120},{... | collective-permute-start | bytes 393224 | tf_op jit(solution)/shard_map/ppermute | solution.py:28
  57.1 6.6 %collective-permute-start.13 = (bf16[64,1024]{1,0:T(8,128)(2,1)S(1)}, bf16[64,1024]{1,0:T(8,128)(2,1)S(1)}, u32[]{:S(2)}, u32[]{:S(2)}) collective-permute-start(bf16[64,1024]{1,0:T(8,128)(2,1)S(1)} %collective-permute-done.9.a1), channel_id=1, source_target_pairs={{0,64},{8,72},{16,80},{24,88},{32,96},{40,104},{48,112},{56,120},{... | collective-permute-start | bytes 393224 | tf_op jit(solution)/shard_map/ppermute | solution.py:28
  59.4 5.8 %collective-permute-start.14 = (bf16[64,1024]{1,0:T(8,128)(2,1)S(1)}, bf16[64,1024]{1,0:T(8,128)(2,1)S(1)}, u32[]{:S(2)}, u32[]{:S(2)}) collective-permute-start(bf16[64,1024]{1,0:T(8,128)(2,1)S(1)} %collective-permute-done.10.a2), channel_id=1, source_target_pairs={{0,64},{8,72},{16,80},{24,88},{32,96},{40,104},{48,112},{56,120},{... | collective-permute-start | bytes 393224 | tf_op jit(solution)/shard_map/ppermute | solution.py:28
  60.4 7.2 %collective-permute-start.15 = (bf16[64,1024]{1,0:T(8,128)(2,1)S(1)}, bf16[64,1024]{1,0:T(8,128)(2,1)S(1)}, u32[]{:S(2)}, u32[]{:S(2)}) collective-permute-start(bf16[64,1024]{1,0:T(8,128)(2,1)S(1)} %collective-permute-done.11.a3), channel_id=1, source_target_pairs={{0,64},{8,72},{16,80},{24,88},{32,96},{40,104},{48,112},{56,120},{... | collective-permute-start | bytes 393224 | tf_op jit(solution)/shard_map/ppermute | solution.py:28
  83.5 7.2 %collective-permute-start.17 = (bf16[64,512]{1,0:T(8,128)(2,1)S(1)}, bf16[64,512]{1,0:T(8,128)(2,1)S(1)}, u32[]{:S(2)}, u32[]{:S(2)}) collective-permute-start(bf16[64,512]{1,0:T(8,128)(2,1)S(1)} %get-tuple-element.50), channel_id=1, source_target_pairs={{0,8},{8,0},{16,24},{24,16},{32,40},{40,32},{48,56},{56,48},{64,72... | collective-permute-start | bytes 196616 | tf_op jit(solution)/shard_map/ppermute | solution.py:28

commit v9 on v8

--- a/solution.py
+++ b/solution.py
@@ -55,17 +55,24 @@
     return jnp.concatenate([ref[:, h * DH : (h + 1) * DH] for h in range(GROUP)], axis=0)
 
 
-def join_kernel(k, v, kv):
-    half = k.shape[0]
-    kv[:half, :] = k[...]
-    kv[half:, :] = v[...]
-
-
-def split(kv, scratch):
-    half = kv.shape[0] // 2
-    scratch[:, :DH] = kv[half:, :]
-    scratch[:, DH:] = jnp.ones((half, DH), kv.dtype)
-    return kv.at[pl.ds(0, half)]
+def join_kernel(k, v, whole, first, second):
+    size = k.shape[0]
+    half = size // 2
+    whole[:size, :] = k[...]
+    whole[size:, :] = v[...]
+    for i, kv in enumerate((first, second)):
+        kv[:half, :] = k[i * half : (i + 1) * half, :]
+        kv[half:, :] = v[i * half : (i + 1) * half, :]
+
+
+def split(parts, keys, values):
+    at = 0
+    for kv in parts:
+        size = kv.shape[0] // 2
+        keys[at : at + size, :] = kv[:size, :]
+        values[at : at + size, :DH] = kv[size:, :]
+        at += size
+    values[:, DH:] = jnp.ones((at, DH), values.dtype)
 
 
 def finish(top, total):
@@ -120,21 +127,21 @@
     )
 
 
-def own_kernel(q, qk, qv, bias, kv, top_out, total_out, values):
-    k = split(kv, values)
+def own_kernel(q, qk, qv, bias, kv, top_out, total_out, k, values):
+    split((kv,), k, values)
     rows = stacked(q)
     scores = scores_of(rows, qk[...]) + jnp.concatenate([bias[...]] * GROUP, axis=0)
-    far = scores_of(rows, k[...])
+    block = scores_of(rows, k[...])
     top, total = add_block(
         *empty(),
         scores,
         jnp.concatenate([qv[...], jnp.ones((ROWS, DH), jnp.bfloat16)], axis=1),
     )
-    top_out[...], total_out[...] = add_block(top, total, far, values[...])
-
-
-def near_kernel(q0, q1, q2, q, kv, top_out, total_out, rows, values):
-    k = split(kv, values)
+    top_out[...], total_out[...] = add_block(top, total, block, values[...])
+
+
+def near_kernel(q0, q1, q2, q, kv, top_out, total_out, rows, k, values):
+    split((kv,), k, values)
     for i, ref in enumerate((q0, q1, q2, q)):
         rows[i] = stacked(ref)
     states = run([(i, rows.at[i], k, values) for i in range(3)], [empty() for _ in range(3)])
@@ -142,34 +149,33 @@
         top_out[i], total_out[i] = top, total
 
 
-def core_kernel(rows, top_in, total_in, kv, top_out, total_out, values):
-    k = split(kv, values)
+def others_kernel(rows, top_in, total_in, *refs):
+    *parts, top_out, total_out, k, values = refs
+    split(parts, k, values)
     states = [(top_in[i], total_in[i]) for i in range(3)]
     states = run([(i, rows.at[i], k, values) for i in range(3)], states)
     for i, (top, total) in enumerate(states):
         top_out[i], total_out[i] = top, total
 
 
-def own_kernel_2(rows, top, total, kv0, kv1, top_out, total_out, values):
-    k0, k1 = split(kv0, values.at[0]), split(kv1, values.at[1])
-    tasks = [(0, rows.at[3], k0, values.at[0]), (0, rows.at[3], k1, values.at[1])]
+def own_kernel_2(rows, top, total, kv, half, other_half, top_out, total_out, k, values):
+    split((kv,), k.at[0], values.at[0])
+    split((half, other_half), k.at[1], values.at[1])
+    tasks = [(0, rows.at[3], k.at[i], values.at[i]) for i in range(2)]
     top_out[...], total_out[...] = run(tasks, [(top[...], total[...])])[0]
 
 
-def far_kernel(rows, top, total, kv0, kv1, *refs, owners):
-    *outs, values = refs
-    k0, k1 = split(kv0, values.at[0]), split(kv1, values.at[1])
-    tasks = []
-    for i, owner in enumerate(owners):
-        tasks.append((i, rows.at[owner], k0, values.at[0]))
-        tasks.append((i, rows.at[owner], k1, values.at[1]))
+def last_kernel(rows, top, total, half, other_half, *refs, owners):
+    *outs, k, values = refs
+    split((half, other_half), k, values)
+    tasks = [(i, rows.at[owner], k, values) for i, owner in enumerate(owners)]
     states = run(tasks, [(top[owner], total[owner]) for owner in owners])
     for state, out in zip(states, outs):
         out[...] = packed(*finish(*state))
 
 
-def own_last_kernel(rows, top, total, kv, r2, result_ref, level_ref, values):
-    k = split(kv, values)
+def own_last_kernel(rows, top, total, half, other_half, r2, result_ref, level_ref, k, values):
+    split((half, other_half), k, values)
     states = run([(0, rows.at[3], k, values)], [(top[...], total[...])])
     result, level = merged([finish(*states[0]), unpacked(r2)])
     result_ref[...] = result
@@ -242,40 +248,45 @@
     own_state = [((LANES, DH), f32), ((LANES, 2 * DH), f32)]
     state = [((3, LANES, DH), f32), ((3, LANES, 2 * DH), f32)]
 
-    (kv,) = call(join_kernel, [((2 * positions, DH), bf16)])(prefix_keys, prefix_values)
-    kv_x = moved(kv, xh=1)
+    kv, *halves = call(
+        join_kernel, [((2 * positions, DH), bf16)] + [((positions, DH), bf16)] * 2
+    )(prefix_keys, prefix_values)
+    x0, x1 = [moved(half, xh=1) for half in halves]
     kv_c = moved(kv, c=1)
     q_z = [moved(queries, z=z) for z in FAR]
     row = jnp.arange(ROWS, dtype=jnp.int32)
     allowed = (question_ids[:, None] == question_ids[None, :]) & (row[None, :] <= row[:, None])
     bias = jnp.where(allowed, 0.0, FLOOR).astype(f32)
-    scratch = [pltpu.VMEM(ones_shape, bf16)]
+    scratch = [pltpu.VMEM((positions, DH), bf16), pltpu.VMEM(ones_shape, bf16)]
     own_top, own_total = call(own_kernel, own_state, scratch)(
-        after(queries, q_z[0]), question_keys, question_values, bias, kv
+        after(queries, *q_z), question_keys, question_values, bias, kv
     )
     top, total, rows = call(near_kernel, state + [((4, LANES, DH), bf16)], scratch)(
         *q_z, after(queries, own_top), kv
     )
-    top, total = call(core_kernel, state, scratch)(rows, top, total, kv_c)
-
-    kv_x, weight, top = lax.optimization_barrier((kv_x, out_weight, top))
-    kv_xc = moved(kv_x, c=1)
+    x0 = after(x0, own_top)
+    xc0 = moved(x0, c=1)
+    top, total = call(others_kernel, state, scratch, flops=1)(rows, top, total, kv_c)
+    top, total = call(others_kernel, state, scratch, flops=1)(rows, top, total, x0, xc0)
+
+    x1, weight, top = lax.optimization_barrier((x1, out_weight, top))
+    xc1 = moved(x1, c=1)
     weight_c = moved(weight, c=1)
-    pair = [pltpu.VMEM((2,) + ones_shape, bf16)]
+    pair = [pltpu.VMEM((2, positions, DH), bf16), pltpu.VMEM((2,) + ones_shape, bf16)]
     own_top, own_total = call(own_kernel_2, own_state, pair, flops=2 * block_flops)(
-        rows, own_top, own_total, kv_c, kv_x
+        after(rows, x1), own_top, own_total, kv_c, x0, xc0
     )
     top = after(top, own_top)
-    (p_far,) = call(functools.partial(far_kernel, owners=(2,)), [part], pair, flops=1)(
-        rows, top, total, kv_x, kv_xc
-    )
-    p_next = call(functools.partial(far_kernel, owners=(0, 1)), [part] * 2, pair, flops=4 * block_flops)(
-        rows, after(top, p_far), total, kv_x, kv_xc
-    )
+    (p_far,) = call(functools.partial(last_kernel, owners=(2,)), [part], scratch, flops=1)(
+        rows, top, total, x1, xc1
+    )
+    p_next = call(
+        functools.partial(last_kernel, owners=(0, 1)), [part] * 2, scratch, flops=4 * block_flops
+    )(rows, after(top, p_far), total, x1, xc1)
     back = [moved(p, z=-z) for p, z in zip((*p_next, p_far), FAR)]
     result, level = call(
         own_last_kernel, [((DH, LANES), f32), ((8, LANES), f32)], scratch, flops=1
-    )(after(rows, *p_next), own_top, own_total, kv_xc, back[2])
+    )(after(rows, *p_next), own_top, own_total, x1, xc1, back[2])
     (att,) = call(
         merge_kernel, [((ROWS, GROUP * DH), bf16)], in_specs=[smem] + [vmem] * 4
     )(live_rows, result, level, *back[:2])

time: 91.6 us -> 95.9 us (1.047)
  starting transfers between devices: 32.8 us -> 29.1 us
  local copies, waits for them, and re-layouts: 2.14 us -> 4.47 us
  waiting for transfers between devices: 14.7 us -> 16.7 us
  blocking collectives: 14.5 us -> 16 us
  Pallas kernels: 25.7 us -> 27.1 us
    ppermute x18 -> x20, starting transfers between devices: 32.8 us -> 29.1 us  [moved(): return lax.ppermute(array, 'blk', pairs)]
    unnamed x14, local copies, waits for them, and re-layouts: 2.14 us -> 4.47 us
    ppermute x18 -> x20, waiting for transfers between devices: 14.7 us -> 16.7 us  [moved(): return lax.ppermute(array, 'blk', pairs)]
    all_to_all x1, blocking collectives: 14.5 us -> 16 us  [shards(): gathered = lax.all_to_all(terms, 'head', 0, 0, tiled=True)]
    pallas_call x4 -> x5, Pallas kernels: 12.3 us -> 13.5 us  [the longest x1 3.91 us: shards(): call(others_kernel, state, scratch, flops=1)(rows, top, total, kv_c)]
  transfers between devices with their start and end apart: 18 -> 20, of which waited for: 8 -> 8; matrix products, arithmetic and copies ran while one was open for 0% -> 1% of each run, Pallas kernels for 27% -> 27%
where the time goes in v9:
time: 95.9 us; the launch traced here: 95.5 us
  starting transfers between devices  29.1 us (30%)
  Pallas kernels  27.1 us (28%)
  waiting for transfers between devices  16.7 us (17%)
  blocking collectives  16 us (17%)
  local copies, waits for them, and re-layouts  4.47 us (5%)
  other arithmetic  1.48 us (2%)
    ppermute x20, starting transfers between devices, moved(): return lax.ppermute(array, 'blk', pairs)  29.1 us
    ppermute x20, waiting for transfers between devices, moved(): return lax.ppermute(array, 'blk', pairs)  16.7 us
    all_to_all x1, blocking collectives, shards(): gathered = lax.all_to_all(terms, 'head', 0, 0, tiled=True)  16 us
    unnamed x14, local copies, waits for them, and re-layouts  4.47 us
    pallas_call x1, Pallas kernels, shards(): call(near_kernel, state + [((4, LANES, DH), bf16)], scratch)  3.96 us
    pallas_call x1, Pallas kernels, shards(): call(others_kernel, state, scratch, flops=1)(rows, top, total, kv_c)  3.91 us
    pallas_call x1, Pallas kernels, shards(): call(others_kernel, state, scratch, flops=1)(rows, top, total, x0, xc0)  3.91 us
    pallas_call x1, Pallas kernels, shards(): call(functools.partial(last_kernel, owners=(0, 1)), [part] * 2, scratch,...  2.88 us
  transfers between devices with their start and end apart: 20, of which 8 were waited for; matrix products, arithmetic and copies ran while one was open for 1% of the time, Pallas kernels for 27%

profile of v9, /device:TPU:1, one launch (start us, length us, event | category | flops | bytes accessed | tf_op | source)
XLA Modules:
  0.0 95.5 jit_solution(2117304271622992974)
XLA Ops:
  0.0 0.0 copy-start.2
  0.0 1.1 %copy-done.3 = bf16[2048,128]{1,0:T(8,128)(2,1)S(1)} copy-done((bf16[2048,128]{1,0:T(8,128)(2,1)S(1)}, bf16[2048,128]{1,0:T(8,128)(2,1)}, u32[]{:S(2)}) %copy-start.3) | copy-done | bytes 524312
  1.1 1.0 %copy-done.4 = bf16[2048,128]{1,0:T(8,128)(2,1)S(1)} copy-done((bf16[2048,128]{1,0:T(8,128)(2,1)S(1)}, bf16[2048,128]{1,0:T(8,128)(2,1)}, u32[]{:S(2)}) %copy-start.4) | copy-done | bytes 524312
  2.1 0.1 shard_map.82
  2.3 1.5 %collective-permute-start.4 = (bf16[4096,128]{1,0:T(8,128)(2,1)S(1)}, bf16[4096,128]{1,0:T(8,128)(2,1)S(1)}, u32[]{:S(2)}, u32[]{:S(2)}) collective-permute-start(bf16[4096,128]{1,0:T(8,128)(2,1)S(1)} %get-tuple-element.36.kv), channel_id=1, source_target_pairs={{0,8},{8,0},{16,24},{24,16},{32,40},{40,32},{48,56},{56,48},{64,72... | collective-permute-start | bytes 3145736 | tf_op jit(solution)/shard_map/ppermute | solution.py:28
  3.8 2.8 %collective-permute-start.5 = (bf16[2048,128]{1,0:T(8,128)(2,1)S(1)}, bf16[2048,128]{1,0:T(8,128)(2,1)S(1)}, u32[]{:S(2)}, u32[]{:S(2)}) collective-permute-start(bf16[2048,128]{1,0:T(8,128)(2,1)S(1)} %get-tuple-element.45), channel_id=1, source_target_pairs={{0,64},{8,72},{16,80},{24,88},{32,96},{40,104},{48,112},{56,120},{... | collective-permute-start | bytes 1572872 | tf_op jit(solution)/shard_map/ppermute | solution.py:28
  6.6 1.6 %collective-permute-start = (bf16[64,1024]{1,0:T(8,128)(2,1)}, bf16[64,1024]{1,0:T(8,128)(2,1)S(1)}, u32[]{:S(2)}, u32[]{:S(2)}) collective-permute-start(bf16[64,1024]{1,0:T(8,128)(2,1)} %q.1), channel_id=1, source_target_pairs={{0,16},{8,24},{16,32},{24,40},{32,48},{40,56},{48,0},{56,8},{64,80... | collective-permute-start | bytes 393224 | tf_op jit(solution)/shard_map/ppermute | solution.py:28
  8.2 2.1 %collective-permute-start.1 = (bf16[64,1024]{1,0:T(8,128)(2,1)}, bf16[64,1024]{1,0:T(8,128)(2,1)S(1)}, u32[]{:S(2)}, u32[]{:S(2)}) collective-permute-start(bf16[64,1024]{1,0:T(8,128)(2,1)} %q.1), channel_id=1, source_target_pairs={{0,48},{8,56},{16,0},{24,8},{32,16},{40,24},{48,32},{56,40},{64,11... | collective-permute-start | bytes 393224 | tf_op jit(solution)/shard_map/ppermute | solution.py:28
  10.4 1.3 %collective-permute-start.2 = (bf16[64,1024]{1,0:T(8,128)(2,1)}, bf16[64,1024]{1,0:T(8,128)(2,1)S(1)}, u32[]{:S(2)}, u32[]{:S(2)}) collective-permute-start(bf16[64,1024]{1,0:T(8,128)(2,1)} %q.1), channel_id=1, source_target_pairs={{0,32},{8,40},{16,48},{24,56},{32,0},{40,8},{48,16},{56,24},{64,96... | collective-permute-start | bytes 393224 | tf_op jit(solution)/shard_map/ppermute | solution.py:28
  11.7 0.8 fusion.1.bias
  12.5 1.7 %collective-permute-done.q0 = bf16[64,1024]{1,0:T(8,128)(2,1)S(1)} collective-permute-done((bf16[64,1024]{1,0:T(8,128)(2,1)}, bf16[64,1024]{1,0:T(8,128)(2,1)S(1)}, u32[]{:S(2)}, u32[]{:S(2)}) %collective-permute-start) | collective-permute-done | bytes 131104 | tf_op jit(solution)/shard_map/ppermute | solution.py:28
  14.2 0.0 collective-permute-done.1.q1
  14.2 3.7 %collective-permute-done.2.q2 = bf16[64,1024]{1,0:T(8,128)(2,1)S(1)} collective-permute-done((bf16[64,1024]{1,0:T(8,128)(2,1)}, bf16[64,1024]{1,0:T(8,128)(2,1)S(1)}, u32[]{:S(2)}, u32[]{:S(2)}) %collective-permute-start.2) | collective-permute-done | bytes 131104 | tf_op jit(solution)/shard_map/ppermute | solution.py:28
  17.8 0.9 copy-done.1
  18.7 0.7 copy-done.5
  19.4 0.7 copy-done.6
  20.2 2.6 %shard_map.83 = (f32[512,128]{1,0:T(8,128)S(1)}, f32[512,256]{1,0:T(8,128)S(1)}) custom-call(bf16[64,1024]{1,0:T(8,128)(2,1)S(1)} %copy-done.1, bf16[64,128]{1,0:T(8,128)(2,1)S(1)} %copy-done.5, bf16[64,128]{1,0:T(8,128)(2,1)S(1)} %copy-done.6, f32[64,64]{1,0:T(8,128)S(1)} %fusion.1.bias, bf16[4096,128]{1,0:T(8,128)(2,1)S(1)} %get-tuple-element.36.kv), custom_call_target="tpu_custom_call" | custom-call | tf_op jit(solution)/shard_map/pallas_call | solution.py:261
  22.8 0.0 collective-permute-done.5.refs_0_.half
  22.8 1.3 %collective-permute-start.6 = (bf16[2048,128]{1,0:T(8,128)(2,1)S(1)}, bf16[2048,128]{1,0:T(8,128)(2,1)S(1)}, u32[]{:S(2)}, u32[]{:S(2)}) collective-permute-start(bf16[2048,128]{1,0:T(8,128)(2,1)S(1)} %collective-permute-done.5.refs_0_.half), channel_id=1, source_target_pairs={{0,8},{8,0},{16,24},{24,16},{32,40},{40,32},{48,56},{56,48},{64,72... | collective-permute-start | bytes 1572872 | tf_op jit(solution)/shard_map/ppermute | solution.py:28
  24.0 0.2 collective-permute-start.3
  24.3 0.0 copy-done.2
  24.3 4.0 %shard_map.84 = (f32[3,512,128]{2,1,0:T(8,128)S(1)}, f32[3,512,256]{2,1,0:T(8,128)S(1)}, bf16[4,512,128]{2,1,0:T(8,128)(2,1)S(1)}) custom-call(bf16[64,1024]{1,0:T(8,128)(2,1)S(1)} %collective-permute-done.q0, bf16[64,1024]{1,0:T(8,128)(2,1)S(1)} %collective-permute-done.1.q1, bf16[64,1024]{1,0:T(8,128)(2,1)S(1)} %collective-permute-done.2.q2, ...), custom_call_target="tpu_custom_call" | custom-call | tf_op jit(solution)/shard_map/pallas_call | solution.py:264
  28.2 0.0 collective-permute-done.4.refs_0_.kv
  28.2 3.9 %shard_map.85 = (f32[3,512,128]{2,1,0:T(8,128)S(1)}, f32[3,512,256]{2,1,0:T(8,128)S(1)}) custom-call(bf16[4,512,128]{2,1,0:T(8,128)(2,1)S(1)} %get-tuple-element.58.rows, f32[3,512,128]{2,1,0:T(8,128)S(1)} %get-tuple-element.41.top_in, f32[3,512,256]{2,1,0:T(8,128)S(1)} %get-tuple-element.42.total_in, bf16[4096,128]{1,0:T(8,128)(2,1)S(1)} %collective-permute-done.4.refs_0_.kv), custom_call_target="tpu_custom_call" | custom-call | flops 1 | tf_op jit(solution)/shard_map/pallas_call | solution.py:269
  32.2 0.0 collective-permute-done.6.refs_1_.other_half
  32.2 0.0 copy-start
  32.2 3.9 %shard_map.86 = (f32[3,512,128]{2,1,0:T(8,128)S(1)}, f32[3,512,256]{2,1,0:T(8,128)S(1)}) custom-call(bf16[4,512,128]{2,1,0:T(8,128)(2,1)S(1)} %get-tuple-element.58.rows, f32[3,512,128]{2,1,0:T(8,128)S(1)} %get-tuple-element.43.top_in, f32[3,512,256]{2,1,0:T(8,128)S(1)} %get-tuple-element.44.total_in, ...), custom_call_target="tpu_custom_call" | custom-call | flops 1 | tf_op jit(solution)/shard_map/pallas_call | solution.py:270
  36.1 2.7 %collective-permute-done.3.half = bf16[2048,128]{1,0:T(8,128)(2,1)S(1)} collective-permute-done((bf16[2048,128]{1,0:T(8,128)(2,1)S(1)}, bf16[2048,128]{1,0:T(8,128)(2,1)S(1)}, u32[]{:S(2)}, u32[]{:S(2)}) %collective-permute-start.3) | collective-permute-done | bytes 524320 | tf_op jit(solution)/shard_map/ppermute | solution.py:28
  38.8 1.1 %collective-permute-start.7 = (bf16[2048,128]{1,0:T(8,128)(2,1)S(1)}, bf16[2048,128]{1,0:T(8,128)(2,1)S(1)}, u32[]{:S(2)}, u32[]{:S(2)}) collective-permute-start(bf16[2048,128]{1,0:T(8,128)(2,1)S(1)} %collective-permute-done.3.half), channel_id=1, source_target_pairs={{0,8},{8,0},{16,24},{24,16},{32,40},{40,32},{48,56},{56,48},{64,72... | collective-permute-start | bytes 1572872 | tf_op jit(solution)/shard_map/ppermute | solution.py:28
  39.9 0.0 copy-done
  39.9 0.0 collective-permute-start.18
  39.9 2.8 %shard_map.87 = (f32[512,128]{1,0:T(8,128)S(1)}, f32[512,256]{1,0:T(8,128)S(1)}) custom-call(bf16[4,512,128]{2,1,0:T(8,128)(2,1)S(1)} %get-tuple-element.58.rows, f32[512,128]{1,0:T(8,128)S(1)} %get-tuple-element.37.top, f32[512,256]{1,0:T(8,128)S(1)} %get-tuple-element.51.total, bf16[4096,128]{1,0:T(8,128)(2,1)S(1)} %collective-permute-done.4.refs_0_.kv, ...), custom_call_target="tpu_custom_call" | custom-call | flops 2147483648 | tf_op jit(solution)/shard_map/pallas_call | solution.py:276
  42.7 0.0 collective-permute-done.7.other_half
  42.7 2.6 %shard_map.88 = bf16[144,512]{1,0:T(8,128)(2,1)S(1)} custom-call(bf16[4,512,128]{2,1,0:T(8,128)(2,1)S(1)} %get-tuple-element.58.rows, f32[3,512,128]{2,1,0:T(8,128)S(1)} %get-tuple-element.55.top, f32[3,512,256]{2,1,0:T(8,128)S(1)} %get-tuple-element.54.total, bf16[2048,128]{1,0:T(8,128)(2,1)S(1)} %collective-permute-done.3.half, ...), custom_call_target="tpu_custom_call" | custom-call | flops 1 | tf_op jit(solution)/shard_map/pallas_call | solution.py:280
  45.4 0.4 collective-permute-start.8
  45.8 2.9 %shard_map.89 = (bf16[144,512]{1,0:T(8,128)(2,1)S(1)}, bf16[144,512]{1,0:T(8,128)(2,1)S(1)}) custom-call(bf16[4,512,128]{2,1,0:T(8,128)(2,1)S(1)} %get-tuple-element.58.rows, f32[3,512,128]{2,1,0:T(8,128)S(1)} %get-tuple-element.55.top, f32[3,512,256]{2,1,0:T(8,128)S(1)} %get-tuple-element.54.total, bf16[2048,128]{1,0:T(8,128)(2,1)S(1)} %collective-permute-done.3.half, ...), custom_call_target="tpu_custom_call" | custom-call | flops 4294967296 | tf_op jit(solution)/shard_map/pallas_call | solution.py:283
  48.6 1.9 %collective-permute-start.10 = (bf16[144,512]{1,0:T(8,128)(2,1)S(1)}, bf16[144,512]{1,0:T(8,128)(2,1)S(1)}, u32[]{:S(2)}, u32[]{:S(2)}) collective-permute-start(bf16[144,512]{1,0:T(8,128)(2,1)S(1)} %get-tuple-element.57), channel_id=1, source_target_pairs={{0,16},{8,24},{16,32},{24,40},{32,48},{40,56},{48,0},{56,8},{64,80... | collective-permute-start | bytes 442376 | tf_op jit(solution)/shard_map/ppermute | solution.py:28
  50.5 1.3 %collective-permute-start.9 = (bf16[144,512]{1,0:T(8,128)(2,1)S(1)}, bf16[144,512]{1,0:T(8,128)(2,1)S(1)}, u32[]{:S(2)}, u32[]{:S(2)}) collective-permute-start(bf16[144,512]{1,0:T(8,128)(2,1)S(1)} %get-tuple-element.56), channel_id=1, source_target_pairs={{0,48},{8,56},{16,0},{24,8},{32,16},{40,24},{48,32},{56,40},{64,11... | collective-permute-start | bytes 442376 | tf_op jit(solution)/shard_map/ppermute | solution.py:28
  52.4 0.0 collective-permute-done.8.r2
  52.4 2.7 %shard_map.90 = (f32[128,512]{1,0:T(8,128)S(1)}, f32[8,512]{1,0:T(8,128)S(1)}) custom-call(bf16[4,512,128]{2,1,0:T(8,128)(2,1)S(1)} %get-tuple-element.58.rows, f32[512,128]{1,0:T(8,128)S(1)} %get-tuple-element.52.top, f32[512,256]{1,0:T(8,128)S(1)} %get-tuple-element.59.total, bf16[2048,128]{1,0:T(8,128)(2,1)S(1)} %collective-permute-done.3.half, ...), custom_call_target="tpu_custom_call" | custom-call | flops 1 | tf_op jit(solution)/shard_map/pallas_call | solution.py:287
  55.1 0.0 collective-permute-done.10.r1
  55.1 0.0 collective-permute-done.9.r0
  55.1 0.2 shard_map.91.a0
  55.3 0.4 collective-permute-start.11
  55.7 2.4 %collective-permute-start.12 = (bf16[64,1024]{1,0:T(8,128)(2,1)S(1)}, bf16[64,1024]{1,0:T(8,128)(2,1)S(1)}, u32[]{:S(2)}, u32[]{:S(2)}) collective-permute-start(bf16[64,1024]{1,0:T(8,128)(2,1)S(1)} %shard_map.91.a0), channel_id=1, source_target_pairs={{0,48},{8,56},{16,0},{24,8},{32,16},{40,24},{48,32},{56,40},{64,11... | collective-permute-start | bytes 393224 | tf_op jit(solution)/shard_map/ppermute | solution.py:28
  58.1 0.9 collective-permute-start.13
  59.0 0.8 collective-permute-start.14
  59.8 0.7 collective-permute-done.11.a1
  60.4 1.6 %collective-permute-start.15 = (bf16[64,1024]{1,0:T(8,128)(2,1)S(1)}, bf16[64,1024]{1,0:T(8,128)(2,1)S(1)}, u32[]{:S(2)}, u32[]{:S(2)}) collective-permute-start(bf16[64,1024]{1,0:T(8,128)(2,1)S(1)} %collective-permute-done.11.a1), channel_id=1, source_target_pairs={{0,64},{8,72},{16,80},{24,88},{32,96},{40,104},{48,112},{56,120},{... | collective-permute-start | bytes 393224 | tf_op jit(solution)/shard_map/ppermute | solution.py:28
  62.0 0.0 collective-permute-done.12.a2
  62.0 1.4 %collective-permute-start.16 = (bf16[64,1024]{1,0:T(8,128)(2,1)S(1)}, bf16[64,1024]{1,0:T(8,128)(2,1)S(1)}, u32[]{:S(2)}, u32[]{:S(2)}) collective-permute-start(bf16[64,1024]{1,0:T(8,128)(2,1)S(1)} %collective-permute-done.12.a2), channel_id=1, source_target_pairs={{0,64},{8,72},{16,80},{24,88},{32,96},{40,104},{48,112},{56,120},{... | collective-permute-start | bytes 393224 | tf_op jit(solution)/shard_map/ppermute | solution.py:28
  63.4 1.3 %collective-permute-done.13.a3 = bf16[64,1024]{1,0:T(8,128)(2,1)S(1)} collective-permute-done((bf16[64,1024]{1,0:T(8,128)(2,1)S(1)}, bf16[64,1024]{1,0:T(8,128)(2,1)S(1)}, u32[]{:S(2)}, u32[]{:S(2)}) %collective-permute-start.13) | collective-permute-done | bytes 131104 | tf_op jit(solution)/shard_map/ppermute | solution.py:28
  64.7 1.4 %collective-permute-start.17 = (bf16[64,1024]{1,0:T(8,128)(2,1)S(1)}, bf16[64,1024]{1,0:T(8,128)(2,1)S(1)}, u32[]{:S(2)}, u32[]{:S(2)}) collective-permute-start(bf16[64,1024]{1,0:T(8,128)(2,1)S(1)} %collective-permute-done.13.a3), channel_id=1, source_target_pairs={{0,64},{8,72},{16,80},{24,88},{32,96},{40,104},{48,112},{56,120},{... | collective-permute-start | bytes 393224 | tf_op jit(solution)/shard_map/ppermute | solution.py:28
  66.0 0.0 collective-permute-done.14.a4
  66.0 0.0 collective-permute-done.15.a5
  66.0 2.8 %collective-permute-done.16.a6 = bf16[64,1024]{1,0:T(8,128)(2,1)S(1)} collective-permute-done((bf16[64,1024]{1,0:T(8,128)(2,1)S(1)}, bf16[64,1024]{1,0:T(8,128)(2,1)S(1)}, u32[]{:S(2)}, u32[]{:S(2)}) %collective-permute-start.16) | collective-permute-done | bytes 131104 | tf_op jit(solution)/shard_map/ppermute | solution.py:28
  68.8 3.0 %collective-permute-done.17.a7 = bf16[64,1024]{1,0:T(8,128)(2,1)S(1)} collective-permute-done((bf16[64,1024]{1,0:T(8,128)(2,1)S(1)}, bf16[64,1024]{1,0:T(8,128)(2,1)S(1)}, u32[]{:S(2)}, u32[]{:S(2)}) %collective-permute-start.17) | collective-permute-done | bytes 131104 | tf_op jit(solution)/shard_map/ppermute | solution.py:28
  71.8 0.0 collective-permute-done.18.wb
  71.8 1.2 %shard_map.92 = bf16[8,64,1024]{2,1,0:T(8,128)(2,1)S(1)} custom-call(s32[1]{0:T(128)} %bitcast.index, bf16[64,1024]{1,0:T(8,128)(2,1)S(1)} %shard_map.91.a0, bf16[64,1024]{1,0:T(8,128)(2,1)S(1)} %collective-permute-done.11.a1, bf16[64,1024]{1,0:T(8,128)(2,1)S(1)} %collective-permute-done.12.a2, bf16[64,1024]{1,0:T(8,128)(2,1)S(1)} %collective-permute-done.13.a3, ...), custom_call_target="tpu_custom_call" | custom-call | tf_op jit(solution)/shard_map/pallas_call | solution.py:297
  73.0 16.0 %all_to_all.5.terms = bf16[8,64,1024]{2,1,0:T(8,128)(2,1)S(1)} all-to-all(bf16[8,64,1024]{2,1,0:T(8,128)(2,1)S(1)} %shard_map.92), channel_id=1, replica_groups=mesh['blk'=16,'head'=8] {'head'}, dimensions={0} | all-to-all | bytes 2097152 | tf_op jit(solution)/shard_map/all_to_all | solution.py:303
  89.0 0.1 shard_map.93
  89.1 4.8 %collective-permute-start.19 = (bf16[64,512]{1,0:T(8,128)(2,1)S(1)}, bf16[64,512]{1,0:T(8,128)(2,1)S(1)}, u32[]{:S(2)}, u32[]{:S(2)}) collective-permute-start(bf16[64,512]{1,0:T(8,128)(2,1)S(1)} %get-tuple-element.64), channel_id=1, source_target_pairs={{0,8},{8,0},{16,24},{24,16},{32,40},{40,32},{48,56},{56,48},{64,72... | collective-permute-start | bytes 196616 | tf_op jit(solution)/shard_map/ppermute | solution.py:28
  94.0 0.9 collective-permute-done.19
  94.9 0.7 maximum_select_fusion
  (5 shorter events, 0.0 us)
Async XLA Ops:
  0.0 24.3 %copy-start.2 = (bf16[64,1024]{1,0:T(8,128)(2,1)S(1)}, bf16[64,1024]{1,0:T(8,128)(2,1)}, u32[]{:S(2)}) copy-start(bf16[64,1024]{1,0:T(8,128)(2,1)} %q.1) | copy-start | bytes 393220
  0.0 1.1 %copy-start.3 = (bf16[2048,128]{1,0:T(8,128)(2,1)S(1)}, bf16[2048,128]{1,0:T(8,128)(2,1)}, u32[]{:S(2)}) copy-start(bf16[2048,128]{1,0:T(8,128)(2,1)} %k.1) | copy-start | bytes 1572868
  1.1 1.0 %copy-start.4 = (bf16[2048,128]{1,0:T(8,128)(2,1)S(1)}, bf16[2048,128]{1,0:T(8,128)(2,1)}, u32[]{:S(2)}) copy-start(bf16[2048,128]{1,0:T(8,128)(2,1)} %v.1) | copy-start | bytes 1572868
  2.3 26.0 %collective-permute-start.4 = (bf16[4096,128]{1,0:T(8,128)(2,1)S(1)}, bf16[4096,128]{1,0:T(8,128)(2,1)S(1)}, u32[]{:S(2)}, u32[]{:S(2)}) collective-permute-start(bf16[4096,128]{1,0:T(8,128)(2,1)S(1)} %get-tuple-element.36.kv), channel_id=1, source_target_pairs={{0,8},{8,0},{16,24},{24,16},{32,40},{40,32},{48,56},{56,48},{64,72... | collective-permute-start | bytes 3145736 | tf_op jit(solution)/shard_map/ppermute | solution.py:28
  3.8 19.0 %collective-permute-start.5 = (bf16[2048,128]{1,0:T(8,128)(2,1)S(1)}, bf16[2048,128]{1,0:T(8,128)(2,1)S(1)}, u32[]{:S(2)}, u32[]{:S(2)}) collective-permute-start(bf16[2048,128]{1,0:T(8,128)(2,1)S(1)} %get-tuple-element.45), channel_id=1, source_target_pairs={{0,64},{8,72},{16,80},{24,88},{32,96},{40,104},{48,112},{56,120},{... | collective-permute-start | bytes 1572872 | tf_op jit(solution)/shard_map/ppermute | solution.py:28
  6.6 7.5 %collective-permute-start = (bf16[64,1024]{1,0:T(8,128)(2,1)}, bf16[64,1024]{1,0:T(8,128)(2,1)S(1)}, u32[]{:S(2)}, u32[]{:S(2)}) collective-permute-start(bf16[64,1024]{1,0:T(8,128)(2,1)} %q.1), channel_id=1, source_target_pairs={{0,16},{8,24},{16,32},{24,40},{32,48},{40,56},{48,0},{56,8},{64,80... | collective-permute-start | bytes 393224 | tf_op jit(solution)/shard_map/ppermute | solution.py:28
  8.2 5.9 %collective-permute-start.1 = (bf16[64,1024]{1,0:T(8,128)(2,1)}, bf16[64,1024]{1,0:T(8,128)(2,1)S(1)}, u32[]{:S(2)}, u32[]{:S(2)}) collective-permute-start(bf16[64,1024]{1,0:T(8,128)(2,1)} %q.1), channel_id=1, source_target_pairs={{0,48},{8,56},{16,0},{24,8},{32,16},{40,24},{48,32},{56,40},{64,11... | collective-permute-start | bytes 393224 | tf_op jit(solution)/shard_map/ppermute | solution.py:28
  10.4 7.5 %collective-permute-start.2 = (bf16[64,1024]{1,0:T(8,128)(2,1)}, bf16[64,1024]{1,0:T(8,128)(2,1)S(1)}, u32[]{:S(2)}, u32[]{:S(2)}) collective-permute-start(bf16[64,1024]{1,0:T(8,128)(2,1)} %q.1), channel_id=1, source_target_pairs={{0,32},{8,40},{16,48},{24,56},{32,0},{40,8},{48,16},{56,24},{64,96... | collective-permute-start | bytes 393224 | tf_op jit(solution)/shard_map/ppermute | solution.py:28
  17.8 0.9 copy-start.1
  18.7 0.7 copy-start.5
  19.4 0.7 copy-start.6
  22.8 9.4 %collective-permute-start.6 = (bf16[2048,128]{1,0:T(8,128)(2,1)S(1)}, bf16[2048,128]{1,0:T(8,128)(2,1)S(1)}, u32[]{:S(2)}, u32[]{:S(2)}) collective-permute-start(bf16[2048,128]{1,0:T(8,128)(2,1)S(1)} %collective-permute-done.5.refs_0_.half), channel_id=1, source_target_pairs={{0,8},{8,0},{16,24},{24,16},{32,40},{40,32},{48,56},{56,48},{64,72... | collective-permute-start | bytes 1572872 | tf_op jit(solution)/shard_map/ppermute | solution.py:28
  24.0 14.8 %collective-permute-start.3 = (bf16[2048,128]{1,0:T(8,128)(2,1)S(1)}, bf16[2048,128]{1,0:T(8,128)(2,1)S(1)}, u32[]{:S(2)}, u32[]{:S(2)}) collective-permute-start(bf16[2048,128]{1,0:T(8,128)(2,1)S(1)} %get-tuple-element.40), channel_id=1, source_target_pairs={{0,64},{8,72},{16,80},{24,88},{32,96},{40,104},{48,112},{56,120},{... | collective-permute-start | bytes 1572872 | tf_op jit(solution)/shard_map/ppermute | solution.py:28
  32.2 7.7 %copy-start = (bf16[1024,512]{1,0:T(8,128)(2,1)S(1)}, bf16[1024,512]{1,0:T(8,128)(2,1)}, u32[]{:S(2)}) copy-start(bf16[1024,512]{1,0:T(8,128)(2,1)} %wa.1) | copy-start | bytes 3145732
  38.8 3.9 %collective-permute-start.7 = (bf16[2048,128]{1,0:T(8,128)(2,1)S(1)}, bf16[2048,128]{1,0:T(8,128)(2,1)S(1)}, u32[]{:S(2)}, u32[]{:S(2)}) collective-permute-start(bf16[2048,128]{1,0:T(8,128)(2,1)S(1)} %collective-permute-done.3.half), channel_id=1, source_target_pairs={{0,8},{8,0},{16,24},{24,16},{32,40},{40,32},{48,56},{56,48},{64,72... | collective-permute-start | bytes 1572872 | tf_op jit(solution)/shard_map/ppermute | solution.py:28
  39.9 31.9 %collective-permute-start.18 = (bf16[1024,512]{1,0:T(8,128)(2,1)S(1)}, bf16[1024,512]{1,0:T(8,128)(2,1)S(1)}, u32[]{:S(2)}, u32[]{:S(2)}) collective-permute-start(bf16[1024,512]{1,0:T(8,128)(2,1)S(1)} %copy-done), channel_id=1, source_target_pairs={{0,8},{8,0},{16,24},{24,16},{32,40},{40,32},{48,56},{56,48},{64,72... | collective-permute-start | bytes 3145736 | tf_op jit(solution)/shard_map/ppermute | solution.py:28
  45.4 7.0 %collective-permute-start.8 = (bf16[144,512]{1,0:T(8,128)(2,1)S(1)}, bf16[144,512]{1,0:T(8,128)(2,1)S(1)}, u32[]{:S(2)}, u32[]{:S(2)}) collective-permute-start(bf16[144,512]{1,0:T(8,128)(2,1)S(1)} %shard_map.88), channel_id=1, source_target_pairs={{0,32},{8,40},{16,48},{24,56},{32,0},{40,8},{48,16},{56,24},{64,96... | collective-permute-start | bytes 442376 | tf_op jit(solution)/shard_map/ppermute | solution.py:28
  48.6 6.5 %collective-permute-start.10 = (bf16[144,512]{1,0:T(8,128)(2,1)S(1)}, bf16[144,512]{1,0:T(8,128)(2,1)S(1)}, u32[]{:S(2)}, u32[]{:S(2)}) collective-permute-start(bf16[144,512]{1,0:T(8,128)(2,1)S(1)} %get-tuple-element.57), channel_id=1, source_target_pairs={{0,16},{8,24},{16,32},{24,40},{32,48},{40,56},{48,0},{56,8},{64,80... | collective-permute-start | bytes 442376 | tf_op jit(solution)/shard_map/ppermute | solution.py:28
  50.5 4.6 %collective-permute-start.9 = (bf16[144,512]{1,0:T(8,128)(2,1)S(1)}, bf16[144,512]{1,0:T(8,128)(2,1)S(1)}, u32[]{:S(2)}, u32[]{:S(2)}) collective-permute-start(bf16[144,512]{1,0:T(8,128)(2,1)S(1)} %get-tuple-element.56), channel_id=1, source_target_pairs={{0,48},{8,56},{16,0},{24,8},{32,16},{40,24},{48,32},{56,40},{64,11... | collective-permute-start | bytes 442376 | tf_op jit(solution)/shard_map/ppermute | solution.py:28
  55.3 5.1 %collective-permute-start.11 = (bf16[64,1024]{1,0:T(8,128)(2,1)S(1)}, bf16[64,1024]{1,0:T(8,128)(2,1)S(1)}, u32[]{:S(2)}, u32[]{:S(2)}) collective-permute-start(bf16[64,1024]{1,0:T(8,128)(2,1)S(1)} %shard_map.91.a0), channel_id=1, source_target_pairs={{0,16},{8,24},{16,32},{24,40},{32,48},{40,56},{48,0},{56,8},{64,80... | collective-permute-start | bytes 393224 | tf_op jit(solution)/shard_map/ppermute | solution.py:28
  55.7 6.3 %collective-permute-start.12 = (bf16[64,1024]{1,0:T(8,128)(2,1)S(1)}, bf16[64,1024]{1,0:T(8,128)(2,1)S(1)}, u32[]{:S(2)}, u32[]{:S(2)}) collective-permute-start(bf16[64,1024]{1,0:T(8,128)(2,1)S(1)} %shard_map.91.a0), channel_id=1, source_target_pairs={{0,48},{8,56},{16,0},{24,8},{32,16},{40,24},{48,32},{56,40},{64,11... | collective-permute-start | bytes 393224 | tf_op jit(solution)/shard_map/ppermute | solution.py:28
  58.1 6.6 %collective-permute-start.13 = (bf16[64,1024]{1,0:T(8,128)(2,1)S(1)}, bf16[64,1024]{1,0:T(8,128)(2,1)S(1)}, u32[]{:S(2)}, u32[]{:S(2)}) collective-permute-start(bf16[64,1024]{1,0:T(8,128)(2,1)S(1)} %shard_map.91.a0), channel_id=1, source_target_pairs={{0,32},{8,40},{16,48},{24,56},{32,0},{40,8},{48,16},{56,24},{64,96... | collective-permute-start | bytes 393224 | tf_op jit(solution)/shard_map/ppermute | solution.py:28
  59.0 7.0 %collective-permute-start.14 = (bf16[64,1024]{1,0:T(8,128)(2,1)S(1)}, bf16[64,1024]{1,0:T(8,128)(2,1)S(1)}, u32[]{:S(2)}, u32[]{:S(2)}) collective-permute-start(bf16[64,1024]{1,0:T(8,128)(2,1)S(1)} %shard_map.91.a0), channel_id=1, source_target_pairs={{0,64},{8,72},{16,80},{24,88},{32,96},{40,104},{48,112},{56,120},{... | collective-permute-start | bytes 393224 | tf_op jit(solution)/shard_map/ppermute | solution.py:28
  60.4 5.6 %collective-permute-start.15 = (bf16[64,1024]{1,0:T(8,128)(2,1)S(1)}, bf16[64,1024]{1,0:T(8,128)(2,1)S(1)}, u32[]{:S(2)}, u32[]{:S(2)}) collective-permute-start(bf16[64,1024]{1,0:T(8,128)(2,1)S(1)} %collective-permute-done.11.a1), channel_id=1, source_target_pairs={{0,64},{8,72},{16,80},{24,88},{32,96},{40,104},{48,112},{56,120},{... | collective-permute-start | bytes 393224 | tf_op jit(solution)/shard_map/ppermute | solution.py:28
  62.0 6.8 %collective-permute-start.16 = (bf16[64,1024]{1,0:T(8,128)(2,1)S(1)}, bf16[64,1024]{1,0:T(8,128)(2,1)S(1)}, u32[]{:S(2)}, u32[]{:S(2)}) collective-permute-start(bf16[64,1024]{1,0:T(8,128)(2,1)S(1)} %collective-permute-done.12.a2), channel_id=1, source_target_pairs={{0,64},{8,72},{16,80},{24,88},{32,96},{40,104},{48,112},{56,120},{... | collective-permute-start | bytes 393224 | tf_op jit(solution)/shard_map/ppermute | solution.py:28
  64.7 7.1 %collective-permute-start.17 = (bf16[64,1024]{1,0:T(8,128)(2,1)S(1)}, bf16[64,1024]{1,0:T(8,128)(2,1)S(1)}, u32[]{:S(2)}, u32[]{:S(2)}) collective-permute-start(bf16[64,1024]{1,0:T(8,128)(2,1)S(1)} %collective-permute-done.13.a3), channel_id=1, source_target_pairs={{0,64},{8,72},{16,80},{24,88},{32,96},{40,104},{48,112},{56,120},{... | collective-permute-start | bytes 393224 | tf_op jit(solution)/shard_map/ppermute | solution.py:28
  89.1 5.7 %collective-permute-start.19 = (bf16[64,512]{1,0:T(8,128)(2,1)S(1)}, bf16[64,512]{1,0:T(8,128)(2,1)S(1)}, u32[]{:S(2)}, u32[]{:S(2)}) collective-permute-start(bf16[64,512]{1,0:T(8,128)(2,1)S(1)} %get-tuple-element.64), channel_id=1, source_target_pairs={{0,8},{8,0},{16,24},{24,16},{32,40},{40,32},{48,56},{56,48},{64,72... | collective-permute-start | bytes 196616 | tf_op jit(solution)/shard_map/ppermute | solution.py:28

commit v10 on v9

--- a/solution.py
+++ b/solution.py
@@ -57,12 +57,12 @@
 
 def join_kernel(k, v, whole, first, second):
     size = k.shape[0]
-    half = size // 2
-    whole[:size, :] = k[...]
-    whole[size:, :] = v[...]
-    for i, kv in enumerate((first, second)):
-        kv[:half, :] = k[i * half : (i + 1) * half, :]
-        kv[half:, :] = v[i * half : (i + 1) * half, :]
+    at = 0
+    for kv in (whole, first, second):
+        count = kv.shape[0] // 2
+        kv[:count, :] = k[at : at + count, :]
+        kv[count:, :] = v[at : at + count, :]
+        at = (at + count) % size
 
 
 def split(parts, keys, values):
@@ -158,10 +158,10 @@
         top_out[i], total_out[i] = top, total
 
 
-def own_kernel_2(rows, top, total, kv, half, other_half, top_out, total_out, k, values):
-    split((kv,), k.at[0], values.at[0])
-    split((half, other_half), k.at[1], values.at[1])
-    tasks = [(0, rows.at[3], k.at[i], values.at[i]) for i in range(2)]
+def own_kernel_2(rows, top, total, kv, half, other_half, top_out, total_out, k0, v0, k1, v1):
+    split((kv,), k0, v0)
+    split((half, other_half), k1, v1)
+    tasks = [(0, rows.at[3], k0, v0), (0, rows.at[3], k1, v1)]
     top_out[...], total_out[...] = run(tasks, [(top[...], total[...])])[0]
 
 
@@ -243,13 +243,14 @@
     smem = pl.BlockSpec(memory_space=pltpu.SMEM)
     block_flops = 8 * LANES * positions * DH
     part = ((DH + EXTRA, LANES), bf16)
-    ones_shape = (positions, 2 * DH)
 
     own_state = [((LANES, DH), f32), ((LANES, 2 * DH), f32)]
     state = [((3, LANES, DH), f32), ((3, LANES, 2 * DH), f32)]
 
+    early = positions * 7 // 16
+    late = positions - early
     kv, *halves = call(
-        join_kernel, [((2 * positions, DH), bf16)] + [((positions, DH), bf16)] * 2
+        join_kernel, [((2 * size, DH), bf16) for size in (positions, early, late)]
     )(prefix_keys, prefix_values)
     x0, x1 = [moved(half, xh=1) for half in halves]
     kv_c = moved(kv, c=1)
@@ -257,35 +258,36 @@
     row = jnp.arange(ROWS, dtype=jnp.int32)
     allowed = (question_ids[:, None] == question_ids[None, :]) & (row[None, :] <= row[:, None])
     bias = jnp.where(allowed, 0.0, FLOOR).astype(f32)
-    scratch = [pltpu.VMEM((positions, DH), bf16), pltpu.VMEM(ones_shape, bf16)]
-    own_top, own_total = call(own_kernel, own_state, scratch)(
-        after(queries, *q_z), question_keys, question_values, bias, kv
-    )
-    top, total, rows = call(near_kernel, state + [((4, LANES, DH), bf16)], scratch)(
-        *q_z, after(queries, own_top), kv
-    )
-    x0 = after(x0, own_top)
+    def scratch(*sizes):
+        return [pltpu.VMEM((size, width), bf16) for size in sizes for width in (DH, 2 * DH)]
+
+    own_top, own_total = call(own_kernel, own_state, scratch(positions))(
+        queries, question_keys, question_values, after(bias, q_z[0]), kv
+    )
+    top, total, rows = call(near_kernel, state + [((4, LANES, DH), bf16)], scratch(positions))(
+        *q_z, queries, kv
+    )
+    x0 = after(x0, own_top, *q_z)
     xc0 = moved(x0, c=1)
-    top, total = call(others_kernel, state, scratch, flops=1)(rows, top, total, kv_c)
-    top, total = call(others_kernel, state, scratch, flops=1)(rows, top, total, x0, xc0)
+    top, total = call(others_kernel, state, scratch(positions), flops=1)(rows, top, total, kv_c)
+    top, total = call(others_kernel, state, scratch(2 * early), flops=1)(rows, top, total, x0, xc0)
 
     x1, weight, top = lax.optimization_barrier((x1, out_weight, top))
     xc1 = moved(x1, c=1)
     weight_c = moved(weight, c=1)
-    pair = [pltpu.VMEM((2, positions, DH), bf16), pltpu.VMEM((2,) + ones_shape, bf16)]
-    own_top, own_total = call(own_kernel_2, own_state, pair, flops=2 * block_flops)(
+    own_top, own_total = call(own_kernel_2, own_state, scratch(positions, 2 * early), flops=2 * block_flops)(
         after(rows, x1), own_top, own_total, kv_c, x0, xc0
     )
     top = after(top, own_top)
-    (p_far,) = call(functools.partial(last_kernel, owners=(2,)), [part], scratch, flops=1)(
+    (p_far,) = call(functools.partial(last_kernel, owners=(2,)), [part], scratch(2 * late), flops=1)(
         rows, top, total, x1, xc1
     )
     p_next = call(
-        functools.partial(last_kernel, owners=(0, 1)), [part] * 2, scratch, flops=4 * block_flops
+        functools.partial(last_kernel, owners=(0, 1)), [part] * 2, scratch(2 * late), flops=4 * block_flops
     )(rows, after(top, p_far), total, x1, xc1)
     back = [moved(p, z=-z) for p, z in zip((*p_next, p_far), FAR)]
     result, level = call(
-        own_last_kernel, [((DH, LANES), f32), ((8, LANES), f32)], scratch, flops=1
+        own_last_kernel, [((DH, LANES), f32), ((8, LANES), f32)], scratch(2 * late), flops=1
     )(after(rows, *p_next), own_top, own_total, x1, xc1, back[2])
     (att,) = call(
         merge_kernel, [((ROWS, GROUP * DH), bf16)], in_specs=[smem] + [vmem] * 4

time: 95.9 us -> 93.2 us (0.972)
  waiting for transfers between devices: 16.7 us -> 9.5 us
  starting transfers between devices: 29.1 us -> 31.8 us
  blocking collectives: 16 us -> 17.1 us
    ppermute x20, waiting for transfers between devices: 16.7 us -> 9.5 us  [moved(): return lax.ppermute(array, 'blk', pairs)]
    ppermute x20, starting transfers between devices: 29.1 us -> 31.8 us  [moved(): return lax.ppermute(array, 'blk', pairs)]
    all_to_all x1, blocking collectives: 16 us -> 17.1 us  [shards(): gathered = lax.all_to_all(terms, 'head', 0, 0, tiled=True)]
  transfers between devices with their start and end apart: 20 -> 20, of which waited for: 8 -> 7; matrix products, arithmetic and copies ran while one was open for 1% -> 1% of each run, Pallas kernels for 27% -> 28%
where the time goes in v10:
time: 93.2 us; the launch traced here: 92.9 us
  starting transfers between devices  31.8 us (34%)
  Pallas kernels  27.6 us (30%)
  blocking collectives  17.1 us (18%)
  waiting for transfers between devices  9.5 us (10%)
  local copies, waits for them, and re-layouts  4.46 us (5%)
  other arithmetic  1.48 us (2%)
    ppermute x20, starting transfers between devices, moved(): return lax.ppermute(array, 'blk', pairs)  31.8 us
    all_to_all x1, blocking collectives, shards(): gathered = lax.all_to_all(terms, 'head', 0, 0, tiled=True)  17.1 us
    ppermute x20, waiting for transfers between devices, moved(): return lax.ppermute(array, 'blk', pairs)  9.5 us
    unnamed x14, local copies, waits for them, and re-layouts  4.46 us
    pallas_call x1, Pallas kernels, shards(): call(near_kernel, state + [((4, LANES, DH), bf16)], scratch(positions))  3.95 us
    pallas_call x1, Pallas kernels, shards(): call(others_kernel, state, scratch(positions), flops=1)  3.91 us
    pallas_call x1, Pallas kernels, shards(): call(others_kernel, state, scratch(2 * early), flops=1)  3.5 us
    pallas_call x1, Pallas kernels, shards(): call(functools.partial(last_kernel, owners=(0, 1)), [part] * 2, scratch(2...  3.18 us
  transfers between devices with their start and end apart: 20, of which 7 were waited for; matrix products, arithmetic and copies ran while one was open for 1% of the time, Pallas kernels for 28%

profile of v10, /device:TPU:1, one launch (start us, length us, event | category | flops | bytes accessed | tf_op | source)
XLA Modules:
  0.0 92.9 jit_solution(76765520911888378)
XLA Ops:
  0.0 0.0 copy-start.3
  0.0 1.1 %copy-done.3 = bf16[2048,128]{1,0:T(8,128)(2,1)S(1)} copy-done((bf16[2048,128]{1,0:T(8,128)(2,1)S(1)}, bf16[2048,128]{1,0:T(8,128)(2,1)}, u32[]{:S(2)}) %copy-start.3) | copy-done | bytes 524312
  1.1 1.0 %copy-done.4 = bf16[2048,128]{1,0:T(8,128)(2,1)S(1)} copy-done((bf16[2048,128]{1,0:T(8,128)(2,1)S(1)}, bf16[2048,128]{1,0:T(8,128)(2,1)}, u32[]{:S(2)}) %copy-start.4) | copy-done | bytes 524312
  2.1 0.1 shard_map.82
  2.3 1.5 %collective-permute-start.4 = (bf16[4096,128]{1,0:T(8,128)(2,1)S(1)}, bf16[4096,128]{1,0:T(8,128)(2,1)S(1)}, u32[]{:S(2)}, u32[]{:S(2)}) collective-permute-start(bf16[4096,128]{1,0:T(8,128)(2,1)S(1)} %get-tuple-element.34.kv), channel_id=1, source_target_pairs={{0,8},{8,0},{16,24},{24,16},{32,40},{40,32},{48,56},{56,48},{64,72... | collective-permute-start | bytes 3145736 | tf_op jit(solution)/shard_map/ppermute | solution.py:28
  3.8 2.8 %collective-permute-start.5 = (bf16[1792,128]{1,0:T(8,128)(2,1)S(1)}, bf16[1792,128]{1,0:T(8,128)(2,1)S(1)}, u32[]{:S(2)}, u32[]{:S(2)}) collective-permute-start(bf16[1792,128]{1,0:T(8,128)(2,1)S(1)} %get-tuple-element.41), channel_id=1, source_target_pairs={{0,64},{8,72},{16,80},{24,88},{32,96},{40,104},{48,112},{56,120},{... | collective-permute-start | bytes 1376264 | tf_op jit(solution)/shard_map/ppermute | solution.py:28
  6.6 1.6 %collective-permute-start = (bf16[64,1024]{1,0:T(8,128)(2,1)}, bf16[64,1024]{1,0:T(8,128)(2,1)S(1)}, u32[]{:S(2)}, u32[]{:S(2)}) collective-permute-start(bf16[64,1024]{1,0:T(8,128)(2,1)} %q.3), channel_id=1, source_target_pairs={{0,16},{8,24},{16,32},{24,40},{32,48},{40,56},{48,0},{56,8},{64,80... | collective-permute-start | bytes 393224 | tf_op jit(solution)/shard_map/ppermute | solution.py:28
  8.2 3.3 %collective-permute-start.2 = (bf16[64,1024]{1,0:T(8,128)(2,1)}, bf16[64,1024]{1,0:T(8,128)(2,1)S(1)}, u32[]{:S(2)}, u32[]{:S(2)}) collective-permute-start(bf16[64,1024]{1,0:T(8,128)(2,1)} %q.3), channel_id=1, source_target_pairs={{0,32},{8,40},{16,48},{24,56},{32,0},{40,8},{48,16},{56,24},{64,96... | collective-permute-start | bytes 393224 | tf_op jit(solution)/shard_map/ppermute | solution.py:28
  11.5 0.7 collective-permute-start.1
  12.3 1.9 %collective-permute-done.q0 = bf16[64,1024]{1,0:T(8,128)(2,1)S(1)} collective-permute-done((bf16[64,1024]{1,0:T(8,128)(2,1)}, bf16[64,1024]{1,0:T(8,128)(2,1)S(1)}, u32[]{:S(2)}, u32[]{:S(2)}) %collective-permute-start) | collective-permute-done | bytes 131104 | tf_op jit(solution)/shard_map/ppermute | solution.py:28
  14.2 0.2 collective-permute-start.3
  14.4 0.8 fusion.1.bias
  15.2 0.9 copy-done.1
  16.1 0.7 copy-done.5
  16.8 0.7 copy-done.6
  17.5 2.6 %shard_map.85 = (f32[512,128]{1,0:T(8,128)S(1)}, f32[512,256]{1,0:T(8,128)S(1)}) custom-call(bf16[64,1024]{1,0:T(8,128)(2,1)S(1)} %copy-done.1, bf16[64,128]{1,0:T(8,128)(2,1)S(1)} %copy-done.5, bf16[64,128]{1,0:T(8,128)(2,1)S(1)} %copy-done.6, f32[64,64]{1,0:T(8,128)S(1)} %fusion.1.bias, bf16[4096,128]{1,0:T(8,128)(2,1)S(1)} %get-tuple-element.34.kv), custom_call_target="tpu_custom_call" | custom-call | tf_op jit(solution)/shard_map/pallas_call | solution.py:264
  20.1 0.0 collective-permute-done.2.q2
  20.1 0.0 collective-permute-done.1.q1
  20.1 0.0 collective-permute-done.5.refs_0_.half
  20.1 1.4 %collective-permute-start.6 = (bf16[1792,128]{1,0:T(8,128)(2,1)S(1)}, bf16[1792,128]{1,0:T(8,128)(2,1)S(1)}, u32[]{:S(2)}, u32[]{:S(2)}) collective-permute-start(bf16[1792,128]{1,0:T(8,128)(2,1)S(1)} %collective-permute-done.5.refs_0_.half), channel_id=1, source_target_pairs={{0,8},{8,0},{16,24},{24,16},{32,40},{40,32},{48,56},{56,48},{64,72... | collective-permute-start | bytes 1376264 | tf_op jit(solution)/shard_map/ppermute | solution.py:28
  21.6 0.0 copy-done.2
  21.6 4.0 %shard_map.83 = (f32[3,512,128]{2,1,0:T(8,128)S(1)}, f32[3,512,256]{2,1,0:T(8,128)S(1)}, bf16[4,512,128]{2,1,0:T(8,128)(2,1)S(1)}) custom-call(bf16[64,1024]{1,0:T(8,128)(2,1)S(1)} %collective-permute-done.q0, bf16[64,1024]{1,0:T(8,128)(2,1)S(1)} %collective-permute-done.1.q1, bf16[64,1024]{1,0:T(8,128)(2,1)S(1)} %collective-permute-done.2.q2, ...), custom_call_target="tpu_custom_call" | custom-call | tf_op jit(solution)/shard_map/pallas_call | solution.py:267
  25.5 0.0 collective-permute-done.4.refs_0_.kv
  25.5 3.9 %shard_map.84 = (f32[3,512,128]{2,1,0:T(8,128)S(1)}, f32[3,512,256]{2,1,0:T(8,128)S(1)}) custom-call(bf16[4,512,128]{2,1,0:T(8,128)(2,1)S(1)} %get-tuple-element.56.rows, f32[3,512,128]{2,1,0:T(8,128)S(1)} %get-tuple-element.37.top_in, f32[3,512,256]{2,1,0:T(8,128)S(1)} %get-tuple-element.38.total_in, bf16[4096,128]{1,0:T(8,128)(2,1)S(1)} %collective-permute-done.4.refs_0_.kv), custom_call_target="tpu_custom_call" | custom-call | flops 1 | tf_op jit(solution)/shard_map/pallas_call | solution.py:272
  29.5 0.0 collective-permute-done.6.refs_1_.other_half
  29.5 0.0 copy-start
  29.5 3.5 %shard_map.86 = (f32[3,512,128]{2,1,0:T(8,128)S(1)}, f32[3,512,256]{2,1,0:T(8,128)S(1)}) custom-call(bf16[4,512,128]{2,1,0:T(8,128)(2,1)S(1)} %get-tuple-element.56.rows, f32[3,512,128]{2,1,0:T(8,128)S(1)} %get-tuple-element.39.top_in, f32[3,512,256]{2,1,0:T(8,128)S(1)} %get-tuple-element.40.total_in, ...), custom_call_target="tpu_custom_call" | custom-call | flops 1 | tf_op jit(solution)/shard_map/pallas_call | solution.py:273
  33.0 0.0 collective-permute-done.3.half
  33.0 0.1 collective-permute-start.7
  33.1 0.0 copy-done
  33.1 0.5 collective-permute-start.18
  33.6 2.9 %shard_map.87 = (f32[512,128]{1,0:T(8,128)S(1)}, f32[512,256]{1,0:T(8,128)S(1)}) custom-call(bf16[4,512,128]{2,1,0:T(8,128)(2,1)S(1)} %get-tuple-element.56.rows, f32[512,128]{1,0:T(8,128)S(1)} %get-tuple-element.43.top, f32[512,256]{1,0:T(8,128)S(1)} %get-tuple-element.49.total, bf16[4096,128]{1,0:T(8,128)(2,1)S(1)} %collective-permute-done.4.refs_0_.kv, ...), custom_call_target="tpu_custom_call" | custom-call | flops 2147483648 | tf_op jit(solution)/shard_map/pallas_call | solution.py:278
  36.5 0.0 collective-permute-done.7.other_half
  36.5 2.9 %shard_map.88 = bf16[144,512]{1,0:T(8,128)(2,1)S(1)} custom-call(bf16[4,512,128]{2,1,0:T(8,128)(2,1)S(1)} %get-tuple-element.56.rows, f32[3,512,128]{2,1,0:T(8,128)S(1)} %get-tuple-element.53.top, f32[3,512,256]{2,1,0:T(8,128)S(1)} %get-tuple-element.52.total, bf16[2304,128]{1,0:T(8,128)(2,1)S(1)} %collective-permute-done.3.half, ...), custom_call_target="tpu_custom_call" | custom-call | flops 1 | tf_op jit(solution)/shard_map/pallas_call | solution.py:282
  39.5 1.4 %collective-permute-start.8 = (bf16[144,512]{1,0:T(8,128)(2,1)S(1)}, bf16[144,512]{1,0:T(8,128)(2,1)S(1)}, u32[]{:S(2)}, u32[]{:S(2)}) collective-permute-start(bf16[144,512]{1,0:T(8,128)(2,1)S(1)} %shard_map.88), channel_id=1, source_target_pairs={{0,32},{8,40},{16,48},{24,56},{32,0},{40,8},{48,16},{56,24},{64,96... | collective-permute-start | bytes 442376 | tf_op jit(solution)/shard_map/ppermute | solution.py:28
  40.9 3.2 %shard_map.89 = (bf16[144,512]{1,0:T(8,128)(2,1)S(1)}, bf16[144,512]{1,0:T(8,128)(2,1)S(1)}) custom-call(bf16[4,512,128]{2,1,0:T(8,128)(2,1)S(1)} %get-tuple-element.56.rows, f32[3,512,128]{2,1,0:T(8,128)S(1)} %get-tuple-element.53.top, f32[3,512,256]{2,1,0:T(8,128)S(1)} %get-tuple-element.52.total, bf16[2304,128]{1,0:T(8,128)(2,1)S(1)} %collective-permute-done.3.half, ...), custom_call_target="tpu_custom_call" | custom-call | flops 4294967296 | tf_op jit(solution)/shard_map/pallas_call | solution.py:285
  44.1 1.0 %collective-permute-start.9 = (bf16[144,512]{1,0:T(8,128)(2,1)S(1)}, bf16[144,512]{1,0:T(8,128)(2,1)S(1)}, u32[]{:S(2)}, u32[]{:S(2)}) collective-permute-start(bf16[144,512]{1,0:T(8,128)(2,1)S(1)} %get-tuple-element.54), channel_id=1, source_target_pairs={{0,48},{8,56},{16,0},{24,8},{32,16},{40,24},{48,32},{56,40},{64,11... | collective-permute-start | bytes 442376 | tf_op jit(solution)/shard_map/ppermute | solution.py:28
  45.1 0.6 collective-permute-start.10
  46.4 0.0 collective-permute-done.8.r2
  46.4 3.0 %shard_map.90 = (f32[128,512]{1,0:T(8,128)S(1)}, f32[8,512]{1,0:T(8,128)S(1)}) custom-call(bf16[4,512,128]{2,1,0:T(8,128)(2,1)S(1)} %get-tuple-element.56.rows, f32[512,128]{1,0:T(8,128)S(1)} %get-tuple-element.50.top, f32[512,256]{1,0:T(8,128)S(1)} %get-tuple-element.57.total, bf16[2304,128]{1,0:T(8,128)(2,1)S(1)} %collective-permute-done.3.half, ...), custom_call_target="tpu_custom_call" | custom-call | flops 1 | tf_op jit(solution)/shard_map/pallas_call | solution.py:289
  49.3 0.0 collective-permute-done.9.r0
  49.4 1.7 %collective-permute-done.10.r1 = bf16[144,512]{1,0:T(8,128)(2,1)S(1)} collective-permute-done((bf16[144,512]{1,0:T(8,128)(2,1)S(1)}, bf16[144,512]{1,0:T(8,128)(2,1)S(1)}, u32[]{:S(2)}, u32[]{:S(2)}) %collective-permute-start.10) | collective-permute-done | bytes 147488 | tf_op jit(solution)/shard_map/ppermute | solution.py:28
  51.1 0.2 shard_map.91.a0
  51.3 1.2 %collective-permute-start.13 = (bf16[64,1024]{1,0:T(8,128)(2,1)S(1)}, bf16[64,1024]{1,0:T(8,128)(2,1)S(1)}, u32[]{:S(2)}, u32[]{:S(2)}) collective-permute-start(bf16[64,1024]{1,0:T(8,128)(2,1)S(1)} %shard_map.91.a0), channel_id=1, source_target_pairs={{0,32},{8,40},{16,48},{24,56},{32,0},{40,8},{48,16},{56,24},{64,96... | collective-permute-start | bytes 393224 | tf_op jit(solution)/shard_map/ppermute | solution.py:28
  52.4 1.2 %collective-permute-start.12 = (bf16[64,1024]{1,0:T(8,128)(2,1)S(1)}, bf16[64,1024]{1,0:T(8,128)(2,1)S(1)}, u32[]{:S(2)}, u32[]{:S(2)}) collective-permute-start(bf16[64,1024]{1,0:T(8,128)(2,1)S(1)} %shard_map.91.a0), channel_id=1, source_target_pairs={{0,48},{8,56},{16,0},{24,8},{32,16},{40,24},{48,32},{56,40},{64,11... | collective-permute-start | bytes 393224 | tf_op jit(solution)/shard_map/ppermute | solution.py:28
  53.7 0.2 collective-permute-start.11
  53.9 2.7 %collective-permute-start.14 = (bf16[64,1024]{1,0:T(8,128)(2,1)S(1)}, bf16[64,1024]{1,0:T(8,128)(2,1)S(1)}, u32[]{:S(2)}, u32[]{:S(2)}) collective-permute-start(bf16[64,1024]{1,0:T(8,128)(2,1)S(1)} %shard_map.91.a0), channel_id=1, source_target_pairs={{0,64},{8,72},{16,80},{24,88},{32,96},{40,104},{48,112},{56,120},{... | collective-permute-start | bytes 393224 | tf_op jit(solution)/shard_map/ppermute | solution.py:28
  56.6 0.3 collective-permute-done.13.a3
  56.9 2.7 %collective-permute-start.17 = (bf16[64,1024]{1,0:T(8,128)(2,1)S(1)}, bf16[64,1024]{1,0:T(8,128)(2,1)S(1)}, u32[]{:S(2)}, u32[]{:S(2)}) collective-permute-start(bf16[64,1024]{1,0:T(8,128)(2,1)S(1)} %collective-permute-done.13.a3), channel_id=1, source_target_pairs={{0,64},{8,72},{16,80},{24,88},{32,96},{40,104},{48,112},{56,120},{... | collective-permute-start | bytes 393224 | tf_op jit(solution)/shard_map/ppermute | solution.py:28
  59.7 0.0 collective-permute-done.12.a2
  59.7 1.3 %collective-permute-start.16 = (bf16[64,1024]{1,0:T(8,128)(2,1)S(1)}, bf16[64,1024]{1,0:T(8,128)(2,1)S(1)}, u32[]{:S(2)}, u32[]{:S(2)}) collective-permute-start(bf16[64,1024]{1,0:T(8,128)(2,1)S(1)} %collective-permute-done.12.a2), channel_id=1, source_target_pairs={{0,64},{8,72},{16,80},{24,88},{32,96},{40,104},{48,112},{56,120},{... | collective-permute-start | bytes 393224 | tf_op jit(solution)/shard_map/ppermute | solution.py:28
  61.0 0.0 collective-permute-done.11.a1
  61.0 2.4 %collective-permute-start.15 = (bf16[64,1024]{1,0:T(8,128)(2,1)S(1)}, bf16[64,1024]{1,0:T(8,128)(2,1)S(1)}, u32[]{:S(2)}, u32[]{:S(2)}) collective-permute-start(bf16[64,1024]{1,0:T(8,128)(2,1)S(1)} %collective-permute-done.11.a1), channel_id=1, source_target_pairs={{0,64},{8,72},{16,80},{24,88},{32,96},{40,104},{48,112},{56,120},{... | collective-permute-start | bytes 393224 | tf_op jit(solution)/shard_map/ppermute | solution.py:28
  63.4 0.0 collective-permute-done.14.a4
  63.4 0.5 collective-permute-done.17.a7
  63.9 1.5 %collective-permute-done.16.a6 = bf16[64,1024]{1,0:T(8,128)(2,1)S(1)} collective-permute-done((bf16[64,1024]{1,0:T(8,128)(2,1)S(1)}, bf16[64,1024]{1,0:T(8,128)(2,1)S(1)}, u32[]{:S(2)}, u32[]{:S(2)}) %collective-permute-start.16) | collective-permute-done | bytes 131104 | tf_op jit(solution)/shard_map/ppermute | solution.py:28
  65.4 2.6 %collective-permute-done.15.a5 = bf16[64,1024]{1,0:T(8,128)(2,1)S(1)} collective-permute-done((bf16[64,1024]{1,0:T(8,128)(2,1)S(1)}, bf16[64,1024]{1,0:T(8,128)(2,1)S(1)}, u32[]{:S(2)}, u32[]{:S(2)}) %collective-permute-start.15) | collective-permute-done | bytes 131104 | tf_op jit(solution)/shard_map/ppermute | solution.py:28
  68.1 0.0 collective-permute-done.18.wb
  68.1 1.2 %shard_map.92 = bf16[8,64,1024]{2,1,0:T(8,128)(2,1)S(1)} custom-call(s32[1]{0:T(128)} %bitcast.index, bf16[64,1024]{1,0:T(8,128)(2,1)S(1)} %shard_map.91.a0, bf16[64,1024]{1,0:T(8,128)(2,1)S(1)} %collective-permute-done.11.a1, bf16[64,1024]{1,0:T(8,128)(2,1)S(1)} %collective-permute-done.12.a2, bf16[64,1024]{1,0:T(8,128)(2,1)S(1)} %collective-permute-done.13.a3, ...), custom_call_target="tpu_custom_call" | custom-call | tf_op jit(solution)/shard_map/pallas_call | solution.py:299
  69.3 17.1 %all_to_all.5.terms = bf16[8,64,1024]{2,1,0:T(8,128)(2,1)S(1)} all-to-all(bf16[8,64,1024]{2,1,0:T(8,128)(2,1)S(1)} %shard_map.92), channel_id=1, replica_groups=mesh['blk'=16,'head'=8] {'head'}, dimensions={0} | all-to-all | bytes 2097152 | tf_op jit(solution)/shard_map/all_to_all | solution.py:305
  86.5 0.1 shard_map.93
  86.6 4.7 %collective-permute-start.19 = (bf16[64,512]{1,0:T(8,128)(2,1)S(1)}, bf16[64,512]{1,0:T(8,128)(2,1)S(1)}, u32[]{:S(2)}, u32[]{:S(2)}) collective-permute-start(bf16[64,512]{1,0:T(8,128)(2,1)S(1)} %get-tuple-element.62), channel_id=1, source_target_pairs={{0,8},{8,0},{16,24},{24,16},{32,40},{40,32},{48,56},{56,48},{64,72... | collective-permute-start | bytes 196616 | tf_op jit(solution)/shard_map/ppermute | solution.py:28
  91.3 0.9 collective-permute-done.19
  92.2 0.7 maximum_select_fusion
  (5 shorter events, 0.0 us)
Async XLA Ops:
  0.0 21.6 %copy-start.2 = (bf16[64,1024]{1,0:T(8,128)(2,1)S(1)}, bf16[64,1024]{1,0:T(8,128)(2,1)}, u32[]{:S(2)}) copy-start(bf16[64,1024]{1,0:T(8,128)(2,1)} %q.3) | copy-start | bytes 393220
  0.0 1.1 %copy-start.3 = (bf16[2048,128]{1,0:T(8,128)(2,1)S(1)}, bf16[2048,128]{1,0:T(8,128)(2,1)}, u32[]{:S(2)}) copy-start(bf16[2048,128]{1,0:T(8,128)(2,1)} %k.1) | copy-start | bytes 1572868
  1.1 1.0 %copy-start.4 = (bf16[2048,128]{1,0:T(8,128)(2,1)S(1)}, bf16[2048,128]{1,0:T(8,128)(2,1)}, u32[]{:S(2)}) copy-start(bf16[2048,128]{1,0:T(8,128)(2,1)} %v.1) | copy-start | bytes 1572868
  2.3 23.3 %collective-permute-start.4 = (bf16[4096,128]{1,0:T(8,128)(2,1)S(1)}, bf16[4096,128]{1,0:T(8,128)(2,1)S(1)}, u32[]{:S(2)}, u32[]{:S(2)}) collective-permute-start(bf16[4096,128]{1,0:T(8,128)(2,1)S(1)} %get-tuple-element.34.kv), channel_id=1, source_target_pairs={{0,8},{8,0},{16,24},{24,16},{32,40},{40,32},{48,56},{56,48},{64,72... | collective-permute-start | bytes 3145736 | tf_op jit(solution)/shard_map/ppermute | solution.py:28
  3.8 16.4 %collective-permute-start.5 = (bf16[1792,128]{1,0:T(8,128)(2,1)S(1)}, bf16[1792,128]{1,0:T(8,128)(2,1)S(1)}, u32[]{:S(2)}, u32[]{:S(2)}) collective-permute-start(bf16[1792,128]{1,0:T(8,128)(2,1)S(1)} %get-tuple-element.41), channel_id=1, source_target_pairs={{0,64},{8,72},{16,80},{24,88},{32,96},{40,104},{48,112},{56,120},{... | collective-permute-start | bytes 1376264 | tf_op jit(solution)/shard_map/ppermute | solution.py:28
  6.6 7.5 %collective-permute-start = (bf16[64,1024]{1,0:T(8,128)(2,1)}, bf16[64,1024]{1,0:T(8,128)(2,1)S(1)}, u32[]{:S(2)}, u32[]{:S(2)}) collective-permute-start(bf16[64,1024]{1,0:T(8,128)(2,1)} %q.3), channel_id=1, source_target_pairs={{0,16},{8,24},{16,32},{24,40},{32,48},{40,56},{48,0},{56,8},{64,80... | collective-permute-start | bytes 393224 | tf_op jit(solution)/shard_map/ppermute | solution.py:28
  8.2 11.9 %collective-permute-start.2 = (bf16[64,1024]{1,0:T(8,128)(2,1)}, bf16[64,1024]{1,0:T(8,128)(2,1)S(1)}, u32[]{:S(2)}, u32[]{:S(2)}) collective-permute-start(bf16[64,1024]{1,0:T(8,128)(2,1)} %q.3), channel_id=1, source_target_pairs={{0,32},{8,40},{16,48},{24,56},{32,0},{40,8},{48,16},{56,24},{64,96... | collective-permute-start | bytes 393224 | tf_op jit(solution)/shard_map/ppermute | solution.py:28
  11.5 8.6 %collective-permute-start.1 = (bf16[64,1024]{1,0:T(8,128)(2,1)}, bf16[64,1024]{1,0:T(8,128)(2,1)S(1)}, u32[]{:S(2)}, u32[]{:S(2)}) collective-permute-start(bf16[64,1024]{1,0:T(8,128)(2,1)} %q.3), channel_id=1, source_target_pairs={{0,48},{8,56},{16,0},{24,8},{32,16},{40,24},{48,32},{56,40},{64,11... | collective-permute-start | bytes 393224 | tf_op jit(solution)/shard_map/ppermute | solution.py:28
  14.2 18.8 %collective-permute-start.3 = (bf16[2304,128]{1,0:T(8,128)(2,1)S(1)}, bf16[2304,128]{1,0:T(8,128)(2,1)S(1)}, u32[]{:S(2)}, u32[]{:S(2)}) collective-permute-start(bf16[2304,128]{1,0:T(8,128)(2,1)S(1)} %get-tuple-element.36), channel_id=1, source_target_pairs={{0,64},{8,72},{16,80},{24,88},{32,96},{40,104},{48,112},{56,120},{... | collective-permute-start | bytes 1769480 | tf_op jit(solution)/shard_map/ppermute | solution.py:28
  15.2 0.9 copy-start.1
  16.1 0.7 copy-start.5
  16.8 0.7 copy-start.6
  20.1 9.3 %collective-permute-start.6 = (bf16[1792,128]{1,0:T(8,128)(2,1)S(1)}, bf16[1792,128]{1,0:T(8,128)(2,1)S(1)}, u32[]{:S(2)}, u32[]{:S(2)}) collective-permute-start(bf16[1792,128]{1,0:T(8,128)(2,1)S(1)} %collective-permute-done.5.refs_0_.half), channel_id=1, source_target_pairs={{0,8},{8,0},{16,24},{24,16},{32,40},{40,32},{48,56},{56,48},{64,72... | collective-permute-start | bytes 1376264 | tf_op jit(solution)/shard_map/ppermute | solution.py:28
  29.5 3.6 %copy-start = (bf16[1024,512]{1,0:T(8,128)(2,1)S(1)}, bf16[1024,512]{1,0:T(8,128)(2,1)}, u32[]{:S(2)}) copy-start(bf16[1024,512]{1,0:T(8,128)(2,1)} %wa.1) | copy-start | bytes 3145732
  33.0 3.5 %collective-permute-start.7 = (bf16[2304,128]{1,0:T(8,128)(2,1)S(1)}, bf16[2304,128]{1,0:T(8,128)(2,1)S(1)}, u32[]{:S(2)}, u32[]{:S(2)}) collective-permute-start(bf16[2304,128]{1,0:T(8,128)(2,1)S(1)} %collective-permute-done.3.half), channel_id=1, source_target_pairs={{0,8},{8,0},{16,24},{24,16},{32,40},{40,32},{48,56},{56,48},{64,72... | collective-permute-start | bytes 1769480 | tf_op jit(solution)/shard_map/ppermute | solution.py:28
  33.1 35.0 %collective-permute-start.18 = (bf16[1024,512]{1,0:T(8,128)(2,1)S(1)}, bf16[1024,512]{1,0:T(8,128)(2,1)S(1)}, u32[]{:S(2)}, u32[]{:S(2)}) collective-permute-start(bf16[1024,512]{1,0:T(8,128)(2,1)S(1)} %copy-done), channel_id=1, source_target_pairs={{0,8},{8,0},{16,24},{24,16},{32,40},{40,32},{48,56},{56,48},{64,72... | collective-permute-start | bytes 3145736 | tf_op jit(solution)/shard_map/ppermute | solution.py:28
  39.5 6.9 %collective-permute-start.8 = (bf16[144,512]{1,0:T(8,128)(2,1)S(1)}, bf16[144,512]{1,0:T(8,128)(2,1)S(1)}, u32[]{:S(2)}, u32[]{:S(2)}) collective-permute-start(bf16[144,512]{1,0:T(8,128)(2,1)S(1)} %shard_map.88), channel_id=1, source_target_pairs={{0,32},{8,40},{16,48},{24,56},{32,0},{40,8},{48,16},{56,24},{64,96... | collective-permute-start | bytes 442376 | tf_op jit(solution)/shard_map/ppermute | solution.py:28
  44.1 5.3 %collective-permute-start.9 = (bf16[144,512]{1,0:T(8,128)(2,1)S(1)}, bf16[144,512]{1,0:T(8,128)(2,1)S(1)}, u32[]{:S(2)}, u32[]{:S(2)}) collective-permute-start(bf16[144,512]{1,0:T(8,128)(2,1)S(1)} %get-tuple-element.54), channel_id=1, source_target_pairs={{0,48},{8,56},{16,0},{24,8},{32,16},{40,24},{48,32},{56,40},{64,11... | collective-permute-start | bytes 442376 | tf_op jit(solution)/shard_map/ppermute | solution.py:28
  45.1 6.0 %collective-permute-start.10 = (bf16[144,512]{1,0:T(8,128)(2,1)S(1)}, bf16[144,512]{1,0:T(8,128)(2,1)S(1)}, u32[]{:S(2)}, u32[]{:S(2)}) collective-permute-start(bf16[144,512]{1,0:T(8,128)(2,1)S(1)} %get-tuple-element.55), channel_id=1, source_target_pairs={{0,16},{8,24},{16,32},{24,40},{32,48},{40,56},{48,0},{56,8},{64,80... | collective-permute-start | bytes 442376 | tf_op jit(solution)/shard_map/ppermute | solution.py:28
  51.3 5.7 %collective-permute-start.13 = (bf16[64,1024]{1,0:T(8,128)(2,1)S(1)}, bf16[64,1024]{1,0:T(8,128)(2,1)S(1)}, u32[]{:S(2)}, u32[]{:S(2)}) collective-permute-start(bf16[64,1024]{1,0:T(8,128)(2,1)S(1)} %shard_map.91.a0), channel_id=1, source_target_pairs={{0,32},{8,40},{16,48},{24,56},{32,0},{40,8},{48,16},{56,24},{64,96... | collective-permute-start | bytes 393224 | tf_op jit(solution)/shard_map/ppermute | solution.py:28
  52.4 7.2 %collective-permute-start.12 = (bf16[64,1024]{1,0:T(8,128)(2,1)S(1)}, bf16[64,1024]{1,0:T(8,128)(2,1)S(1)}, u32[]{:S(2)}, u32[]{:S(2)}) collective-permute-start(bf16[64,1024]{1,0:T(8,128)(2,1)S(1)} %shard_map.91.a0), channel_id=1, source_target_pairs={{0,48},{8,56},{16,0},{24,8},{32,16},{40,24},{48,32},{56,40},{64,11... | collective-permute-start | bytes 393224 | tf_op jit(solution)/shard_map/ppermute | solution.py:28
  53.7 7.3 %collective-permute-start.11 = (bf16[64,1024]{1,0:T(8,128)(2,1)S(1)}, bf16[64,1024]{1,0:T(8,128)(2,1)S(1)}, u32[]{:S(2)}, u32[]{:S(2)}) collective-permute-start(bf16[64,1024]{1,0:T(8,128)(2,1)S(1)} %shard_map.91.a0), channel_id=1, source_target_pairs={{0,16},{8,24},{16,32},{24,40},{32,48},{40,56},{48,0},{56,8},{64,80... | collective-permute-start | bytes 393224 | tf_op jit(solution)/shard_map/ppermute | solution.py:28
  53.9 9.5 %collective-permute-start.14 = (bf16[64,1024]{1,0:T(8,128)(2,1)S(1)}, bf16[64,1024]{1,0:T(8,128)(2,1)S(1)}, u32[]{:S(2)}, u32[]{:S(2)}) collective-permute-start(bf16[64,1024]{1,0:T(8,128)(2,1)S(1)} %shard_map.91.a0), channel_id=1, source_target_pairs={{0,64},{8,72},{16,80},{24,88},{32,96},{40,104},{48,112},{56,120},{... | collective-permute-start | bytes 393224 | tf_op jit(solution)/shard_map/ppermute | solution.py:28
  56.9 7.0 %collective-permute-start.17 = (bf16[64,1024]{1,0:T(8,128)(2,1)S(1)}, bf16[64,1024]{1,0:T(8,128)(2,1)S(1)}, u32[]{:S(2)}, u32[]{:S(2)}) collective-permute-start(bf16[64,1024]{1,0:T(8,128)(2,1)S(1)} %collective-permute-done.13.a3), channel_id=1, source_target_pairs={{0,64},{8,72},{16,80},{24,88},{32,96},{40,104},{48,112},{56,120},{... | collective-permute-start | bytes 393224 | tf_op jit(solution)/shard_map/ppermute | solution.py:28
  59.7 5.8 %collective-permute-start.16 = (bf16[64,1024]{1,0:T(8,128)(2,1)S(1)}, bf16[64,1024]{1,0:T(8,128)(2,1)S(1)}, u32[]{:S(2)}, u32[]{:S(2)}) collective-permute-start(bf16[64,1024]{1,0:T(8,128)(2,1)S(1)} %collective-permute-done.12.a2), channel_id=1, source_target_pairs={{0,64},{8,72},{16,80},{24,88},{32,96},{40,104},{48,112},{56,120},{... | collective-permute-start | bytes 393224 | tf_op jit(solution)/shard_map/ppermute | solution.py:28
  61.0 7.1 %collective-permute-start.15 = (bf16[64,1024]{1,0:T(8,128)(2,1)S(1)}, bf16[64,1024]{1,0:T(8,128)(2,1)S(1)}, u32[]{:S(2)}, u32[]{:S(2)}) collective-permute-start(bf16[64,1024]{1,0:T(8,128)(2,1)S(1)} %collective-permute-done.11.a1), channel_id=1, source_target_pairs={{0,64},{8,72},{16,80},{24,88},{32,96},{40,104},{48,112},{56,120},{... | collective-permute-start | bytes 393224 | tf_op jit(solution)/shard_map/ppermute | solution.py:28
  86.6 5.6 %collective-permute-start.19 = (bf16[64,512]{1,0:T(8,128)(2,1)S(1)}, bf16[64,512]{1,0:T(8,128)(2,1)S(1)}, u32[]{:S(2)}, u32[]{:S(2)}) collective-permute-start(bf16[64,512]{1,0:T(8,128)(2,1)S(1)} %get-tuple-element.62), channel_id=1, source_target_pairs={{0,8},{8,0},{16,24},{24,16},{32,40},{40,32},{48,56},{56,48},{64,72... | collective-permute-start | bytes 196616 | tf_op jit(solution)/shard_map/ppermute | solution.py:28

commit v11 on v10

--- a/solution.py
+++ b/solution.py
@@ -127,25 +127,26 @@
     )
 
 
-def own_kernel(q, qk, qv, bias, kv, top_out, total_out, k, values):
+def own_kernel(q, qkv, bias, kv, top_out, total_out, k, values):
     split((kv,), k, values)
     rows = stacked(q)
-    scores = scores_of(rows, qk[...]) + jnp.concatenate([bias[...]] * GROUP, axis=0)
+    scores = scores_of(rows, qkv[:ROWS, :]) + jnp.concatenate([bias[...]] * GROUP, axis=0)
     block = scores_of(rows, k[...])
     top, total = add_block(
         *empty(),
         scores,
-        jnp.concatenate([qv[...], jnp.ones((ROWS, DH), jnp.bfloat16)], axis=1),
+        jnp.concatenate([qkv[ROWS:, :], jnp.ones((ROWS, DH), jnp.bfloat16)], axis=1),
     )
     top_out[...], total_out[...] = add_block(top, total, block, values[...])
 
 
-def near_kernel(q0, q1, q2, q, kv, top_out, total_out, rows, k, values):
-    split((kv,), k, values)
+def near_kernel(q0, q1, q2, q, kv, kv_c, top_out, total_out, rows, k0, v0, k1, v1):
+    split((kv,), k0, v0)
+    split((kv_c,), k1, v1)
     for i, ref in enumerate((q0, q1, q2, q)):
         rows[i] = stacked(ref)
-    states = run([(i, rows.at[i], k, values) for i in range(3)], [empty() for _ in range(3)])
-    for i, (top, total) in enumerate(states):
+    tasks = [(i, rows.at[i], k, v) for k, v in ((k0, v0), (k1, v1)) for i in range(3)]
+    for i, (top, total) in enumerate(run(tasks, [empty() for _ in range(3)])):
         top_out[i], total_out[i] = top, total
 
 
@@ -262,22 +263,21 @@
         return [pltpu.VMEM((size, width), bf16) for size in sizes for width in (DH, 2 * DH)]
 
     own_top, own_total = call(own_kernel, own_state, scratch(positions))(
-        queries, question_keys, question_values, after(bias, q_z[0]), kv
-    )
-    top, total, rows = call(near_kernel, state + [((4, LANES, DH), bf16)], scratch(positions))(
-        *q_z, queries, kv
+        queries, jnp.concatenate([question_keys, question_values]), bias, after(kv, q_z[0])
     )
     x0 = after(x0, own_top, *q_z)
     xc0 = moved(x0, c=1)
-    top, total = call(others_kernel, state, scratch(positions), flops=1)(rows, top, total, kv_c)
+    top, total, rows = call(
+        near_kernel, state + [((4, LANES, DH), bf16)], scratch(positions, positions), flops=1
+    )(*q_z, queries, kv, kv_c)
     top, total = call(others_kernel, state, scratch(2 * early), flops=1)(rows, top, total, x0, xc0)
 
     x1, weight, top = lax.optimization_barrier((x1, out_weight, top))
     xc1 = moved(x1, c=1)
     weight_c = moved(weight, c=1)
-    own_top, own_total = call(own_kernel_2, own_state, scratch(positions, 2 * early), flops=2 * block_flops)(
-        after(rows, x1), own_top, own_total, kv_c, x0, xc0
-    )
+    own_top, own_total = call(
+        own_kernel_2, own_state, scratch(positions, 2 * early), flops=2 * block_flops
+    )(after(rows, x1), own_top, own_total, kv_c, x0, xc0)
     top = after(top, own_top)
     (p_far,) = call(functools.partial(last_kernel, owners=(2,)), [part], scratch(2 * late), flops=1)(
         rows, top, total, x1, xc1

time: 93.2 us -> 94.5 us (1.014)
  starting transfers between devices: 31.8 us -> 35.5 us
  waiting for transfers between devices: 9.5 us -> 7.53 us
  local copies, waits for them, and re-layouts: 4.46 us -> 2.99 us
    ppermute x20, starting transfers between devices: 31.8 us -> 35.5 us  [moved(): return lax.ppermute(array, 'blk', pairs)]
    ppermute x20, waiting for transfers between devices: 9.5 us -> 7.53 us  [moved(): return lax.ppermute(array, 'blk', pairs)]
    unnamed x14 -> x8, local copies, waits for them, and re-layouts: 4.46 us -> 2.99 us
    pallas_call x2 -> x1, Pallas kernels: 7.86 us -> 7.92 us  [shards(): call(near_kernel, state + [((4, LANES, DH), bf16)], scratch(positions, po...]
  transfers between devices with their start and end apart: 20 -> 20, of which waited for: 7 -> 5; matrix products, arithmetic and copies ran while one was open for 1% -> 2% of each run, Pallas kernels for 28% -> 28%
where the time goes in v11:
time: 94.5 us; the launch traced here: 94.2 us
  starting transfers between devices  35.5 us (38%)
  Pallas kernels  27.7 us (29%)
  blocking collectives  17.3 us (18%)
  waiting for transfers between devices  7.53 us (8%)
  local copies, waits for them, and re-layouts  2.99 us (3%)
  other arithmetic  2.22 us (2%)
    ppermute x20, starting transfers between devices, moved(): return lax.ppermute(array, 'blk', pairs)  35.5 us
    all_to_all x1, blocking collectives, shards(): gathered = lax.all_to_all(terms, 'head', 0, 0, tiled=True)  17.3 us
    pallas_call x1, Pallas kernels, shards(): call(near_kernel, state + [((4, LANES, DH), bf16)], scratch(positions, po...  7.92 us
    ppermute x20, waiting for transfers between devices, moved(): return lax.ppermute(array, 'blk', pairs)  7.53 us
    pallas_call x1, Pallas kernels, shards(): call(others_kernel, state, scratch(2 * early), flops=1)  3.5 us
    pallas_call x1, Pallas kernels, shards(): call(functools.partial(last_kernel, owners=(0, 1)), [part] * 2, scratch(2...  3.18 us
    unnamed x8, local copies, waits for them, and re-layouts  2.99 us
    pallas_call x1, Pallas kernels, shards(): call(own_last_kernel, [((DH, LANES), f32), ((8, LANES), f32)], scratch(2...  2.97 us
  transfers between devices with their start and end apart: 20, of which 5 were waited for; matrix products, arithmetic and copies ran while one was open for 2% of the time, Pallas kernels for 28%

profile of v11, /device:TPU:1, one launch (start us, length us, event | category | flops | bytes accessed | tf_op | source)
XLA Modules:
  0.0 94.2 jit_solution(6085449367599131925)
XLA Ops:
  0.0 0.0 copy-start.2
  0.0 1.0 %copy-done.2 = bf16[2048,128]{1,0:T(8,128)(2,1)S(1)} copy-done((bf16[2048,128]{1,0:T(8,128)(2,1)S(1)}, bf16[2048,128]{1,0:T(8,128)(2,1)}, u32[]{:S(2)}) %copy-start.2) | copy-done | bytes 524312
  1.0 0.0 copy-start.3
  1.0 1.0 %copy-done.3 = bf16[2048,128]{1,0:T(8,128)(2,1)S(1)} copy-done((bf16[2048,128]{1,0:T(8,128)(2,1)S(1)}, bf16[2048,128]{1,0:T(8,128)(2,1)}, u32[]{:S(2)}) %copy-start.3) | copy-done | bytes 524312
  2.1 0.1 shard_map.82
  2.2 1.5 %collective-permute-start.3 = (bf16[4096,128]{1,0:T(8,128)(2,1)S(1)}, bf16[4096,128]{1,0:T(8,128)(2,1)S(1)}, u32[]{:S(2)}, u32[]{:S(2)}) collective-permute-start(bf16[4096,128]{1,0:T(8,128)(2,1)S(1)} %get-tuple-element.38.kv), channel_id=1, source_target_pairs={{0,8},{8,0},{16,24},{24,16},{32,40},{40,32},{48,56},{56,48},{64,72... | collective-permute-start | bytes 3145736 | tf_op jit(solution)/shard_map/ppermute | solution.py:28
  3.7 1.7 %collective-permute-start = (bf16[64,1024]{1,0:T(8,128)(2,1)}, bf16[64,1024]{1,0:T(8,128)(2,1)S(1)}, u32[]{:S(2)}, u32[]{:S(2)}) collective-permute-start(bf16[64,1024]{1,0:T(8,128)(2,1)} %q.3), channel_id=1, source_target_pairs={{0,16},{8,24},{16,32},{24,40},{32,48},{40,56},{48,0},{56,8},{64,80... | collective-permute-start | bytes 393224 | tf_op jit(solution)/shard_map/ppermute | solution.py:28
  5.5 2.7 %collective-permute-start.5 = (bf16[1792,128]{1,0:T(8,128)(2,1)S(1)}, bf16[1792,128]{1,0:T(8,128)(2,1)S(1)}, u32[]{:S(2)}, u32[]{:S(2)}) collective-permute-start(bf16[1792,128]{1,0:T(8,128)(2,1)S(1)} %get-tuple-element.37), channel_id=1, source_target_pairs={{0,64},{8,72},{16,80},{24,88},{32,96},{40,104},{48,112},{56,120},{... | collective-permute-start | bytes 1376264 | tf_op jit(solution)/shard_map/ppermute | solution.py:28
  8.2 2.1 %collective-permute-start.1 = (bf16[64,1024]{1,0:T(8,128)(2,1)}, bf16[64,1024]{1,0:T(8,128)(2,1)S(1)}, u32[]{:S(2)}, u32[]{:S(2)}) collective-permute-start(bf16[64,1024]{1,0:T(8,128)(2,1)} %q.3), channel_id=1, source_target_pairs={{0,48},{8,56},{16,0},{24,8},{32,16},{40,24},{48,32},{56,40},{64,11... | collective-permute-start | bytes 393224 | tf_op jit(solution)/shard_map/ppermute | solution.py:28
  10.3 1.3 %collective-permute-start.2 = (bf16[64,1024]{1,0:T(8,128)(2,1)}, bf16[64,1024]{1,0:T(8,128)(2,1)S(1)}, u32[]{:S(2)}, u32[]{:S(2)}) collective-permute-start(bf16[64,1024]{1,0:T(8,128)(2,1)} %q.3), channel_id=1, source_target_pairs={{0,32},{8,40},{16,48},{24,56},{32,0},{40,8},{48,16},{56,24},{64,96... | collective-permute-start | bytes 393224 | tf_op jit(solution)/shard_map/ppermute | solution.py:28
  11.6 0.0 collective-permute-done.q0
  11.6 2.7 %collective-permute-start.4 = (bf16[2304,128]{1,0:T(8,128)(2,1)S(1)}, bf16[2304,128]{1,0:T(8,128)(2,1)S(1)}, u32[]{:S(2)}, u32[]{:S(2)}) collective-permute-start(bf16[2304,128]{1,0:T(8,128)(2,1)S(1)} %get-tuple-element.34), channel_id=1, source_target_pairs={{0,64},{8,72},{16,80},{24,88},{32,96},{40,104},{48,112},{56,120},{... | collective-permute-start | bytes 1769480 | tf_op jit(solution)/shard_map/ppermute | solution.py:28
  14.3 0.8 fusion.1.bias
  15.1 0.7 pad_maximum_fusion.qkv
  15.9 0.0 copy-start.1
  15.9 0.9 copy-done.1
  16.8 2.6 %shard_map.84 = (f32[512,128]{1,0:T(8,128)S(1)}, f32[512,256]{1,0:T(8,128)S(1)}) custom-call(bf16[64,1024]{1,0:T(8,128)(2,1)S(1)} %copy-done.1, bf16[128,128]{1,0:T(8,128)(2,1)S(1)} %pad_maximum_fusion.qkv, f32[64,64]{1,0:T(8,128)S(1)} %fusion.1.bias, bf16[4096,128]{1,0:T(8,128)(2,1)S(1)} %get-tuple-element.38.kv), custom_call_target="tpu_custom_call" | custom-call | tf_op jit(solution)/shard_map/pallas_call | solution.py:265
  19.4 0.0 collective-permute-done.1.q1
  19.4 0.0 collective-permute-done.2.q2
  19.4 0.0 collective-permute-done.5.refs_0_.half
  19.4 1.3 %collective-permute-start.6 = (bf16[1792,128]{1,0:T(8,128)(2,1)S(1)}, bf16[1792,128]{1,0:T(8,128)(2,1)S(1)}, u32[]{:S(2)}, u32[]{:S(2)}) collective-permute-start(bf16[1792,128]{1,0:T(8,128)(2,1)S(1)} %collective-permute-done.5.refs_0_.half), channel_id=1, source_target_pairs={{0,8},{8,0},{16,24},{24,16},{32,40},{40,32},{48,56},{56,48},{64,72... | collective-permute-start | bytes 1376264 | tf_op jit(solution)/shard_map/ppermute | solution.py:28
  20.7 0.0 collective-permute-done.3.kv_c.kv
  20.7 7.9 %shard_map.83 = (f32[3,512,128]{2,1,0:T(8,128)S(1)}, f32[3,512,256]{2,1,0:T(8,128)S(1)}, bf16[4,512,128]{2,1,0:T(8,128)(2,1)S(1)}) custom-call(bf16[64,1024]{1,0:T(8,128)(2,1)S(1)} %collective-permute-done.q0, bf16[64,1024]{1,0:T(8,128)(2,1)S(1)} %collective-permute-done.1.q1, bf16[64,1024]{1,0:T(8,128)(2,1)S(1)} %collective-permute-done.2.q2, ...), custom_call_target="tpu_custom_call" | custom-call | flops 1 | tf_op jit(solution)/shard_map/pallas_call | solution.py:270
  28.6 0.0 collective-permute-done.6.refs_1_.other_half
  28.6 0.0 copy-start
  28.6 3.5 %shard_map.85 = (f32[3,512,128]{2,1,0:T(8,128)S(1)}, f32[3,512,256]{2,1,0:T(8,128)S(1)}) custom-call(bf16[4,512,128]{2,1,0:T(8,128)(2,1)S(1)} %get-tuple-element.52.rows, f32[3,512,128]{2,1,0:T(8,128)S(1)} %get-tuple-element.35.top_in, f32[3,512,256]{2,1,0:T(8,128)S(1)} %get-tuple-element.36.total_in, ...), custom_call_target="tpu_custom_call" | custom-call | flops 1 | tf_op jit(solution)/shard_map/pallas_call | solution.py:273
  32.1 0.0 collective-permute-done.4.half
  32.2 0.4 collective-permute-start.7
  32.5 0.0 copy-done
  32.5 0.2 collective-permute-start.18
  32.7 2.9 %shard_map.86 = (f32[512,128]{1,0:T(8,128)S(1)}, f32[512,256]{1,0:T(8,128)S(1)}) custom-call(bf16[4,512,128]{2,1,0:T(8,128)(2,1)S(1)} %get-tuple-element.52.rows, f32[512,128]{1,0:T(8,128)S(1)} %get-tuple-element.39.top, f32[512,256]{1,0:T(8,128)S(1)} %get-tuple-element.45.total, bf16[4096,128]{1,0:T(8,128)(2,1)S(1)} %collective-permute-done.3.kv_c.kv, ...), custom_call_target="tpu_custom_call" | custom-call | flops 2147483648 | tf_op jit(solution)/shard_map/pallas_call | solution.py:278
  35.7 0.0 collective-permute-done.7.other_half
  35.7 2.9 %shard_map.87 = bf16[144,512]{1,0:T(8,128)(2,1)S(1)} custom-call(bf16[4,512,128]{2,1,0:T(8,128)(2,1)S(1)} %get-tuple-element.52.rows, f32[3,512,128]{2,1,0:T(8,128)S(1)} %get-tuple-element.49.top, f32[3,512,256]{2,1,0:T(8,128)S(1)} %get-tuple-element.48.total, bf16[2304,128]{1,0:T(8,128)(2,1)S(1)} %collective-permute-done.4.half, ...), custom_call_target="tpu_custom_call" | custom-call | flops 1 | tf_op jit(solution)/shard_map/pallas_call | solution.py:282
  38.6 3.4 %collective-permute-start.8 = (bf16[144,512]{1,0:T(8,128)(2,1)S(1)}, bf16[144,512]{1,0:T(8,128)(2,1)S(1)}, u32[]{:S(2)}, u32[]{:S(2)}) collective-permute-start(bf16[144,512]{1,0:T(8,128)(2,1)S(1)} %shard_map.87), channel_id=1, source_target_pairs={{0,32},{8,40},{16,48},{24,56},{32,0},{40,8},{48,16},{56,24},{64,96... | collective-permute-start | bytes 442376 | tf_op jit(solution)/shard_map/ppermute | solution.py:28
  42.0 3.2 %shard_map.88 = (bf16[144,512]{1,0:T(8,128)(2,1)S(1)}, bf16[144,512]{1,0:T(8,128)(2,1)S(1)}) custom-call(bf16[4,512,128]{2,1,0:T(8,128)(2,1)S(1)} %get-tuple-element.52.rows, f32[3,512,128]{2,1,0:T(8,128)S(1)} %get-tuple-element.49.top, f32[3,512,256]{2,1,0:T(8,128)S(1)} %get-tuple-element.48.total, bf16[2304,128]{1,0:T(8,128)(2,1)S(1)} %collective-permute-done.4.half, ...), custom_call_target="tpu_custom_call" | custom-call | flops 4294967296 | tf_op jit(solution)/shard_map/pallas_call | solution.py:285
  45.2 0.1 collective-permute-start.10
  45.3 2.7 %collective-permute-start.9 = (bf16[144,512]{1,0:T(8,128)(2,1)S(1)}, bf16[144,512]{1,0:T(8,128)(2,1)S(1)}, u32[]{:S(2)}, u32[]{:S(2)}) collective-permute-start(bf16[144,512]{1,0:T(8,128)(2,1)S(1)} %get-tuple-element.50), channel_id=1, source_target_pairs={{0,48},{8,56},{16,0},{24,8},{32,16},{40,24},{48,32},{56,40},{64,11... | collective-permute-start | bytes 442376 | tf_op jit(solution)/shard_map/ppermute | solution.py:28
  48.6 0.0 collective-permute-done.8.r2
  48.6 3.0 %shard_map.89 = (f32[128,512]{1,0:T(8,128)S(1)}, f32[8,512]{1,0:T(8,128)S(1)}) custom-call(bf16[4,512,128]{2,1,0:T(8,128)(2,1)S(1)} %get-tuple-element.52.rows, f32[512,128]{1,0:T(8,128)S(1)} %get-tuple-element.46.top, f32[512,256]{1,0:T(8,128)S(1)} %get-tuple-element.53.total, bf16[2304,128]{1,0:T(8,128)(2,1)S(1)} %collective-permute-done.4.half, ...), custom_call_target="tpu_custom_call" | custom-call | flops 1 | tf_op jit(solution)/shard_map/pallas_call | solution.py:289
  51.6 0.0 collective-permute-done.10.r1
  51.6 0.0 collective-permute-done.9.r0
  51.6 0.2 shard_map.90.a0
  51.8 0.3 collective-permute-start.11
  52.1 2.7 %collective-permute-start.12 = (bf16[64,1024]{1,0:T(8,128)(2,1)S(1)}, bf16[64,1024]{1,0:T(8,128)(2,1)S(1)}, u32[]{:S(2)}, u32[]{:S(2)}) collective-permute-start(bf16[64,1024]{1,0:T(8,128)(2,1)S(1)} %shard_map.90.a0), channel_id=1, source_target_pairs={{0,48},{8,56},{16,0},{24,8},{32,16},{40,24},{48,32},{56,40},{64,11... | collective-permute-start | bytes 393224 | tf_op jit(solution)/shard_map/ppermute | solution.py:28
  54.8 0.5 collective-permute-start.13
  55.3 2.7 %collective-permute-start.14 = (bf16[64,1024]{1,0:T(8,128)(2,1)S(1)}, bf16[64,1024]{1,0:T(8,128)(2,1)S(1)}, u32[]{:S(2)}, u32[]{:S(2)}) collective-permute-start(bf16[64,1024]{1,0:T(8,128)(2,1)S(1)} %shard_map.90.a0), channel_id=1, source_target_pairs={{0,64},{8,72},{16,80},{24,88},{32,96},{40,104},{48,112},{56,120},{... | collective-permute-start | bytes 393224 | tf_op jit(solution)/shard_map/ppermute | solution.py:28
  58.1 0.0 collective-permute-done.11.a1
  58.1 1.8 %collective-permute-start.15 = (bf16[64,1024]{1,0:T(8,128)(2,1)S(1)}, bf16[64,1024]{1,0:T(8,128)(2,1)S(1)}, u32[]{:S(2)}, u32[]{:S(2)}) collective-permute-start(bf16[64,1024]{1,0:T(8,128)(2,1)S(1)} %collective-permute-done.11.a1), channel_id=1, source_target_pairs={{0,64},{8,72},{16,80},{24,88},{32,96},{40,104},{48,112},{56,120},{... | collective-permute-start | bytes 393224 | tf_op jit(solution)/shard_map/ppermute | solution.py:28
  59.9 0.0 collective-permute-done.12.a2
  59.9 1.2 %collective-permute-start.16 = (bf16[64,1024]{1,0:T(8,128)(2,1)S(1)}, bf16[64,1024]{1,0:T(8,128)(2,1)S(1)}, u32[]{:S(2)}, u32[]{:S(2)}) collective-permute-start(bf16[64,1024]{1,0:T(8,128)(2,1)S(1)} %collective-permute-done.12.a2), channel_id=1, source_target_pairs={{0,64},{8,72},{16,80},{24,88},{32,96},{40,104},{48,112},{56,120},{... | collective-permute-start | bytes 393224 | tf_op jit(solution)/shard_map/ppermute | solution.py:28
  61.0 0.8 collective-permute-done.13.a3
  61.8 2.7 %collective-permute-start.17 = (bf16[64,1024]{1,0:T(8,128)(2,1)S(1)}, bf16[64,1024]{1,0:T(8,128)(2,1)S(1)}, u32[]{:S(2)}, u32[]{:S(2)}) collective-permute-start(bf16[64,1024]{1,0:T(8,128)(2,1)S(1)} %collective-permute-done.13.a3), channel_id=1, source_target_pairs={{0,64},{8,72},{16,80},{24,88},{32,96},{40,104},{48,112},{56,120},{... | collective-permute-start | bytes 393224 | tf_op jit(solution)/shard_map/ppermute | solution.py:28
  64.5 0.0 collective-permute-done.14.a4
  64.5 0.5 collective-permute-done.15.a5
  65.0 2.5 %collective-permute-done.16.a6 = bf16[64,1024]{1,0:T(8,128)(2,1)S(1)} collective-permute-done((bf16[64,1024]{1,0:T(8,128)(2,1)S(1)}, bf16[64,1024]{1,0:T(8,128)(2,1)S(1)}, u32[]{:S(2)}, u32[]{:S(2)}) %collective-permute-start.16) | collective-permute-done | bytes 131104 | tf_op jit(solution)/shard_map/ppermute | solution.py:28
  67.6 2.8 %collective-permute-done.17.a7 = bf16[64,1024]{1,0:T(8,128)(2,1)S(1)} collective-permute-done((bf16[64,1024]{1,0:T(8,128)(2,1)S(1)}, bf16[64,1024]{1,0:T(8,128)(2,1)S(1)}, u32[]{:S(2)}, u32[]{:S(2)}) %collective-permute-start.17) | collective-permute-done | bytes 131104 | tf_op jit(solution)/shard_map/ppermute | solution.py:28
  70.4 0.0 collective-permute-done.18.wb
  70.4 1.2 %shard_map.91 = bf16[8,64,1024]{2,1,0:T(8,128)(2,1)S(1)} custom-call(s32[1]{0:T(128)} %bitcast.index, bf16[64,1024]{1,0:T(8,128)(2,1)S(1)} %shard_map.90.a0, bf16[64,1024]{1,0:T(8,128)(2,1)S(1)} %collective-permute-done.11.a1, bf16[64,1024]{1,0:T(8,128)(2,1)S(1)} %collective-permute-done.12.a2, bf16[64,1024]{1,0:T(8,128)(2,1)S(1)} %collective-permute-done.13.a3, ...), custom_call_target="tpu_custom_call" | custom-call | tf_op jit(solution)/shard_map/pallas_call | solution.py:299
  71.6 17.3 %all_to_all.5.terms = bf16[8,64,1024]{2,1,0:T(8,128)(2,1)S(1)} all-to-all(bf16[8,64,1024]{2,1,0:T(8,128)(2,1)S(1)} %shard_map.91), channel_id=1, replica_groups=mesh['blk'=16,'head'=8] {'head'}, dimensions={0} | all-to-all | bytes 2097152 | tf_op jit(solution)/shard_map/all_to_all | solution.py:305
  89.0 0.1 shard_map.92
  89.1 3.5 %collective-permute-start.19 = (bf16[64,512]{1,0:T(8,128)(2,1)S(1)}, bf16[64,512]{1,0:T(8,128)(2,1)S(1)}, u32[]{:S(2)}, u32[]{:S(2)}) collective-permute-start(bf16[64,512]{1,0:T(8,128)(2,1)S(1)} %get-tuple-element.58), channel_id=1, source_target_pairs={{0,8},{8,0},{16,24},{24,16},{32,40},{40,32},{48,56},{56,48},{64,72... | collective-permute-start | bytes 196616 | tf_op jit(solution)/shard_map/ppermute | solution.py:28
  92.6 0.9 collective-permute-done.19
  93.5 0.7 maximum_select_fusion
Async XLA Ops:
  0.0 1.0 %copy-start.2 = (bf16[2048,128]{1,0:T(8,128)(2,1)S(1)}, bf16[2048,128]{1,0:T(8,128)(2,1)}, u32[]{:S(2)}) copy-start(bf16[2048,128]{1,0:T(8,128)(2,1)} %k.1) | copy-start | bytes 1572868
  1.0 1.0 %copy-start.3 = (bf16[2048,128]{1,0:T(8,128)(2,1)S(1)}, bf16[2048,128]{1,0:T(8,128)(2,1)}, u32[]{:S(2)}) copy-start(bf16[2048,128]{1,0:T(8,128)(2,1)} %v.1) | copy-start | bytes 1572868
  2.2 18.5 %collective-permute-start.3 = (bf16[4096,128]{1,0:T(8,128)(2,1)S(1)}, bf16[4096,128]{1,0:T(8,128)(2,1)S(1)}, u32[]{:S(2)}, u32[]{:S(2)}) collective-permute-start(bf16[4096,128]{1,0:T(8,128)(2,1)S(1)} %get-tuple-element.38.kv), channel_id=1, source_target_pairs={{0,8},{8,0},{16,24},{24,16},{32,40},{40,32},{48,56},{56,48},{64,72... | collective-permute-start | bytes 3145736 | tf_op jit(solution)/shard_map/ppermute | solution.py:28
  3.7 7.9 %collective-permute-start = (bf16[64,1024]{1,0:T(8,128)(2,1)}, bf16[64,1024]{1,0:T(8,128)(2,1)S(1)}, u32[]{:S(2)}, u32[]{:S(2)}) collective-permute-start(bf16[64,1024]{1,0:T(8,128)(2,1)} %q.3), channel_id=1, source_target_pairs={{0,16},{8,24},{16,32},{24,40},{32,48},{40,56},{48,0},{56,8},{64,80... | collective-permute-start | bytes 393224 | tf_op jit(solution)/shard_map/ppermute | solution.py:28
  5.5 13.9 %collective-permute-start.5 = (bf16[1792,128]{1,0:T(8,128)(2,1)S(1)}, bf16[1792,128]{1,0:T(8,128)(2,1)S(1)}, u32[]{:S(2)}, u32[]{:S(2)}) collective-permute-start(bf16[1792,128]{1,0:T(8,128)(2,1)S(1)} %get-tuple-element.37), channel_id=1, source_target_pairs={{0,64},{8,72},{16,80},{24,88},{32,96},{40,104},{48,112},{56,120},{... | collective-permute-start | bytes 1376264 | tf_op jit(solution)/shard_map/ppermute | solution.py:28
  8.2 11.1 %collective-permute-start.1 = (bf16[64,1024]{1,0:T(8,128)(2,1)}, bf16[64,1024]{1,0:T(8,128)(2,1)S(1)}, u32[]{:S(2)}, u32[]{:S(2)}) collective-permute-start(bf16[64,1024]{1,0:T(8,128)(2,1)} %q.3), channel_id=1, source_target_pairs={{0,48},{8,56},{16,0},{24,8},{32,16},{40,24},{48,32},{56,40},{64,11... | collective-permute-start | bytes 393224 | tf_op jit(solution)/shard_map/ppermute | solution.py:28
  10.3 9.1 %collective-permute-start.2 = (bf16[64,1024]{1,0:T(8,128)(2,1)}, bf16[64,1024]{1,0:T(8,128)(2,1)S(1)}, u32[]{:S(2)}, u32[]{:S(2)}) collective-permute-start(bf16[64,1024]{1,0:T(8,128)(2,1)} %q.3), channel_id=1, source_target_pairs={{0,32},{8,40},{16,48},{24,56},{32,0},{40,8},{48,16},{56,24},{64,96... | collective-permute-start | bytes 393224 | tf_op jit(solution)/shard_map/ppermute | solution.py:28
  11.6 20.5 %collective-permute-start.4 = (bf16[2304,128]{1,0:T(8,128)(2,1)S(1)}, bf16[2304,128]{1,0:T(8,128)(2,1)S(1)}, u32[]{:S(2)}, u32[]{:S(2)}) collective-permute-start(bf16[2304,128]{1,0:T(8,128)(2,1)S(1)} %get-tuple-element.34), channel_id=1, source_target_pairs={{0,64},{8,72},{16,80},{24,88},{32,96},{40,104},{48,112},{56,120},{... | collective-permute-start | bytes 1769480 | tf_op jit(solution)/shard_map/ppermute | solution.py:28
  15.9 0.9 copy-start.1
  19.4 9.2 %collective-permute-start.6 = (bf16[1792,128]{1,0:T(8,128)(2,1)S(1)}, bf16[1792,128]{1,0:T(8,128)(2,1)S(1)}, u32[]{:S(2)}, u32[]{:S(2)}) collective-permute-start(bf16[1792,128]{1,0:T(8,128)(2,1)S(1)} %collective-permute-done.5.refs_0_.half), channel_id=1, source_target_pairs={{0,8},{8,0},{16,24},{24,16},{32,40},{40,32},{48,56},{56,48},{64,72... | collective-permute-start | bytes 1376264 | tf_op jit(solution)/shard_map/ppermute | solution.py:28
  28.6 3.9 %copy-start = (bf16[1024,512]{1,0:T(8,128)(2,1)S(1)}, bf16[1024,512]{1,0:T(8,128)(2,1)}, u32[]{:S(2)}) copy-start(bf16[1024,512]{1,0:T(8,128)(2,1)} %wa.1) | copy-start | bytes 3145732
  32.2 3.5 %collective-permute-start.7 = (bf16[2304,128]{1,0:T(8,128)(2,1)S(1)}, bf16[2304,128]{1,0:T(8,128)(2,1)S(1)}, u32[]{:S(2)}, u32[]{:S(2)}) collective-permute-start(bf16[2304,128]{1,0:T(8,128)(2,1)S(1)} %collective-permute-done.4.half), channel_id=1, source_target_pairs={{0,8},{8,0},{16,24},{24,16},{32,40},{40,32},{48,56},{56,48},{64,72... | collective-permute-start | bytes 1769480 | tf_op jit(solution)/shard_map/ppermute | solution.py:28
  32.5 37.8 %collective-permute-start.18 = (bf16[1024,512]{1,0:T(8,128)(2,1)S(1)}, bf16[1024,512]{1,0:T(8,128)(2,1)S(1)}, u32[]{:S(2)}, u32[]{:S(2)}) collective-permute-start(bf16[1024,512]{1,0:T(8,128)(2,1)S(1)} %copy-done), channel_id=1, source_target_pairs={{0,8},{8,0},{16,24},{24,16},{32,40},{40,32},{48,56},{56,48},{64,72... | collective-permute-start | bytes 3145736 | tf_op jit(solution)/shard_map/ppermute | solution.py:28
  38.6 10.0 %collective-permute-start.8 = (bf16[144,512]{1,0:T(8,128)(2,1)S(1)}, bf16[144,512]{1,0:T(8,128)(2,1)S(1)}, u32[]{:S(2)}, u32[]{:S(2)}) collective-permute-start(bf16[144,512]{1,0:T(8,128)(2,1)S(1)} %shard_map.87), channel_id=1, source_target_pairs={{0,32},{8,40},{16,48},{24,56},{32,0},{40,8},{48,16},{56,24},{64,96... | collective-permute-start | bytes 442376 | tf_op jit(solution)/shard_map/ppermute | solution.py:28
  45.2 6.4 %collective-permute-start.10 = (bf16[144,512]{1,0:T(8,128)(2,1)S(1)}, bf16[144,512]{1,0:T(8,128)(2,1)S(1)}, u32[]{:S(2)}, u32[]{:S(2)}) collective-permute-start(bf16[144,512]{1,0:T(8,128)(2,1)S(1)} %get-tuple-element.51), channel_id=1, source_target_pairs={{0,16},{8,24},{16,32},{24,40},{32,48},{40,56},{48,0},{56,8},{64,80... | collective-permute-start | bytes 442376 | tf_op jit(solution)/shard_map/ppermute | solution.py:28
  45.3 6.3 %collective-permute-start.9 = (bf16[144,512]{1,0:T(8,128)(2,1)S(1)}, bf16[144,512]{1,0:T(8,128)(2,1)S(1)}, u32[]{:S(2)}, u32[]{:S(2)}) collective-permute-start(bf16[144,512]{1,0:T(8,128)(2,1)S(1)} %get-tuple-element.50), channel_id=1, source_target_pairs={{0,48},{8,56},{16,0},{24,8},{32,16},{40,24},{48,32},{56,40},{64,11... | collective-permute-start | bytes 442376 | tf_op jit(solution)/shard_map/ppermute | solution.py:28
  51.8 6.3 %collective-permute-start.11 = (bf16[64,1024]{1,0:T(8,128)(2,1)S(1)}, bf16[64,1024]{1,0:T(8,128)(2,1)S(1)}, u32[]{:S(2)}, u32[]{:S(2)}) collective-permute-start(bf16[64,1024]{1,0:T(8,128)(2,1)S(1)} %shard_map.90.a0), channel_id=1, source_target_pairs={{0,16},{8,24},{16,32},{24,40},{32,48},{40,56},{48,0},{56,8},{64,80... | collective-permute-start | bytes 393224 | tf_op jit(solution)/shard_map/ppermute | solution.py:28
  52.1 7.8 %collective-permute-start.12 = (bf16[64,1024]{1,0:T(8,128)(2,1)S(1)}, bf16[64,1024]{1,0:T(8,128)(2,1)S(1)}, u32[]{:S(2)}, u32[]{:S(2)}) collective-permute-start(bf16[64,1024]{1,0:T(8,128)(2,1)S(1)} %shard_map.90.a0), channel_id=1, source_target_pairs={{0,48},{8,56},{16,0},{24,8},{32,16},{40,24},{48,32},{56,40},{64,11... | collective-permute-start | bytes 393224 | tf_op jit(solution)/shard_map/ppermute | solution.py:28
  54.8 7.0 %collective-permute-start.13 = (bf16[64,1024]{1,0:T(8,128)(2,1)S(1)}, bf16[64,1024]{1,0:T(8,128)(2,1)S(1)}, u32[]{:S(2)}, u32[]{:S(2)}) collective-permute-start(bf16[64,1024]{1,0:T(8,128)(2,1)S(1)} %shard_map.90.a0), channel_id=1, source_target_pairs={{0,32},{8,40},{16,48},{24,56},{32,0},{40,8},{48,16},{56,24},{64,96... | collective-permute-start | bytes 393224 | tf_op jit(solution)/shard_map/ppermute | solution.py:28
  55.3 9.2 %collective-permute-start.14 = (bf16[64,1024]{1,0:T(8,128)(2,1)S(1)}, bf16[64,1024]{1,0:T(8,128)(2,1)S(1)}, u32[]{:S(2)}, u32[]{:S(2)}) collective-permute-start(bf16[64,1024]{1,0:T(8,128)(2,1)S(1)} %shard_map.90.a0), channel_id=1, source_target_pairs={{0,64},{8,72},{16,80},{24,88},{32,96},{40,104},{48,112},{56,120},{... | collective-permute-start | bytes 393224 | tf_op jit(solution)/shard_map/ppermute | solution.py:28
  58.1 7.0 %collective-permute-start.15 = (bf16[64,1024]{1,0:T(8,128)(2,1)S(1)}, bf16[64,1024]{1,0:T(8,128)(2,1)S(1)}, u32[]{:S(2)}, u32[]{:S(2)}) collective-permute-start(bf16[64,1024]{1,0:T(8,128)(2,1)S(1)} %collective-permute-done.11.a1), channel_id=1, source_target_pairs={{0,64},{8,72},{16,80},{24,88},{32,96},{40,104},{48,112},{56,120},{... | collective-permute-start | bytes 393224 | tf_op jit(solution)/shard_map/ppermute | solution.py:28
  59.9 7.7 %collective-permute-start.16 = (bf16[64,1024]{1,0:T(8,128)(2,1)S(1)}, bf16[64,1024]{1,0:T(8,128)(2,1)S(1)}, u32[]{:S(2)}, u32[]{:S(2)}) collective-permute-start(bf16[64,1024]{1,0:T(8,128)(2,1)S(1)} %collective-permute-done.12.a2), channel_id=1, source_target_pairs={{0,64},{8,72},{16,80},{24,88},{32,96},{40,104},{48,112},{56,120},{... | collective-permute-start | bytes 393224 | tf_op jit(solution)/shard_map/ppermute | solution.py:28
  61.8 8.6 %collective-permute-start.17 = (bf16[64,1024]{1,0:T(8,128)(2,1)S(1)}, bf16[64,1024]{1,0:T(8,128)(2,1)S(1)}, u32[]{:S(2)}, u32[]{:S(2)}) collective-permute-start(bf16[64,1024]{1,0:T(8,128)(2,1)S(1)} %collective-permute-done.13.a3), channel_id=1, source_target_pairs={{0,64},{8,72},{16,80},{24,88},{32,96},{40,104},{48,112},{56,120},{... | collective-permute-start | bytes 393224 | tf_op jit(solution)/shard_map/ppermute | solution.py:28
  89.1 4.4 %collective-permute-start.19 = (bf16[64,512]{1,0:T(8,128)(2,1)S(1)}, bf16[64,512]{1,0:T(8,128)(2,1)S(1)}, u32[]{:S(2)}, u32[]{:S(2)}) collective-permute-start(bf16[64,512]{1,0:T(8,128)(2,1)S(1)} %get-tuple-element.58), channel_id=1, source_target_pairs={{0,8},{8,0},{16,24},{24,16},{32,40},{40,32},{48,56},{56,48},{64,72... | collective-permute-start | bytes 196616 | tf_op jit(solution)/shard_map/ppermute | solution.py:28

commit v12 on v11

--- a/solution.py
+++ b/solution.py
@@ -159,11 +159,11 @@
         top_out[i], total_out[i] = top, total
 
 
-def own_kernel_2(rows, top, total, kv, half, other_half, top_out, total_out, k0, v0, k1, v1):
-    split((kv,), k0, v0)
-    split((half, other_half), k1, v1)
-    tasks = [(0, rows.at[3], k0, v0), (0, rows.at[3], k1, v1)]
-    top_out[...], total_out[...] = run(tasks, [(top[...], total[...])])[0]
+def own_more_kernel(rows, top, total, *refs):
+    *parts, top_out, total_out, k, values = refs
+    split(parts, k, values)
+    states = run([(0, rows.at[3], k, values)], [(top[...], total[...])])
+    top_out[...], total_out[...] = states[0]
 
 
 def last_kernel(rows, top, total, half, other_half, *refs, owners):
@@ -265,19 +265,24 @@
     own_top, own_total = call(own_kernel, own_state, scratch(positions))(
         queries, jnp.concatenate([question_keys, question_values]), bias, after(kv, q_z[0])
     )
-    x0 = after(x0, own_top, *q_z)
-    xc0 = moved(x0, c=1)
     top, total, rows = call(
         near_kernel, state + [((4, LANES, DH), bf16)], scratch(positions, positions), flops=1
-    )(*q_z, queries, kv, kv_c)
-    top, total = call(others_kernel, state, scratch(2 * early), flops=1)(rows, top, total, x0, xc0)
+    )(*q_z, queries, after(kv, own_top), kv_c)
+    x0, top = lax.optimization_barrier((x0, top))
+    xc0 = moved(x0, c=1)
+    own_top, own_total = call(own_more_kernel, own_state, scratch(positions), flops=block_flops)(
+        after(rows, x0), own_top, own_total, kv_c
+    )
+    top, total = call(others_kernel, state, scratch(2 * early), flops=1)(
+        rows, after(top, own_top), total, x0, xc0
+    )
 
     x1, weight, top = lax.optimization_barrier((x1, out_weight, top))
     xc1 = moved(x1, c=1)
     weight_c = moved(weight, c=1)
-    own_top, own_total = call(
-        own_kernel_2, own_state, scratch(positions, 2 * early), flops=2 * block_flops
-    )(after(rows, x1), own_top, own_total, kv_c, x0, xc0)
+    own_top, own_total = call(own_more_kernel, own_state, scratch(2 * early), flops=2 * block_flops)(
+        after(rows, x1), own_top, own_total, x0, xc0
+    )
     top = after(top, own_top)
     (p_far,) = call(functools.partial(last_kernel, owners=(2,)), [part], scratch(2 * late), flops=1)(
         rows, top, total, x1, xc1
@@ -293,8 +298,8 @@
         merge_kernel, [((ROWS, GROUP * DH), bf16)], in_specs=[smem] + [vmem] * 4
     )(live_rows, result, level, *back[:2])
 
-    held = [att] + [moved(att, z=z) for z in FAR]
-    held = held + [moved(rows, xh=1) for rows in held]
+    att_x = moved(att, xh=1)
+    held = [att] + [moved(att, z=z) for z in FAR] + [att_x] + [moved(att_x, z=z) for z in FAR]
     width = out_weight.shape[1]
     (terms,) = call(
         project_kernel,

time: 94.5 us -> 93 us (0.984)
  starting transfers between devices: 35.5 us -> 28.9 us
  waiting for transfers between devices: 7.53 us -> 10.9 us
  Pallas kernels: 27.7 us -> 29.6 us
    ppermute x20, starting transfers between devices: 35.5 us -> 28.9 us  [moved(): return lax.ppermute(array, 'blk', pairs)]
    ppermute x20, waiting for transfers between devices: 7.53 us -> 10.9 us  [moved(): return lax.ppermute(array, 'blk', pairs)]
    pallas_call x1 -> x2, Pallas kernels: 2.91 us -> 4.83 us  [the longest x1 2.55 us: shards(): call(own_more_kernel, own_state, scratch(positions), flops=block_flops)]
  transfers between devices with their start and end apart: 20 -> 20, of which waited for: 5 -> 7; matrix products, arithmetic and copies ran while one was open for 2% -> 2% of each run, Pallas kernels for 28% -> 30%
where the time goes in v12:
time: 93 us; the launch traced here: 92.7 us
  Pallas kernels  29.6 us (32%)
  starting transfers between devices  28.9 us (31%)
  blocking collectives  17.2 us (18%)
  waiting for transfers between devices  10.9 us (12%)
  local copies, waits for them, and re-layouts  2.99 us (3%)
  other arithmetic  2.22 us (2%)
    ppermute x20, starting transfers between devices, moved(): return lax.ppermute(array, 'blk', pairs)  28.9 us
    all_to_all x1, blocking collectives, shards(): gathered = lax.all_to_all(terms, 'head', 0, 0, tiled=True)  17.2 us
    ppermute x20, waiting for transfers between devices, moved(): return lax.ppermute(array, 'blk', pairs)  10.9 us
    pallas_call x1, Pallas kernels, shards(): call(near_kernel, state + [((4, LANES, DH), bf16)], scratch(positions, po...  7.93 us
    pallas_call x1, Pallas kernels, shards(): call(others_kernel, state, scratch(2 * early), flops=1)  3.5 us
    pallas_call x1, Pallas kernels, shards(): call(functools.partial(last_kernel, owners=(0, 1)), [part] * 2, scratch(2...  3.17 us
    unnamed x8, local copies, waits for them, and re-layouts  2.99 us
    pallas_call x1, Pallas kernels, shards(): call(own_last_kernel, [((DH, LANES), f32), ((8, LANES), f32)], scratch(2...  2.97 us
  transfers between devices with their start and end apart: 20, of which 7 were waited for; matrix products, arithmetic and copies ran while one was open for 2% of the time, Pallas kernels for 30%

profile of v12, /device:TPU:1, one launch (start us, length us, event | category | flops | bytes accessed | tf_op | source)
XLA Modules:
  0.0 92.7 jit_solution(9533194869717340563)
XLA Ops:
  0.0 0.0 copy-start.2
  0.0 1.0 %copy-done.2 = bf16[2048,128]{1,0:T(8,128)(2,1)S(1)} copy-done((bf16[2048,128]{1,0:T(8,128)(2,1)S(1)}, bf16[2048,128]{1,0:T(8,128)(2,1)}, u32[]{:S(2)}) %copy-start.2) | copy-done | bytes 524312
  1.0 0.0 copy-start.3
  1.0 1.0 %copy-done.3 = bf16[2048,128]{1,0:T(8,128)(2,1)S(1)} copy-done((bf16[2048,128]{1,0:T(8,128)(2,1)S(1)}, bf16[2048,128]{1,0:T(8,128)(2,1)}, u32[]{:S(2)}) %copy-start.3) | copy-done | bytes 524312
  2.1 0.1 shard_map.82
  2.2 1.5 %collective-permute-start.3 = (bf16[4096,128]{1,0:T(8,128)(2,1)S(1)}, bf16[4096,128]{1,0:T(8,128)(2,1)S(1)}, u32[]{:S(2)}, u32[]{:S(2)}) collective-permute-start(bf16[4096,128]{1,0:T(8,128)(2,1)S(1)} %get-tuple-element.41.kv), channel_id=1, source_target_pairs={{0,8},{8,0},{16,24},{24,16},{32,40},{40,32},{48,56},{56,48},{64,72... | collective-permute-start | bytes 3145736 | tf_op jit(solution)/shard_map/ppermute | solution.py:28
  3.7 1.7 %collective-permute-start = (bf16[64,1024]{1,0:T(8,128)(2,1)}, bf16[64,1024]{1,0:T(8,128)(2,1)S(1)}, u32[]{:S(2)}, u32[]{:S(2)}) collective-permute-start(bf16[64,1024]{1,0:T(8,128)(2,1)} %q.3), channel_id=1, source_target_pairs={{0,16},{8,24},{16,32},{24,40},{32,48},{40,56},{48,0},{56,8},{64,80... | collective-permute-start | bytes 393224 | tf_op jit(solution)/shard_map/ppermute | solution.py:28
  5.5 2.7 %collective-permute-start.5 = (bf16[1792,128]{1,0:T(8,128)(2,1)S(1)}, bf16[1792,128]{1,0:T(8,128)(2,1)S(1)}, u32[]{:S(2)}, u32[]{:S(2)}) collective-permute-start(bf16[1792,128]{1,0:T(8,128)(2,1)S(1)} %get-tuple-element.44), channel_id=1, source_target_pairs={{0,64},{8,72},{16,80},{24,88},{32,96},{40,104},{48,112},{56,120},{... | collective-permute-start | bytes 1376264 | tf_op jit(solution)/shard_map/ppermute | solution.py:28
  8.2 2.1 %collective-permute-start.1 = (bf16[64,1024]{1,0:T(8,128)(2,1)}, bf16[64,1024]{1,0:T(8,128)(2,1)S(1)}, u32[]{:S(2)}, u32[]{:S(2)}) collective-permute-start(bf16[64,1024]{1,0:T(8,128)(2,1)} %q.3), channel_id=1, source_target_pairs={{0,48},{8,56},{16,0},{24,8},{32,16},{40,24},{48,32},{56,40},{64,11... | collective-permute-start | bytes 393224 | tf_op jit(solution)/shard_map/ppermute | solution.py:28
  10.3 1.3 %collective-permute-start.2 = (bf16[64,1024]{1,0:T(8,128)(2,1)}, bf16[64,1024]{1,0:T(8,128)(2,1)S(1)}, u32[]{:S(2)}, u32[]{:S(2)}) collective-permute-start(bf16[64,1024]{1,0:T(8,128)(2,1)} %q.3), channel_id=1, source_target_pairs={{0,32},{8,40},{16,48},{24,56},{32,0},{40,8},{48,16},{56,24},{64,96... | collective-permute-start | bytes 393224 | tf_op jit(solution)/shard_map/ppermute | solution.py:28
  11.6 0.0 collective-permute-done.q0
  11.6 2.7 %collective-permute-start.4 = (bf16[2304,128]{1,0:T(8,128)(2,1)S(1)}, bf16[2304,128]{1,0:T(8,128)(2,1)S(1)}, u32[]{:S(2)}, u32[]{:S(2)}) collective-permute-start(bf16[2304,128]{1,0:T(8,128)(2,1)S(1)} %get-tuple-element.43), channel_id=1, source_target_pairs={{0,64},{8,72},{16,80},{24,88},{32,96},{40,104},{48,112},{56,120},{... | collective-permute-start | bytes 1769480 | tf_op jit(solution)/shard_map/ppermute | solution.py:28
  14.3 0.8 fusion.1.bias
  15.1 0.7 pad_maximum_fusion.qkv
  15.9 0.0 copy-start.1
  15.9 0.9 copy-done.1
  16.8 2.6 %shard_map.83 = (f32[512,128]{1,0:T(8,128)S(1)}, f32[512,256]{1,0:T(8,128)S(1)}) custom-call(bf16[64,1024]{1,0:T(8,128)(2,1)S(1)} %copy-done.1, bf16[128,128]{1,0:T(8,128)(2,1)S(1)} %pad_maximum_fusion.qkv, f32[64,64]{1,0:T(8,128)S(1)} %fusion.1.bias, bf16[4096,128]{1,0:T(8,128)(2,1)S(1)} %get-tuple-element.41.kv), custom_call_target="tpu_custom_call" | custom-call | tf_op jit(solution)/shard_map/pallas_call | solution.py:265
  19.4 0.0 collective-permute-done.1.q1
  19.4 0.0 collective-permute-done.2.q2
  19.4 0.0 collective-permute-done.3.kv_c.refs_0_
  19.4 7.9 %shard_map.84 = (f32[3,512,128]{2,1,0:T(8,128)S(1)}, f32[3,512,256]{2,1,0:T(8,128)S(1)}, bf16[4,512,128]{2,1,0:T(8,128)(2,1)S(1)}) custom-call(bf16[64,1024]{1,0:T(8,128)(2,1)S(1)} %collective-permute-done.q0, bf16[64,1024]{1,0:T(8,128)(2,1)S(1)} %collective-permute-done.1.q1, bf16[64,1024]{1,0:T(8,128)(2,1)S(1)} %collective-permute-done.2.q2, ...), custom_call_target="tpu_custom_call" | custom-call | flops 1 | tf_op jit(solution)/shard_map/pallas_call | solution.py:268
  27.3 0.0 collective-permute-done.5.refs_0_
  27.3 1.2 %collective-permute-start.6 = (bf16[1792,128]{1,0:T(8,128)(2,1)S(1)}, bf16[1792,128]{1,0:T(8,128)(2,1)S(1)}, u32[]{:S(2)}, u32[]{:S(2)}) collective-permute-start(bf16[1792,128]{1,0:T(8,128)(2,1)S(1)} %collective-permute-done.5.refs_0_), channel_id=1, source_target_pairs={{0,8},{8,0},{16,24},{24,16},{32,40},{40,32},{48,56},{56,48},{64,72... | collective-permute-start | bytes 1376264 | tf_op jit(solution)/shard_map/ppermute | solution.py:28
  28.5 2.6 %shard_map.85 = (f32[512,128]{1,0:T(8,128)S(1)}, f32[512,256]{1,0:T(8,128)S(1)}) custom-call(bf16[4,512,128]{2,1,0:T(8,128)(2,1)S(1)} %get-tuple-element.64.rows, f32[512,128]{1,0:T(8,128)S(1)} %get-tuple-element.40.top, f32[512,256]{1,0:T(8,128)S(1)} %get-tuple-element.49.total, bf16[4096,128]{1,0:T(8,128)(2,1)S(1)} %collective-permute-done.3.kv_c.refs_0_), custom_call_target="tpu_custom_call" | custom-call | flops 1073741824 | tf_op jit(solution)/shard_map/pallas_call | solution.py:273
  31.1 0.0 collective-permute-done.6.refs_1_
  31.1 0.0 copy-start
  31.1 3.5 %shard_map.86 = (f32[3,512,128]{2,1,0:T(8,128)S(1)}, f32[3,512,256]{2,1,0:T(8,128)S(1)}) custom-call(bf16[4,512,128]{2,1,0:T(8,128)(2,1)S(1)} %get-tuple-element.64.rows, f32[3,512,128]{2,1,0:T(8,128)S(1)} %get-tuple-element.51.top_in, f32[3,512,256]{2,1,0:T(8,128)S(1)} %get-tuple-element.52.total_in, bf16[1792,128]{1,0:T(8,128)(2,1)S(1)} %collective-permute-done.5.refs_0_, ...), custom_call_target="tpu_custom_call" | custom-call | flops 1 | tf_op jit(solution)/shard_map/pallas_call | solution.py:276
  34.6 0.0 collective-permute-done.4.half
  34.6 0.1 collective-permute-start.7
  34.7 0.0 copy-done
  34.7 0.5 collective-permute-start.18
  35.2 2.3 %shard_map.87 = (f32[512,128]{1,0:T(8,128)S(1)}, f32[512,256]{1,0:T(8,128)S(1)}) custom-call(bf16[4,512,128]{2,1,0:T(8,128)(2,1)S(1)} %get-tuple-element.64.rows, f32[512,128]{1,0:T(8,128)S(1)} %get-tuple-element.50.top, f32[512,256]{1,0:T(8,128)S(1)} %get-tuple-element.57.total, bf16[1792,128]{1,0:T(8,128)(2,1)S(1)} %collective-permute-done.5.refs_0_, ...), custom_call_target="tpu_custom_call" | custom-call | flops 2147483648 | tf_op jit(solution)/shard_map/pallas_call | solution.py:283
  37.5 0.0 collective-permute-done.7.other_half
  37.5 2.9 %shard_map.88 = bf16[144,512]{1,0:T(8,128)(2,1)S(1)} custom-call(bf16[4,512,128]{2,1,0:T(8,128)(2,1)S(1)} %get-tuple-element.64.rows, f32[3,512,128]{2,1,0:T(8,128)S(1)} %get-tuple-element.61.top, f32[3,512,256]{2,1,0:T(8,128)S(1)} %get-tuple-element.60.total, bf16[2304,128]{1,0:T(8,128)(2,1)S(1)} %collective-permute-done.4.half, ...), custom_call_target="tpu_custom_call" | custom-call | flops 1 | tf_op jit(solution)/shard_map/pallas_call | solution.py:287
  40.5 1.6 %collective-permute-start.8 = (bf16[144,512]{1,0:T(8,128)(2,1)S(1)}, bf16[144,512]{1,0:T(8,128)(2,1)S(1)}, u32[]{:S(2)}, u32[]{:S(2)}) collective-permute-start(bf16[144,512]{1,0:T(8,128)(2,1)S(1)} %shard_map.88), channel_id=1, source_target_pairs={{0,32},{8,40},{16,48},{24,56},{32,0},{40,8},{48,16},{56,24},{64,96... | collective-permute-start | bytes 442376 | tf_op jit(solution)/shard_map/ppermute | solution.py:28
  42.1 3.2 %shard_map.89 = (bf16[144,512]{1,0:T(8,128)(2,1)S(1)}, bf16[144,512]{1,0:T(8,128)(2,1)S(1)}) custom-call(bf16[4,512,128]{2,1,0:T(8,128)(2,1)S(1)} %get-tuple-element.64.rows, f32[3,512,128]{2,1,0:T(8,128)S(1)} %get-tuple-element.61.top, f32[3,512,256]{2,1,0:T(8,128)S(1)} %get-tuple-element.60.total, bf16[2304,128]{1,0:T(8,128)(2,1)S(1)} %collective-permute-done.4.half, ...), custom_call_target="tpu_custom_call" | custom-call | flops 4294967296 | tf_op jit(solution)/shard_map/pallas_call | solution.py:290
  45.3 1.3 %collective-permute-start.10 = (bf16[144,512]{1,0:T(8,128)(2,1)S(1)}, bf16[144,512]{1,0:T(8,128)(2,1)S(1)}, u32[]{:S(2)}, u32[]{:S(2)}) collective-permute-start(bf16[144,512]{1,0:T(8,128)(2,1)S(1)} %get-tuple-element.63), channel_id=1, source_target_pairs={{0,16},{8,24},{16,32},{24,40},{32,48},{40,56},{48,0},{56,8},{64,80... | collective-permute-start | bytes 442376 | tf_op jit(solution)/shard_map/ppermute | solution.py:28
  46.5 1.5 %collective-permute-start.9 = (bf16[144,512]{1,0:T(8,128)(2,1)S(1)}, bf16[144,512]{1,0:T(8,128)(2,1)S(1)}, u32[]{:S(2)}, u32[]{:S(2)}) collective-permute-start(bf16[144,512]{1,0:T(8,128)(2,1)S(1)} %get-tuple-element.62), channel_id=1, source_target_pairs={{0,48},{8,56},{16,0},{24,8},{32,16},{40,24},{48,32},{56,40},{64,11... | collective-permute-start | bytes 442376 | tf_op jit(solution)/shard_map/ppermute | solution.py:28
  48.7 0.0 collective-permute-done.8.r2
  48.7 3.0 %shard_map.90 = (f32[128,512]{1,0:T(8,128)S(1)}, f32[8,512]{1,0:T(8,128)S(1)}) custom-call(bf16[4,512,128]{2,1,0:T(8,128)(2,1)S(1)} %get-tuple-element.64.rows, f32[512,128]{1,0:T(8,128)S(1)} %get-tuple-element.58.top, f32[512,256]{1,0:T(8,128)S(1)} %get-tuple-element.65.total, bf16[2304,128]{1,0:T(8,128)(2,1)S(1)} %collective-permute-done.4.half, ...), custom_call_target="tpu_custom_call" | custom-call | flops 1 | tf_op jit(solution)/shard_map/pallas_call | solution.py:294
  51.7 0.0 collective-permute-done.10.r1
  51.7 0.0 collective-permute-done.9.r0
  51.7 0.2 shard_map.91.a0
  51.9 2.1 %collective-permute-start.14 = (bf16[64,1024]{1,0:T(8,128)(2,1)S(1)}, bf16[64,1024]{1,0:T(8,128)(2,1)S(1)}, u32[]{:S(2)}, u32[]{:S(2)}) collective-permute-start(bf16[64,1024]{1,0:T(8,128)(2,1)S(1)} %shard_map.91.a0), channel_id=1, source_target_pairs={{0,64},{8,72},{16,80},{24,88},{32,96},{40,104},{48,112},{56,120},{... | collective-permute-start | bytes 393224 | tf_op jit(solution)/shard_map/ppermute | solution.py:28
  54.0 0.0 collective-permute-start.11
  54.0 2.7 %collective-permute-start.12 = (bf16[64,1024]{1,0:T(8,128)(2,1)S(1)}, bf16[64,1024]{1,0:T(8,128)(2,1)S(1)}, u32[]{:S(2)}, u32[]{:S(2)}) collective-permute-start(bf16[64,1024]{1,0:T(8,128)(2,1)S(1)} %shard_map.91.a0), channel_id=1, source_target_pairs={{0,48},{8,56},{16,0},{24,8},{32,16},{40,24},{48,32},{56,40},{64,11... | collective-permute-start | bytes 393224 | tf_op jit(solution)/shard_map/ppermute | solution.py:28
  56.7 0.0 collective-permute-start.13
  56.7 0.6 collective-permute-done.14.a4
  57.3 0.3 collective-permute-start.15
  57.6 1.6 %collective-permute-done.11.a1 = bf16[64,1024]{1,0:T(8,128)(2,1)S(1)} collective-permute-done((bf16[64,1024]{1,0:T(8,128)(2,1)S(1)}, bf16[64,1024]{1,0:T(8,128)(2,1)S(1)}, u32[]{:S(2)}, u32[]{:S(2)}) %collective-permute-start.11) | collective-permute-done | bytes 131104 | tf_op jit(solution)/shard_map/ppermute | solution.py:28
  59.2 0.8 collective-permute-start.16
  60.0 0.0 collective-permute-done.12.a2
  60.0 1.2 %collective-permute-start.17 = (bf16[64,1024]{1,0:T(8,128)(2,1)S(1)}, bf16[64,1024]{1,0:T(8,128)(2,1)S(1)}, u32[]{:S(2)}, u32[]{:S(2)}) collective-permute-start(bf16[64,1024]{1,0:T(8,128)(2,1)S(1)} %collective-permute-done.14.a4), channel_id=1, source_target_pairs={{0,32},{8,40},{16,48},{24,56},{32,0},{40,8},{48,16},{56,24},{64,96... | collective-permute-start | bytes 393224 | tf_op jit(solution)/shard_map/ppermute | solution.py:28
  61.1 2.2 %collective-permute-done.13.a3 = bf16[64,1024]{1,0:T(8,128)(2,1)S(1)} collective-permute-done((bf16[64,1024]{1,0:T(8,128)(2,1)S(1)}, bf16[64,1024]{1,0:T(8,128)(2,1)S(1)}, u32[]{:S(2)}, u32[]{:S(2)}) %collective-permute-start.13) | collective-permute-done | bytes 131104 | tf_op jit(solution)/shard_map/ppermute | solution.py:28
  63.3 1.6 %collective-permute-done.15.a5 = bf16[64,1024]{1,0:T(8,128)(2,1)S(1)} collective-permute-done((bf16[64,1024]{1,0:T(8,128)(2,1)S(1)}, bf16[64,1024]{1,0:T(8,128)(2,1)S(1)}, u32[]{:S(2)}, u32[]{:S(2)}) %collective-permute-start.15) | collective-permute-done | bytes 131104 | tf_op jit(solution)/shard_map/ppermute | solution.py:28
  65.0 0.7 collective-permute-done.16.a6
  65.7 3.2 %collective-permute-done.17.a7 = bf16[64,1024]{1,0:T(8,128)(2,1)S(1)} collective-permute-done((bf16[64,1024]{1,0:T(8,128)(2,1)S(1)}, bf16[64,1024]{1,0:T(8,128)(2,1)S(1)}, u32[]{:S(2)}, u32[]{:S(2)}) %collective-permute-start.17) | collective-permute-done | bytes 131104 | tf_op jit(solution)/shard_map/ppermute | solution.py:28
  68.9 0.0 collective-permute-done.18.wb
  68.9 1.2 %shard_map.92 = bf16[8,64,1024]{2,1,0:T(8,128)(2,1)S(1)} custom-call(s32[1]{0:T(128)} %bitcast.index, bf16[64,1024]{1,0:T(8,128)(2,1)S(1)} %shard_map.91.a0, bf16[64,1024]{1,0:T(8,128)(2,1)S(1)} %collective-permute-done.11.a1, bf16[64,1024]{1,0:T(8,128)(2,1)S(1)} %collective-permute-done.12.a2, bf16[64,1024]{1,0:T(8,128)(2,1)S(1)} %collective-permute-done.13.a3, ...), custom_call_target="tpu_custom_call" | custom-call | tf_op jit(solution)/shard_map/pallas_call | solution.py:304
  70.2 17.2 %all_to_all.5.terms = bf16[8,64,1024]{2,1,0:T(8,128)(2,1)S(1)} all-to-all(bf16[8,64,1024]{2,1,0:T(8,128)(2,1)S(1)} %shard_map.92), channel_id=1, replica_groups=mesh['blk'=16,'head'=8] {'head'}, dimensions={0} | all-to-all | bytes 2097152 | tf_op jit(solution)/shard_map/all_to_all | solution.py:310
  87.4 0.1 shard_map.93
  87.5 3.6 %collective-permute-start.19 = (bf16[64,512]{1,0:T(8,128)(2,1)S(1)}, bf16[64,512]{1,0:T(8,128)(2,1)S(1)}, u32[]{:S(2)}, u32[]{:S(2)}) collective-permute-start(bf16[64,512]{1,0:T(8,128)(2,1)S(1)} %get-tuple-element.70), channel_id=1, source_target_pairs={{0,8},{8,0},{16,24},{24,16},{32,40},{40,32},{48,56},{56,48},{64,72... | collective-permute-start | bytes 196616 | tf_op jit(solution)/shard_map/ppermute | solution.py:28
  91.1 0.9 collective-permute-done.19
  92.0 0.7 maximum_select_fusion
Async XLA Ops:
  0.0 1.0 %copy-start.2 = (bf16[2048,128]{1,0:T(8,128)(2,1)S(1)}, bf16[2048,128]{1,0:T(8,128)(2,1)}, u32[]{:S(2)}) copy-start(bf16[2048,128]{1,0:T(8,128)(2,1)} %k.1) | copy-start | bytes 1572868
  1.0 1.0 %copy-start.3 = (bf16[2048,128]{1,0:T(8,128)(2,1)S(1)}, bf16[2048,128]{1,0:T(8,128)(2,1)}, u32[]{:S(2)}) copy-start(bf16[2048,128]{1,0:T(8,128)(2,1)} %v.1) | copy-start | bytes 1572868
  2.2 17.2 %collective-permute-start.3 = (bf16[4096,128]{1,0:T(8,128)(2,1)S(1)}, bf16[4096,128]{1,0:T(8,128)(2,1)S(1)}, u32[]{:S(2)}, u32[]{:S(2)}) collective-permute-start(bf16[4096,128]{1,0:T(8,128)(2,1)S(1)} %get-tuple-element.41.kv), channel_id=1, source_target_pairs={{0,8},{8,0},{16,24},{24,16},{32,40},{40,32},{48,56},{56,48},{64,72... | collective-permute-start | bytes 3145736 | tf_op jit(solution)/shard_map/ppermute | solution.py:28
  3.7 7.9 %collective-permute-start = (bf16[64,1024]{1,0:T(8,128)(2,1)}, bf16[64,1024]{1,0:T(8,128)(2,1)S(1)}, u32[]{:S(2)}, u32[]{:S(2)}) collective-permute-start(bf16[64,1024]{1,0:T(8,128)(2,1)} %q.3), channel_id=1, source_target_pairs={{0,16},{8,24},{16,32},{24,40},{32,48},{40,56},{48,0},{56,8},{64,80... | collective-permute-start | bytes 393224 | tf_op jit(solution)/shard_map/ppermute | solution.py:28
  5.5 21.9 %collective-permute-start.5 = (bf16[1792,128]{1,0:T(8,128)(2,1)S(1)}, bf16[1792,128]{1,0:T(8,128)(2,1)S(1)}, u32[]{:S(2)}, u32[]{:S(2)}) collective-permute-start(bf16[1792,128]{1,0:T(8,128)(2,1)S(1)} %get-tuple-element.44), channel_id=1, source_target_pairs={{0,64},{8,72},{16,80},{24,88},{32,96},{40,104},{48,112},{56,120},{... | collective-permute-start | bytes 1376264 | tf_op jit(solution)/shard_map/ppermute | solution.py:28
  8.2 11.1 %collective-permute-start.1 = (bf16[64,1024]{1,0:T(8,128)(2,1)}, bf16[64,1024]{1,0:T(8,128)(2,1)S(1)}, u32[]{:S(2)}, u32[]{:S(2)}) collective-permute-start(bf16[64,1024]{1,0:T(8,128)(2,1)} %q.3), channel_id=1, source_target_pairs={{0,48},{8,56},{16,0},{24,8},{32,16},{40,24},{48,32},{56,40},{64,11... | collective-permute-start | bytes 393224 | tf_op jit(solution)/shard_map/ppermute | solution.py:28
  10.3 9.1 %collective-permute-start.2 = (bf16[64,1024]{1,0:T(8,128)(2,1)}, bf16[64,1024]{1,0:T(8,128)(2,1)S(1)}, u32[]{:S(2)}, u32[]{:S(2)}) collective-permute-start(bf16[64,1024]{1,0:T(8,128)(2,1)} %q.3), channel_id=1, source_target_pairs={{0,32},{8,40},{16,48},{24,56},{32,0},{40,8},{48,16},{56,24},{64,96... | collective-permute-start | bytes 393224 | tf_op jit(solution)/shard_map/ppermute | solution.py:28
  11.6 23.0 %collective-permute-start.4 = (bf16[2304,128]{1,0:T(8,128)(2,1)S(1)}, bf16[2304,128]{1,0:T(8,128)(2,1)S(1)}, u32[]{:S(2)}, u32[]{:S(2)}) collective-permute-start(bf16[2304,128]{1,0:T(8,128)(2,1)S(1)} %get-tuple-element.43), channel_id=1, source_target_pairs={{0,64},{8,72},{16,80},{24,88},{32,96},{40,104},{48,112},{56,120},{... | collective-permute-start | bytes 1769480 | tf_op jit(solution)/shard_map/ppermute | solution.py:28
  15.9 0.9 copy-start.1
  27.3 3.8 %collective-permute-start.6 = (bf16[1792,128]{1,0:T(8,128)(2,1)S(1)}, bf16[1792,128]{1,0:T(8,128)(2,1)S(1)}, u32[]{:S(2)}, u32[]{:S(2)}) collective-permute-start(bf16[1792,128]{1,0:T(8,128)(2,1)S(1)} %collective-permute-done.5.refs_0_), channel_id=1, source_target_pairs={{0,8},{8,0},{16,24},{24,16},{32,40},{40,32},{48,56},{56,48},{64,72... | collective-permute-start | bytes 1376264 | tf_op jit(solution)/shard_map/ppermute | solution.py:28
  31.1 3.6 %copy-start = (bf16[1024,512]{1,0:T(8,128)(2,1)S(1)}, bf16[1024,512]{1,0:T(8,128)(2,1)}, u32[]{:S(2)}) copy-start(bf16[1024,512]{1,0:T(8,128)(2,1)} %wa.1) | copy-start | bytes 3145732
  34.6 2.9 %collective-permute-start.7 = (bf16[2304,128]{1,0:T(8,128)(2,1)S(1)}, bf16[2304,128]{1,0:T(8,128)(2,1)S(1)}, u32[]{:S(2)}, u32[]{:S(2)}) collective-permute-start(bf16[2304,128]{1,0:T(8,128)(2,1)S(1)} %collective-permute-done.4.half), channel_id=1, source_target_pairs={{0,8},{8,0},{16,24},{24,16},{32,40},{40,32},{48,56},{56,48},{64,72... | collective-permute-start | bytes 1769480 | tf_op jit(solution)/shard_map/ppermute | solution.py:28
  34.7 34.2 %collective-permute-start.18 = (bf16[1024,512]{1,0:T(8,128)(2,1)S(1)}, bf16[1024,512]{1,0:T(8,128)(2,1)S(1)}, u32[]{:S(2)}, u32[]{:S(2)}) collective-permute-start(bf16[1024,512]{1,0:T(8,128)(2,1)S(1)} %copy-done), channel_id=1, source_target_pairs={{0,8},{8,0},{16,24},{24,16},{32,40},{40,32},{48,56},{56,48},{64,72... | collective-permute-start | bytes 3145736 | tf_op jit(solution)/shard_map/ppermute | solution.py:28
  40.5 8.2 %collective-permute-start.8 = (bf16[144,512]{1,0:T(8,128)(2,1)S(1)}, bf16[144,512]{1,0:T(8,128)(2,1)S(1)}, u32[]{:S(2)}, u32[]{:S(2)}) collective-permute-start(bf16[144,512]{1,0:T(8,128)(2,1)S(1)} %shard_map.88), channel_id=1, source_target_pairs={{0,32},{8,40},{16,48},{24,56},{32,0},{40,8},{48,16},{56,24},{64,96... | collective-permute-start | bytes 442376 | tf_op jit(solution)/shard_map/ppermute | solution.py:28
  45.3 6.4 %collective-permute-start.10 = (bf16[144,512]{1,0:T(8,128)(2,1)S(1)}, bf16[144,512]{1,0:T(8,128)(2,1)S(1)}, u32[]{:S(2)}, u32[]{:S(2)}) collective-permute-start(bf16[144,512]{1,0:T(8,128)(2,1)S(1)} %get-tuple-element.63), channel_id=1, source_target_pairs={{0,16},{8,24},{16,32},{24,40},{32,48},{40,56},{48,0},{56,8},{64,80... | collective-permute-start | bytes 442376 | tf_op jit(solution)/shard_map/ppermute | solution.py:28
  46.5 5.1 %collective-permute-start.9 = (bf16[144,512]{1,0:T(8,128)(2,1)S(1)}, bf16[144,512]{1,0:T(8,128)(2,1)S(1)}, u32[]{:S(2)}, u32[]{:S(2)}) collective-permute-start(bf16[144,512]{1,0:T(8,128)(2,1)S(1)} %get-tuple-element.62), channel_id=1, source_target_pairs={{0,48},{8,56},{16,0},{24,8},{32,16},{40,24},{48,32},{56,40},{64,11... | collective-permute-start | bytes 442376 | tf_op jit(solution)/shard_map/ppermute | solution.py:28
  51.9 5.4 %collective-permute-start.14 = (bf16[64,1024]{1,0:T(8,128)(2,1)S(1)}, bf16[64,1024]{1,0:T(8,128)(2,1)S(1)}, u32[]{:S(2)}, u32[]{:S(2)}) collective-permute-start(bf16[64,1024]{1,0:T(8,128)(2,1)S(1)} %shard_map.91.a0), channel_id=1, source_target_pairs={{0,64},{8,72},{16,80},{24,88},{32,96},{40,104},{48,112},{56,120},{... | collective-permute-start | bytes 393224 | tf_op jit(solution)/shard_map/ppermute | solution.py:28
  54.0 5.2 %collective-permute-start.11 = (bf16[64,1024]{1,0:T(8,128)(2,1)S(1)}, bf16[64,1024]{1,0:T(8,128)(2,1)S(1)}, u32[]{:S(2)}, u32[]{:S(2)}) collective-permute-start(bf16[64,1024]{1,0:T(8,128)(2,1)S(1)} %shard_map.91.a0), channel_id=1, source_target_pairs={{0,16},{8,24},{16,32},{24,40},{32,48},{40,56},{48,0},{56,8},{64,80... | collective-permute-start | bytes 393224 | tf_op jit(solution)/shard_map/ppermute | solution.py:28
  54.0 6.0 %collective-permute-start.12 = (bf16[64,1024]{1,0:T(8,128)(2,1)S(1)}, bf16[64,1024]{1,0:T(8,128)(2,1)S(1)}, u32[]{:S(2)}, u32[]{:S(2)}) collective-permute-start(bf16[64,1024]{1,0:T(8,128)(2,1)S(1)} %shard_map.91.a0), channel_id=1, source_target_pairs={{0,48},{8,56},{16,0},{24,8},{32,16},{40,24},{48,32},{56,40},{64,11... | collective-permute-start | bytes 393224 | tf_op jit(solution)/shard_map/ppermute | solution.py:28
  56.7 6.6 %collective-permute-start.13 = (bf16[64,1024]{1,0:T(8,128)(2,1)S(1)}, bf16[64,1024]{1,0:T(8,128)(2,1)S(1)}, u32[]{:S(2)}, u32[]{:S(2)}) collective-permute-start(bf16[64,1024]{1,0:T(8,128)(2,1)S(1)} %shard_map.91.a0), channel_id=1, source_target_pairs={{0,32},{8,40},{16,48},{24,56},{32,0},{40,8},{48,16},{56,24},{64,96... | collective-permute-start | bytes 393224 | tf_op jit(solution)/shard_map/ppermute | solution.py:28
  57.3 7.7 %collective-permute-start.15 = (bf16[64,1024]{1,0:T(8,128)(2,1)S(1)}, bf16[64,1024]{1,0:T(8,128)(2,1)S(1)}, u32[]{:S(2)}, u32[]{:S(2)}) collective-permute-start(bf16[64,1024]{1,0:T(8,128)(2,1)S(1)} %collective-permute-done.14.a4), channel_id=1, source_target_pairs={{0,16},{8,24},{16,32},{24,40},{32,48},{40,56},{48,0},{56,8},{64,80... | collective-permute-start | bytes 393224 | tf_op jit(solution)/shard_map/ppermute | solution.py:28
  59.2 6.5 %collective-permute-start.16 = (bf16[64,1024]{1,0:T(8,128)(2,1)S(1)}, bf16[64,1024]{1,0:T(8,128)(2,1)S(1)}, u32[]{:S(2)}, u32[]{:S(2)}) collective-permute-start(bf16[64,1024]{1,0:T(8,128)(2,1)S(1)} %collective-permute-done.14.a4), channel_id=1, source_target_pairs={{0,48},{8,56},{16,0},{24,8},{32,16},{40,24},{48,32},{56,40},{64,11... | collective-permute-start | bytes 393224 | tf_op jit(solution)/shard_map/ppermute | solution.py:28
  60.0 9.0 %collective-permute-start.17 = (bf16[64,1024]{1,0:T(8,128)(2,1)S(1)}, bf16[64,1024]{1,0:T(8,128)(2,1)S(1)}, u32[]{:S(2)}, u32[]{:S(2)}) collective-permute-start(bf16[64,1024]{1,0:T(8,128)(2,1)S(1)} %collective-permute-done.14.a4), channel_id=1, source_target_pairs={{0,32},{8,40},{16,48},{24,56},{32,0},{40,8},{48,16},{56,24},{64,96... | collective-permute-start | bytes 393224 | tf_op jit(solution)/shard_map/ppermute | solution.py:28
  87.5 4.5 %collective-permute-start.19 = (bf16[64,512]{1,0:T(8,128)(2,1)S(1)}, bf16[64,512]{1,0:T(8,128)(2,1)S(1)}, u32[]{:S(2)}, u32[]{:S(2)}) collective-permute-start(bf16[64,512]{1,0:T(8,128)(2,1)S(1)} %get-tuple-element.70), channel_id=1, source_target_pairs={{0,8},{8,0},{16,24},{24,16},{32,40},{40,32},{48,56},{56,48},{64,72... | collective-permute-start | bytes 196616 | tf_op jit(solution)/shard_map/ppermute | solution.py:28

commit v13 on v12

--- a/solution.py
+++ b/solution.py
@@ -127,8 +127,8 @@
     )
 
 
-def own_kernel(q, qkv, bias, kv, top_out, total_out, k, values):
-    split((kv,), k, values)
+def own_kernel(q, qkv, bias, kv, top_out, total_out, k, v):
+    split((kv,), k, v)
     rows = stacked(q)
     scores = scores_of(rows, qkv[:ROWS, :]) + jnp.concatenate([bias[...]] * GROUP, axis=0)
     block = scores_of(rows, k[...])
@@ -137,11 +137,10 @@
         scores,
         jnp.concatenate([qkv[ROWS:, :], jnp.ones((ROWS, DH), jnp.bfloat16)], axis=1),
     )
-    top_out[...], total_out[...] = add_block(top, total, block, values[...])
-
-
-def near_kernel(q0, q1, q2, q, kv, kv_c, top_out, total_out, rows, k0, v0, k1, v1):
-    split((kv,), k0, v0)
+    top_out[...], total_out[...] = add_block(top, total, block, v[...])
+
+
+def near_kernel(q0, q1, q2, q, k0, v0, kv_c, top_out, total_out, rows, k1, v1):
     split((kv_c,), k1, v1)
     for i, ref in enumerate((q0, q1, q2, q)):
         rows[i] = stacked(ref)
@@ -150,34 +149,34 @@
         top_out[i], total_out[i] = top, total
 
 
-def others_kernel(rows, top_in, total_in, *refs):
-    *parts, top_out, total_out, k, values = refs
-    split(parts, k, values)
+def others_kernel(rows, top_in, total_in, part, other_part, top_out, total_out, k, v):
+    split((part, other_part), k, v)
     states = [(top_in[i], total_in[i]) for i in range(3)]
-    states = run([(i, rows.at[i], k, values) for i in range(3)], states)
+    states = run([(i, rows.at[i], k, v) for i in range(3)], states)
     for i, (top, total) in enumerate(states):
         top_out[i], total_out[i] = top, total
 
 
-def own_more_kernel(rows, top, total, *refs):
-    *parts, top_out, total_out, k, values = refs
-    split(parts, k, values)
-    states = run([(0, rows.at[3], k, values)], [(top[...], total[...])])
+def own_more_kernel(rows, top, total, k, v, top_out, total_out):
+    states = run([(0, rows.at[3], k, v)], [(top[...], total[...])])
     top_out[...], total_out[...] = states[0]
 
 
-def last_kernel(rows, top, total, half, other_half, *refs, owners):
-    *outs, k, values = refs
-    split((half, other_half), k, values)
-    tasks = [(i, rows.at[owner], k, values) for i, owner in enumerate(owners)]
-    states = run(tasks, [(top[owner], total[owner]) for owner in owners])
+def far_kernel(rows, top, total, part, other_part, out, k, v):
+    split((part, other_part), k, v)
+    states = run([(0, rows.at[2], k, v)], [(top[2], total[2])])
+    out[...] = packed(*finish(*states[0]))
+
+
+def next_kernel(rows, top, total, k, v, *outs):
+    states = [(top[i], total[i]) for i in range(2)]
+    states = run([(i, rows.at[i], k, v) for i in range(2)], states)
     for state, out in zip(states, outs):
         out[...] = packed(*finish(*state))
 
 
-def own_last_kernel(rows, top, total, half, other_half, r2, result_ref, level_ref, k, values):
-    split((half, other_half), k, values)
-    states = run([(0, rows.at[3], k, values)], [(top[...], total[...])])
+def own_last_kernel(rows, top, total, k, v, r2, result_ref, level_ref):
+    states = run([(0, rows.at[3], k, v)], [(top[...], total[...])])
     result, level = merged([finish(*states[0]), unpacked(r2)])
     result_ref[...] = result
     level_ref[...] = jnp.broadcast_to(level, (8, LANES))
@@ -197,7 +196,7 @@
         rows[i * ROWS : (i + 1) * ROWS, :] = ref[...]
     width = wa.shape[1]
     xh, z = index[0] // (Z * CORE), (index[0] // CORE) % Z
-    slots = [((xh + dx) % XH) * Z + (z + Z - dz) % Z for dx in range(XH) for dz in (0,) + FAR]
+    slots = [((xh + dx) % XH) * Z + (z + Z - dz) % Z for dx in range(XH) for dz in (0, 2, 1, 3)]
     for side, w in enumerate((wa, wb)):
         terms = jnp.dot(rows[...], w[...], preferred_element_type=jnp.float32).astype(jnp.bfloat16)
         for i in range(8):
@@ -211,6 +210,11 @@
     acc = acc.astype(jnp.bfloat16)
     mine[...] = acc[:, :width]
     other[...] = acc[:, width:]
+
+
+def place_kernel(core, mine, theirs, out):
+    out[pl.ds(pl.multiple_of(core[0] * ROWS, ROWS), ROWS), :] = mine[...]
+    out[pl.ds(pl.multiple_of((1 - core[0]) * ROWS, ROWS), ROWS), :] = theirs[...]
 
 
 def call(kernel, outs, scratch=(), flops=0, **kwargs):
@@ -259,47 +263,47 @@
     row = jnp.arange(ROWS, dtype=jnp.int32)
     allowed = (question_ids[:, None] == question_ids[None, :]) & (row[None, :] <= row[:, None])
     bias = jnp.where(allowed, 0.0, FLOOR).astype(f32)
-    def scratch(*sizes):
-        return [pltpu.VMEM((size, width), bf16) for size in sizes for width in (DH, 2 * DH)]
-
-    own_top, own_total = call(own_kernel, own_state, scratch(positions))(
+    def layout(size):
+        return [((size, DH), bf16), ((size, 2 * DH), bf16)]
+
+    own_top, own_total, *block = call(own_kernel, own_state + layout(positions))(
         queries, jnp.concatenate([question_keys, question_values]), bias, after(kv, q_z[0])
     )
-    top, total, rows = call(
-        near_kernel, state + [((4, LANES, DH), bf16)], scratch(positions, positions), flops=1
-    )(*q_z, queries, after(kv, own_top), kv_c)
+    top, total, rows, *block = call(
+        near_kernel, state + [((4, LANES, DH), bf16)] + layout(positions), flops=1
+    )(*q_z, queries, *block, kv_c)
     x0, top = lax.optimization_barrier((x0, top))
     xc0 = moved(x0, c=1)
-    own_top, own_total = call(own_more_kernel, own_state, scratch(positions), flops=block_flops)(
-        after(rows, x0), own_top, own_total, kv_c
-    )
-    top, total = call(others_kernel, state, scratch(2 * early), flops=1)(
+    own_top, own_total = call(own_more_kernel, own_state, flops=block_flops)(
+        after(rows, x0), own_top, own_total, *block
+    )
+    top, total, *block = call(others_kernel, state + layout(2 * early), flops=1)(
         rows, after(top, own_top), total, x0, xc0
     )
 
     x1, weight, top = lax.optimization_barrier((x1, out_weight, top))
     xc1 = moved(x1, c=1)
     weight_c = moved(weight, c=1)
-    own_top, own_total = call(own_more_kernel, own_state, scratch(2 * early), flops=2 * block_flops)(
-        after(rows, x1), own_top, own_total, x0, xc0
-    )
-    top = after(top, own_top)
-    (p_far,) = call(functools.partial(last_kernel, owners=(2,)), [part], scratch(2 * late), flops=1)(
-        rows, top, total, x1, xc1
-    )
-    p_next = call(
-        functools.partial(last_kernel, owners=(0, 1)), [part] * 2, scratch(2 * late), flops=4 * block_flops
-    )(rows, after(top, p_far), total, x1, xc1)
+    own_top, own_total = call(own_more_kernel, own_state, flops=2 * block_flops)(
+        after(rows, x1), own_top, own_total, *block
+    )
+    p_far, *block = call(far_kernel, [part] + layout(2 * late), flops=1)(
+        rows, after(top, own_top), total, x1, xc1
+    )
+    p_next = call(next_kernel, [part] * 2, flops=4 * block_flops)(
+        rows, after(top, p_far), total, *block
+    )
     back = [moved(p, z=-z) for p, z in zip((*p_next, p_far), FAR)]
-    result, level = call(
-        own_last_kernel, [((DH, LANES), f32), ((8, LANES), f32)], scratch(2 * late), flops=1
-    )(after(rows, *p_next), own_top, own_total, x1, xc1, back[2])
+    result, level = call(own_last_kernel, [((DH, LANES), f32), ((8, LANES), f32)], flops=1)(
+        after(rows, *p_next), own_top, own_total, *block, back[2]
+    )
     (att,) = call(
         merge_kernel, [((ROWS, GROUP * DH), bf16)], in_specs=[smem] + [vmem] * 4
     )(live_rows, result, level, *back[:2])
 
     att_x = moved(att, xh=1)
-    held = [att] + [moved(att, z=z) for z in FAR] + [att_x] + [moved(att_x, z=z) for z in FAR]
+    steps = (2, 1, 3)
+    held = [att] + [moved(att, z=z) for z in steps] + [att_x] + [moved(att_x, z=z) for z in steps]
     width = out_weight.shape[1]
     (terms,) = call(
         project_kernel,
@@ -313,11 +317,10 @@
         [((ROWS, width), bf16), ((ROWS, width), bf16)],
     )(gathered)
     theirs = moved(other, c=1)
-    return jnp.where(
-        core == 0,
-        jnp.concatenate([mine, theirs], axis=0),
-        jnp.concatenate([theirs, mine], axis=0),
-    )
+    (projected,) = call(
+        place_kernel, [((CORE * ROWS, width), bf16)], in_specs=[smem, vmem, vmem]
+    )(core.reshape(1), mine, theirs)
+    return projected
 
 
 def solution(mesh):

time: 93 us -> 91.7 us (0.986)
  starting transfers between devices: 28.9 us -> 31.5 us
  blocking collectives: 17.2 us -> 14.8 us
    ppermute x20, starting transfers between devices: 28.9 us -> 31.5 us  [moved(): return lax.ppermute(array, 'blk', pairs)]
    all_to_all x1, blocking collectives: 17.2 us -> 14.8 us  [shards(): gathered = lax.all_to_all(terms, 'head', 0, 0, tiled=True)]
    pallas_call x8 -> x9, Pallas kernels: 27.9 us -> 27.6 us  [the longest x1 7.68 us: shards(): call(near_kernel, state + [((4, LANES, DH), bf16)] + layout(positions), f...]
  transfers between devices with their start and end apart: 20 -> 20, of which waited for: 7 -> 6; matrix products, arithmetic and copies ran while one was open for 2% -> 2% of each run, Pallas kernels for 30% -> 30%
where the time goes in v13:
time: 91.7 us; the launch traced here: 91.3 us
  starting transfers between devices  31.5 us (34%)
  Pallas kernels  29.3 us (32%)
  blocking collectives  14.8 us (16%)
  waiting for transfers between devices  10.3 us (11%)
  local copies, waits for them, and re-layouts  2.99 us (3%)
  other arithmetic  1.54 us (2%)
    ppermute x20, starting transfers between devices, moved(): return lax.ppermute(array, 'blk', pairs)  31.5 us
    all_to_all x1, blocking collectives, shards(): gathered = lax.all_to_all(terms, 'head', 0, 0, tiled=True)  14.8 us
    ppermute x20, waiting for transfers between devices, moved(): return lax.ppermute(array, 'blk', pairs)  10.3 us
    pallas_call x1, Pallas kernels, shards(): call(near_kernel, state + [((4, LANES, DH), bf16)] + layout(positions), f...  7.68 us
    pallas_call x1, Pallas kernels, shards(): call(others_kernel, state + layout(2 * early), flops=1)  3.49 us
    unnamed x8, local copies, waits for them, and re-layouts  2.99 us
    pallas_call x1, Pallas kernels, shards(): call(next_kernel, [part] * 2, flops=4 * block_flops)  2.95 us
    pallas_call x1, Pallas kernels, shards(): call(far_kernel, [part] + layout(2 * late), flops=1)  2.92 us
  transfers between devices with their start and end apart: 20, of which 6 were waited for; matrix products, arithmetic and copies ran while one was open for 2% of the time, Pallas kernels for 30%

profile of v13, /device:TPU:1, one launch (start us, length us, event | category | flops | bytes accessed | tf_op | source)
XLA Modules:
  0.0 91.3 jit_solution(16192060680764881233)
XLA Ops:
  0.0 0.0 copy-start.2
  0.0 1.0 %copy-done.2 = bf16[2048,128]{1,0:T(8,128)(2,1)S(1)} copy-done((bf16[2048,128]{1,0:T(8,128)(2,1)S(1)}, bf16[2048,128]{1,0:T(8,128)(2,1)}, u32[]{:S(2)}) %copy-start.2) | copy-done | bytes 524312
  1.0 0.0 copy-start.3
  1.0 1.0 %copy-done.3 = bf16[2048,128]{1,0:T(8,128)(2,1)S(1)} copy-done((bf16[2048,128]{1,0:T(8,128)(2,1)S(1)}, bf16[2048,128]{1,0:T(8,128)(2,1)}, u32[]{:S(2)}) %copy-start.3) | copy-done | bytes 524312
  2.1 0.1 shard_map.82
  2.2 1.5 %collective-permute-start.3 = (bf16[4096,128]{1,0:T(8,128)(2,1)S(1)}, bf16[4096,128]{1,0:T(8,128)(2,1)S(1)}, u32[]{:S(2)}, u32[]{:S(2)}) collective-permute-start(bf16[4096,128]{1,0:T(8,128)(2,1)S(1)} %get-tuple-element.47.kv), channel_id=1, source_target_pairs={{0,8},{8,0},{16,24},{24,16},{32,40},{40,32},{48,56},{56,48},{64,72... | collective-permute-start | bytes 3145736 | tf_op jit(solution)/shard_map/ppermute | solution.py:28
  3.7 1.7 %collective-permute-start = (bf16[64,1024]{1,0:T(8,128)(2,1)}, bf16[64,1024]{1,0:T(8,128)(2,1)S(1)}, u32[]{:S(2)}, u32[]{:S(2)}) collective-permute-start(bf16[64,1024]{1,0:T(8,128)(2,1)} %q.3), channel_id=1, source_target_pairs={{0,16},{8,24},{16,32},{24,40},{32,48},{40,56},{48,0},{56,8},{64,80... | collective-permute-start | bytes 393224 | tf_op jit(solution)/shard_map/ppermute | solution.py:28
  5.5 2.7 %collective-permute-start.5 = (bf16[1792,128]{1,0:T(8,128)(2,1)S(1)}, bf16[1792,128]{1,0:T(8,128)(2,1)S(1)}, u32[]{:S(2)}, u32[]{:S(2)}) collective-permute-start(bf16[1792,128]{1,0:T(8,128)(2,1)S(1)} %get-tuple-element.52), channel_id=1, source_target_pairs={{0,64},{8,72},{16,80},{24,88},{32,96},{40,104},{48,112},{56,120},{... | collective-permute-start | bytes 1376264 | tf_op jit(solution)/shard_map/ppermute | solution.py:28
  8.2 2.1 %collective-permute-start.1 = (bf16[64,1024]{1,0:T(8,128)(2,1)}, bf16[64,1024]{1,0:T(8,128)(2,1)S(1)}, u32[]{:S(2)}, u32[]{:S(2)}) collective-permute-start(bf16[64,1024]{1,0:T(8,128)(2,1)} %q.3), channel_id=1, source_target_pairs={{0,48},{8,56},{16,0},{24,8},{32,16},{40,24},{48,32},{56,40},{64,11... | collective-permute-start | bytes 393224 | tf_op jit(solution)/shard_map/ppermute | solution.py:28
  10.3 1.3 %collective-permute-start.2 = (bf16[64,1024]{1,0:T(8,128)(2,1)}, bf16[64,1024]{1,0:T(8,128)(2,1)S(1)}, u32[]{:S(2)}, u32[]{:S(2)}) collective-permute-start(bf16[64,1024]{1,0:T(8,128)(2,1)} %q.3), channel_id=1, source_target_pairs={{0,32},{8,40},{16,48},{24,56},{32,0},{40,8},{48,16},{56,24},{64,96... | collective-permute-start | bytes 393224 | tf_op jit(solution)/shard_map/ppermute | solution.py:28
  11.6 0.0 collective-permute-done.q0
  11.6 2.7 %collective-permute-start.4 = (bf16[2304,128]{1,0:T(8,128)(2,1)S(1)}, bf16[2304,128]{1,0:T(8,128)(2,1)S(1)}, u32[]{:S(2)}, u32[]{:S(2)}) collective-permute-start(bf16[2304,128]{1,0:T(8,128)(2,1)S(1)} %get-tuple-element.51), channel_id=1, source_target_pairs={{0,64},{8,72},{16,80},{24,88},{32,96},{40,104},{48,112},{56,120},{... | collective-permute-start | bytes 1769480 | tf_op jit(solution)/shard_map/ppermute | solution.py:28
  14.3 0.8 fusion.1.bias
  15.1 0.7 pad_maximum_fusion.qkv
  15.9 0.0 copy-start.1
  15.9 0.9 copy-done.1
  16.8 2.6 %shard_map.83 = (f32[512,128]{1,0:T(8,128)S(1)}, f32[512,256]{1,0:T(8,128)S(1)}, bf16[2048,128]{1,0:T(8,128)(2,1)S(1)}, bf16[2048,256]{1,0:T(8,128)(2,1)S(1)}) custom-call(bf16[64,1024]{1,0:T(8,128)(2,1)S(1)} %copy-done.1, bf16[128,128]{1,0:T(8,128)(2,1)S(1)} %pad_maximum_fusion.qkv, f32[64,64]{1,0:T(8,128)S(1)} %fusion.1.bias, ...), custom_call_target="tpu_custom_call" | custom-call | tf_op jit(solution)/shard_map/pallas_call | solution.py:269
  19.3 0.0 collective-permute-done.1.q1
  19.4 0.0 collective-permute-done.2.q2
  19.4 0.0 collective-permute-done.3.kv_c
  19.4 7.7 %shard_map.84 = (f32[3,512,128]{2,1,0:T(8,128)S(1)}, f32[3,512,256]{2,1,0:T(8,128)S(1)}, bf16[4,512,128]{2,1,0:T(8,128)(2,1)S(1)}, bf16[2048,128]{1,0:T(8,128)(2,1)S(1)}, bf16[2048,256]{1,0:T(8,128)(2,1)S(1)}) custom-call(bf16[64,1024]{1,0:T(8,128)(2,1)S(1)} %collective-permute-done.q0, bf16[64,1024]{1,0:T(8,128)(2,1)S(1)} %collective-permute-done.1.q1, ...), custom_call_target="tpu_custom_call" | custom-call | flops 1 | tf_op jit(solution)/shard_map/pallas_call | solution.py:272
  27.1 0.0 collective-permute-done.5.part
  27.1 1.2 %collective-permute-start.6 = (bf16[1792,128]{1,0:T(8,128)(2,1)S(1)}, bf16[1792,128]{1,0:T(8,128)(2,1)S(1)}, u32[]{:S(2)}, u32[]{:S(2)}) collective-permute-start(bf16[1792,128]{1,0:T(8,128)(2,1)S(1)} %collective-permute-done.5.part), channel_id=1, source_target_pairs={{0,8},{8,0},{16,24},{24,16},{32,40},{40,32},{48,56},{56,48},{64,72... | collective-permute-start | bytes 1376264 | tf_op jit(solution)/shard_map/ppermute | solution.py:28
  28.3 2.4 %shard_map.85 = (f32[512,128]{1,0:T(8,128)S(1)}, f32[512,256]{1,0:T(8,128)S(1)}) custom-call(bf16[4,512,128]{2,1,0:T(8,128)(2,1)S(1)} %get-tuple-element.80.rows, f32[512,128]{1,0:T(8,128)S(1)} %get-tuple-element.57.top, f32[512,256]{1,0:T(8,128)S(1)} %get-tuple-element.58.total, bf16[2048,128]{1,0:T(8,128)(2,1)S(1)} %get-tuple-element.59.k, ...), custom_call_target="tpu_custom_call" | custom-call | flops 1073741824 | tf_op jit(solution)/shard_map/pallas_call | solution.py:277
  30.7 0.0 collective-permute-done.6.other_part
  30.7 0.0 copy-start
  30.7 3.5 %shard_map.86 = (f32[3,512,128]{2,1,0:T(8,128)S(1)}, f32[3,512,256]{2,1,0:T(8,128)S(1)}, bf16[1792,128]{1,0:T(8,128)(2,1)S(1)}, bf16[1792,256]{1,0:T(8,128)(2,1)S(1)}) custom-call(bf16[4,512,128]{2,1,0:T(8,128)(2,1)S(1)} %get-tuple-element.80.rows, f32[3,512,128]{2,1,0:T(8,128)S(1)} %get-tuple-element.62.top_in, ...), custom_call_target="tpu_custom_call" | custom-call | flops 1 | tf_op jit(solution)/shard_map/pallas_call | solution.py:280
  34.2 0.0 collective-permute-done.4.part
  34.2 0.1 collective-permute-start.7
  34.3 0.0 copy-done
  34.3 0.5 collective-permute-start.18
  34.8 2.1 %shard_map.87 = (f32[512,128]{1,0:T(8,128)S(1)}, f32[512,256]{1,0:T(8,128)S(1)}) custom-call(bf16[4,512,128]{2,1,0:T(8,128)(2,1)S(1)} %get-tuple-element.80.rows, f32[512,128]{1,0:T(8,128)S(1)} %get-tuple-element.61.top, f32[512,256]{1,0:T(8,128)S(1)} %get-tuple-element.68.total, bf16[1792,128]{1,0:T(8,128)(2,1)S(1)} %get-tuple-element.69.k, ...), custom_call_target="tpu_custom_call" | custom-call | flops 2147483648 | tf_op jit(solution)/shard_map/pallas_call | solution.py:287
  36.9 0.0 collective-permute-done.7.other_part
  36.9 2.9 %shard_map.88 = (bf16[144,512]{1,0:T(8,128)(2,1)S(1)}, bf16[2304,128]{1,0:T(8,128)(2,1)S(1)}, bf16[2304,256]{1,0:T(8,128)(2,1)S(1)}) custom-call(bf16[4,512,128]{2,1,0:T(8,128)(2,1)S(1)} %get-tuple-element.80.rows, f32[3,512,128]{2,1,0:T(8,128)S(1)} %get-tuple-element.75.top, f32[3,512,256]{2,1,0:T(8,128)S(1)} %get-tuple-element.73.total, ...), custom_call_target="tpu_custom_call" | custom-call | flops 1 | tf_op jit(solution)/shard_map/pallas_call | solution.py:290
  39.9 1.6 %collective-permute-start.8 = (bf16[144,512]{1,0:T(8,128)(2,1)S(1)}, bf16[144,512]{1,0:T(8,128)(2,1)S(1)}, u32[]{:S(2)}, u32[]{:S(2)}) collective-permute-start(bf16[144,512]{1,0:T(8,128)(2,1)S(1)} %get-tuple-element.74), channel_id=1, source_target_pairs={{0,32},{8,40},{16,48},{24,56},{32,0},{40,8},{48,16},{56,24},{64,96... | collective-permute-start | bytes 442376 | tf_op jit(solution)/shard_map/ppermute | solution.py:28
  41.5 2.9 %shard_map.89 = (bf16[144,512]{1,0:T(8,128)(2,1)S(1)}, bf16[144,512]{1,0:T(8,128)(2,1)S(1)}) custom-call(bf16[4,512,128]{2,1,0:T(8,128)(2,1)S(1)} %get-tuple-element.80.rows, f32[3,512,128]{2,1,0:T(8,128)S(1)} %get-tuple-element.75.top, f32[3,512,256]{2,1,0:T(8,128)S(1)} %get-tuple-element.73.total, bf16[2304,128]{1,0:T(8,128)(2,1)S(1)} %get-tuple-element.76.k, ...), custom_call_target="tpu_custom_call" | custom-call | flops 4294967296 | tf_op jit(solution)/shard_map/pallas_call | solution.py:293
  44.4 1.3 %collective-permute-start.10 = (bf16[144,512]{1,0:T(8,128)(2,1)S(1)}, bf16[144,512]{1,0:T(8,128)(2,1)S(1)}, u32[]{:S(2)}, u32[]{:S(2)}) collective-permute-start(bf16[144,512]{1,0:T(8,128)(2,1)S(1)} %get-tuple-element.79), channel_id=1, source_target_pairs={{0,16},{8,24},{16,32},{24,40},{32,48},{40,56},{48,0},{56,8},{64,80... | collective-permute-start | bytes 442376 | tf_op jit(solution)/shard_map/ppermute | solution.py:28
  45.7 1.5 %collective-permute-start.9 = (bf16[144,512]{1,0:T(8,128)(2,1)S(1)}, bf16[144,512]{1,0:T(8,128)(2,1)S(1)}, u32[]{:S(2)}, u32[]{:S(2)}) collective-permute-start(bf16[144,512]{1,0:T(8,128)(2,1)S(1)} %get-tuple-element.78), channel_id=1, source_target_pairs={{0,48},{8,56},{16,0},{24,8},{32,16},{40,24},{48,32},{56,40},{64,11... | collective-permute-start | bytes 442376 | tf_op jit(solution)/shard_map/ppermute | solution.py:28
  47.8 0.0 collective-permute-done.8.r2
  47.8 2.8 %shard_map.90 = (f32[128,512]{1,0:T(8,128)S(1)}, f32[8,512]{1,0:T(8,128)S(1)}) custom-call(bf16[4,512,128]{2,1,0:T(8,128)(2,1)S(1)} %get-tuple-element.80.rows, f32[512,128]{1,0:T(8,128)S(1)} %get-tuple-element.71.top, f32[512,256]{1,0:T(8,128)S(1)} %get-tuple-element.81.total, bf16[2304,128]{1,0:T(8,128)(2,1)S(1)} %get-tuple-element.76.k, ...), custom_call_target="tpu_custom_call" | custom-call | flops 1 | tf_op jit(solution)/shard_map/pallas_call | solution.py:297
  50.6 0.0 collective-permute-done.10.r1
  50.6 0.0 collective-permute-done.9.r0
  50.6 0.2 shard_map.91.a0
  50.8 2.6 %collective-permute-start.14 = (bf16[64,1024]{1,0:T(8,128)(2,1)S(1)}, bf16[64,1024]{1,0:T(8,128)(2,1)S(1)}, u32[]{:S(2)}, u32[]{:S(2)}) collective-permute-start(bf16[64,1024]{1,0:T(8,128)(2,1)S(1)} %shard_map.91.a0), channel_id=1, source_target_pairs={{0,64},{8,72},{16,80},{24,88},{32,96},{40,104},{48,112},{56,120},{... | collective-permute-start | bytes 393224 | tf_op jit(solution)/shard_map/ppermute | solution.py:28
  53.4 1.3 %collective-permute-start.11 = (bf16[64,1024]{1,0:T(8,128)(2,1)S(1)}, bf16[64,1024]{1,0:T(8,128)(2,1)S(1)}, u32[]{:S(2)}, u32[]{:S(2)}) collective-permute-start(bf16[64,1024]{1,0:T(8,128)(2,1)S(1)} %shard_map.91.a0), channel_id=1, source_target_pairs={{0,32},{8,40},{16,48},{24,56},{32,0},{40,8},{48,16},{56,24},{64,96... | collective-permute-start | bytes 393224 | tf_op jit(solution)/shard_map/ppermute | solution.py:28
  54.7 1.0 %collective-permute-start.12 = (bf16[64,1024]{1,0:T(8,128)(2,1)S(1)}, bf16[64,1024]{1,0:T(8,128)(2,1)S(1)}, u32[]{:S(2)}, u32[]{:S(2)}) collective-permute-start(bf16[64,1024]{1,0:T(8,128)(2,1)S(1)} %shard_map.91.a0), channel_id=1, source_target_pairs={{0,16},{8,24},{16,32},{24,40},{32,48},{40,56},{48,0},{56,8},{64,80... | collective-permute-start | bytes 393224 | tf_op jit(solution)/shard_map/ppermute | solution.py:28
  55.7 1.6 %collective-permute-start.13 = (bf16[64,1024]{1,0:T(8,128)(2,1)S(1)}, bf16[64,1024]{1,0:T(8,128)(2,1)S(1)}, u32[]{:S(2)}, u32[]{:S(2)}) collective-permute-start(bf16[64,1024]{1,0:T(8,128)(2,1)S(1)} %shard_map.91.a0), channel_id=1, source_target_pairs={{0,48},{8,56},{16,0},{24,8},{32,16},{40,24},{48,32},{56,40},{64,11... | collective-permute-start | bytes 393224 | tf_op jit(solution)/shard_map/ppermute | solution.py:28
  57.3 0.0 collective-permute-done.14.a4
  57.3 0.5 collective-permute-start.15
  57.8 0.9 %collective-permute-done.11.a1 = bf16[64,1024]{1,0:T(8,128)(2,1)S(1)} collective-permute-done((bf16[64,1024]{1,0:T(8,128)(2,1)S(1)}, bf16[64,1024]{1,0:T(8,128)(2,1)S(1)}, u32[]{:S(2)}, u32[]{:S(2)}) %collective-permute-start.11) | collective-permute-done | bytes 131104 | tf_op jit(solution)/shard_map/ppermute | solution.py:28
  58.8 0.4 collective-permute-start.16
  59.1 2.4 %collective-permute-done.12.a2 = bf16[64,1024]{1,0:T(8,128)(2,1)S(1)} collective-permute-done((bf16[64,1024]{1,0:T(8,128)(2,1)S(1)}, bf16[64,1024]{1,0:T(8,128)(2,1)S(1)}, u32[]{:S(2)}, u32[]{:S(2)}) %collective-permute-start.12) | collective-permute-done | bytes 131104 | tf_op jit(solution)/shard_map/ppermute | solution.py:28
  61.5 0.0 collective-permute-start.17
  61.5 0.4 collective-permute-done.13.a3
  61.9 2.3 %collective-permute-done.15.a5 = bf16[64,1024]{1,0:T(8,128)(2,1)S(1)} collective-permute-done((bf16[64,1024]{1,0:T(8,128)(2,1)S(1)}, bf16[64,1024]{1,0:T(8,128)(2,1)S(1)}, u32[]{:S(2)}, u32[]{:S(2)}) %collective-permute-start.15) | collective-permute-done | bytes 131104 | tf_op jit(solution)/shard_map/ppermute | solution.py:28
  64.1 3.4 %collective-permute-done.16.a6 = bf16[64,1024]{1,0:T(8,128)(2,1)S(1)} collective-permute-done((bf16[64,1024]{1,0:T(8,128)(2,1)S(1)}, bf16[64,1024]{1,0:T(8,128)(2,1)S(1)}, u32[]{:S(2)}, u32[]{:S(2)}) %collective-permute-start.16) | collective-permute-done | bytes 131104 | tf_op jit(solution)/shard_map/ppermute | solution.py:28
  67.6 0.0 collective-permute-done.17.a7
  67.6 0.0 collective-permute-done.18.wb
  67.6 1.2 %shard_map.92 = bf16[8,64,1024]{2,1,0:T(8,128)(2,1)S(1)} custom-call(s32[1]{0:T(128)} %bitcast.1.index, bf16[64,1024]{1,0:T(8,128)(2,1)S(1)} %shard_map.91.a0, bf16[64,1024]{1,0:T(8,128)(2,1)S(1)} %collective-permute-done.11.a1, bf16[64,1024]{1,0:T(8,128)(2,1)S(1)} %collective-permute-done.12.a2, bf16[64,1024]{1,0:T(8,128)(2,1)S(1)} %collective-permute-done.13.a3, ...), custom_call_target="tpu_custom_call" | custom-call | tf_op jit(solution)/shard_map/pallas_call | solution.py:308
  68.8 14.8 %all_to_all.5.terms = bf16[8,64,1024]{2,1,0:T(8,128)(2,1)S(1)} all-to-all(bf16[8,64,1024]{2,1,0:T(8,128)(2,1)S(1)} %shard_map.92), channel_id=1, replica_groups=mesh['blk'=16,'head'=8] {'head'}, dimensions={0} | all-to-all | bytes 2097152 | tf_op jit(solution)/shard_map/all_to_all | solution.py:314
  83.7 0.1 shard_map.93
  83.8 5.9 %collective-permute-start.19 = (bf16[64,512]{1,0:T(8,128)(2,1)S(1)}, bf16[64,512]{1,0:T(8,128)(2,1)S(1)}, u32[]{:S(2)}, u32[]{:S(2)}) collective-permute-start(bf16[64,512]{1,0:T(8,128)(2,1)S(1)} %get-tuple-element.86), channel_id=1, source_target_pairs={{0,8},{8,0},{16,24},{24,16},{32,40},{40,32},{48,56},{56,48},{64,72... | collective-permute-start | bytes 196616 | tf_op jit(solution)/shard_map/ppermute | solution.py:28
  89.7 0.9 collective-permute-done.19.theirs
  90.6 0.7 shard_map.94
Async XLA Ops:
  0.0 1.0 %copy-start.2 = (bf16[2048,128]{1,0:T(8,128)(2,1)S(1)}, bf16[2048,128]{1,0:T(8,128)(2,1)}, u32[]{:S(2)}) copy-start(bf16[2048,128]{1,0:T(8,128)(2,1)} %k.1) | copy-start | bytes 1572868
  1.0 1.0 %copy-start.3 = (bf16[2048,128]{1,0:T(8,128)(2,1)S(1)}, bf16[2048,128]{1,0:T(8,128)(2,1)}, u32[]{:S(2)}) copy-start(bf16[2048,128]{1,0:T(8,128)(2,1)} %v.1) | copy-start | bytes 1572868
  2.2 17.1 %collective-permute-start.3 = (bf16[4096,128]{1,0:T(8,128)(2,1)S(1)}, bf16[4096,128]{1,0:T(8,128)(2,1)S(1)}, u32[]{:S(2)}, u32[]{:S(2)}) collective-permute-start(bf16[4096,128]{1,0:T(8,128)(2,1)S(1)} %get-tuple-element.47.kv), channel_id=1, source_target_pairs={{0,8},{8,0},{16,24},{24,16},{32,40},{40,32},{48,56},{56,48},{64,72... | collective-permute-start | bytes 3145736 | tf_op jit(solution)/shard_map/ppermute | solution.py:28
  3.7 7.9 %collective-permute-start = (bf16[64,1024]{1,0:T(8,128)(2,1)}, bf16[64,1024]{1,0:T(8,128)(2,1)S(1)}, u32[]{:S(2)}, u32[]{:S(2)}) collective-permute-start(bf16[64,1024]{1,0:T(8,128)(2,1)} %q.3), channel_id=1, source_target_pairs={{0,16},{8,24},{16,32},{24,40},{32,48},{40,56},{48,0},{56,8},{64,80... | collective-permute-start | bytes 393224 | tf_op jit(solution)/shard_map/ppermute | solution.py:28
  5.5 21.6 %collective-permute-start.5 = (bf16[1792,128]{1,0:T(8,128)(2,1)S(1)}, bf16[1792,128]{1,0:T(8,128)(2,1)S(1)}, u32[]{:S(2)}, u32[]{:S(2)}) collective-permute-start(bf16[1792,128]{1,0:T(8,128)(2,1)S(1)} %get-tuple-element.52), channel_id=1, source_target_pairs={{0,64},{8,72},{16,80},{24,88},{32,96},{40,104},{48,112},{56,120},{... | collective-permute-start | bytes 1376264 | tf_op jit(solution)/shard_map/ppermute | solution.py:28
  8.2 11.1 %collective-permute-start.1 = (bf16[64,1024]{1,0:T(8,128)(2,1)}, bf16[64,1024]{1,0:T(8,128)(2,1)S(1)}, u32[]{:S(2)}, u32[]{:S(2)}) collective-permute-start(bf16[64,1024]{1,0:T(8,128)(2,1)} %q.3), channel_id=1, source_target_pairs={{0,48},{8,56},{16,0},{24,8},{32,16},{40,24},{48,32},{56,40},{64,11... | collective-permute-start | bytes 393224 | tf_op jit(solution)/shard_map/ppermute | solution.py:28
  10.3 9.0 %collective-permute-start.2 = (bf16[64,1024]{1,0:T(8,128)(2,1)}, bf16[64,1024]{1,0:T(8,128)(2,1)S(1)}, u32[]{:S(2)}, u32[]{:S(2)}) collective-permute-start(bf16[64,1024]{1,0:T(8,128)(2,1)} %q.3), channel_id=1, source_target_pairs={{0,32},{8,40},{16,48},{24,56},{32,0},{40,8},{48,16},{56,24},{64,96... | collective-permute-start | bytes 393224 | tf_op jit(solution)/shard_map/ppermute | solution.py:28
  11.6 22.6 %collective-permute-start.4 = (bf16[2304,128]{1,0:T(8,128)(2,1)S(1)}, bf16[2304,128]{1,0:T(8,128)(2,1)S(1)}, u32[]{:S(2)}, u32[]{:S(2)}) collective-permute-start(bf16[2304,128]{1,0:T(8,128)(2,1)S(1)} %get-tuple-element.51), channel_id=1, source_target_pairs={{0,64},{8,72},{16,80},{24,88},{32,96},{40,104},{48,112},{56,120},{... | collective-permute-start | bytes 1769480 | tf_op jit(solution)/shard_map/ppermute | solution.py:28
  15.9 0.9 copy-start.1
  27.1 3.6 %collective-permute-start.6 = (bf16[1792,128]{1,0:T(8,128)(2,1)S(1)}, bf16[1792,128]{1,0:T(8,128)(2,1)S(1)}, u32[]{:S(2)}, u32[]{:S(2)}) collective-permute-start(bf16[1792,128]{1,0:T(8,128)(2,1)S(1)} %collective-permute-done.5.part), channel_id=1, source_target_pairs={{0,8},{8,0},{16,24},{24,16},{32,40},{40,32},{48,56},{56,48},{64,72... | collective-permute-start | bytes 1376264 | tf_op jit(solution)/shard_map/ppermute | solution.py:28
  30.7 3.6 %copy-start = (bf16[1024,512]{1,0:T(8,128)(2,1)S(1)}, bf16[1024,512]{1,0:T(8,128)(2,1)}, u32[]{:S(2)}) copy-start(bf16[1024,512]{1,0:T(8,128)(2,1)} %wa.1) | copy-start | bytes 3145732
  34.2 2.7 %collective-permute-start.7 = (bf16[2304,128]{1,0:T(8,128)(2,1)S(1)}, bf16[2304,128]{1,0:T(8,128)(2,1)S(1)}, u32[]{:S(2)}, u32[]{:S(2)}) collective-permute-start(bf16[2304,128]{1,0:T(8,128)(2,1)S(1)} %collective-permute-done.4.part), channel_id=1, source_target_pairs={{0,8},{8,0},{16,24},{24,16},{32,40},{40,32},{48,56},{56,48},{64,72... | collective-permute-start | bytes 1769480 | tf_op jit(solution)/shard_map/ppermute | solution.py:28
  34.3 33.3 %collective-permute-start.18 = (bf16[1024,512]{1,0:T(8,128)(2,1)S(1)}, bf16[1024,512]{1,0:T(8,128)(2,1)S(1)}, u32[]{:S(2)}, u32[]{:S(2)}) collective-permute-start(bf16[1024,512]{1,0:T(8,128)(2,1)S(1)} %copy-done), channel_id=1, source_target_pairs={{0,8},{8,0},{16,24},{24,16},{32,40},{40,32},{48,56},{56,48},{64,72... | collective-permute-start | bytes 3145736 | tf_op jit(solution)/shard_map/ppermute | solution.py:28
  39.9 8.0 %collective-permute-start.8 = (bf16[144,512]{1,0:T(8,128)(2,1)S(1)}, bf16[144,512]{1,0:T(8,128)(2,1)S(1)}, u32[]{:S(2)}, u32[]{:S(2)}) collective-permute-start(bf16[144,512]{1,0:T(8,128)(2,1)S(1)} %get-tuple-element.74), channel_id=1, source_target_pairs={{0,32},{8,40},{16,48},{24,56},{32,0},{40,8},{48,16},{56,24},{64,96... | collective-permute-start | bytes 442376 | tf_op jit(solution)/shard_map/ppermute | solution.py:28
  44.4 6.2 %collective-permute-start.10 = (bf16[144,512]{1,0:T(8,128)(2,1)S(1)}, bf16[144,512]{1,0:T(8,128)(2,1)S(1)}, u32[]{:S(2)}, u32[]{:S(2)}) collective-permute-start(bf16[144,512]{1,0:T(8,128)(2,1)S(1)} %get-tuple-element.79), channel_id=1, source_target_pairs={{0,16},{8,24},{16,32},{24,40},{32,48},{40,56},{48,0},{56,8},{64,80... | collective-permute-start | bytes 442376 | tf_op jit(solution)/shard_map/ppermute | solution.py:28
  45.7 4.9 %collective-permute-start.9 = (bf16[144,512]{1,0:T(8,128)(2,1)S(1)}, bf16[144,512]{1,0:T(8,128)(2,1)S(1)}, u32[]{:S(2)}, u32[]{:S(2)}) collective-permute-start(bf16[144,512]{1,0:T(8,128)(2,1)S(1)} %get-tuple-element.78), channel_id=1, source_target_pairs={{0,48},{8,56},{16,0},{24,8},{32,16},{40,24},{48,32},{56,40},{64,11... | collective-permute-start | bytes 442376 | tf_op jit(solution)/shard_map/ppermute | solution.py:28
  50.8 6.5 %collective-permute-start.14 = (bf16[64,1024]{1,0:T(8,128)(2,1)S(1)}, bf16[64,1024]{1,0:T(8,128)(2,1)S(1)}, u32[]{:S(2)}, u32[]{:S(2)}) collective-permute-start(bf16[64,1024]{1,0:T(8,128)(2,1)S(1)} %shard_map.91.a0), channel_id=1, source_target_pairs={{0,64},{8,72},{16,80},{24,88},{32,96},{40,104},{48,112},{56,120},{... | collective-permute-start | bytes 393224 | tf_op jit(solution)/shard_map/ppermute | solution.py:28
  53.4 5.4 %collective-permute-start.11 = (bf16[64,1024]{1,0:T(8,128)(2,1)S(1)}, bf16[64,1024]{1,0:T(8,128)(2,1)S(1)}, u32[]{:S(2)}, u32[]{:S(2)}) collective-permute-start(bf16[64,1024]{1,0:T(8,128)(2,1)S(1)} %shard_map.91.a0), channel_id=1, source_target_pairs={{0,32},{8,40},{16,48},{24,56},{32,0},{40,8},{48,16},{56,24},{64,96... | collective-permute-start | bytes 393224 | tf_op jit(solution)/shard_map/ppermute | solution.py:28
  54.7 6.8 %collective-permute-start.12 = (bf16[64,1024]{1,0:T(8,128)(2,1)S(1)}, bf16[64,1024]{1,0:T(8,128)(2,1)S(1)}, u32[]{:S(2)}, u32[]{:S(2)}) collective-permute-start(bf16[64,1024]{1,0:T(8,128)(2,1)S(1)} %shard_map.91.a0), channel_id=1, source_target_pairs={{0,16},{8,24},{16,32},{24,40},{32,48},{40,56},{48,0},{56,8},{64,80... | collective-permute-start | bytes 393224 | tf_op jit(solution)/shard_map/ppermute | solution.py:28
  55.7 6.2 %collective-permute-start.13 = (bf16[64,1024]{1,0:T(8,128)(2,1)S(1)}, bf16[64,1024]{1,0:T(8,128)(2,1)S(1)}, u32[]{:S(2)}, u32[]{:S(2)}) collective-permute-start(bf16[64,1024]{1,0:T(8,128)(2,1)S(1)} %shard_map.91.a0), channel_id=1, source_target_pairs={{0,48},{8,56},{16,0},{24,8},{32,16},{40,24},{48,32},{56,40},{64,11... | collective-permute-start | bytes 393224 | tf_op jit(solution)/shard_map/ppermute | solution.py:28
  57.3 6.8 %collective-permute-start.15 = (bf16[64,1024]{1,0:T(8,128)(2,1)S(1)}, bf16[64,1024]{1,0:T(8,128)(2,1)S(1)}, u32[]{:S(2)}, u32[]{:S(2)}) collective-permute-start(bf16[64,1024]{1,0:T(8,128)(2,1)S(1)} %collective-permute-done.14.a4), channel_id=1, source_target_pairs={{0,32},{8,40},{16,48},{24,56},{32,0},{40,8},{48,16},{56,24},{64,96... | collective-permute-start | bytes 393224 | tf_op jit(solution)/shard_map/ppermute | solution.py:28
  58.8 8.8 %collective-permute-start.16 = (bf16[64,1024]{1,0:T(8,128)(2,1)S(1)}, bf16[64,1024]{1,0:T(8,128)(2,1)S(1)}, u32[]{:S(2)}, u32[]{:S(2)}) collective-permute-start(bf16[64,1024]{1,0:T(8,128)(2,1)S(1)} %collective-permute-done.14.a4), channel_id=1, source_target_pairs={{0,16},{8,24},{16,32},{24,40},{32,48},{40,56},{48,0},{56,8},{64,80... | collective-permute-start | bytes 393224 | tf_op jit(solution)/shard_map/ppermute | solution.py:28
  61.5 6.1 %collective-permute-start.17 = (bf16[64,1024]{1,0:T(8,128)(2,1)S(1)}, bf16[64,1024]{1,0:T(8,128)(2,1)S(1)}, u32[]{:S(2)}, u32[]{:S(2)}) collective-permute-start(bf16[64,1024]{1,0:T(8,128)(2,1)S(1)} %collective-permute-done.14.a4), channel_id=1, source_target_pairs={{0,48},{8,56},{16,0},{24,8},{32,16},{40,24},{48,32},{56,40},{64,11... | collective-permute-start | bytes 393224 | tf_op jit(solution)/shard_map/ppermute | solution.py:28
  83.8 6.8 %collective-permute-start.19 = (bf16[64,512]{1,0:T(8,128)(2,1)S(1)}, bf16[64,512]{1,0:T(8,128)(2,1)S(1)}, u32[]{:S(2)}, u32[]{:S(2)}) collective-permute-start(bf16[64,512]{1,0:T(8,128)(2,1)S(1)} %get-tuple-element.86), channel_id=1, source_target_pairs={{0,8},{8,0},{16,24},{24,16},{32,40},{40,32},{48,56},{56,48},{64,72... | collective-permute-start | bytes 196616 | tf_op jit(solution)/shard_map/ppermute | solution.py:28

commit v14 on v13

--- a/solution.py
+++ b/solution.py
@@ -302,8 +302,8 @@
     )(live_rows, result, level, *back[:2])
 
     att_x = moved(att, xh=1)
-    steps = (2, 1, 3)
-    held = [att] + [moved(att, z=z) for z in steps] + [att_x] + [moved(att_x, z=z) for z in steps]
+    held = [att] + [moved(att, z=z) for z in (2, 1, 3)]
+    held += [att_x, moved(held[1], xh=1)] + [moved(att_x, z=z) for z in (1, 3)]
     width = out_weight.shape[1]
     (terms,) = call(
         project_kernel,

time: 91.7 us -> 88.8 us (0.968)
  waiting for transfers between devices: 10.3 us -> 5.12 us
  starting transfers between devices: 31.5 us -> 33.9 us
    ppermute x20, waiting for transfers between devices: 10.3 us -> 5.12 us  [moved(): return lax.ppermute(array, 'blk', pairs)]
    ppermute x20, starting transfers between devices: 31.5 us -> 33.9 us  [moved(): return lax.ppermute(array, 'blk', pairs)]
  transfers between devices with their start and end apart: 20 -> 20, of which waited for: 6 -> 5; matrix products, arithmetic and copies ran while one was open for 2% -> 2% of each run, Pallas kernels for 30% -> 31%
where the time goes in v14:
time: 88.8 us; the launch traced here: 88.5 us
  starting transfers between devices  33.9 us (38%)
  Pallas kernels  29.3 us (33%)
  blocking collectives  14.8 us (17%)
  waiting for transfers between devices  5.12 us (6%)
  local copies, waits for them, and re-layouts  2.99 us (3%)
  other arithmetic  1.54 us (2%)
    ppermute x20, starting transfers between devices, moved(): return lax.ppermute(array, 'blk', pairs)  33.9 us
    all_to_all x1, blocking collectives, shards(): gathered = lax.all_to_all(terms, 'head', 0, 0, tiled=True)  14.8 us
    pallas_call x1, Pallas kernels, shards(): call(near_kernel, state + [((4, LANES, DH), bf16)] + layout(positions), f...  7.68 us
    ppermute x20, waiting for transfers between devices, moved(): return lax.ppermute(array, 'blk', pairs)  5.12 us
    pallas_call x1, Pallas kernels, shards(): call(others_kernel, state + layout(2 * early), flops=1)  3.49 us
    unnamed x8, local copies, waits for them, and re-layouts  2.99 us
    pallas_call x1, Pallas kernels, shards(): call(next_kernel, [part] * 2, flops=4 * block_flops)  2.95 us
    pallas_call x1, Pallas kernels, shards(): call(far_kernel, [part] + layout(2 * late), flops=1)  2.92 us
  transfers between devices with their start and end apart: 20, of which 5 were waited for; matrix products, arithmetic and copies ran while one was open for 2% of the time, Pallas kernels for 31%

profile of v14, /device:TPU:1, one launch (start us, length us, event | category | flops | bytes accessed | tf_op | source)
XLA Modules:
  0.0 88.5 jit_solution(8196587088983270)
XLA Ops:
  0.0 0.0 copy-start.2
  0.0 1.0 %copy-done.2 = bf16[2048,128]{1,0:T(8,128)(2,1)S(1)} copy-done((bf16[2048,128]{1,0:T(8,128)(2,1)S(1)}, bf16[2048,128]{1,0:T(8,128)(2,1)}, u32[]{:S(2)}) %copy-start.2) | copy-done | bytes 524312
  1.0 0.0 copy-start.3
  1.0 1.0 %copy-done.3 = bf16[2048,128]{1,0:T(8,128)(2,1)S(1)} copy-done((bf16[2048,128]{1,0:T(8,128)(2,1)S(1)}, bf16[2048,128]{1,0:T(8,128)(2,1)}, u32[]{:S(2)}) %copy-start.3) | copy-done | bytes 524312
  2.1 0.1 shard_map.82
  2.2 1.5 %collective-permute-start.3 = (bf16[4096,128]{1,0:T(8,128)(2,1)S(1)}, bf16[4096,128]{1,0:T(8,128)(2,1)S(1)}, u32[]{:S(2)}, u32[]{:S(2)}) collective-permute-start(bf16[4096,128]{1,0:T(8,128)(2,1)S(1)} %get-tuple-element.47.kv), channel_id=1, source_target_pairs={{0,8},{8,0},{16,24},{24,16},{32,40},{40,32},{48,56},{56,48},{64,72... | collective-permute-start | bytes 3145736 | tf_op jit(solution)/shard_map/ppermute | solution.py:28
  3.7 1.7 %collective-permute-start = (bf16[64,1024]{1,0:T(8,128)(2,1)}, bf16[64,1024]{1,0:T(8,128)(2,1)S(1)}, u32[]{:S(2)}, u32[]{:S(2)}) collective-permute-start(bf16[64,1024]{1,0:T(8,128)(2,1)} %q.3), channel_id=1, source_target_pairs={{0,16},{8,24},{16,32},{24,40},{32,48},{40,56},{48,0},{56,8},{64,80... | collective-permute-start | bytes 393224 | tf_op jit(solution)/shard_map/ppermute | solution.py:28
  5.5 2.7 %collective-permute-start.5 = (bf16[1792,128]{1,0:T(8,128)(2,1)S(1)}, bf16[1792,128]{1,0:T(8,128)(2,1)S(1)}, u32[]{:S(2)}, u32[]{:S(2)}) collective-permute-start(bf16[1792,128]{1,0:T(8,128)(2,1)S(1)} %get-tuple-element.52), channel_id=1, source_target_pairs={{0,64},{8,72},{16,80},{24,88},{32,96},{40,104},{48,112},{56,120},{... | collective-permute-start | bytes 1376264 | tf_op jit(solution)/shard_map/ppermute | solution.py:28
  8.2 2.1 %collective-permute-start.1 = (bf16[64,1024]{1,0:T(8,128)(2,1)}, bf16[64,1024]{1,0:T(8,128)(2,1)S(1)}, u32[]{:S(2)}, u32[]{:S(2)}) collective-permute-start(bf16[64,1024]{1,0:T(8,128)(2,1)} %q.3), channel_id=1, source_target_pairs={{0,48},{8,56},{16,0},{24,8},{32,16},{40,24},{48,32},{56,40},{64,11... | collective-permute-start | bytes 393224 | tf_op jit(solution)/shard_map/ppermute | solution.py:28
  10.3 1.3 %collective-permute-start.2 = (bf16[64,1024]{1,0:T(8,128)(2,1)}, bf16[64,1024]{1,0:T(8,128)(2,1)S(1)}, u32[]{:S(2)}, u32[]{:S(2)}) collective-permute-start(bf16[64,1024]{1,0:T(8,128)(2,1)} %q.3), channel_id=1, source_target_pairs={{0,32},{8,40},{16,48},{24,56},{32,0},{40,8},{48,16},{56,24},{64,96... | collective-permute-start | bytes 393224 | tf_op jit(solution)/shard_map/ppermute | solution.py:28
  11.6 0.0 collective-permute-done.q0
  11.6 2.7 %collective-permute-start.4 = (bf16[2304,128]{1,0:T(8,128)(2,1)S(1)}, bf16[2304,128]{1,0:T(8,128)(2,1)S(1)}, u32[]{:S(2)}, u32[]{:S(2)}) collective-permute-start(bf16[2304,128]{1,0:T(8,128)(2,1)S(1)} %get-tuple-element.51), channel_id=1, source_target_pairs={{0,64},{8,72},{16,80},{24,88},{32,96},{40,104},{48,112},{56,120},{... | collective-permute-start | bytes 1769480 | tf_op jit(solution)/shard_map/ppermute | solution.py:28
  14.3 0.8 fusion.1.bias
  15.1 0.7 pad_maximum_fusion.qkv
  15.9 0.0 copy-start.1
  15.9 0.9 %copy-done.1 = bf16[64,1024]{1,0:T(8,128)(2,1)S(1)} copy-done((bf16[64,1024]{1,0:T(8,128)(2,1)S(1)}, bf16[64,1024]{1,0:T(8,128)(2,1)}, u32[]{:S(2)}) %copy-start.1) | copy-done | bytes 131096
  16.8 2.6 %shard_map.83 = (f32[512,128]{1,0:T(8,128)S(1)}, f32[512,256]{1,0:T(8,128)S(1)}, bf16[2048,128]{1,0:T(8,128)(2,1)S(1)}, bf16[2048,256]{1,0:T(8,128)(2,1)S(1)}) custom-call(bf16[64,1024]{1,0:T(8,128)(2,1)S(1)} %copy-done.1, bf16[128,128]{1,0:T(8,128)(2,1)S(1)} %pad_maximum_fusion.qkv, f32[64,64]{1,0:T(8,128)S(1)} %fusion.1.bias, ...), custom_call_target="tpu_custom_call" | custom-call | tf_op jit(solution)/shard_map/pallas_call | solution.py:269
  19.3 0.0 collective-permute-done.1.q1
  19.4 0.0 collective-permute-done.2.q2
  19.4 0.0 collective-permute-done.3.kv_c
  19.4 7.7 %shard_map.84 = (f32[3,512,128]{2,1,0:T(8,128)S(1)}, f32[3,512,256]{2,1,0:T(8,128)S(1)}, bf16[4,512,128]{2,1,0:T(8,128)(2,1)S(1)}, bf16[2048,128]{1,0:T(8,128)(2,1)S(1)}, bf16[2048,256]{1,0:T(8,128)(2,1)S(1)}) custom-call(bf16[64,1024]{1,0:T(8,128)(2,1)S(1)} %collective-permute-done.q0, bf16[64,1024]{1,0:T(8,128)(2,1)S(1)} %collective-permute-done.1.q1, ...), custom_call_target="tpu_custom_call" | custom-call | flops 1 | tf_op jit(solution)/shard_map/pallas_call | solution.py:272
  27.1 0.0 collective-permute-done.5.part
  27.1 1.2 %collective-permute-start.6 = (bf16[1792,128]{1,0:T(8,128)(2,1)S(1)}, bf16[1792,128]{1,0:T(8,128)(2,1)S(1)}, u32[]{:S(2)}, u32[]{:S(2)}) collective-permute-start(bf16[1792,128]{1,0:T(8,128)(2,1)S(1)} %collective-permute-done.5.part), channel_id=1, source_target_pairs={{0,8},{8,0},{16,24},{24,16},{32,40},{40,32},{48,56},{56,48},{64,72... | collective-permute-start | bytes 1376264 | tf_op jit(solution)/shard_map/ppermute | solution.py:28
  28.3 2.4 %shard_map.85 = (f32[512,128]{1,0:T(8,128)S(1)}, f32[512,256]{1,0:T(8,128)S(1)}) custom-call(bf16[4,512,128]{2,1,0:T(8,128)(2,1)S(1)} %get-tuple-element.80.rows, f32[512,128]{1,0:T(8,128)S(1)} %get-tuple-element.57.top, f32[512,256]{1,0:T(8,128)S(1)} %get-tuple-element.58.total, bf16[2048,128]{1,0:T(8,128)(2,1)S(1)} %get-tuple-element.59.k, ...), custom_call_target="tpu_custom_call" | custom-call | flops 1073741824 | tf_op jit(solution)/shard_map/pallas_call | solution.py:277
  30.7 0.0 collective-permute-done.6.other_part
  30.7 0.0 copy-start
  30.7 3.5 %shard_map.86 = (f32[3,512,128]{2,1,0:T(8,128)S(1)}, f32[3,512,256]{2,1,0:T(8,128)S(1)}, bf16[1792,128]{1,0:T(8,128)(2,1)S(1)}, bf16[1792,256]{1,0:T(8,128)(2,1)S(1)}) custom-call(bf16[4,512,128]{2,1,0:T(8,128)(2,1)S(1)} %get-tuple-element.80.rows, f32[3,512,128]{2,1,0:T(8,128)S(1)} %get-tuple-element.62.top_in, ...), custom_call_target="tpu_custom_call" | custom-call | flops 1 | tf_op jit(solution)/shard_map/pallas_call | solution.py:280
  34.2 0.0 collective-permute-done.4.part
  34.2 0.1 collective-permute-start.7
  34.3 0.0 copy-done
  34.3 0.5 collective-permute-start.18
  34.8 2.1 %shard_map.87 = (f32[512,128]{1,0:T(8,128)S(1)}, f32[512,256]{1,0:T(8,128)S(1)}) custom-call(bf16[4,512,128]{2,1,0:T(8,128)(2,1)S(1)} %get-tuple-element.80.rows, f32[512,128]{1,0:T(8,128)S(1)} %get-tuple-element.61.top, f32[512,256]{1,0:T(8,128)S(1)} %get-tuple-element.68.total, bf16[1792,128]{1,0:T(8,128)(2,1)S(1)} %get-tuple-element.69.k, ...), custom_call_target="tpu_custom_call" | custom-call | flops 2147483648 | tf_op jit(solution)/shard_map/pallas_call | solution.py:287
  36.9 0.0 collective-permute-done.7.other_part
  36.9 2.9 %shard_map.88 = (bf16[144,512]{1,0:T(8,128)(2,1)S(1)}, bf16[2304,128]{1,0:T(8,128)(2,1)S(1)}, bf16[2304,256]{1,0:T(8,128)(2,1)S(1)}) custom-call(bf16[4,512,128]{2,1,0:T(8,128)(2,1)S(1)} %get-tuple-element.80.rows, f32[3,512,128]{2,1,0:T(8,128)S(1)} %get-tuple-element.75.top, f32[3,512,256]{2,1,0:T(8,128)S(1)} %get-tuple-element.73.total, ...), custom_call_target="tpu_custom_call" | custom-call | flops 1 | tf_op jit(solution)/shard_map/pallas_call | solution.py:290
  39.9 1.6 %collective-permute-start.8 = (bf16[144,512]{1,0:T(8,128)(2,1)S(1)}, bf16[144,512]{1,0:T(8,128)(2,1)S(1)}, u32[]{:S(2)}, u32[]{:S(2)}) collective-permute-start(bf16[144,512]{1,0:T(8,128)(2,1)S(1)} %get-tuple-element.74), channel_id=1, source_target_pairs={{0,32},{8,40},{16,48},{24,56},{32,0},{40,8},{48,16},{56,24},{64,96... | collective-permute-start | bytes 442376 | tf_op jit(solution)/shard_map/ppermute | solution.py:28
  41.5 2.9 %shard_map.89 = (bf16[144,512]{1,0:T(8,128)(2,1)S(1)}, bf16[144,512]{1,0:T(8,128)(2,1)S(1)}) custom-call(bf16[4,512,128]{2,1,0:T(8,128)(2,1)S(1)} %get-tuple-element.80.rows, f32[3,512,128]{2,1,0:T(8,128)S(1)} %get-tuple-element.75.top, f32[3,512,256]{2,1,0:T(8,128)S(1)} %get-tuple-element.73.total, bf16[2304,128]{1,0:T(8,128)(2,1)S(1)} %get-tuple-element.76.k, ...), custom_call_target="tpu_custom_call" | custom-call | flops 4294967296 | tf_op jit(solution)/shard_map/pallas_call | solution.py:293
  44.4 1.3 %collective-permute-start.10 = (bf16[144,512]{1,0:T(8,128)(2,1)S(1)}, bf16[144,512]{1,0:T(8,128)(2,1)S(1)}, u32[]{:S(2)}, u32[]{:S(2)}) collective-permute-start(bf16[144,512]{1,0:T(8,128)(2,1)S(1)} %get-tuple-element.79), channel_id=1, source_target_pairs={{0,16},{8,24},{16,32},{24,40},{32,48},{40,56},{48,0},{56,8},{64,80... | collective-permute-start | bytes 442376 | tf_op jit(solution)/shard_map/ppermute | solution.py:28
  45.7 1.5 %collective-permute-start.9 = (bf16[144,512]{1,0:T(8,128)(2,1)S(1)}, bf16[144,512]{1,0:T(8,128)(2,1)S(1)}, u32[]{:S(2)}, u32[]{:S(2)}) collective-permute-start(bf16[144,512]{1,0:T(8,128)(2,1)S(1)} %get-tuple-element.78), channel_id=1, source_target_pairs={{0,48},{8,56},{16,0},{24,8},{32,16},{40,24},{48,32},{56,40},{64,11... | collective-permute-start | bytes 442376 | tf_op jit(solution)/shard_map/ppermute | solution.py:28
  47.8 0.0 collective-permute-done.8.r2
  47.8 2.8 %shard_map.90 = (f32[128,512]{1,0:T(8,128)S(1)}, f32[8,512]{1,0:T(8,128)S(1)}) custom-call(bf16[4,512,128]{2,1,0:T(8,128)(2,1)S(1)} %get-tuple-element.80.rows, f32[512,128]{1,0:T(8,128)S(1)} %get-tuple-element.71.top, f32[512,256]{1,0:T(8,128)S(1)} %get-tuple-element.81.total, bf16[2304,128]{1,0:T(8,128)(2,1)S(1)} %get-tuple-element.76.k, ...), custom_call_target="tpu_custom_call" | custom-call | flops 1 | tf_op jit(solution)/shard_map/pallas_call | solution.py:297
  50.6 0.0 collective-permute-done.10.r1
  50.6 0.0 collective-permute-done.9.r0
  50.6 0.2 shard_map.91.a0
  50.8 1.2 %collective-permute-start.11 = (bf16[64,1024]{1,0:T(8,128)(2,1)S(1)}, bf16[64,1024]{1,0:T(8,128)(2,1)S(1)}, u32[]{:S(2)}, u32[]{:S(2)}) collective-permute-start(bf16[64,1024]{1,0:T(8,128)(2,1)S(1)} %shard_map.91.a0), channel_id=1, source_target_pairs={{0,32},{8,40},{16,48},{24,56},{32,0},{40,8},{48,16},{56,24},{64,96... | collective-permute-start | bytes 393224 | tf_op jit(solution)/shard_map/ppermute | solution.py:28
  52.0 2.6 %collective-permute-start.14 = (bf16[64,1024]{1,0:T(8,128)(2,1)S(1)}, bf16[64,1024]{1,0:T(8,128)(2,1)S(1)}, u32[]{:S(2)}, u32[]{:S(2)}) collective-permute-start(bf16[64,1024]{1,0:T(8,128)(2,1)S(1)} %shard_map.91.a0), channel_id=1, source_target_pairs={{0,64},{8,72},{16,80},{24,88},{32,96},{40,104},{48,112},{56,120},{... | collective-permute-start | bytes 393224 | tf_op jit(solution)/shard_map/ppermute | solution.py:28
  54.7 1.0 %collective-permute-start.12 = (bf16[64,1024]{1,0:T(8,128)(2,1)S(1)}, bf16[64,1024]{1,0:T(8,128)(2,1)S(1)}, u32[]{:S(2)}, u32[]{:S(2)}) collective-permute-start(bf16[64,1024]{1,0:T(8,128)(2,1)S(1)} %shard_map.91.a0), channel_id=1, source_target_pairs={{0,16},{8,24},{16,32},{24,40},{32,48},{40,56},{48,0},{56,8},{64,80... | collective-permute-start | bytes 393224 | tf_op jit(solution)/shard_map/ppermute | solution.py:28
  55.7 1.6 %collective-permute-start.13 = (bf16[64,1024]{1,0:T(8,128)(2,1)S(1)}, bf16[64,1024]{1,0:T(8,128)(2,1)S(1)}, u32[]{:S(2)}, u32[]{:S(2)}) collective-permute-start(bf16[64,1024]{1,0:T(8,128)(2,1)S(1)} %shard_map.91.a0), channel_id=1, source_target_pairs={{0,48},{8,56},{16,0},{24,8},{32,16},{40,24},{48,32},{56,40},{64,11... | collective-permute-start | bytes 393224 | tf_op jit(solution)/shard_map/ppermute | solution.py:28
  57.3 0.0 collective-permute-done.11.a1
  57.3 1.4 %collective-permute-start.15 = (bf16[64,1024]{1,0:T(8,128)(2,1)S(1)}, bf16[64,1024]{1,0:T(8,128)(2,1)S(1)}, u32[]{:S(2)}, u32[]{:S(2)}) collective-permute-start(bf16[64,1024]{1,0:T(8,128)(2,1)S(1)} %collective-permute-done.11.a1), channel_id=1, source_target_pairs={{0,64},{8,72},{16,80},{24,88},{32,96},{40,104},{48,112},{56,120},{... | collective-permute-start | bytes 393224 | tf_op jit(solution)/shard_map/ppermute | solution.py:28
  58.7 0.0 collective-permute-done.14.a4
  58.7 0.4 collective-permute-start.16
  59.1 0.8 collective-permute-done.12.a2
  59.9 1.5 %collective-permute-start.17 = (bf16[64,1024]{1,0:T(8,128)(2,1)S(1)}, bf16[64,1024]{1,0:T(8,128)(2,1)S(1)}, u32[]{:S(2)}, u32[]{:S(2)}) collective-permute-start(bf16[64,1024]{1,0:T(8,128)(2,1)S(1)} %collective-permute-done.14.a4), channel_id=1, source_target_pairs={{0,48},{8,56},{16,0},{24,8},{32,16},{40,24},{48,32},{56,40},{64,11... | collective-permute-start | bytes 393224 | tf_op jit(solution)/shard_map/ppermute | solution.py:28
  61.4 0.0 collective-permute-done.13.a3
  61.4 1.3 %collective-permute-done.15.a5 = bf16[64,1024]{1,0:T(8,128)(2,1)S(1)} collective-permute-done((bf16[64,1024]{1,0:T(8,128)(2,1)S(1)}, bf16[64,1024]{1,0:T(8,128)(2,1)S(1)}, u32[]{:S(2)}, u32[]{:S(2)}) %collective-permute-start.15) | collective-permute-done | bytes 131104 | tf_op jit(solution)/shard_map/ppermute | solution.py:28
  62.7 1.1 %collective-permute-done.16.a6 = bf16[64,1024]{1,0:T(8,128)(2,1)S(1)} collective-permute-done((bf16[64,1024]{1,0:T(8,128)(2,1)S(1)}, bf16[64,1024]{1,0:T(8,128)(2,1)S(1)}, u32[]{:S(2)}, u32[]{:S(2)}) %collective-permute-start.16) | collective-permute-done | bytes 131104 | tf_op jit(solution)/shard_map/ppermute | solution.py:28
  63.8 1.0 %collective-permute-done.17.a7 = bf16[64,1024]{1,0:T(8,128)(2,1)S(1)} collective-permute-done((bf16[64,1024]{1,0:T(8,128)(2,1)S(1)}, bf16[64,1024]{1,0:T(8,128)(2,1)S(1)}, u32[]{:S(2)}, u32[]{:S(2)}) %collective-permute-start.17) | collective-permute-done | bytes 131104 | tf_op jit(solution)/shard_map/ppermute | solution.py:28
  64.8 0.0 collective-permute-done.18.wb
  64.8 1.2 %shard_map.92 = bf16[8,64,1024]{2,1,0:T(8,128)(2,1)S(1)} custom-call(s32[1]{0:T(128)} %bitcast.1.index, bf16[64,1024]{1,0:T(8,128)(2,1)S(1)} %shard_map.91.a0, bf16[64,1024]{1,0:T(8,128)(2,1)S(1)} %collective-permute-done.11.a1, bf16[64,1024]{1,0:T(8,128)(2,1)S(1)} %collective-permute-done.12.a2, bf16[64,1024]{1,0:T(8,128)(2,1)S(1)} %collective-permute-done.13.a3, ...), custom_call_target="tpu_custom_call" | custom-call | tf_op jit(solution)/shard_map/pallas_call | solution.py:308
  66.0 14.8 %all_to_all.5.terms = bf16[8,64,1024]{2,1,0:T(8,128)(2,1)S(1)} all-to-all(bf16[8,64,1024]{2,1,0:T(8,128)(2,1)S(1)} %shard_map.92), channel_id=1, replica_groups=mesh['blk'=16,'head'=8] {'head'}, dimensions={0} | all-to-all | bytes 2097152 | tf_op jit(solution)/shard_map/all_to_all | solution.py:314
  80.8 0.1 shard_map.93
  81.0 5.9 %collective-permute-start.19 = (bf16[64,512]{1,0:T(8,128)(2,1)S(1)}, bf16[64,512]{1,0:T(8,128)(2,1)S(1)}, u32[]{:S(2)}, u32[]{:S(2)}) collective-permute-start(bf16[64,512]{1,0:T(8,128)(2,1)S(1)} %get-tuple-element.86), channel_id=1, source_target_pairs={{0,8},{8,0},{16,24},{24,16},{32,40},{40,32},{48,56},{56,48},{64,72... | collective-permute-start | bytes 196616 | tf_op jit(solution)/shard_map/ppermute | solution.py:28
  86.9 0.9 %collective-permute-done.19.theirs = bf16[64,512]{1,0:T(8,128)(2,1)S(1)} collective-permute-done((bf16[64,512]{1,0:T(8,128)(2,1)S(1)}, bf16[64,512]{1,0:T(8,128)(2,1)S(1)}, u32[]{:S(2)}, u32[]{:S(2)}) %collective-permute-start.19) | collective-permute-done | bytes 65568 | tf_op jit(solution)/shard_map/ppermute | solution.py:28
  87.8 0.7 shard_map.94
Async XLA Ops:
  0.0 1.0 %copy-start.2 = (bf16[2048,128]{1,0:T(8,128)(2,1)S(1)}, bf16[2048,128]{1,0:T(8,128)(2,1)}, u32[]{:S(2)}) copy-start(bf16[2048,128]{1,0:T(8,128)(2,1)} %k.1) | copy-start | bytes 1572868
  1.0 1.0 %copy-start.3 = (bf16[2048,128]{1,0:T(8,128)(2,1)S(1)}, bf16[2048,128]{1,0:T(8,128)(2,1)}, u32[]{:S(2)}) copy-start(bf16[2048,128]{1,0:T(8,128)(2,1)} %v.1) | copy-start | bytes 1572868
  2.2 17.1 %collective-permute-start.3 = (bf16[4096,128]{1,0:T(8,128)(2,1)S(1)}, bf16[4096,128]{1,0:T(8,128)(2,1)S(1)}, u32[]{:S(2)}, u32[]{:S(2)}) collective-permute-start(bf16[4096,128]{1,0:T(8,128)(2,1)S(1)} %get-tuple-element.47.kv), channel_id=1, source_target_pairs={{0,8},{8,0},{16,24},{24,16},{32,40},{40,32},{48,56},{56,48},{64,72... | collective-permute-start | bytes 3145736 | tf_op jit(solution)/shard_map/ppermute | solution.py:28
  3.7 7.9 %collective-permute-start = (bf16[64,1024]{1,0:T(8,128)(2,1)}, bf16[64,1024]{1,0:T(8,128)(2,1)S(1)}, u32[]{:S(2)}, u32[]{:S(2)}) collective-permute-start(bf16[64,1024]{1,0:T(8,128)(2,1)} %q.3), channel_id=1, source_target_pairs={{0,16},{8,24},{16,32},{24,40},{32,48},{40,56},{48,0},{56,8},{64,80... | collective-permute-start | bytes 393224 | tf_op jit(solution)/shard_map/ppermute | solution.py:28
  5.5 21.6 %collective-permute-start.5 = (bf16[1792,128]{1,0:T(8,128)(2,1)S(1)}, bf16[1792,128]{1,0:T(8,128)(2,1)S(1)}, u32[]{:S(2)}, u32[]{:S(2)}) collective-permute-start(bf16[1792,128]{1,0:T(8,128)(2,1)S(1)} %get-tuple-element.52), channel_id=1, source_target_pairs={{0,64},{8,72},{16,80},{24,88},{32,96},{40,104},{48,112},{56,120},{... | collective-permute-start | bytes 1376264 | tf_op jit(solution)/shard_map/ppermute | solution.py:28
  8.2 11.1 %collective-permute-start.1 = (bf16[64,1024]{1,0:T(8,128)(2,1)}, bf16[64,1024]{1,0:T(8,128)(2,1)S(1)}, u32[]{:S(2)}, u32[]{:S(2)}) collective-permute-start(bf16[64,1024]{1,0:T(8,128)(2,1)} %q.3), channel_id=1, source_target_pairs={{0,48},{8,56},{16,0},{24,8},{32,16},{40,24},{48,32},{56,40},{64,11... | collective-permute-start | bytes 393224 | tf_op jit(solution)/shard_map/ppermute | solution.py:28
  10.3 9.0 %collective-permute-start.2 = (bf16[64,1024]{1,0:T(8,128)(2,1)}, bf16[64,1024]{1,0:T(8,128)(2,1)S(1)}, u32[]{:S(2)}, u32[]{:S(2)}) collective-permute-start(bf16[64,1024]{1,0:T(8,128)(2,1)} %q.3), channel_id=1, source_target_pairs={{0,32},{8,40},{16,48},{24,56},{32,0},{40,8},{48,16},{56,24},{64,96... | collective-permute-start | bytes 393224 | tf_op jit(solution)/shard_map/ppermute | solution.py:28
  11.6 22.6 %collective-permute-start.4 = (bf16[2304,128]{1,0:T(8,128)(2,1)S(1)}, bf16[2304,128]{1,0:T(8,128)(2,1)S(1)}, u32[]{:S(2)}, u32[]{:S(2)}) collective-permute-start(bf16[2304,128]{1,0:T(8,128)(2,1)S(1)} %get-tuple-element.51), channel_id=1, source_target_pairs={{0,64},{8,72},{16,80},{24,88},{32,96},{40,104},{48,112},{56,120},{... | collective-permute-start | bytes 1769480 | tf_op jit(solution)/shard_map/ppermute | solution.py:28
  15.9 0.9 %copy-start.1 = (bf16[64,1024]{1,0:T(8,128)(2,1)S(1)}, bf16[64,1024]{1,0:T(8,128)(2,1)}, u32[]{:S(2)}) copy-start(bf16[64,1024]{1,0:T(8,128)(2,1)} %q.3) | copy-start | bytes 393220
  27.1 3.6 %collective-permute-start.6 = (bf16[1792,128]{1,0:T(8,128)(2,1)S(1)}, bf16[1792,128]{1,0:T(8,128)(2,1)S(1)}, u32[]{:S(2)}, u32[]{:S(2)}) collective-permute-start(bf16[1792,128]{1,0:T(8,128)(2,1)S(1)} %collective-permute-done.5.part), channel_id=1, source_target_pairs={{0,8},{8,0},{16,24},{24,16},{32,40},{40,32},{48,56},{56,48},{64,72... | collective-permute-start | bytes 1376264 | tf_op jit(solution)/shard_map/ppermute | solution.py:28
  30.7 3.6 %copy-start = (bf16[1024,512]{1,0:T(8,128)(2,1)S(1)}, bf16[1024,512]{1,0:T(8,128)(2,1)}, u32[]{:S(2)}) copy-start(bf16[1024,512]{1,0:T(8,128)(2,1)} %wa.1) | copy-start | bytes 3145732
  34.2 2.7 %collective-permute-start.7 = (bf16[2304,128]{1,0:T(8,128)(2,1)S(1)}, bf16[2304,128]{1,0:T(8,128)(2,1)S(1)}, u32[]{:S(2)}, u32[]{:S(2)}) collective-permute-start(bf16[2304,128]{1,0:T(8,128)(2,1)S(1)} %collective-permute-done.4.part), channel_id=1, source_target_pairs={{0,8},{8,0},{16,24},{24,16},{32,40},{40,32},{48,56},{56,48},{64,72... | collective-permute-start | bytes 1769480 | tf_op jit(solution)/shard_map/ppermute | solution.py:28
  34.3 30.5 %collective-permute-start.18 = (bf16[1024,512]{1,0:T(8,128)(2,1)S(1)}, bf16[1024,512]{1,0:T(8,128)(2,1)S(1)}, u32[]{:S(2)}, u32[]{:S(2)}) collective-permute-start(bf16[1024,512]{1,0:T(8,128)(2,1)S(1)} %copy-done), channel_id=1, source_target_pairs={{0,8},{8,0},{16,24},{24,16},{32,40},{40,32},{48,56},{56,48},{64,72... | collective-permute-start | bytes 3145736 | tf_op jit(solution)/shard_map/ppermute | solution.py:28
  39.9 8.0 %collective-permute-start.8 = (bf16[144,512]{1,0:T(8,128)(2,1)S(1)}, bf16[144,512]{1,0:T(8,128)(2,1)S(1)}, u32[]{:S(2)}, u32[]{:S(2)}) collective-permute-start(bf16[144,512]{1,0:T(8,128)(2,1)S(1)} %get-tuple-element.74), channel_id=1, source_target_pairs={{0,32},{8,40},{16,48},{24,56},{32,0},{40,8},{48,16},{56,24},{64,96... | collective-permute-start | bytes 442376 | tf_op jit(solution)/shard_map/ppermute | solution.py:28
  44.4 6.2 %collective-permute-start.10 = (bf16[144,512]{1,0:T(8,128)(2,1)S(1)}, bf16[144,512]{1,0:T(8,128)(2,1)S(1)}, u32[]{:S(2)}, u32[]{:S(2)}) collective-permute-start(bf16[144,512]{1,0:T(8,128)(2,1)S(1)} %get-tuple-element.79), channel_id=1, source_target_pairs={{0,16},{8,24},{16,32},{24,40},{32,48},{40,56},{48,0},{56,8},{64,80... | collective-permute-start | bytes 442376 | tf_op jit(solution)/shard_map/ppermute | solution.py:28
  45.7 4.9 %collective-permute-start.9 = (bf16[144,512]{1,0:T(8,128)(2,1)S(1)}, bf16[144,512]{1,0:T(8,128)(2,1)S(1)}, u32[]{:S(2)}, u32[]{:S(2)}) collective-permute-start(bf16[144,512]{1,0:T(8,128)(2,1)S(1)} %get-tuple-element.78), channel_id=1, source_target_pairs={{0,48},{8,56},{16,0},{24,8},{32,16},{40,24},{48,32},{56,40},{64,11... | collective-permute-start | bytes 442376 | tf_op jit(solution)/shard_map/ppermute | solution.py:28
  50.8 6.5 %collective-permute-start.11 = (bf16[64,1024]{1,0:T(8,128)(2,1)S(1)}, bf16[64,1024]{1,0:T(8,128)(2,1)S(1)}, u32[]{:S(2)}, u32[]{:S(2)}) collective-permute-start(bf16[64,1024]{1,0:T(8,128)(2,1)S(1)} %shard_map.91.a0), channel_id=1, source_target_pairs={{0,32},{8,40},{16,48},{24,56},{32,0},{40,8},{48,16},{56,24},{64,96... | collective-permute-start | bytes 393224 | tf_op jit(solution)/shard_map/ppermute | solution.py:28
  52.0 6.7 %collective-permute-start.14 = (bf16[64,1024]{1,0:T(8,128)(2,1)S(1)}, bf16[64,1024]{1,0:T(8,128)(2,1)S(1)}, u32[]{:S(2)}, u32[]{:S(2)}) collective-permute-start(bf16[64,1024]{1,0:T(8,128)(2,1)S(1)} %shard_map.91.a0), channel_id=1, source_target_pairs={{0,64},{8,72},{16,80},{24,88},{32,96},{40,104},{48,112},{56,120},{... | collective-permute-start | bytes 393224 | tf_op jit(solution)/shard_map/ppermute | solution.py:28
  54.7 5.3 %collective-permute-start.12 = (bf16[64,1024]{1,0:T(8,128)(2,1)S(1)}, bf16[64,1024]{1,0:T(8,128)(2,1)S(1)}, u32[]{:S(2)}, u32[]{:S(2)}) collective-permute-start(bf16[64,1024]{1,0:T(8,128)(2,1)S(1)} %shard_map.91.a0), channel_id=1, source_target_pairs={{0,16},{8,24},{16,32},{24,40},{32,48},{40,56},{48,0},{56,8},{64,80... | collective-permute-start | bytes 393224 | tf_op jit(solution)/shard_map/ppermute | solution.py:28
  55.7 5.7 %collective-permute-start.13 = (bf16[64,1024]{1,0:T(8,128)(2,1)S(1)}, bf16[64,1024]{1,0:T(8,128)(2,1)S(1)}, u32[]{:S(2)}, u32[]{:S(2)}) collective-permute-start(bf16[64,1024]{1,0:T(8,128)(2,1)S(1)} %shard_map.91.a0), channel_id=1, source_target_pairs={{0,48},{8,56},{16,0},{24,8},{32,16},{40,24},{48,32},{56,40},{64,11... | collective-permute-start | bytes 393224 | tf_op jit(solution)/shard_map/ppermute | solution.py:28
  57.3 5.3 %collective-permute-start.15 = (bf16[64,1024]{1,0:T(8,128)(2,1)S(1)}, bf16[64,1024]{1,0:T(8,128)(2,1)S(1)}, u32[]{:S(2)}, u32[]{:S(2)}) collective-permute-start(bf16[64,1024]{1,0:T(8,128)(2,1)S(1)} %collective-permute-done.11.a1), channel_id=1, source_target_pairs={{0,64},{8,72},{16,80},{24,88},{32,96},{40,104},{48,112},{56,120},{... | collective-permute-start | bytes 393224 | tf_op jit(solution)/shard_map/ppermute | solution.py:28
  58.7 5.0 %collective-permute-start.16 = (bf16[64,1024]{1,0:T(8,128)(2,1)S(1)}, bf16[64,1024]{1,0:T(8,128)(2,1)S(1)}, u32[]{:S(2)}, u32[]{:S(2)}) collective-permute-start(bf16[64,1024]{1,0:T(8,128)(2,1)S(1)} %collective-permute-done.14.a4), channel_id=1, source_target_pairs={{0,16},{8,24},{16,32},{24,40},{32,48},{40,56},{48,0},{56,8},{64,80... | collective-permute-start | bytes 393224 | tf_op jit(solution)/shard_map/ppermute | solution.py:28
  59.9 4.9 %collective-permute-start.17 = (bf16[64,1024]{1,0:T(8,128)(2,1)S(1)}, bf16[64,1024]{1,0:T(8,128)(2,1)S(1)}, u32[]{:S(2)}, u32[]{:S(2)}) collective-permute-start(bf16[64,1024]{1,0:T(8,128)(2,1)S(1)} %collective-permute-done.14.a4), channel_id=1, source_target_pairs={{0,48},{8,56},{16,0},{24,8},{32,16},{40,24},{48,32},{56,40},{64,11... | collective-permute-start | bytes 393224 | tf_op jit(solution)/shard_map/ppermute | solution.py:28
  81.0 6.8 %collective-permute-start.19 = (bf16[64,512]{1,0:T(8,128)(2,1)S(1)}, bf16[64,512]{1,0:T(8,128)(2,1)S(1)}, u32[]{:S(2)}, u32[]{:S(2)}) collective-permute-start(bf16[64,512]{1,0:T(8,128)(2,1)S(1)} %get-tuple-element.86), channel_id=1, source_target_pairs={{0,8},{8,0},{16,24},{24,16},{32,40},{40,32},{48,56},{56,48},{64,72... | collective-permute-start | bytes 196616 | tf_op jit(solution)/shard_map/ppermute | solution.py:28

commit v15 on v14

--- a/solution.py
+++ b/solution.py
@@ -127,26 +127,25 @@
     )
 
 
-def own_kernel(q, qkv, bias, kv, top_out, total_out, k, v):
-    split((kv,), k, v)
-    rows = stacked(q)
-    scores = scores_of(rows, qkv[:ROWS, :]) + jnp.concatenate([bias[...]] * GROUP, axis=0)
-    block = scores_of(rows, k[...])
-    top, total = add_block(
+def near_kernel(
+    q0, q1, q2, q, qkv, bias, kv, kv_c,
+    top_out, total_out, own_top, own_total, rows, k1, v1, k0, v0,
+):
+    split((kv,), k0, v0)
+    split((kv_c,), k1, v1)
+    for i, ref in enumerate((q0, q1, q2, q)):
+        rows[i] = stacked(ref)
+    scores = scores_of(rows[3], qkv[:ROWS, :]) + jnp.concatenate([bias[...]] * GROUP, axis=0)
+    own = add_block(
         *empty(),
         scores,
         jnp.concatenate([qkv[ROWS:, :], jnp.ones((ROWS, DH), jnp.bfloat16)], axis=1),
     )
-    top_out[...], total_out[...] = add_block(top, total, block, v[...])
-
-
-def near_kernel(q0, q1, q2, q, k0, v0, kv_c, top_out, total_out, rows, k1, v1):
-    split((kv_c,), k1, v1)
-    for i, ref in enumerate((q0, q1, q2, q)):
-        rows[i] = stacked(ref)
-    tasks = [(i, rows.at[i], k, v) for k, v in ((k0, v0), (k1, v1)) for i in range(3)]
-    for i, (top, total) in enumerate(run(tasks, [empty() for _ in range(3)])):
-        top_out[i], total_out[i] = top, total
+    tasks = [(i, rows.at[i], k0, v0) for i in range(4)] + [(i, rows.at[i], k1, v1) for i in range(3)]
+    states = run(tasks, [empty() for _ in range(3)] + [own])
+    for i in range(3):
+        top_out[i], total_out[i] = states[i]
+    own_top[...], own_total[...] = states[3]
 
 
 def others_kernel(rows, top_in, total_in, part, other_part, top_out, total_out, k, v):
@@ -266,12 +265,12 @@
     def layout(size):
         return [((size, DH), bf16), ((size, 2 * DH), bf16)]
 
-    own_top, own_total, *block = call(own_kernel, own_state + layout(positions))(
-        queries, jnp.concatenate([question_keys, question_values]), bias, after(kv, q_z[0])
-    )
-    top, total, rows, *block = call(
-        near_kernel, state + [((4, LANES, DH), bf16)] + layout(positions), flops=1
-    )(*q_z, queries, *block, kv_c)
+    top, total, own_top, own_total, rows, *block = call(
+        near_kernel,
+        state + own_state + [((4, LANES, DH), bf16)] + layout(positions),
+        [pltpu.VMEM((positions, DH), bf16), pltpu.VMEM((positions, 2 * DH), bf16)],
+        flops=1,
+    )(*q_z, queries, jnp.concatenate([question_keys, question_values]), bias, kv, kv_c)
     x0, top = lax.optimization_barrier((x0, top))
     xc0 = moved(x0, c=1)
     own_top, own_total = call(own_more_kernel, own_state, flops=block_flops)(

time: 88.8 us -> 88.7 us (level)
  Pallas kernels: 29.3 us -> 28.2 us
    pallas_call x2 -> x1, Pallas kernels: 10.3 us -> 9.15 us  [shards(): call(near_kernel, state + own_state + [((4, LANES, DH), bf16)] + layout(p...]
  transfers between devices with their start and end apart: 20 -> 20, of which waited for: 5 -> 7; matrix products, arithmetic and copies ran while one was open for 2% -> 2% of each run, Pallas kernels for 31% -> 29%
where the time goes in v15:
time: 88.7 us; the launch traced here: 88.3 us
  starting transfers between devices  34.6 us (39%)
  Pallas kernels  28.2 us (32%)
  blocking collectives  15.1 us (17%)
  waiting for transfers between devices  5.08 us (6%)
  local copies, waits for them, and re-layouts  2.99 us (3%)
  other arithmetic  1.54 us (2%)
    ppermute x20, starting transfers between devices, moved(): return lax.ppermute(array, 'blk', pairs)  34.6 us
    all_to_all x1, blocking collectives, shards(): gathered = lax.all_to_all(terms, 'head', 0, 0, tiled=True)  15.1 us
    pallas_call x1, Pallas kernels, shards(): call(near_kernel, state + own_state + [((4, LANES, DH), bf16)] + layout(p...  9.15 us
    ppermute x20, waiting for transfers between devices, moved(): return lax.ppermute(array, 'blk', pairs)  5.08 us
    pallas_call x1, Pallas kernels, shards(): call(others_kernel, state + layout(2 * early), flops=1)  3.49 us
    unnamed x8, local copies, waits for them, and re-layouts  2.99 us
    pallas_call x1, Pallas kernels, shards(): call(next_kernel, [part] * 2, flops=4 * block_flops)  2.95 us
    pallas_call x1, Pallas kernels, shards(): call(far_kernel, [part] + layout(2 * late), flops=1)  2.92 us
  transfers between devices with their start and end apart: 20, of which 7 were waited for; matrix products, arithmetic and copies ran while one was open for 2% of the time, Pallas kernels for 29%

profile of v15, /device:TPU:1, one launch (start us, length us, event | category | flops | bytes accessed | tf_op | source)
XLA Modules:
  0.0 88.3 jit_solution(13048930855043218802)
XLA Ops:
  0.0 0.0 copy-start.1
  0.0 1.0 %copy-done.1 = bf16[2048,128]{1,0:T(8,128)(2,1)S(1)} copy-done((bf16[2048,128]{1,0:T(8,128)(2,1)S(1)}, bf16[2048,128]{1,0:T(8,128)(2,1)}, u32[]{:S(2)}) %copy-start.1) | copy-done | bytes 524312
  1.0 0.0 copy-start.2
  1.0 1.0 %copy-done.2 = bf16[2048,128]{1,0:T(8,128)(2,1)S(1)} copy-done((bf16[2048,128]{1,0:T(8,128)(2,1)S(1)}, bf16[2048,128]{1,0:T(8,128)(2,1)}, u32[]{:S(2)}) %copy-start.2) | copy-done | bytes 524312
  2.1 0.1 shard_map.82
  2.2 1.5 %collective-permute-start.3 = (bf16[4096,128]{1,0:T(8,128)(2,1)S(1)}, bf16[4096,128]{1,0:T(8,128)(2,1)S(1)}, u32[]{:S(2)}, u32[]{:S(2)}) collective-permute-start(bf16[4096,128]{1,0:T(8,128)(2,1)S(1)} %get-tuple-element.43.kv), channel_id=1, source_target_pairs={{0,8},{8,0},{16,24},{24,16},{32,40},{40,32},{48,56},{56,48},{64,72... | collective-permute-start | bytes 3145736 | tf_op jit(solution)/shard_map/ppermute | solution.py:28
  3.7 1.7 %collective-permute-start = (bf16[64,1024]{1,0:T(8,128)(2,1)}, bf16[64,1024]{1,0:T(8,128)(2,1)S(1)}, u32[]{:S(2)}, u32[]{:S(2)}) collective-permute-start(bf16[64,1024]{1,0:T(8,128)(2,1)} %q.1), channel_id=1, source_target_pairs={{0,16},{8,24},{16,32},{24,40},{32,48},{40,56},{48,0},{56,8},{64,80... | collective-permute-start | bytes 393224 | tf_op jit(solution)/shard_map/ppermute | solution.py:28
  5.5 2.7 %collective-permute-start.5 = (bf16[1792,128]{1,0:T(8,128)(2,1)S(1)}, bf16[1792,128]{1,0:T(8,128)(2,1)S(1)}, u32[]{:S(2)}, u32[]{:S(2)}) collective-permute-start(bf16[1792,128]{1,0:T(8,128)(2,1)S(1)} %get-tuple-element.46), channel_id=1, source_target_pairs={{0,64},{8,72},{16,80},{24,88},{32,96},{40,104},{48,112},{56,120},{... | collective-permute-start | bytes 1376264 | tf_op jit(solution)/shard_map/ppermute | solution.py:28
  8.2 2.1 %collective-permute-start.1 = (bf16[64,1024]{1,0:T(8,128)(2,1)}, bf16[64,1024]{1,0:T(8,128)(2,1)S(1)}, u32[]{:S(2)}, u32[]{:S(2)}) collective-permute-start(bf16[64,1024]{1,0:T(8,128)(2,1)} %q.1), channel_id=1, source_target_pairs={{0,48},{8,56},{16,0},{24,8},{32,16},{40,24},{48,32},{56,40},{64,11... | collective-permute-start | bytes 393224 | tf_op jit(solution)/shard_map/ppermute | solution.py:28
  10.3 1.3 %collective-permute-start.2 = (bf16[64,1024]{1,0:T(8,128)(2,1)}, bf16[64,1024]{1,0:T(8,128)(2,1)S(1)}, u32[]{:S(2)}, u32[]{:S(2)}) collective-permute-start(bf16[64,1024]{1,0:T(8,128)(2,1)} %q.1), channel_id=1, source_target_pairs={{0,32},{8,40},{16,48},{24,56},{32,0},{40,8},{48,16},{56,24},{64,96... | collective-permute-start | bytes 393224 | tf_op jit(solution)/shard_map/ppermute | solution.py:28
  11.6 0.0 collective-permute-done.q0
  11.6 2.7 %collective-permute-start.4 = (bf16[2304,128]{1,0:T(8,128)(2,1)S(1)}, bf16[2304,128]{1,0:T(8,128)(2,1)S(1)}, u32[]{:S(2)}, u32[]{:S(2)}) collective-permute-start(bf16[2304,128]{1,0:T(8,128)(2,1)S(1)} %get-tuple-element.45), channel_id=1, source_target_pairs={{0,64},{8,72},{16,80},{24,88},{32,96},{40,104},{48,112},{56,120},{... | collective-permute-start | bytes 1769480 | tf_op jit(solution)/shard_map/ppermute | solution.py:28
  14.3 0.8 fusion.1.bias
  15.1 0.7 pad_maximum_fusion.qkv
  15.9 0.0 collective-permute-done.1.q1
  15.9 0.5 collective-permute-done.2.q2
  16.3 0.0 collective-permute-done.3.kv_c
  16.3 0.0 copy-start.3
  16.3 0.9 %copy-done.3 = bf16[64,1024]{1,0:T(8,128)(2,1)S(1)} copy-done((bf16[64,1024]{1,0:T(8,128)(2,1)S(1)}, bf16[64,1024]{1,0:T(8,128)(2,1)}, u32[]{:S(2)}) %copy-start.3) | copy-done | bytes 131096
  17.2 9.1 %shard_map.83 = (f32[3,512,128]{2,1,0:T(8,128)S(1)}, f32[3,512,256]{2,1,0:T(8,128)S(1)}, f32[512,128]{1,0:T(8,128)S(1)}, f32[512,256]{1,0:T(8,128)S(1)}, bf16[4,...) custom-call(bf16[64,1024]{1,0:T(8,128)(2,1)S(1)} %collective-permute-done.q0, ...), custom_call_target="tpu_custom_call" | custom-call | flops 1 | tf_op jit(solution)/shard_map/pallas_call | solution.py:268
  26.4 0.0 collective-permute-done.5.part
  26.4 1.9 %collective-permute-start.6 = (bf16[1792,128]{1,0:T(8,128)(2,1)S(1)}, bf16[1792,128]{1,0:T(8,128)(2,1)S(1)}, u32[]{:S(2)}, u32[]{:S(2)}) collective-permute-start(bf16[1792,128]{1,0:T(8,128)(2,1)S(1)} %collective-permute-done.5.part), channel_id=1, source_target_pairs={{0,8},{8,0},{16,24},{24,16},{32,40},{40,32},{48,56},{56,48},{64,72... | collective-permute-start | bytes 1376264 | tf_op jit(solution)/shard_map/ppermute | solution.py:28
  28.3 2.4 %shard_map.84 = (f32[512,128]{1,0:T(8,128)S(1)}, f32[512,256]{1,0:T(8,128)S(1)}) custom-call(bf16[4,512,128]{2,1,0:T(8,128)(2,1)S(1)} %get-tuple-element.74.rows, f32[512,128]{1,0:T(8,128)S(1)} %get-tuple-element.51.top, f32[512,256]{1,0:T(8,128)S(1)} %get-tuple-element.52.total, bf16[2048,128]{1,0:T(8,128)(2,1)S(1)} %get-tuple-element.53.k, ...), custom_call_target="tpu_custom_call" | custom-call | flops 1073741824 | tf_op jit(solution)/shard_map/pallas_call | solution.py:276
  30.7 0.0 collective-permute-done.6.other_part
  30.7 0.0 copy-start
  30.7 3.5 %shard_map.85 = (f32[3,512,128]{2,1,0:T(8,128)S(1)}, f32[3,512,256]{2,1,0:T(8,128)S(1)}, bf16[1792,128]{1,0:T(8,128)(2,1)S(1)}, bf16[1792,256]{1,0:T(8,128)(2,1)S(1)}) custom-call(bf16[4,512,128]{2,1,0:T(8,128)(2,1)S(1)} %get-tuple-element.74.rows, f32[3,512,128]{2,1,0:T(8,128)S(1)} %get-tuple-element.56.top_in, ...), custom_call_target="tpu_custom_call" | custom-call | flops 1 | tf_op jit(solution)/shard_map/pallas_call | solution.py:279
  34.2 0.0 collective-permute-done.4.part
  34.2 0.1 collective-permute-start.7
  34.3 0.0 copy-done
  34.3 0.5 collective-permute-start.18
  34.8 2.1 %shard_map.86 = (f32[512,128]{1,0:T(8,128)S(1)}, f32[512,256]{1,0:T(8,128)S(1)}) custom-call(bf16[4,512,128]{2,1,0:T(8,128)(2,1)S(1)} %get-tuple-element.74.rows, f32[512,128]{1,0:T(8,128)S(1)} %get-tuple-element.55.top, f32[512,256]{1,0:T(8,128)S(1)} %get-tuple-element.62.total, bf16[1792,128]{1,0:T(8,128)(2,1)S(1)} %get-tuple-element.63.k, ...), custom_call_target="tpu_custom_call" | custom-call | flops 2147483648 | tf_op jit(solution)/shard_map/pallas_call | solution.py:286
  36.9 0.0 collective-permute-done.7.other_part
  36.9 2.9 %shard_map.87 = (bf16[144,512]{1,0:T(8,128)(2,1)S(1)}, bf16[2304,128]{1,0:T(8,128)(2,1)S(1)}, bf16[2304,256]{1,0:T(8,128)(2,1)S(1)}) custom-call(bf16[4,512,128]{2,1,0:T(8,128)(2,1)S(1)} %get-tuple-element.74.rows, f32[3,512,128]{2,1,0:T(8,128)S(1)} %get-tuple-element.69.top, f32[3,512,256]{2,1,0:T(8,128)S(1)} %get-tuple-element.67.total, ...), custom_call_target="tpu_custom_call" | custom-call | flops 1 | tf_op jit(solution)/shard_map/pallas_call | solution.py:289
  39.9 1.6 %collective-permute-start.8 = (bf16[144,512]{1,0:T(8,128)(2,1)S(1)}, bf16[144,512]{1,0:T(8,128)(2,1)S(1)}, u32[]{:S(2)}, u32[]{:S(2)}) collective-permute-start(bf16[144,512]{1,0:T(8,128)(2,1)S(1)} %get-tuple-element.68), channel_id=1, source_target_pairs={{0,32},{8,40},{16,48},{24,56},{32,0},{40,8},{48,16},{56,24},{64,96... | collective-permute-start | bytes 442376 | tf_op jit(solution)/shard_map/ppermute | solution.py:28
  41.5 2.9 %shard_map.88 = (bf16[144,512]{1,0:T(8,128)(2,1)S(1)}, bf16[144,512]{1,0:T(8,128)(2,1)S(1)}) custom-call(bf16[4,512,128]{2,1,0:T(8,128)(2,1)S(1)} %get-tuple-element.74.rows, f32[3,512,128]{2,1,0:T(8,128)S(1)} %get-tuple-element.69.top, f32[3,512,256]{2,1,0:T(8,128)S(1)} %get-tuple-element.67.total, bf16[2304,128]{1,0:T(8,128)(2,1)S(1)} %get-tuple-element.70.k, ...), custom_call_target="tpu_custom_call" | custom-call | flops 4294967296 | tf_op jit(solution)/shard_map/pallas_call | solution.py:292
  44.4 1.9 %collective-permute-start.10 = (bf16[144,512]{1,0:T(8,128)(2,1)S(1)}, bf16[144,512]{1,0:T(8,128)(2,1)S(1)}, u32[]{:S(2)}, u32[]{:S(2)}) collective-permute-start(bf16[144,512]{1,0:T(8,128)(2,1)S(1)} %get-tuple-element.73), channel_id=1, source_target_pairs={{0,16},{8,24},{16,32},{24,40},{32,48},{40,56},{48,0},{56,8},{64,80... | collective-permute-start | bytes 442376 | tf_op jit(solution)/shard_map/ppermute | solution.py:28
  46.3 1.3 %collective-permute-start.9 = (bf16[144,512]{1,0:T(8,128)(2,1)S(1)}, bf16[144,512]{1,0:T(8,128)(2,1)S(1)}, u32[]{:S(2)}, u32[]{:S(2)}) collective-permute-start(bf16[144,512]{1,0:T(8,128)(2,1)S(1)} %get-tuple-element.72), channel_id=1, source_target_pairs={{0,48},{8,56},{16,0},{24,8},{32,16},{40,24},{48,32},{56,40},{64,11... | collective-permute-start | bytes 442376 | tf_op jit(solution)/shard_map/ppermute | solution.py:28
  48.2 0.0 collective-permute-done.8.r2
  48.2 2.8 %shard_map.89 = (f32[128,512]{1,0:T(8,128)S(1)}, f32[8,512]{1,0:T(8,128)S(1)}) custom-call(bf16[4,512,128]{2,1,0:T(8,128)(2,1)S(1)} %get-tuple-element.74.rows, f32[512,128]{1,0:T(8,128)S(1)} %get-tuple-element.65.top, f32[512,256]{1,0:T(8,128)S(1)} %get-tuple-element.75.total, bf16[2304,128]{1,0:T(8,128)(2,1)S(1)} %get-tuple-element.70.k, ...), custom_call_target="tpu_custom_call" | custom-call | flops 1 | tf_op jit(solution)/shard_map/pallas_call | solution.py:296
  51.0 0.3 collective-permute-done.10.r1
  51.3 0.0 collective-permute-done.9.r0
  51.3 0.2 shard_map.90.a0
  51.5 2.2 %collective-permute-start.11 = (bf16[64,1024]{1,0:T(8,128)(2,1)S(1)}, bf16[64,1024]{1,0:T(8,128)(2,1)S(1)}, u32[]{:S(2)}, u32[]{:S(2)}) collective-permute-start(bf16[64,1024]{1,0:T(8,128)(2,1)S(1)} %shard_map.90.a0), channel_id=1, source_target_pairs={{0,32},{8,40},{16,48},{24,56},{32,0},{40,8},{48,16},{56,24},{64,96... | collective-permute-start | bytes 393224 | tf_op jit(solution)/shard_map/ppermute | solution.py:28
  53.7 1.0 %collective-permute-start.14 = (bf16[64,1024]{1,0:T(8,128)(2,1)S(1)}, bf16[64,1024]{1,0:T(8,128)(2,1)S(1)}, u32[]{:S(2)}, u32[]{:S(2)}) collective-permute-start(bf16[64,1024]{1,0:T(8,128)(2,1)S(1)} %shard_map.90.a0), channel_id=1, source_target_pairs={{0,64},{8,72},{16,80},{24,88},{32,96},{40,104},{48,112},{56,120},{... | collective-permute-start | bytes 393224 | tf_op jit(solution)/shard_map/ppermute | solution.py:28
  54.7 1.0 %collective-permute-start.12 = (bf16[64,1024]{1,0:T(8,128)(2,1)S(1)}, bf16[64,1024]{1,0:T(8,128)(2,1)S(1)}, u32[]{:S(2)}, u32[]{:S(2)}) collective-permute-start(bf16[64,1024]{1,0:T(8,128)(2,1)S(1)} %shard_map.90.a0), channel_id=1, source_target_pairs={{0,16},{8,24},{16,32},{24,40},{32,48},{40,56},{48,0},{56,8},{64,80... | collective-permute-start | bytes 393224 | tf_op jit(solution)/shard_map/ppermute | solution.py:28
  55.7 1.7 %collective-permute-start.13 = (bf16[64,1024]{1,0:T(8,128)(2,1)S(1)}, bf16[64,1024]{1,0:T(8,128)(2,1)S(1)}, u32[]{:S(2)}, u32[]{:S(2)}) collective-permute-start(bf16[64,1024]{1,0:T(8,128)(2,1)S(1)} %shard_map.90.a0), channel_id=1, source_target_pairs={{0,48},{8,56},{16,0},{24,8},{32,16},{40,24},{48,32},{56,40},{64,11... | collective-permute-start | bytes 393224 | tf_op jit(solution)/shard_map/ppermute | solution.py:28
  57.4 0.0 collective-permute-done.11.a1
  57.4 2.0 %collective-permute-start.15 = (bf16[64,1024]{1,0:T(8,128)(2,1)S(1)}, bf16[64,1024]{1,0:T(8,128)(2,1)S(1)}, u32[]{:S(2)}, u32[]{:S(2)}) collective-permute-start(bf16[64,1024]{1,0:T(8,128)(2,1)S(1)} %collective-permute-done.11.a1), channel_id=1, source_target_pairs={{0,64},{8,72},{16,80},{24,88},{32,96},{40,104},{48,112},{56,120},{... | collective-permute-start | bytes 393224 | tf_op jit(solution)/shard_map/ppermute | solution.py:28
  59.3 0.0 collective-permute-done.14.a4
  59.4 0.6 collective-permute-start.16
  60.0 0.8 collective-permute-done.12.a2
  60.8 1.2 %collective-permute-start.17 = (bf16[64,1024]{1,0:T(8,128)(2,1)S(1)}, bf16[64,1024]{1,0:T(8,128)(2,1)S(1)}, u32[]{:S(2)}, u32[]{:S(2)}) collective-permute-start(bf16[64,1024]{1,0:T(8,128)(2,1)S(1)} %collective-permute-done.14.a4), channel_id=1, source_target_pairs={{0,48},{8,56},{16,0},{24,8},{32,16},{40,24},{48,32},{56,40},{64,11... | collective-permute-start | bytes 393224 | tf_op jit(solution)/shard_map/ppermute | solution.py:28
  62.0 0.0 collective-permute-done.13.a3
  62.0 0.7 collective-permute-done.15.a5
  62.7 1.7 %collective-permute-done.16.a6 = bf16[64,1024]{1,0:T(8,128)(2,1)S(1)} collective-permute-done((bf16[64,1024]{1,0:T(8,128)(2,1)S(1)}, bf16[64,1024]{1,0:T(8,128)(2,1)S(1)}, u32[]{:S(2)}, u32[]{:S(2)}) %collective-permute-start.16) | collective-permute-done | bytes 131104 | tf_op jit(solution)/shard_map/ppermute | solution.py:28
  64.4 0.2 collective-permute-done.17.a7
  64.6 0.0 collective-permute-done.18.wb
  64.6 1.2 %shard_map.91 = bf16[8,64,1024]{2,1,0:T(8,128)(2,1)S(1)} custom-call(s32[1]{0:T(128)} %bitcast.1.index, bf16[64,1024]{1,0:T(8,128)(2,1)S(1)} %shard_map.90.a0, bf16[64,1024]{1,0:T(8,128)(2,1)S(1)} %collective-permute-done.11.a1, bf16[64,1024]{1,0:T(8,128)(2,1)S(1)} %collective-permute-done.12.a2, bf16[64,1024]{1,0:T(8,128)(2,1)S(1)} %collective-permute-done.13.a3, ...), custom_call_target="tpu_custom_call" | custom-call | tf_op jit(solution)/shard_map/pallas_call | solution.py:307
  65.9 15.1 %all_to_all.5.terms = bf16[8,64,1024]{2,1,0:T(8,128)(2,1)S(1)} all-to-all(bf16[8,64,1024]{2,1,0:T(8,128)(2,1)S(1)} %shard_map.91), channel_id=1, replica_groups=mesh['blk'=16,'head'=8] {'head'}, dimensions={0} | all-to-all | bytes 2097152 | tf_op jit(solution)/shard_map/all_to_all | solution.py:313
  81.0 0.1 shard_map.92
  81.1 5.6 %collective-permute-start.19 = (bf16[64,512]{1,0:T(8,128)(2,1)S(1)}, bf16[64,512]{1,0:T(8,128)(2,1)S(1)}, u32[]{:S(2)}, u32[]{:S(2)}) collective-permute-start(bf16[64,512]{1,0:T(8,128)(2,1)S(1)} %get-tuple-element.80), channel_id=1, source_target_pairs={{0,8},{8,0},{16,24},{24,16},{32,40},{40,32},{48,56},{56,48},{64,72... | collective-permute-start | bytes 196616 | tf_op jit(solution)/shard_map/ppermute | solution.py:28
  86.7 0.9 %collective-permute-done.19.theirs = bf16[64,512]{1,0:T(8,128)(2,1)S(1)} collective-permute-done((bf16[64,512]{1,0:T(8,128)(2,1)S(1)}, bf16[64,512]{1,0:T(8,128)(2,1)S(1)}, u32[]{:S(2)}, u32[]{:S(2)}) %collective-permute-start.19) | collective-permute-done | bytes 65568 | tf_op jit(solution)/shard_map/ppermute | solution.py:28
  87.6 0.7 shard_map.93
Async XLA Ops:
  0.0 1.0 %copy-start.1 = (bf16[2048,128]{1,0:T(8,128)(2,1)S(1)}, bf16[2048,128]{1,0:T(8,128)(2,1)}, u32[]{:S(2)}) copy-start(bf16[2048,128]{1,0:T(8,128)(2,1)} %k.1) | copy-start | bytes 1572868
  1.0 1.0 %copy-start.2 = (bf16[2048,128]{1,0:T(8,128)(2,1)S(1)}, bf16[2048,128]{1,0:T(8,128)(2,1)}, u32[]{:S(2)}) copy-start(bf16[2048,128]{1,0:T(8,128)(2,1)} %v.1) | copy-start | bytes 1572868
  2.2 14.1 %collective-permute-start.3 = (bf16[4096,128]{1,0:T(8,128)(2,1)S(1)}, bf16[4096,128]{1,0:T(8,128)(2,1)S(1)}, u32[]{:S(2)}, u32[]{:S(2)}) collective-permute-start(bf16[4096,128]{1,0:T(8,128)(2,1)S(1)} %get-tuple-element.43.kv), channel_id=1, source_target_pairs={{0,8},{8,0},{16,24},{24,16},{32,40},{40,32},{48,56},{56,48},{64,72... | collective-permute-start | bytes 3145736 | tf_op jit(solution)/shard_map/ppermute | solution.py:28
  3.7 7.9 %collective-permute-start = (bf16[64,1024]{1,0:T(8,128)(2,1)}, bf16[64,1024]{1,0:T(8,128)(2,1)S(1)}, u32[]{:S(2)}, u32[]{:S(2)}) collective-permute-start(bf16[64,1024]{1,0:T(8,128)(2,1)} %q.1), channel_id=1, source_target_pairs={{0,16},{8,24},{16,32},{24,40},{32,48},{40,56},{48,0},{56,8},{64,80... | collective-permute-start | bytes 393224 | tf_op jit(solution)/shard_map/ppermute | solution.py:28
  5.5 20.9 %collective-permute-start.5 = (bf16[1792,128]{1,0:T(8,128)(2,1)S(1)}, bf16[1792,128]{1,0:T(8,128)(2,1)S(1)}, u32[]{:S(2)}, u32[]{:S(2)}) collective-permute-start(bf16[1792,128]{1,0:T(8,128)(2,1)S(1)} %get-tuple-element.46), channel_id=1, source_target_pairs={{0,64},{8,72},{16,80},{24,88},{32,96},{40,104},{48,112},{56,120},{... | collective-permute-start | bytes 1376264 | tf_op jit(solution)/shard_map/ppermute | solution.py:28
  8.2 7.6 %collective-permute-start.1 = (bf16[64,1024]{1,0:T(8,128)(2,1)}, bf16[64,1024]{1,0:T(8,128)(2,1)S(1)}, u32[]{:S(2)}, u32[]{:S(2)}) collective-permute-start(bf16[64,1024]{1,0:T(8,128)(2,1)} %q.1), channel_id=1, source_target_pairs={{0,48},{8,56},{16,0},{24,8},{32,16},{40,24},{48,32},{56,40},{64,11... | collective-permute-start | bytes 393224 | tf_op jit(solution)/shard_map/ppermute | solution.py:28
  10.3 6.0 %collective-permute-start.2 = (bf16[64,1024]{1,0:T(8,128)(2,1)}, bf16[64,1024]{1,0:T(8,128)(2,1)S(1)}, u32[]{:S(2)}, u32[]{:S(2)}) collective-permute-start(bf16[64,1024]{1,0:T(8,128)(2,1)} %q.1), channel_id=1, source_target_pairs={{0,32},{8,40},{16,48},{24,56},{32,0},{40,8},{48,16},{56,24},{64,96... | collective-permute-start | bytes 393224 | tf_op jit(solution)/shard_map/ppermute | solution.py:28
  11.6 22.6 %collective-permute-start.4 = (bf16[2304,128]{1,0:T(8,128)(2,1)S(1)}, bf16[2304,128]{1,0:T(8,128)(2,1)S(1)}, u32[]{:S(2)}, u32[]{:S(2)}) collective-permute-start(bf16[2304,128]{1,0:T(8,128)(2,1)S(1)} %get-tuple-element.45), channel_id=1, source_target_pairs={{0,64},{8,72},{16,80},{24,88},{32,96},{40,104},{48,112},{56,120},{... | collective-permute-start | bytes 1769480 | tf_op jit(solution)/shard_map/ppermute | solution.py:28
  16.3 0.9 %copy-start.3 = (bf16[64,1024]{1,0:T(8,128)(2,1)S(1)}, bf16[64,1024]{1,0:T(8,128)(2,1)}, u32[]{:S(2)}) copy-start(bf16[64,1024]{1,0:T(8,128)(2,1)} %q.1) | copy-start | bytes 393220
  26.4 4.3 %collective-permute-start.6 = (bf16[1792,128]{1,0:T(8,128)(2,1)S(1)}, bf16[1792,128]{1,0:T(8,128)(2,1)S(1)}, u32[]{:S(2)}, u32[]{:S(2)}) collective-permute-start(bf16[1792,128]{1,0:T(8,128)(2,1)S(1)} %collective-permute-done.5.part), channel_id=1, source_target_pairs={{0,8},{8,0},{16,24},{24,16},{32,40},{40,32},{48,56},{56,48},{64,72... | collective-permute-start | bytes 1376264 | tf_op jit(solution)/shard_map/ppermute | solution.py:28
  30.7 3.6 %copy-start = (bf16[1024,512]{1,0:T(8,128)(2,1)S(1)}, bf16[1024,512]{1,0:T(8,128)(2,1)}, u32[]{:S(2)}) copy-start(bf16[1024,512]{1,0:T(8,128)(2,1)} %wa.1) | copy-start | bytes 3145732
  34.2 2.7 %collective-permute-start.7 = (bf16[2304,128]{1,0:T(8,128)(2,1)S(1)}, bf16[2304,128]{1,0:T(8,128)(2,1)S(1)}, u32[]{:S(2)}, u32[]{:S(2)}) collective-permute-start(bf16[2304,128]{1,0:T(8,128)(2,1)S(1)} %collective-permute-done.4.part), channel_id=1, source_target_pairs={{0,8},{8,0},{16,24},{24,16},{32,40},{40,32},{48,56},{56,48},{64,72... | collective-permute-start | bytes 1769480 | tf_op jit(solution)/shard_map/ppermute | solution.py:28
  34.3 30.3 %collective-permute-start.18 = (bf16[1024,512]{1,0:T(8,128)(2,1)S(1)}, bf16[1024,512]{1,0:T(8,128)(2,1)S(1)}, u32[]{:S(2)}, u32[]{:S(2)}) collective-permute-start(bf16[1024,512]{1,0:T(8,128)(2,1)S(1)} %copy-done), channel_id=1, source_target_pairs={{0,8},{8,0},{16,24},{24,16},{32,40},{40,32},{48,56},{56,48},{64,72... | collective-permute-start | bytes 3145736 | tf_op jit(solution)/shard_map/ppermute | solution.py:28
  39.9 8.4 %collective-permute-start.8 = (bf16[144,512]{1,0:T(8,128)(2,1)S(1)}, bf16[144,512]{1,0:T(8,128)(2,1)S(1)}, u32[]{:S(2)}, u32[]{:S(2)}) collective-permute-start(bf16[144,512]{1,0:T(8,128)(2,1)S(1)} %get-tuple-element.68), channel_id=1, source_target_pairs={{0,32},{8,40},{16,48},{24,56},{32,0},{40,8},{48,16},{56,24},{64,96... | collective-permute-start | bytes 442376 | tf_op jit(solution)/shard_map/ppermute | solution.py:28
  44.4 6.8 %collective-permute-start.10 = (bf16[144,512]{1,0:T(8,128)(2,1)S(1)}, bf16[144,512]{1,0:T(8,128)(2,1)S(1)}, u32[]{:S(2)}, u32[]{:S(2)}) collective-permute-start(bf16[144,512]{1,0:T(8,128)(2,1)S(1)} %get-tuple-element.73), channel_id=1, source_target_pairs={{0,16},{8,24},{16,32},{24,40},{32,48},{40,56},{48,0},{56,8},{64,80... | collective-permute-start | bytes 442376 | tf_op jit(solution)/shard_map/ppermute | solution.py:28
  46.3 5.0 %collective-permute-start.9 = (bf16[144,512]{1,0:T(8,128)(2,1)S(1)}, bf16[144,512]{1,0:T(8,128)(2,1)S(1)}, u32[]{:S(2)}, u32[]{:S(2)}) collective-permute-start(bf16[144,512]{1,0:T(8,128)(2,1)S(1)} %get-tuple-element.72), channel_id=1, source_target_pairs={{0,48},{8,56},{16,0},{24,8},{32,16},{40,24},{48,32},{56,40},{64,11... | collective-permute-start | bytes 442376 | tf_op jit(solution)/shard_map/ppermute | solution.py:28
  51.5 5.9 %collective-permute-start.11 = (bf16[64,1024]{1,0:T(8,128)(2,1)S(1)}, bf16[64,1024]{1,0:T(8,128)(2,1)S(1)}, u32[]{:S(2)}, u32[]{:S(2)}) collective-permute-start(bf16[64,1024]{1,0:T(8,128)(2,1)S(1)} %shard_map.90.a0), channel_id=1, source_target_pairs={{0,32},{8,40},{16,48},{24,56},{32,0},{40,8},{48,16},{56,24},{64,96... | collective-permute-start | bytes 393224 | tf_op jit(solution)/shard_map/ppermute | solution.py:28
  53.7 5.7 %collective-permute-start.14 = (bf16[64,1024]{1,0:T(8,128)(2,1)S(1)}, bf16[64,1024]{1,0:T(8,128)(2,1)S(1)}, u32[]{:S(2)}, u32[]{:S(2)}) collective-permute-start(bf16[64,1024]{1,0:T(8,128)(2,1)S(1)} %shard_map.90.a0), channel_id=1, source_target_pairs={{0,64},{8,72},{16,80},{24,88},{32,96},{40,104},{48,112},{56,120},{... | collective-permute-start | bytes 393224 | tf_op jit(solution)/shard_map/ppermute | solution.py:28
  54.7 6.1 %collective-permute-start.12 = (bf16[64,1024]{1,0:T(8,128)(2,1)S(1)}, bf16[64,1024]{1,0:T(8,128)(2,1)S(1)}, u32[]{:S(2)}, u32[]{:S(2)}) collective-permute-start(bf16[64,1024]{1,0:T(8,128)(2,1)S(1)} %shard_map.90.a0), channel_id=1, source_target_pairs={{0,16},{8,24},{16,32},{24,40},{32,48},{40,56},{48,0},{56,8},{64,80... | collective-permute-start | bytes 393224 | tf_op jit(solution)/shard_map/ppermute | solution.py:28
  55.7 6.3 %collective-permute-start.13 = (bf16[64,1024]{1,0:T(8,128)(2,1)S(1)}, bf16[64,1024]{1,0:T(8,128)(2,1)S(1)}, u32[]{:S(2)}, u32[]{:S(2)}) collective-permute-start(bf16[64,1024]{1,0:T(8,128)(2,1)S(1)} %shard_map.90.a0), channel_id=1, source_target_pairs={{0,48},{8,56},{16,0},{24,8},{32,16},{40,24},{48,32},{56,40},{64,11... | collective-permute-start | bytes 393224 | tf_op jit(solution)/shard_map/ppermute | solution.py:28
  57.4 5.3 %collective-permute-start.15 = (bf16[64,1024]{1,0:T(8,128)(2,1)S(1)}, bf16[64,1024]{1,0:T(8,128)(2,1)S(1)}, u32[]{:S(2)}, u32[]{:S(2)}) collective-permute-start(bf16[64,1024]{1,0:T(8,128)(2,1)S(1)} %collective-permute-done.11.a1), channel_id=1, source_target_pairs={{0,64},{8,72},{16,80},{24,88},{32,96},{40,104},{48,112},{56,120},{... | collective-permute-start | bytes 393224 | tf_op jit(solution)/shard_map/ppermute | solution.py:28
  59.4 5.0 %collective-permute-start.16 = (bf16[64,1024]{1,0:T(8,128)(2,1)S(1)}, bf16[64,1024]{1,0:T(8,128)(2,1)S(1)}, u32[]{:S(2)}, u32[]{:S(2)}) collective-permute-start(bf16[64,1024]{1,0:T(8,128)(2,1)S(1)} %collective-permute-done.14.a4), channel_id=1, source_target_pairs={{0,16},{8,24},{16,32},{24,40},{32,48},{40,56},{48,0},{56,8},{64,80... | collective-permute-start | bytes 393224 | tf_op jit(solution)/shard_map/ppermute | solution.py:28
  60.8 3.8 %collective-permute-start.17 = (bf16[64,1024]{1,0:T(8,128)(2,1)S(1)}, bf16[64,1024]{1,0:T(8,128)(2,1)S(1)}, u32[]{:S(2)}, u32[]{:S(2)}) collective-permute-start(bf16[64,1024]{1,0:T(8,128)(2,1)S(1)} %collective-permute-done.14.a4), channel_id=1, source_target_pairs={{0,48},{8,56},{16,0},{24,8},{32,16},{40,24},{48,32},{56,40},{64,11... | collective-permute-start | bytes 393224 | tf_op jit(solution)/shard_map/ppermute | solution.py:28
  81.1 6.5 %collective-permute-start.19 = (bf16[64,512]{1,0:T(8,128)(2,1)S(1)}, bf16[64,512]{1,0:T(8,128)(2,1)S(1)}, u32[]{:S(2)}, u32[]{:S(2)}) collective-permute-start(bf16[64,512]{1,0:T(8,128)(2,1)S(1)} %get-tuple-element.80), channel_id=1, source_target_pairs={{0,8},{8,0},{16,24},{24,16},{32,40},{40,32},{48,56},{56,48},{64,72... | collective-permute-start | bytes 196616 | tf_op jit(solution)/shard_map/ppermute | solution.py:28

commit v16 on v14

--- a/solution.py
+++ b/solution.py
@@ -303,7 +303,7 @@
 
     att_x = moved(att, xh=1)
     held = [att] + [moved(att, z=z) for z in (2, 1, 3)]
-    held += [att_x, moved(held[1], xh=1)] + [moved(att_x, z=z) for z in (1, 3)]
+    held += [att_x, moved(held[1], xh=1), moved(att_x, z=1), moved(held[3], xh=1)]
     width = out_weight.shape[1]
     (terms,) = call(
         project_kernel,

time: 88.8 us -> 90.9 us (1.024)
  waiting for transfers between devices: 5.12 us -> 6.65 us
  blocking collectives: 14.8 us -> 16.1 us
    ppermute x20, waiting for transfers between devices: 5.12 us -> 6.65 us  [moved(): return lax.ppermute(array, 'blk', pairs)]
    all_to_all x1, blocking collectives: 14.8 us -> 16.1 us  [shards(): gathered = lax.all_to_all(terms, 'head', 0, 0, tiled=True)]
  transfers between devices with their start and end apart: 20 -> 20, of which waited for: 5 -> 6; matrix products, arithmetic and copies ran while one was open for 2% -> 2% of each run, Pallas kernels for 31% -> 30%
where the time goes in v16:
time: 90.9 us; the launch traced here: 90.6 us
  starting transfers between devices  33.1 us (36%)
  Pallas kernels  29.3 us (32%)
  blocking collectives  16.1 us (18%)
  waiting for transfers between devices  6.65 us (7%)
  local copies, waits for them, and re-layouts  2.99 us (3%)
  other arithmetic  1.54 us (2%)
    ppermute x20, starting transfers between devices, moved(): return lax.ppermute(array, 'blk', pairs)  33.1 us
    all_to_all x1, blocking collectives, shards(): gathered = lax.all_to_all(terms, 'head', 0, 0, tiled=True)  16.1 us
    pallas_call x1, Pallas kernels, shards(): call(near_kernel, state + [((4, LANES, DH), bf16)] + layout(positions), f...  7.68 us
    ppermute x20, waiting for transfers between devices, moved(): return lax.ppermute(array, 'blk', pairs)  6.65 us
    pallas_call x1, Pallas kernels, shards(): call(others_kernel, state + layout(2 * early), flops=1)  3.49 us
    unnamed x8, local copies, waits for them, and re-layouts  2.99 us
    pallas_call x1, Pallas kernels, shards(): call(next_kernel, [part] * 2, flops=4 * block_flops)  2.95 us
    pallas_call x1, Pallas kernels, shards(): call(far_kernel, [part] + layout(2 * late), flops=1)  2.92 us
  transfers between devices with their start and end apart: 20, of which 6 were waited for; matrix products, arithmetic and copies ran while one was open for 2% of the time, Pallas kernels for 30%

profile of v16, /device:TPU:1, one launch (start us, length us, event | category | flops | bytes accessed | tf_op | source)
XLA Modules:
  0.0 90.6 jit_solution(10668395855224663288)
XLA Ops:
  0.0 0.0 copy-start.2
  0.0 1.0 %copy-done.2 = bf16[2048,128]{1,0:T(8,128)(2,1)S(1)} copy-done((bf16[2048,128]{1,0:T(8,128)(2,1)S(1)}, bf16[2048,128]{1,0:T(8,128)(2,1)}, u32[]{:S(2)}) %copy-start.2) | copy-done | bytes 524312
  1.0 0.0 copy-start.3
  1.0 1.0 %copy-done.3 = bf16[2048,128]{1,0:T(8,128)(2,1)S(1)} copy-done((bf16[2048,128]{1,0:T(8,128)(2,1)S(1)}, bf16[2048,128]{1,0:T(8,128)(2,1)}, u32[]{:S(2)}) %copy-start.3) | copy-done | bytes 524312
  2.1 0.1 shard_map.82
  2.2 1.5 %collective-permute-start.3 = (bf16[4096,128]{1,0:T(8,128)(2,1)S(1)}, bf16[4096,128]{1,0:T(8,128)(2,1)S(1)}, u32[]{:S(2)}, u32[]{:S(2)}) collective-permute-start(bf16[4096,128]{1,0:T(8,128)(2,1)S(1)} %get-tuple-element.47.kv), channel_id=1, source_target_pairs={{0,8},{8,0},{16,24},{24,16},{32,40},{40,32},{48,56},{56,48},{64,72... | collective-permute-start | bytes 3145736 | tf_op jit(solution)/shard_map/ppermute | solution.py:28
  3.7 1.7 %collective-permute-start = (bf16[64,1024]{1,0:T(8,128)(2,1)}, bf16[64,1024]{1,0:T(8,128)(2,1)S(1)}, u32[]{:S(2)}, u32[]{:S(2)}) collective-permute-start(bf16[64,1024]{1,0:T(8,128)(2,1)} %q.3), channel_id=1, source_target_pairs={{0,16},{8,24},{16,32},{24,40},{32,48},{40,56},{48,0},{56,8},{64,80... | collective-permute-start | bytes 393224 | tf_op jit(solution)/shard_map/ppermute | solution.py:28
  5.5 2.7 %collective-permute-start.5 = (bf16[1792,128]{1,0:T(8,128)(2,1)S(1)}, bf16[1792,128]{1,0:T(8,128)(2,1)S(1)}, u32[]{:S(2)}, u32[]{:S(2)}) collective-permute-start(bf16[1792,128]{1,0:T(8,128)(2,1)S(1)} %get-tuple-element.52), channel_id=1, source_target_pairs={{0,64},{8,72},{16,80},{24,88},{32,96},{40,104},{48,112},{56,120},{... | collective-permute-start | bytes 1376264 | tf_op jit(solution)/shard_map/ppermute | solution.py:28
  8.2 2.1 %collective-permute-start.1 = (bf16[64,1024]{1,0:T(8,128)(2,1)}, bf16[64,1024]{1,0:T(8,128)(2,1)S(1)}, u32[]{:S(2)}, u32[]{:S(2)}) collective-permute-start(bf16[64,1024]{1,0:T(8,128)(2,1)} %q.3), channel_id=1, source_target_pairs={{0,48},{8,56},{16,0},{24,8},{32,16},{40,24},{48,32},{56,40},{64,11... | collective-permute-start | bytes 393224 | tf_op jit(solution)/shard_map/ppermute | solution.py:28
  10.3 1.3 %collective-permute-start.2 = (bf16[64,1024]{1,0:T(8,128)(2,1)}, bf16[64,1024]{1,0:T(8,128)(2,1)S(1)}, u32[]{:S(2)}, u32[]{:S(2)}) collective-permute-start(bf16[64,1024]{1,0:T(8,128)(2,1)} %q.3), channel_id=1, source_target_pairs={{0,32},{8,40},{16,48},{24,56},{32,0},{40,8},{48,16},{56,24},{64,96... | collective-permute-start | bytes 393224 | tf_op jit(solution)/shard_map/ppermute | solution.py:28
  11.6 0.0 collective-permute-done.q0
  11.6 2.7 %collective-permute-start.4 = (bf16[2304,128]{1,0:T(8,128)(2,1)S(1)}, bf16[2304,128]{1,0:T(8,128)(2,1)S(1)}, u32[]{:S(2)}, u32[]{:S(2)}) collective-permute-start(bf16[2304,128]{1,0:T(8,128)(2,1)S(1)} %get-tuple-element.51), channel_id=1, source_target_pairs={{0,64},{8,72},{16,80},{24,88},{32,96},{40,104},{48,112},{56,120},{... | collective-permute-start | bytes 1769480 | tf_op jit(solution)/shard_map/ppermute | solution.py:28
  14.3 0.8 fusion.1.bias
  15.1 0.7 pad_maximum_fusion.qkv
  15.9 0.0 copy-start.1
  15.9 0.9 copy-done.1
  16.8 2.6 %shard_map.83 = (f32[512,128]{1,0:T(8,128)S(1)}, f32[512,256]{1,0:T(8,128)S(1)}, bf16[2048,128]{1,0:T(8,128)(2,1)S(1)}, bf16[2048,256]{1,0:T(8,128)(2,1)S(1)}) custom-call(bf16[64,1024]{1,0:T(8,128)(2,1)S(1)} %copy-done.1, bf16[128,128]{1,0:T(8,128)(2,1)S(1)} %pad_maximum_fusion.qkv, f32[64,64]{1,0:T(8,128)S(1)} %fusion.1.bias, ...), custom_call_target="tpu_custom_call" | custom-call | tf_op jit(solution)/shard_map/pallas_call | solution.py:269
  19.3 0.0 collective-permute-done.1.q1
  19.4 0.0 collective-permute-done.2.q2
  19.4 0.0 collective-permute-done.3.kv_c
  19.4 7.7 %shard_map.84 = (f32[3,512,128]{2,1,0:T(8,128)S(1)}, f32[3,512,256]{2,1,0:T(8,128)S(1)}, bf16[4,512,128]{2,1,0:T(8,128)(2,1)S(1)}, bf16[2048,128]{1,0:T(8,128)(2,1)S(1)}, bf16[2048,256]{1,0:T(8,128)(2,1)S(1)}) custom-call(bf16[64,1024]{1,0:T(8,128)(2,1)S(1)} %collective-permute-done.q0, bf16[64,1024]{1,0:T(8,128)(2,1)S(1)} %collective-permute-done.1.q1, ...), custom_call_target="tpu_custom_call" | custom-call | flops 1 | tf_op jit(solution)/shard_map/pallas_call | solution.py:272
  27.1 0.0 collective-permute-done.5.part
  27.1 1.2 %collective-permute-start.6 = (bf16[1792,128]{1,0:T(8,128)(2,1)S(1)}, bf16[1792,128]{1,0:T(8,128)(2,1)S(1)}, u32[]{:S(2)}, u32[]{:S(2)}) collective-permute-start(bf16[1792,128]{1,0:T(8,128)(2,1)S(1)} %collective-permute-done.5.part), channel_id=1, source_target_pairs={{0,8},{8,0},{16,24},{24,16},{32,40},{40,32},{48,56},{56,48},{64,72... | collective-permute-start | bytes 1376264 | tf_op jit(solution)/shard_map/ppermute | solution.py:28
  28.3 2.4 %shard_map.85 = (f32[512,128]{1,0:T(8,128)S(1)}, f32[512,256]{1,0:T(8,128)S(1)}) custom-call(bf16[4,512,128]{2,1,0:T(8,128)(2,1)S(1)} %get-tuple-element.80.rows, f32[512,128]{1,0:T(8,128)S(1)} %get-tuple-element.57.top, f32[512,256]{1,0:T(8,128)S(1)} %get-tuple-element.58.total, bf16[2048,128]{1,0:T(8,128)(2,1)S(1)} %get-tuple-element.59.k, ...), custom_call_target="tpu_custom_call" | custom-call | flops 1073741824 | tf_op jit(solution)/shard_map/pallas_call | solution.py:277
  30.7 0.0 collective-permute-done.6.other_part
  30.7 0.0 copy-start
  30.7 3.5 %shard_map.86 = (f32[3,512,128]{2,1,0:T(8,128)S(1)}, f32[3,512,256]{2,1,0:T(8,128)S(1)}, bf16[1792,128]{1,0:T(8,128)(2,1)S(1)}, bf16[1792,256]{1,0:T(8,128)(2,1)S(1)}) custom-call(bf16[4,512,128]{2,1,0:T(8,128)(2,1)S(1)} %get-tuple-element.80.rows, f32[3,512,128]{2,1,0:T(8,128)S(1)} %get-tuple-element.62.top_in, ...), custom_call_target="tpu_custom_call" | custom-call | flops 1 | tf_op jit(solution)/shard_map/pallas_call | solution.py:280
  34.2 0.0 collective-permute-done.4.part
  34.2 0.1 collective-permute-start.7
  34.3 0.0 copy-done
  34.3 0.5 collective-permute-start.18
  34.8 2.1 %shard_map.87 = (f32[512,128]{1,0:T(8,128)S(1)}, f32[512,256]{1,0:T(8,128)S(1)}) custom-call(bf16[4,512,128]{2,1,0:T(8,128)(2,1)S(1)} %get-tuple-element.80.rows, f32[512,128]{1,0:T(8,128)S(1)} %get-tuple-element.61.top, f32[512,256]{1,0:T(8,128)S(1)} %get-tuple-element.68.total, bf16[1792,128]{1,0:T(8,128)(2,1)S(1)} %get-tuple-element.69.k, ...), custom_call_target="tpu_custom_call" | custom-call | flops 2147483648 | tf_op jit(solution)/shard_map/pallas_call | solution.py:287
  36.9 0.0 collective-permute-done.7.other_part
  36.9 2.9 %shard_map.88 = (bf16[144,512]{1,0:T(8,128)(2,1)S(1)}, bf16[2304,128]{1,0:T(8,128)(2,1)S(1)}, bf16[2304,256]{1,0:T(8,128)(2,1)S(1)}) custom-call(bf16[4,512,128]{2,1,0:T(8,128)(2,1)S(1)} %get-tuple-element.80.rows, f32[3,512,128]{2,1,0:T(8,128)S(1)} %get-tuple-element.75.top, f32[3,512,256]{2,1,0:T(8,128)S(1)} %get-tuple-element.73.total, ...), custom_call_target="tpu_custom_call" | custom-call | flops 1 | tf_op jit(solution)/shard_map/pallas_call | solution.py:290
  39.9 1.6 %collective-permute-start.8 = (bf16[144,512]{1,0:T(8,128)(2,1)S(1)}, bf16[144,512]{1,0:T(8,128)(2,1)S(1)}, u32[]{:S(2)}, u32[]{:S(2)}) collective-permute-start(bf16[144,512]{1,0:T(8,128)(2,1)S(1)} %get-tuple-element.74), channel_id=1, source_target_pairs={{0,32},{8,40},{16,48},{24,56},{32,0},{40,8},{48,16},{56,24},{64,96... | collective-permute-start | bytes 442376 | tf_op jit(solution)/shard_map/ppermute | solution.py:28
  41.5 2.9 %shard_map.89 = (bf16[144,512]{1,0:T(8,128)(2,1)S(1)}, bf16[144,512]{1,0:T(8,128)(2,1)S(1)}) custom-call(bf16[4,512,128]{2,1,0:T(8,128)(2,1)S(1)} %get-tuple-element.80.rows, f32[3,512,128]{2,1,0:T(8,128)S(1)} %get-tuple-element.75.top, f32[3,512,256]{2,1,0:T(8,128)S(1)} %get-tuple-element.73.total, bf16[2304,128]{1,0:T(8,128)(2,1)S(1)} %get-tuple-element.76.k, ...), custom_call_target="tpu_custom_call" | custom-call | flops 4294967296 | tf_op jit(solution)/shard_map/pallas_call | solution.py:293
  44.4 1.3 %collective-permute-start.10 = (bf16[144,512]{1,0:T(8,128)(2,1)S(1)}, bf16[144,512]{1,0:T(8,128)(2,1)S(1)}, u32[]{:S(2)}, u32[]{:S(2)}) collective-permute-start(bf16[144,512]{1,0:T(8,128)(2,1)S(1)} %get-tuple-element.79), channel_id=1, source_target_pairs={{0,16},{8,24},{16,32},{24,40},{32,48},{40,56},{48,0},{56,8},{64,80... | collective-permute-start | bytes 442376 | tf_op jit(solution)/shard_map/ppermute | solution.py:28
  45.7 1.5 %collective-permute-start.9 = (bf16[144,512]{1,0:T(8,128)(2,1)S(1)}, bf16[144,512]{1,0:T(8,128)(2,1)S(1)}, u32[]{:S(2)}, u32[]{:S(2)}) collective-permute-start(bf16[144,512]{1,0:T(8,128)(2,1)S(1)} %get-tuple-element.78), channel_id=1, source_target_pairs={{0,48},{8,56},{16,0},{24,8},{32,16},{40,24},{48,32},{56,40},{64,11... | collective-permute-start | bytes 442376 | tf_op jit(solution)/shard_map/ppermute | solution.py:28
  47.8 0.0 collective-permute-done.8.r2
  47.8 2.8 %shard_map.90 = (f32[128,512]{1,0:T(8,128)S(1)}, f32[8,512]{1,0:T(8,128)S(1)}) custom-call(bf16[4,512,128]{2,1,0:T(8,128)(2,1)S(1)} %get-tuple-element.80.rows, f32[512,128]{1,0:T(8,128)S(1)} %get-tuple-element.71.top, f32[512,256]{1,0:T(8,128)S(1)} %get-tuple-element.81.total, bf16[2304,128]{1,0:T(8,128)(2,1)S(1)} %get-tuple-element.76.k, ...), custom_call_target="tpu_custom_call" | custom-call | flops 1 | tf_op jit(solution)/shard_map/pallas_call | solution.py:297
  50.6 0.0 collective-permute-done.10.r1
  50.6 0.0 collective-permute-done.9.r0
  50.6 0.2 shard_map.91.a0
  50.8 1.2 %collective-permute-start.11 = (bf16[64,1024]{1,0:T(8,128)(2,1)S(1)}, bf16[64,1024]{1,0:T(8,128)(2,1)S(1)}, u32[]{:S(2)}, u32[]{:S(2)}) collective-permute-start(bf16[64,1024]{1,0:T(8,128)(2,1)S(1)} %shard_map.91.a0), channel_id=1, source_target_pairs={{0,32},{8,40},{16,48},{24,56},{32,0},{40,8},{48,16},{56,24},{64,96... | collective-permute-start | bytes 393224 | tf_op jit(solution)/shard_map/ppermute | solution.py:28
  52.0 2.6 %collective-permute-start.14 = (bf16[64,1024]{1,0:T(8,128)(2,1)S(1)}, bf16[64,1024]{1,0:T(8,128)(2,1)S(1)}, u32[]{:S(2)}, u32[]{:S(2)}) collective-permute-start(bf16[64,1024]{1,0:T(8,128)(2,1)S(1)} %shard_map.91.a0), channel_id=1, source_target_pairs={{0,64},{8,72},{16,80},{24,88},{32,96},{40,104},{48,112},{56,120},{... | collective-permute-start | bytes 393224 | tf_op jit(solution)/shard_map/ppermute | solution.py:28
  54.7 0.6 collective-permute-start.13
  55.2 0.9 %collective-permute-start.12 = (bf16[64,1024]{1,0:T(8,128)(2,1)S(1)}, bf16[64,1024]{1,0:T(8,128)(2,1)S(1)}, u32[]{:S(2)}, u32[]{:S(2)}) collective-permute-start(bf16[64,1024]{1,0:T(8,128)(2,1)S(1)} %shard_map.91.a0), channel_id=1, source_target_pairs={{0,16},{8,24},{16,32},{24,40},{32,48},{40,56},{48,0},{56,8},{64,80... | collective-permute-start | bytes 393224 | tf_op jit(solution)/shard_map/ppermute | solution.py:28
  56.1 0.1 collective-permute-done.11.a1
  56.2 2.5 %collective-permute-start.15 = (bf16[64,1024]{1,0:T(8,128)(2,1)S(1)}, bf16[64,1024]{1,0:T(8,128)(2,1)S(1)}, u32[]{:S(2)}, u32[]{:S(2)}) collective-permute-start(bf16[64,1024]{1,0:T(8,128)(2,1)S(1)} %collective-permute-done.11.a1), channel_id=1, source_target_pairs={{0,64},{8,72},{16,80},{24,88},{32,96},{40,104},{48,112},{56,120},{... | collective-permute-start | bytes 393224 | tf_op jit(solution)/shard_map/ppermute | solution.py:28
  58.7 0.0 collective-permute-done.14.a4
  58.7 0.4 collective-permute-start.16
  59.1 0.7 collective-permute-done.13.a3
  59.8 1.5 %collective-permute-start.17 = (bf16[64,1024]{1,0:T(8,128)(2,1)S(1)}, bf16[64,1024]{1,0:T(8,128)(2,1)S(1)}, u32[]{:S(2)}, u32[]{:S(2)}) collective-permute-start(bf16[64,1024]{1,0:T(8,128)(2,1)S(1)} %collective-permute-done.13.a3), channel_id=1, source_target_pairs={{0,64},{8,72},{16,80},{24,88},{32,96},{40,104},{48,112},{56,120},{... | collective-permute-start | bytes 393224 | tf_op jit(solution)/shard_map/ppermute | solution.py:28
  61.3 0.0 collective-permute-done.12.a2
  61.3 0.2 collective-permute-done.15.a5
  61.6 3.7 %collective-permute-done.16.a6 = bf16[64,1024]{1,0:T(8,128)(2,1)S(1)} collective-permute-done((bf16[64,1024]{1,0:T(8,128)(2,1)S(1)}, bf16[64,1024]{1,0:T(8,128)(2,1)S(1)}, u32[]{:S(2)}, u32[]{:S(2)}) %collective-permute-start.16) | collective-permute-done | bytes 131104 | tf_op jit(solution)/shard_map/ppermute | solution.py:28
  65.2 1.0 %collective-permute-done.17.a7 = bf16[64,1024]{1,0:T(8,128)(2,1)S(1)} collective-permute-done((bf16[64,1024]{1,0:T(8,128)(2,1)S(1)}, bf16[64,1024]{1,0:T(8,128)(2,1)S(1)}, u32[]{:S(2)}, u32[]{:S(2)}) %collective-permute-start.17) | collective-permute-done | bytes 131104 | tf_op jit(solution)/shard_map/ppermute | solution.py:28
  66.3 0.0 collective-permute-done.18.wb
  66.3 1.2 %shard_map.92 = bf16[8,64,1024]{2,1,0:T(8,128)(2,1)S(1)} custom-call(s32[1]{0:T(128)} %bitcast.1.index, bf16[64,1024]{1,0:T(8,128)(2,1)S(1)} %shard_map.91.a0, bf16[64,1024]{1,0:T(8,128)(2,1)S(1)} %collective-permute-done.11.a1, bf16[64,1024]{1,0:T(8,128)(2,1)S(1)} %collective-permute-done.12.a2, bf16[64,1024]{1,0:T(8,128)(2,1)S(1)} %collective-permute-done.13.a3, ...), custom_call_target="tpu_custom_call" | custom-call | tf_op jit(solution)/shard_map/pallas_call | solution.py:308
  67.5 16.1 %all_to_all.5.terms = bf16[8,64,1024]{2,1,0:T(8,128)(2,1)S(1)} all-to-all(bf16[8,64,1024]{2,1,0:T(8,128)(2,1)S(1)} %shard_map.92), channel_id=1, replica_groups=mesh['blk'=16,'head'=8] {'head'}, dimensions={0} | all-to-all | bytes 2097152 | tf_op jit(solution)/shard_map/all_to_all | solution.py:314
  83.7 0.1 shard_map.93
  83.8 5.2 %collective-permute-start.19 = (bf16[64,512]{1,0:T(8,128)(2,1)S(1)}, bf16[64,512]{1,0:T(8,128)(2,1)S(1)}, u32[]{:S(2)}, u32[]{:S(2)}) collective-permute-start(bf16[64,512]{1,0:T(8,128)(2,1)S(1)} %get-tuple-element.86), channel_id=1, source_target_pairs={{0,8},{8,0},{16,24},{24,16},{32,40},{40,32},{48,56},{56,48},{64,72... | collective-permute-start | bytes 196616 | tf_op jit(solution)/shard_map/ppermute | solution.py:28
  89.0 0.9 collective-permute-done.19.theirs
  89.9 0.7 shard_map.94
Async XLA Ops:
  0.0 1.0 %copy-start.2 = (bf16[2048,128]{1,0:T(8,128)(2,1)S(1)}, bf16[2048,128]{1,0:T(8,128)(2,1)}, u32[]{:S(2)}) copy-start(bf16[2048,128]{1,0:T(8,128)(2,1)} %k.1) | copy-start | bytes 1572868
  1.0 1.0 %copy-start.3 = (bf16[2048,128]{1,0:T(8,128)(2,1)S(1)}, bf16[2048,128]{1,0:T(8,128)(2,1)}, u32[]{:S(2)}) copy-start(bf16[2048,128]{1,0:T(8,128)(2,1)} %v.1) | copy-start | bytes 1572868
  2.2 17.1 %collective-permute-start.3 = (bf16[4096,128]{1,0:T(8,128)(2,1)S(1)}, bf16[4096,128]{1,0:T(8,128)(2,1)S(1)}, u32[]{:S(2)}, u32[]{:S(2)}) collective-permute-start(bf16[4096,128]{1,0:T(8,128)(2,1)S(1)} %get-tuple-element.47.kv), channel_id=1, source_target_pairs={{0,8},{8,0},{16,24},{24,16},{32,40},{40,32},{48,56},{56,48},{64,72... | collective-permute-start | bytes 3145736 | tf_op jit(solution)/shard_map/ppermute | solution.py:28
  3.7 7.9 %collective-permute-start = (bf16[64,1024]{1,0:T(8,128)(2,1)}, bf16[64,1024]{1,0:T(8,128)(2,1)S(1)}, u32[]{:S(2)}, u32[]{:S(2)}) collective-permute-start(bf16[64,1024]{1,0:T(8,128)(2,1)} %q.3), channel_id=1, source_target_pairs={{0,16},{8,24},{16,32},{24,40},{32,48},{40,56},{48,0},{56,8},{64,80... | collective-permute-start | bytes 393224 | tf_op jit(solution)/shard_map/ppermute | solution.py:28
  5.5 21.6 %collective-permute-start.5 = (bf16[1792,128]{1,0:T(8,128)(2,1)S(1)}, bf16[1792,128]{1,0:T(8,128)(2,1)S(1)}, u32[]{:S(2)}, u32[]{:S(2)}) collective-permute-start(bf16[1792,128]{1,0:T(8,128)(2,1)S(1)} %get-tuple-element.52), channel_id=1, source_target_pairs={{0,64},{8,72},{16,80},{24,88},{32,96},{40,104},{48,112},{56,120},{... | collective-permute-start | bytes 1376264 | tf_op jit(solution)/shard_map/ppermute | solution.py:28
  8.2 11.1 %collective-permute-start.1 = (bf16[64,1024]{1,0:T(8,128)(2,1)}, bf16[64,1024]{1,0:T(8,128)(2,1)S(1)}, u32[]{:S(2)}, u32[]{:S(2)}) collective-permute-start(bf16[64,1024]{1,0:T(8,128)(2,1)} %q.3), channel_id=1, source_target_pairs={{0,48},{8,56},{16,0},{24,8},{32,16},{40,24},{48,32},{56,40},{64,11... | collective-permute-start | bytes 393224 | tf_op jit(solution)/shard_map/ppermute | solution.py:28
  10.3 9.0 %collective-permute-start.2 = (bf16[64,1024]{1,0:T(8,128)(2,1)}, bf16[64,1024]{1,0:T(8,128)(2,1)S(1)}, u32[]{:S(2)}, u32[]{:S(2)}) collective-permute-start(bf16[64,1024]{1,0:T(8,128)(2,1)} %q.3), channel_id=1, source_target_pairs={{0,32},{8,40},{16,48},{24,56},{32,0},{40,8},{48,16},{56,24},{64,96... | collective-permute-start | bytes 393224 | tf_op jit(solution)/shard_map/ppermute | solution.py:28
  11.6 22.6 %collective-permute-start.4 = (bf16[2304,128]{1,0:T(8,128)(2,1)S(1)}, bf16[2304,128]{1,0:T(8,128)(2,1)S(1)}, u32[]{:S(2)}, u32[]{:S(2)}) collective-permute-start(bf16[2304,128]{1,0:T(8,128)(2,1)S(1)} %get-tuple-element.51), channel_id=1, source_target_pairs={{0,64},{8,72},{16,80},{24,88},{32,96},{40,104},{48,112},{56,120},{... | collective-permute-start | bytes 1769480 | tf_op jit(solution)/shard_map/ppermute | solution.py:28
  15.9 0.9 copy-start.1
  27.1 3.6 %collective-permute-start.6 = (bf16[1792,128]{1,0:T(8,128)(2,1)S(1)}, bf16[1792,128]{1,0:T(8,128)(2,1)S(1)}, u32[]{:S(2)}, u32[]{:S(2)}) collective-permute-start(bf16[1792,128]{1,0:T(8,128)(2,1)S(1)} %collective-permute-done.5.part), channel_id=1, source_target_pairs={{0,8},{8,0},{16,24},{24,16},{32,40},{40,32},{48,56},{56,48},{64,72... | collective-permute-start | bytes 1376264 | tf_op jit(solution)/shard_map/ppermute | solution.py:28
  30.7 3.6 %copy-start = (bf16[1024,512]{1,0:T(8,128)(2,1)S(1)}, bf16[1024,512]{1,0:T(8,128)(2,1)}, u32[]{:S(2)}) copy-start(bf16[1024,512]{1,0:T(8,128)(2,1)} %wa.1) | copy-start | bytes 3145732
  34.2 2.7 %collective-permute-start.7 = (bf16[2304,128]{1,0:T(8,128)(2,1)S(1)}, bf16[2304,128]{1,0:T(8,128)(2,1)S(1)}, u32[]{:S(2)}, u32[]{:S(2)}) collective-permute-start(bf16[2304,128]{1,0:T(8,128)(2,1)S(1)} %collective-permute-done.4.part), channel_id=1, source_target_pairs={{0,8},{8,0},{16,24},{24,16},{32,40},{40,32},{48,56},{56,48},{64,72... | collective-permute-start | bytes 1769480 | tf_op jit(solution)/shard_map/ppermute | solution.py:28
  34.3 32.0 %collective-permute-start.18 = (bf16[1024,512]{1,0:T(8,128)(2,1)S(1)}, bf16[1024,512]{1,0:T(8,128)(2,1)S(1)}, u32[]{:S(2)}, u32[]{:S(2)}) collective-permute-start(bf16[1024,512]{1,0:T(8,128)(2,1)S(1)} %copy-done), channel_id=1, source_target_pairs={{0,8},{8,0},{16,24},{24,16},{32,40},{40,32},{48,56},{56,48},{64,72... | collective-permute-start | bytes 3145736 | tf_op jit(solution)/shard_map/ppermute | solution.py:28
  39.9 8.0 %collective-permute-start.8 = (bf16[144,512]{1,0:T(8,128)(2,1)S(1)}, bf16[144,512]{1,0:T(8,128)(2,1)S(1)}, u32[]{:S(2)}, u32[]{:S(2)}) collective-permute-start(bf16[144,512]{1,0:T(8,128)(2,1)S(1)} %get-tuple-element.74), channel_id=1, source_target_pairs={{0,32},{8,40},{16,48},{24,56},{32,0},{40,8},{48,16},{56,24},{64,96... | collective-permute-start | bytes 442376 | tf_op jit(solution)/shard_map/ppermute | solution.py:28
  44.4 6.2 %collective-permute-start.10 = (bf16[144,512]{1,0:T(8,128)(2,1)S(1)}, bf16[144,512]{1,0:T(8,128)(2,1)S(1)}, u32[]{:S(2)}, u32[]{:S(2)}) collective-permute-start(bf16[144,512]{1,0:T(8,128)(2,1)S(1)} %get-tuple-element.79), channel_id=1, source_target_pairs={{0,16},{8,24},{16,32},{24,40},{32,48},{40,56},{48,0},{56,8},{64,80... | collective-permute-start | bytes 442376 | tf_op jit(solution)/shard_map/ppermute | solution.py:28
  45.7 4.9 %collective-permute-start.9 = (bf16[144,512]{1,0:T(8,128)(2,1)S(1)}, bf16[144,512]{1,0:T(8,128)(2,1)S(1)}, u32[]{:S(2)}, u32[]{:S(2)}) collective-permute-start(bf16[144,512]{1,0:T(8,128)(2,1)S(1)} %get-tuple-element.78), channel_id=1, source_target_pairs={{0,48},{8,56},{16,0},{24,8},{32,16},{40,24},{48,32},{56,40},{64,11... | collective-permute-start | bytes 442376 | tf_op jit(solution)/shard_map/ppermute | solution.py:28
  50.8 5.4 %collective-permute-start.11 = (bf16[64,1024]{1,0:T(8,128)(2,1)S(1)}, bf16[64,1024]{1,0:T(8,128)(2,1)S(1)}, u32[]{:S(2)}, u32[]{:S(2)}) collective-permute-start(bf16[64,1024]{1,0:T(8,128)(2,1)S(1)} %shard_map.91.a0), channel_id=1, source_target_pairs={{0,32},{8,40},{16,48},{24,56},{32,0},{40,8},{48,16},{56,24},{64,96... | collective-permute-start | bytes 393224 | tf_op jit(solution)/shard_map/ppermute | solution.py:28
  52.0 6.7 %collective-permute-start.14 = (bf16[64,1024]{1,0:T(8,128)(2,1)S(1)}, bf16[64,1024]{1,0:T(8,128)(2,1)S(1)}, u32[]{:S(2)}, u32[]{:S(2)}) collective-permute-start(bf16[64,1024]{1,0:T(8,128)(2,1)S(1)} %shard_map.91.a0), channel_id=1, source_target_pairs={{0,64},{8,72},{16,80},{24,88},{32,96},{40,104},{48,112},{56,120},{... | collective-permute-start | bytes 393224 | tf_op jit(solution)/shard_map/ppermute | solution.py:28
  54.7 5.1 %collective-permute-start.13 = (bf16[64,1024]{1,0:T(8,128)(2,1)S(1)}, bf16[64,1024]{1,0:T(8,128)(2,1)S(1)}, u32[]{:S(2)}, u32[]{:S(2)}) collective-permute-start(bf16[64,1024]{1,0:T(8,128)(2,1)S(1)} %shard_map.91.a0), channel_id=1, source_target_pairs={{0,48},{8,56},{16,0},{24,8},{32,16},{40,24},{48,32},{56,40},{64,11... | collective-permute-start | bytes 393224 | tf_op jit(solution)/shard_map/ppermute | solution.py:28
  55.2 6.1 %collective-permute-start.12 = (bf16[64,1024]{1,0:T(8,128)(2,1)S(1)}, bf16[64,1024]{1,0:T(8,128)(2,1)S(1)}, u32[]{:S(2)}, u32[]{:S(2)}) collective-permute-start(bf16[64,1024]{1,0:T(8,128)(2,1)S(1)} %shard_map.91.a0), channel_id=1, source_target_pairs={{0,16},{8,24},{16,32},{24,40},{32,48},{40,56},{48,0},{56,8},{64,80... | collective-permute-start | bytes 393224 | tf_op jit(solution)/shard_map/ppermute | solution.py:28
  56.2 5.3 %collective-permute-start.15 = (bf16[64,1024]{1,0:T(8,128)(2,1)S(1)}, bf16[64,1024]{1,0:T(8,128)(2,1)S(1)}, u32[]{:S(2)}, u32[]{:S(2)}) collective-permute-start(bf16[64,1024]{1,0:T(8,128)(2,1)S(1)} %collective-permute-done.11.a1), channel_id=1, source_target_pairs={{0,64},{8,72},{16,80},{24,88},{32,96},{40,104},{48,112},{56,120},{... | collective-permute-start | bytes 393224 | tf_op jit(solution)/shard_map/ppermute | solution.py:28
  58.7 6.5 %collective-permute-start.16 = (bf16[64,1024]{1,0:T(8,128)(2,1)S(1)}, bf16[64,1024]{1,0:T(8,128)(2,1)S(1)}, u32[]{:S(2)}, u32[]{:S(2)}) collective-permute-start(bf16[64,1024]{1,0:T(8,128)(2,1)S(1)} %collective-permute-done.14.a4), channel_id=1, source_target_pairs={{0,16},{8,24},{16,32},{24,40},{32,48},{40,56},{48,0},{56,8},{64,80... | collective-permute-start | bytes 393224 | tf_op jit(solution)/shard_map/ppermute | solution.py:28
  59.8 6.5 %collective-permute-start.17 = (bf16[64,1024]{1,0:T(8,128)(2,1)S(1)}, bf16[64,1024]{1,0:T(8,128)(2,1)S(1)}, u32[]{:S(2)}, u32[]{:S(2)}) collective-permute-start(bf16[64,1024]{1,0:T(8,128)(2,1)S(1)} %collective-permute-done.13.a3), channel_id=1, source_target_pairs={{0,64},{8,72},{16,80},{24,88},{32,96},{40,104},{48,112},{56,120},{... | collective-permute-start | bytes 393224 | tf_op jit(solution)/shard_map/ppermute | solution.py:28
  83.8 6.1 %collective-permute-start.19 = (bf16[64,512]{1,0:T(8,128)(2,1)S(1)}, bf16[64,512]{1,0:T(8,128)(2,1)S(1)}, u32[]{:S(2)}, u32[]{:S(2)}) collective-permute-start(bf16[64,512]{1,0:T(8,128)(2,1)S(1)} %get-tuple-element.86), channel_id=1, source_target_pairs={{0,8},{8,0},{16,24},{24,16},{32,40},{40,32},{48,56},{56,48},{64,72... | collective-permute-start | bytes 196616 | tf_op jit(solution)/shard_map/ppermute | solution.py:28
